TPU v7x, 32 devices: a whole 2x2x4 slice. The times are simulated.
32 devices in a mesh: seq: 16 (over z, y, x), chan: 2 (over core).
Axes of the slice: x: 2, y: 2, z: 4, core: 2. Of those that a mesh axis runs over, the one named last changes fastest.
Arguments:
- values: bfloat16 [4096, 4096], P('seq', 'chan'), may hold values from -6 to 6
- gates: bfloat16 [4096, 4096], P('seq', 'chan'), may hold values from -144 to 144
- filter_taps: bfloat16 [4096, 4096], P('seq', 'chan'), may hold values from -0.0625 to 0.0625, as said below
- skip_gain: float32 [4096], P('chan'), may hold values from -0.125 to 0.125
- out_weight: bfloat16 [4096, 2048], P('chan'), may hold values from -0.09375 to 0.09375
Outputs:
- projected: bfloat16 [2048, 4096], P('chan', 'seq')
Inputs may be any that keep to these rules, and one draw needn't show every extreme that they name: `filter_taps`: a causal filter for each channel.
All inputs are finite; a program needn't handle non-finite values.
Results may differ from a plain program's by a relative error of at most 0.0049.
Values may be sent and summed in bfloat16 or wider, within the bound.
No kernel may reach another device: no remote copies, remote signals or barrier semaphores. Data moves between devices by JAX's collectives and lax.ppermute only.
A program may use at most 128 MiB of HBM per device.

v0:
```python
import functools
import math

import jax
import jax.numpy as jnp
import ml_dtypes
import numpy as np
from jax import lax
from jax.experimental import pallas as pl
from jax.experimental.pallas import tpu as pltpu
from jax.sharding import PartitionSpec as P

TWO_PI = 2.0 * math.pi
HIGH = lax.Precision.HIGHEST
RADIX = 16
LANES = 128
VMEM_BYTES = 56 * 1024 * 1024


def angle_table(first, second, period):
    product = first[:, None] * second[None, :] % period
    angles = product.astype(jnp.float32) * (TWO_PI / period)
    return (jnp.cos(angles), jnp.sin(angles))


def mix(equation, left, right):
    return jnp.einsum(equation, left, right, precision=HIGH)


def outer_forward(data, outer_cos, outer_sin, twist_cos, twist_sin, equation):
    source = data.astype(jnp.float32)
    real = mix(equation, outer_cos, source)
    imag = -mix(equation, outer_sin, source)
    cos_part = twist_cos[:, :, None]
    sin_part = twist_sin[:, :, None]
    return (real * cos_part + imag * sin_part, imag * cos_part - real * sin_part)


def inner_filter(spectra, inner_cos, inner_sin):
    value_re, value_im, taps_re, taps_im = spectra

    def forward(real, imag):
        out_re = mix("kr,jrc->jkc", inner_cos, real) + mix("kr,jrc->jkc", inner_sin, imag)
        out_im = mix("kr,jrc->jkc", inner_cos, imag) - mix("kr,jrc->jkc", inner_sin, real)
        return (out_re, out_im)

    value_fre, value_fim = forward(value_re, value_im)
    taps_fre, taps_fim = forward(taps_re, taps_im)
    prod_re = value_fre * taps_fre - value_fim * taps_fim
    prod_im = value_fre * taps_fim + value_fim * taps_fre
    back_re = mix("rk,jkc->jrc", inner_cos, prod_re) - mix("rk,jkc->jrc", inner_sin, prod_im)
    back_im = mix("rk,jkc->jrc", inner_cos, prod_im) + mix("rk,jkc->jrc", inner_sin, prod_re)
    return (back_re, back_im)


def untwist(real, imag, twist_cos, twist_sin):
    cos_part = twist_cos[:, :, None]
    sin_part = twist_sin[:, :, None]
    return (real * cos_part - imag * sin_part, imag * cos_part + real * sin_part)


def channels_plan(values, filter_taps):
    rows, width = values.shape
    blocks = lax.axis_size("seq")
    length = 2 * blocks * rows
    narrow = width // blocks
    whole_values, whole_taps = (
        lax.all_to_all(values, "seq", split_axis=1, concat_axis=0, tiled=True),
        lax.all_to_all(filter_taps, "seq", split_axis=1, concat_axis=0, tiled=True),
    )
    freq_ids = jnp.arange(2 * blocks, dtype=jnp.int32)
    block_ids = jnp.arange(blocks, dtype=jnp.int32)
    all_rows = jnp.arange(rows, dtype=jnp.int32)
    outer_cos, outer_sin = angle_table(freq_ids, block_ids, 2 * blocks)
    twist_cos, twist_sin = angle_table(freq_ids, all_rows, length)
    tables = (outer_cos, outer_sin, twist_cos, twist_sin, "ka,arc->krc")
    value_re, value_im = outer_forward(whole_values.reshape(blocks, rows, narrow), *tables)
    taps_re, taps_im = outer_forward(whole_taps.reshape(blocks, rows, narrow), *tables)
    inner_cos, inner_sin = angle_table(all_rows, all_rows, rows)
    back_re, back_im = inner_filter((value_re, value_im, taps_re, taps_im), inner_cos, inner_sin)
    turned_re, turned_im = untwist(back_re, back_im, twist_cos, twist_sin)
    final_cos, final_sin = angle_table(block_ids, freq_ids, 2 * blocks)
    signal = (
        mix("ak,krc->arc", final_cos, turned_re) - mix("ak,krc->arc", final_sin, turned_im)
    ) / length
    returned = lax.all_to_all(signal, "seq", split_axis=0, concat_axis=2, tiled=True)
    return returned[0]


def general_local(values, gates, filter_taps, skip_gain, out_weight):
    conv = channels_plan(values, filter_taps)
    gated = (
        gates.astype(jnp.float32) * (conv + skip_gain[None, :] * values.astype(jnp.float32))
    ).astype(jnp.bfloat16)
    projected = lax.psum_scatter(
        lax.dot_general(
            out_weight, gated, (((0,), (1,)), ((), ())), preferred_element_type=jnp.float32
        ),
        "chan",
        scatter_dimension=0,
        tiled=True,
    )
    return projected.astype(jnp.bfloat16)


def split_table(table):
    high = table.astype(ml_dtypes.bfloat16)
    low = (table - high.astype(np.float64)).astype(ml_dtypes.bfloat16)
    return high, low


@functools.lru_cache(maxsize=None)
def transform_tables(length):
    inner = length // RADIX
    q = np.arange(RADIX)[:, None, None]
    k = np.arange(inner)[None, :, None]
    m = np.arange(inner)[None, None, :]
    phase = ((RADIX * m + q) * (4 * k + 1)) % (4 * length)
    angles = phase * (TWO_PI / (4 * length))
    table = np.concatenate([np.cos(angles), -np.sin(angles)], axis=1)
    forward = np.stack(split_table(table), axis=1)
    backward = np.stack(split_table(table.transpose(0, 2, 1) / length), axis=1)
    return forward, backward


@functools.lru_cache(maxsize=None)
def row_order(rows):
    chunk = rows // RADIX
    order = np.zeros((rows, rows), np.float32)
    for q in range(RADIX):
        for j in range(chunk):
            order[q * chunk + j, RADIX * j + q] = 1.0
    return order.astype(ml_dtypes.bfloat16)


def turn(point, index, sign):
    re, im = point
    index %= 16
    if index == 0:
        return point
    if index == 4:
        return (-im, re) if sign > 0 else (im, -re)
    if index == 8:
        return (-re, -im)
    half = math.sqrt(0.5)
    if index == 2:
        return ((re - im) * half, (re + im) * half) if sign > 0 else ((re + im) * half, (im - re) * half)
    if index == 6:
        return ((-re - im) * half, (re - im) * half) if sign > 0 else ((im - re) * half, (-re - im) * half)
    cos = math.cos(TWO_PI * index / 16)
    sin = sign * math.sin(TWO_PI * index / 16)
    return (re * cos - im * sin, re * sin + im * cos)


def four_points(points, sign):
    a, b, c, d = points
    ac = (a[0] + c[0], a[1] + c[1])
    am = (a[0] - c[0], a[1] - c[1])
    bd = (b[0] + d[0], b[1] + d[1])
    bm = (b[0] - d[0], b[1] - d[1])
    if sign < 0:
        side = (bm[1], -bm[0])
    else:
        side = (-bm[1], bm[0])
    return (
        (ac[0] + bd[0], ac[1] + bd[1]),
        (am[0] + side[0], am[1] + side[1]),
        (ac[0] - bd[0], ac[1] - bd[1]),
        (am[0] - side[0], am[1] - side[1]),
    )


def sixteen_points(points, sign):
    out = [None] * 16
    columns = []
    for low in range(4):
        column = four_points([points[low + 4 * high] for high in range(4)], sign)
        columns.append([turn(column[k], low * k, sign) for k in range(4)])
    for k in range(4):
        row = four_points([columns[low][k] for low in range(4)], sign)
        for high in range(4):
            out[k + 4 * high] = row[high]
    return out


def arrange_kernel(group, order_ref, values_ref, taps_ref, out_ref):
    order = order_ref[...]
    for index, source in enumerate((values_ref, taps_ref)):
        moved = jnp.dot(order, source[...], preferred_element_type=jnp.float32).astype(jnp.bfloat16)
        for part in range(group):
            out_ref[part, index] = moved[:, part * LANES : (part + 1) * LANES]


def arrange(values, taps, blocks):
    rows, width = values.shape
    group = 4
    return pl.pallas_call(
        functools.partial(arrange_kernel, group),
        grid=(blocks // group,),
        out_shape=jax.ShapeDtypeStruct((blocks, 2, rows, LANES), jnp.bfloat16),
        in_specs=[
            pl.BlockSpec((rows, rows), lambda i: (0, 0)),
            pl.BlockSpec((rows, group * LANES), lambda i: (0, i)),
            pl.BlockSpec((rows, group * LANES), lambda i: (0, i)),
        ],
        out_specs=pl.BlockSpec((group, 2, rows, LANES), lambda i: (i, 0, 0, 0)),
        compiler_params=pltpu.CompilerParams(vmem_limit_bytes=VMEM_BYTES),
        name="arrange_rows",
    )(jnp.asarray(row_order(rows)), values, taps)


def convolve_kernel(step_q, steps, streams_ref, forward_ref, backward_ref, out_ref, spectra):
    phase, step = pl.program_id(0), pl.program_id(1)
    blocks, _, _, chunk, lanes = streams_ref.shape
    inner = blocks * chunk
    half = inner

    @pl.when(phase == 0)
    def _():
        for part in range(step_q):
            q = step * step_q + part
            value = streams_ref[:, 0, pl.ds(q, 1), :, :].reshape(inner, lanes)
            taps = streams_ref[:, 1, pl.ds(q, 1), :, :].reshape(inner, lanes)
            pair = jnp.concatenate([value, taps], axis=1)
            spectra[q] = jnp.dot(
                forward_ref[part, 0], pair, preferred_element_type=jnp.float32
            ) + jnp.dot(forward_ref[part, 1], pair, preferred_element_type=jnp.float32)

    @pl.when((phase == 0) & (step == steps - 1))
    def _():
        def rows_step(index, carry):
            upper = pl.ds(pl.multiple_of(index * 8, 8), 8)
            lower = pl.ds(pl.multiple_of(half + index * 8, 8), 8)
            left, right = pl.ds(0, lanes), pl.ds(lanes, lanes)
            value = sixteen_points(
                [(spectra[q, upper, left], spectra[q, lower, left]) for q in range(RADIX)], -1
            )
            taps = sixteen_points(
                [(spectra[q, upper, right], spectra[q, lower, right]) for q in range(RADIX)], -1
            )
            product = [
                (a[0] * b[0] - a[1] * b[1], a[0] * b[1] + a[1] * b[0]) for a, b in zip(value, taps)
            ]
            back = sixteen_points(product, 1)
            for q in range(RADIX):
                spectra[q, upper, left] = back[q][0]
                spectra[q, lower, left] = back[q][1]
            return carry

        lax.fori_loop(0, half // 8, rows_step, 0)

    @pl.when(phase == 1)
    def _():
        for part in range(step_q):
            q = step * step_q + part
            points = spectra[q, :, pl.ds(0, lanes)]
            high = points.astype(jnp.bfloat16)
            low = (points - high.astype(jnp.float32)).astype(jnp.bfloat16)
            both = jnp.dot(
                backward_ref[part, 0],
                jnp.concatenate([high, low], axis=1),
                preferred_element_type=jnp.float32,
            )
            signal = (
                both[:, :lanes]
                + both[:, lanes:]
                + jnp.dot(backward_ref[part, 1], high, preferred_element_type=jnp.float32)
            )
            out_ref[:, part] = signal.astype(jnp.bfloat16).reshape(blocks, chunk, lanes)


def convolve(streams, blocks, rows):
    length = blocks * rows
    chunk = rows // RADIX
    inner = length // RADIX
    forward, backward = transform_tables(length)
    step_q = 2
    steps = RADIX // step_q
    return pl.pallas_call(
        functools.partial(convolve_kernel, step_q, steps),
        grid=(2, steps),
        out_shape=jax.ShapeDtypeStruct((blocks, RADIX, chunk, LANES), jnp.bfloat16),
        in_specs=[
            pl.BlockSpec((blocks, 2, RADIX, chunk, LANES), lambda p, i: (0, 0, 0, 0, 0)),
            pl.BlockSpec(
                (step_q, 2, 2 * inner, inner),
                lambda p, i: (i * (1 - p) + (steps - 1) * p, 0, 0, 0),
            ),
            pl.BlockSpec((step_q, 2, inner, 2 * inner), lambda p, i: (i * p, 0, 0, 0)),
        ],
        out_specs=pl.BlockSpec((blocks, step_q, chunk, LANES), lambda p, i: (0, i * p, 0, 0)),
        scratch_shapes=[pltpu.VMEM((RADIX, 2 * inner, 2 * LANES), jnp.float32)],
        compiler_params=pltpu.CompilerParams(vmem_limit_bytes=VMEM_BYTES),
        name="long_convolution",
    )(
        streams.reshape(blocks, 2, RADIX, chunk, LANES),
        jnp.asarray(forward),
        jnp.asarray(backward),
    )


def gate_kernel(group, half_ref, order_ref, conv_ref, gates_ref, values_ref, skip_ref, weight_ref, gated_ref, out_ref):
    del half_ref
    step = pl.program_id(0)
    conv = jnp.concatenate([conv_ref[part] for part in range(group)], axis=1)
    conv = jnp.dot(order_ref[...], conv, preferred_element_type=jnp.float32)
    direct = skip_ref[...] * values_ref[...].astype(jnp.float32)
    gated = (gates_ref[...].astype(jnp.float32) * (conv + direct)).astype(jnp.bfloat16)
    gated_ref[...] = gated
    term = jnp.dot(gated, weight_ref[...], preferred_element_type=jnp.float32)

    @pl.when(step == 0)
    def _():
        out_ref[...] = term

    @pl.when(step > 0)
    def _():
        out_ref[...] += term


def gate_and_project(half, conv, gates, values, skip_gain, out_weight):
    blocks, rows, lanes = conv.shape
    width, features = out_weight.shape
    group = 4
    wide = group * lanes
    return pl.pallas_call(
        functools.partial(gate_kernel, group),
        grid_spec=pltpu.PrefetchScalarGridSpec(
            num_scalar_prefetch=1,
            grid=(blocks // group,),
            in_specs=[
                pl.BlockSpec((rows, rows), lambda i, h: (0, 0)),
                pl.BlockSpec((group, rows, lanes), lambda i, h: (i, 0, 0)),
                pl.BlockSpec((rows, wide), lambda i, h: (0, i)),
                pl.BlockSpec((rows, wide), lambda i, h: (0, i)),
                pl.BlockSpec((1, wide), lambda i, h: (0, i)),
                pl.BlockSpec((wide, features // 2), lambda i, h: (i, 1 - h[0])),
            ],
            out_specs=[
                pl.BlockSpec((rows, wide), lambda i, h: (0, i)),
                pl.BlockSpec((rows, features // 2), lambda i, h: (0, 0)),
            ],
        ),
        out_shape=[
            jax.ShapeDtypeStruct((rows, width), jnp.bfloat16),
            jax.ShapeDtypeStruct((rows, features // 2), jnp.float32),
        ],
        compiler_params=pltpu.CompilerParams(vmem_limit_bytes=VMEM_BYTES),
        cost_estimate=pl.CostEstimate(
            flops=rows * width * features, bytes_accessed=width * features + 8 * rows * width, transcendentals=0
        ),
        name="gate_project_sent",
    )(half, jnp.asarray(row_order(rows).T), conv, gates, values, skip_gain[None, :], out_weight)


def kept_kernel(half_ref, gated_ref, weight_ref, out_ref):
    del half_ref
    step = pl.program_id(0)
    term = jnp.dot(gated_ref[...], weight_ref[...], preferred_element_type=jnp.float32)

    @pl.when(step == 0)
    def _():
        out_ref[...] = term

    @pl.when(step > 0)
    def _():
        out_ref[...] += term


def project_kept(half, gated, out_weight):
    rows, width = gated.shape
    features = out_weight.shape[1]
    deep = width // 4
    return pl.pallas_call(
        kept_kernel,
        grid_spec=pltpu.PrefetchScalarGridSpec(
            num_scalar_prefetch=1,
            grid=(4,),
            in_specs=[
                pl.BlockSpec((rows, deep), lambda i, h: (0, i)),
                pl.BlockSpec((deep, features // 2), lambda i, h: (i, h[0])),
            ],
            out_specs=pl.BlockSpec((rows, features // 2), lambda i, h: (0, 0)),
        ),
        out_shape=jax.ShapeDtypeStruct((rows, features // 2), jnp.float32),
        compiler_params=pltpu.CompilerParams(vmem_limit_bytes=VMEM_BYTES),
        cost_estimate=pl.CostEstimate(
            flops=rows * width * features, bytes_accessed=width * features + 4 * rows * width, transcendentals=0
        ),
        name="project_kept",
    )(half, gated, out_weight)


def join_kernel(kept_ref, came_ref, out_ref):
    out_ref[...] = (kept_ref[...] + came_ref[...]).T.astype(jnp.bfloat16)


def join(kept, came):
    rows, features = kept.shape
    wide = features // 4
    return pl.pallas_call(
        join_kernel,
        grid=(4,),
        in_specs=[pl.BlockSpec((rows, wide), lambda i: (0, i))] * 2,
        out_specs=pl.BlockSpec((wide, rows), lambda i: (i, 0)),
        out_shape=jax.ShapeDtypeStruct((features, rows), jnp.bfloat16),
        compiler_params=pltpu.CompilerParams(vmem_limit_bytes=VMEM_BYTES),
        name="join_halves",
    )(kept, came)


def kernel_local(values, gates, filter_taps, skip_gain, out_weight):
    rows, _ = values.shape
    blocks = lax.axis_size("seq")
    streams = arrange(values, filter_taps, blocks)
    streams = lax.all_to_all(streams, "seq", split_axis=0, concat_axis=0, tiled=True)
    conv = convolve(streams, blocks, rows).reshape(blocks, rows, LANES)
    conv = lax.all_to_all(conv, "seq", split_axis=0, concat_axis=0, tiled=True)
    half = lax.axis_index("chan").astype(jnp.int32)[None]
    gated, sent = gate_and_project(half, conv, gates, values, skip_gain, out_weight)
    came = lax.ppermute(sent, "chan", [(0, 1), (1, 0)])
    kept = project_kept(half, gated, out_weight)
    return join(kept, came)


def takes_kernels(mesh, values, out_weight):
    blocks, halves = mesh.shape["seq"], mesh.shape["chan"]
    rows = values.shape[0] // blocks
    return (
        halves == 2
        and blocks % 4 == 0
        and rows == 256
        and blocks * rows == 4096
        and values.shape[1] == halves * blocks * LANES
        and out_weight.shape[1] % (8 * LANES) == 0
    )


def solution(mesh):
    placed = (P("seq", "chan"), P("seq", "chan"), P("seq", "chan"), P("chan"), P("chan", None))

    def whole(values, gates, filter_taps, skip_gain, out_weight):
        local = kernel_local if takes_kernels(mesh, values, out_weight) else general_local
        return jax.shard_map(
            local, mesh=mesh, in_specs=placed, out_specs=P("chan", "seq"), check_vma=False
        )(values, gates, filter_taps, skip_gain, out_weight)

    return whole
```

profile of v0, /device:TPU:0, one launch (start us, length us, event | category | flops | bytes accessed | tf_op | source)
XLA Modules:
  0.0 126.1 jit_solution(6921734815090608455)
XLA Ops:
  0.0 4.3 %arrange_rows.1 = bf16[16,2,256,128]{3,2,1,0:T(8,128)(2,1)} custom-call(bf16[256,256]{1,0:T(8,128)(2,1)} %constant.10.clone.order_ref, bf16[256,2048]{1,0:T(8,128)(2,1)} %values_ref.3, bf16[256,2048]{1,0:T(8,128)(2,1)} %taps_ref.1), custom_call_target="tpu_custom_call" | custom-call | tf_op jit(solution)/shard_map/arrange_rows/pallas_call | solution.py:197
  4.3 57.3 %all_to_all.10 = bf16[16,2,256,128]{3,2,1,0:T(8,128)(2,1)} all-to-all(bf16[16,2,256,128]{3,2,1,0:T(8,128)(2,1)} %arrange_rows.1), channel_id=1, replica_groups=mesh['seq'=16,'chan'=2] {'seq'}, dimensions={0} | all-to-all | bytes 4194304 | tf_op jit(solution)/shard_map/all_to_all | solution.py:416
  61.6 19.5 %long_convolution.1 = bf16[16,16,16,128]{3,2,1,0:T(8,128)(2,1)} custom-call(bf16[16,2,16,16,128]{4,3,2,1,0:T(8,128)(2,1)} %bitcast.4, bf16[16,2,512,256]{3,2,1,0:T(8,128)(2,1)} %constant.11.clone.forward_ref, bf16[16,2,256,512]{3,2,1,0:T(8,128)(2,1)} %constant.12.clone.backward_ref), custom_call_target="tpu_custom_call" | custom-call | tf_op jit(solution)/shard_map/long_convolution/pallas_call | solution.py:279
  81.1 3.9 %all-to-all-start.1 = ((bf16[16,256,128]{2,1,0:T(8,128)(2,1)}), bf16[16,256,128]{2,1,0:T(8,128)(2,1)S(1)}, u32[]{:S(2)}, u32[]{:S(2)}) async-start(bf16[16,256,128]{2,1,0:T(8,128)(2,1)} %bitcast.5), calls=%async_computation.1 | async-start | bytes 2097152 | tf_op jit(solution)/shard_map/all_to_all | solution.py:418
  85.1 23.7 %all-to-all-done.1.conv_ref = bf16[16,256,128]{2,1,0:T(8,128)(2,1)S(1)} async-done(((bf16[16,256,128]{2,1,0:T(8,128)(2,1)}), bf16[16,256,128]{2,1,0:T(8,128)(2,1)S(1)}, u32[]{:S(2)}, u32[]{:S(2)}) %all-to-all-start.1) | async-done | bytes 1048608 | tf_op jit(solution)/shard_map/all_to_all | solution.py:418
  108.7 0.0 copy-start
  108.7 1.0 copy-done
  109.7 6.5 %gate_project_sent.1 = (bf16[256,2048]{1,0:T(8,128)(2,1)}, f32[256,1024]{1,0:T(8,128)}) custom-call(s32[1]{0:T(128)} %bitcast.half_ref, bf16[256,256]{1,0:T(8,128)(2,1)} %constant.10.clone.order_ref, bf16[16,256,128]{2,1,0:T(8,128)(2,1)} %copy-done, bf16[256,2048]{1,0:T(8,128)(2,1)} %gates_ref.1, bf16[256,2048]{1,0:T(8,128)(2,1)} %values_ref.3, ...), custom_call_target="tpu_custom_call" | custom-call | flops 1073741824 | bytes 8388608 | tf_op jit(solution)/shard_map/gate_project_sent/pallas_call | solution.py:326
  116.2 0.0 collective-permute-start
  116.2 5.3 %project_kept.1.kept_ref = f32[256,1024]{1,0:T(8,128)} custom-call(s32[1]{0:T(128)} %bitcast.half_ref, bf16[256,2048]{1,0:T(8,128)(2,1)} %get-tuple-element.7.gated_ref, bf16[2048,2048]{1,0:T(8,128)(2,1)} %weight_ref.3), custom_call_target="tpu_custom_call" | custom-call | flops 1073741824 | bytes 6291456 | tf_op jit(solution)/shard_map/project_kept/pallas_call | solution.py:374
  121.5 0.0 collective-permute-done.came_ref
  121.5 0.0 copy-start.1
  121.5 1.0 copy-done.1
  122.5 3.6 %join_halves.1 = bf16[1024,256]{1,0:T(8,128)(2,1)} custom-call(f32[256,1024]{1,0:T(8,128)} %project_kept.1.kept_ref, f32[256,1024]{1,0:T(8,128)} %copy-done.1), custom_call_target="tpu_custom_call" | custom-call | tf_op jit(solution)/shard_map/join_halves/pallas_call | solution.py:401
Async XLA Ops:
  81.1 27.6 %all-to-all-start.1 = ((bf16[16,256,128]{2,1,0:T(8,128)(2,1)}), bf16[16,256,128]{2,1,0:T(8,128)(2,1)S(1)}, u32[]{:S(2)}, u32[]{:S(2)}) async-start(bf16[16,256,128]{2,1,0:T(8,128)(2,1)} %bitcast.5), calls=%async_computation.1 | async-start | bytes 2097152 | tf_op jit(solution)/shard_map/all_to_all | solution.py:418
  108.7 1.0 copy-start
  116.2 5.3 %collective-permute-start = (f32[256,1024]{1,0:T(8,128)}, f32[256,1024]{1,0:T(8,128)S(1)}, u32[]{:S(2)}, u32[]{:S(2)}) collective-permute-start(f32[256,1024]{1,0:T(8,128)} %get-tuple-element.8), channel_id=1, source_target_pairs={{0,1},{1,0},{2,3},{3,2},{4,5},{5,4},{6,7},{7,6},{8,9},{9,8},{10,11... | collective-permute-start | bytes 3145736 | tf_op jit(solution)/shard_map/ppermute | solution.py:421
  121.5 1.0 copy-start.1
where the time goes:
time: 128 us; the launch traced here: 126 us
  blocking collectives  57.3 us (45%)
  Pallas kernels  39.3 us (31%)
  waiting for transfers between devices  23.7 us (19%)
  starting transfers between devices  3.91 us (3%)
  local copies, waits for them, and re-layouts  1.96 us (2%)
    all_to_all x1, blocking collectives, kernel_local(): lax.all_to_all(streams, 'seq', split_axis=0, concat_axis=0, tiled=True)  57.3 us
    all_to_all x1, waiting for transfers between devices, kernel_local(): conv = lax.all_to_all(conv, 'seq', split_axis=0, concat_axis=0, tiled=True)  23.7 us
    pallas_call x1, Pallas kernels, convolve(): pl.pallas_call(functools.partial(convolve_kernel, step_q, steps), grid=(2...  19.5 us
    pallas_call x1, Pallas kernels, gate_and_project(): pl.pallas_call(functools.partial(gate_kernel, group), grid_spec=pltpu.Pre...  6.5 us
    pallas_call x1, Pallas kernels, project_kept(): pl.pallas_call(kept_kernel, grid_spec=pltpu.PrefetchScalarGridSpec(num_sc...  5.31 us
    pallas_call x1, Pallas kernels, arrange(): pl.pallas_call(functools.partial(arrange_kernel, group), grid=(blocks //...  4.33 us
    all_to_all x1, starting transfers between devices, kernel_local(): conv = lax.all_to_all(conv, 'seq', split_axis=0, concat_axis=0, tiled=True)  3.91 us
    pallas_call x1, Pallas kernels, join(): pl.pallas_call(join_kernel, grid=(4,), in_specs=[pl.BlockSpec((rows, wide...  3.62 us
  transfers between devices with their start and end apart: 2, of which 1 were waited for; matrix products, arithmetic and copies ran while one was open for 0% of the time, Pallas kernels for 4%

commit v1 on v0

v1 whole, which is shorter than its diff:
```python
import functools
import math

import jax
import jax.numpy as jnp
import ml_dtypes
import numpy as np
from jax import lax
from jax.experimental import pallas as pl
from jax.experimental.pallas import tpu as pltpu
from jax.sharding import PartitionSpec as P

TWO_PI = 2.0 * math.pi
HIGH = lax.Precision.HIGHEST
RADIX = 16
LANES = 128
HALF = 64
VMEM_BYTES = 40 * 1024 * 1024
SMALL_BYTES = 24 * 1024 * 1024


def angle_table(first, second, period):
    product = first[:, None] * second[None, :] % period
    angles = product.astype(jnp.float32) * (TWO_PI / period)
    return (jnp.cos(angles), jnp.sin(angles))


def mix(equation, left, right):
    return jnp.einsum(equation, left, right, precision=HIGH)


def outer_forward(data, outer_cos, outer_sin, twist_cos, twist_sin, equation):
    source = data.astype(jnp.float32)
    real = mix(equation, outer_cos, source)
    imag = -mix(equation, outer_sin, source)
    cos_part = twist_cos[:, :, None]
    sin_part = twist_sin[:, :, None]
    return (real * cos_part + imag * sin_part, imag * cos_part - real * sin_part)


def inner_filter(spectra, inner_cos, inner_sin):
    value_re, value_im, taps_re, taps_im = spectra

    def forward(real, imag):
        out_re = mix("kr,jrc->jkc", inner_cos, real) + mix("kr,jrc->jkc", inner_sin, imag)
        out_im = mix("kr,jrc->jkc", inner_cos, imag) - mix("kr,jrc->jkc", inner_sin, real)
        return (out_re, out_im)

    value_fre, value_fim = forward(value_re, value_im)
    taps_fre, taps_fim = forward(taps_re, taps_im)
    prod_re = value_fre * taps_fre - value_fim * taps_fim
    prod_im = value_fre * taps_fim + value_fim * taps_fre
    back_re = mix("rk,jkc->jrc", inner_cos, prod_re) - mix("rk,jkc->jrc", inner_sin, prod_im)
    back_im = mix("rk,jkc->jrc", inner_cos, prod_im) + mix("rk,jkc->jrc", inner_sin, prod_re)
    return (back_re, back_im)


def untwist(real, imag, twist_cos, twist_sin):
    cos_part = twist_cos[:, :, None]
    sin_part = twist_sin[:, :, None]
    return (real * cos_part - imag * sin_part, imag * cos_part + real * sin_part)


def channels_plan(values, filter_taps):
    rows, width = values.shape
    blocks = lax.axis_size("seq")
    length = 2 * blocks * rows
    narrow = width // blocks
    whole_values, whole_taps = (
        lax.all_to_all(values, "seq", split_axis=1, concat_axis=0, tiled=True),
        lax.all_to_all(filter_taps, "seq", split_axis=1, concat_axis=0, tiled=True),
    )
    freq_ids = jnp.arange(2 * blocks, dtype=jnp.int32)
    block_ids = jnp.arange(blocks, dtype=jnp.int32)
    all_rows = jnp.arange(rows, dtype=jnp.int32)
    outer_cos, outer_sin = angle_table(freq_ids, block_ids, 2 * blocks)
    twist_cos, twist_sin = angle_table(freq_ids, all_rows, length)
    tables = (outer_cos, outer_sin, twist_cos, twist_sin, "ka,arc->krc")
    value_re, value_im = outer_forward(whole_values.reshape(blocks, rows, narrow), *tables)
    taps_re, taps_im = outer_forward(whole_taps.reshape(blocks, rows, narrow), *tables)
    inner_cos, inner_sin = angle_table(all_rows, all_rows, rows)
    back_re, back_im = inner_filter((value_re, value_im, taps_re, taps_im), inner_cos, inner_sin)
    turned_re, turned_im = untwist(back_re, back_im, twist_cos, twist_sin)
    final_cos, final_sin = angle_table(block_ids, freq_ids, 2 * blocks)
    signal = (
        mix("ak,krc->arc", final_cos, turned_re) - mix("ak,krc->arc", final_sin, turned_im)
    ) / length
    returned = lax.all_to_all(signal, "seq", split_axis=0, concat_axis=2, tiled=True)
    return returned[0]


def general_local(values, gates, filter_taps, skip_gain, out_weight):
    conv = channels_plan(values, filter_taps)
    gated = (
        gates.astype(jnp.float32) * (conv + skip_gain[None, :] * values.astype(jnp.float32))
    ).astype(jnp.bfloat16)
    projected = lax.psum_scatter(
        lax.dot_general(
            out_weight, gated, (((0,), (1,)), ((), ())), preferred_element_type=jnp.float32
        ),
        "chan",
        scatter_dimension=0,
        tiled=True,
    )
    return projected.astype(jnp.bfloat16)


def split_table(table):
    high = table.astype(ml_dtypes.bfloat16)
    low = (table - high.astype(np.float64)).astype(ml_dtypes.bfloat16)
    return high, low


@functools.lru_cache(maxsize=None)
def transform_tables(length):
    inner = length // RADIX
    q = np.arange(RADIX)[:, None, None]
    k = np.arange(inner)[None, :, None]
    m = np.arange(inner)[None, None, :]
    phase = ((RADIX * m + q) * (4 * k + 1)) % (4 * length)
    angles = phase * (TWO_PI / (4 * length))
    table = np.concatenate([np.cos(angles), -np.sin(angles)], axis=1)
    forward = np.concatenate(split_table(table), axis=2)
    backward = np.concatenate(split_table(table.transpose(0, 2, 1) / length), axis=1)
    return tuple(
        np.ascontiguousarray(part.reshape(2, RADIX // 2, *part.shape[1:]).swapaxes(0, 1))
        for part in (forward, backward)
    )


@functools.lru_cache(maxsize=None)
def row_order(rows):
    chunk = rows // RADIX
    order = np.zeros((rows, rows), np.float32)
    for q in range(RADIX):
        for j in range(chunk):
            order[q * chunk + j, RADIX * j + q] = 1.0
    return order.astype(ml_dtypes.bfloat16)


def turn(point, index, sign):
    re, im = point
    index %= 16
    if index == 0:
        return point
    if index == 4:
        return (-im, re) if sign > 0 else (im, -re)
    if index == 8:
        return (-re, -im)
    half = math.sqrt(0.5)
    if index == 2:
        return ((re - im) * half, (re + im) * half) if sign > 0 else ((re + im) * half, (im - re) * half)
    if index == 6:
        return ((-re - im) * half, (re - im) * half) if sign > 0 else ((im - re) * half, (-re - im) * half)
    cos = math.cos(TWO_PI * index / 16)
    sin = sign * math.sin(TWO_PI * index / 16)
    return (re * cos - im * sin, re * sin + im * cos)


def four_points(points, sign):
    a, b, c, d = points
    ac = (a[0] + c[0], a[1] + c[1])
    am = (a[0] - c[0], a[1] - c[1])
    bd = (b[0] + d[0], b[1] + d[1])
    bm = (b[0] - d[0], b[1] - d[1])
    if sign < 0:
        side = (bm[1], -bm[0])
    else:
        side = (-bm[1], bm[0])
    return (
        (ac[0] + bd[0], ac[1] + bd[1]),
        (am[0] + side[0], am[1] + side[1]),
        (ac[0] - bd[0], ac[1] - bd[1]),
        (am[0] - side[0], am[1] - side[1]),
    )


def sixteen_points(points, sign):
    out = [None] * 16
    columns = []
    for low in range(4):
        column = four_points([points[low + 4 * high] for high in range(4)], sign)
        columns.append([turn(column[k], low * k, sign) for k in range(4)])
    for k in range(4):
        row = four_points([columns[low][k] for low in range(4)], sign)
        for high in range(4):
            out[k + 4 * high] = row[high]
    return out


def left_lanes(rows):
    return lax.broadcasted_iota(jnp.int32, (rows, LANES), 1) < HALF


def swap_halves(block):
    return pltpu.roll(block, HALF, 1)


def arrange_kernel(blocks, me_ref, order_ref, values_ref, taps_ref, *rest):
    outs, packed = rest[:blocks], rest[blocks]
    me = me_ref[0]
    order = order_ref[...]
    left = left_lanes(order.shape[0])
    for pair in range(blocks // 2):
        lanes = pl.ds(pair * LANES, LANES)
        both = jnp.concatenate([values_ref[:, lanes], taps_ref[:, lanes]], axis=1)
        moved = jnp.dot(order, both, preferred_element_type=jnp.float32)
        value, taps = moved[:, :LANES], moved[:, LANES:]
        packed[2 * pair] = jnp.where(left, value, swap_halves(taps)).astype(jnp.bfloat16)
        packed[2 * pair + 1] = jnp.where(left, swap_halves(value), taps).astype(jnp.bfloat16)
    for slot in range(blocks):
        outs[slot][...] = packed[me ^ slot]


def arrange(me, values, taps, blocks, chunk):
    rows = values.shape[0]
    wide = blocks * HALF
    return pl.pallas_call(
        functools.partial(arrange_kernel, blocks),
        grid_spec=pltpu.PrefetchScalarGridSpec(
            num_scalar_prefetch=1,
            grid=(1,),
            in_specs=[
                pl.BlockSpec((rows, rows), lambda i, me: (0, 0)),
                pl.BlockSpec((rows, wide), lambda i, me: (0, chunk)),
                pl.BlockSpec((rows, wide), lambda i, me: (0, chunk)),
            ],
            out_specs=[pl.BlockSpec((rows, LANES), lambda i, me: (0, 0))] * blocks,
            scratch_shapes=[pltpu.VMEM((blocks, rows, LANES), jnp.bfloat16)],
        ),
        out_shape=[jax.ShapeDtypeStruct((rows, LANES), jnp.bfloat16)] * blocks,
        compiler_params=pltpu.CompilerParams(vmem_limit_bytes=VMEM_BYTES),
        name=f"arrange_{chunk}",
    )(me, jnp.asarray(row_order(rows)), values, taps)


def convolve_kernel(blocks, pairs, me_ref, *rest):
    slots = rest[:blocks]
    forward_ref, backward_ref = rest[blocks : blocks + 2]
    outs = rest[blocks + 2 : 2 * blocks + 2]
    streams, spectra, signals = rest[2 * blocks + 2 :]
    me = me_ref[0]
    phase, step = pl.program_id(0), pl.program_id(1)
    chunk = streams.shape[2]
    inner = blocks * chunk
    part_rows = inner // 2

    @pl.when((phase == 0) & (step == 0))
    def _():
        for slot in range(blocks):
            streams[me ^ slot] = slots[slot][...].reshape(RADIX, chunk, LANES)

    @pl.when(phase == 0)
    def _():
        for part in range(2):
            q = step + part * pairs
            stream = streams[:, pl.ds(q, 1)].reshape(inner, LANES)
            spectra[q] = jnp.dot(
                forward_ref[0, part],
                jnp.concatenate([stream, stream], axis=0),
                preferred_element_type=jnp.float32,
            )

    @pl.when((phase == 0) & (step == pairs - 1))
    def _():
        left = left_lanes(8)

        def rows_step(index, carry):
            starts = [pl.multiple_of(base + index * 8, 8) for base in range(0, 2 * inner, part_rows)]
            first_re, second_re, first_im, second_im = [pl.ds(start, 8) for start in starts]
            first = sixteen_points([(spectra[q, first_re], spectra[q, first_im]) for q in range(RADIX)], -1)
            second = sixteen_points([(spectra[q, second_re], spectra[q, second_im]) for q in range(RADIX)], -1)
            product = []
            for one, two in zip(first, second):
                a = [jnp.where(left, x, y) for x, y in zip(one, two)]
                b = [swap_halves(jnp.where(left, y, x)) for x, y in zip(one, two)]
                product.append((a[0] * b[0] - a[1] * b[1], a[0] * b[1] + a[1] * b[0]))
            back = sixteen_points(product, 1)
            for q in range(RADIX):
                spectra[q, first_re] = back[q][0]
                spectra[q, first_im] = back[q][1]
            return carry

        lax.fori_loop(0, part_rows // 8, rows_step, 0)

    @pl.when(phase == 1)
    def _():
        left = left_lanes(part_rows)
        sides = []
        for part in range(2):
            q = step + part * pairs
            pieces = []
            for base in (0, inner):
                points = spectra[q, pl.ds(base, part_rows)]
                high = points.astype(jnp.bfloat16).astype(jnp.float32)
                low = points - high
                pieces.append(jnp.where(left, high, swap_halves(low)).astype(jnp.bfloat16))
                pieces.append(jnp.where(left, swap_halves(high), low).astype(jnp.bfloat16))
            terms = jnp.dot(
                backward_ref[0, part],
                jnp.concatenate(pieces, axis=0),
                preferred_element_type=jnp.float32,
            )
            total = terms[:inner] + terms[inner:]
            sides.append(total + swap_halves(total))
        signal = jnp.where(left_lanes(inner), sides[0], sides[1]).astype(jnp.bfloat16)
        signals[:, pl.ds(step, 1)] = signal.reshape(blocks, 1, chunk, LANES)

    @pl.when((phase == 1) & (step == pairs - 1))
    def _():
        for slot in range(blocks):
            outs[slot][...] = signals[me ^ slot].reshape(pairs * chunk, LANES)


def convolve(me, slots, blocks, chunk_id):
    rows = slots[0].shape[0]
    length = blocks * rows
    chunk = rows // RADIX
    inner = length // RADIX
    pairs = RADIX // 2
    forward, backward = transform_tables(length)
    whole = lambda p, i, me: (0, 0)
    table = (1, 2, 2 * inner, 2 * inner)
    return pl.pallas_call(
        functools.partial(convolve_kernel, blocks, pairs),
        grid_spec=pltpu.PrefetchScalarGridSpec(
            num_scalar_prefetch=1,
            grid=(2, pairs),
            in_specs=[pl.BlockSpec((rows, LANES), whole)] * blocks
            + [
                pl.BlockSpec(table, lambda p, i, me: (i * (1 - p) + (pairs - 1) * p, 0, 0, 0)),
                pl.BlockSpec(table, lambda p, i, me: (i * p, 0, 0, 0)),
            ],
            out_specs=[pl.BlockSpec((pairs * chunk, LANES), whole)] * blocks,
            scratch_shapes=[
                pltpu.VMEM((blocks, RADIX, chunk, LANES), jnp.bfloat16),
                pltpu.VMEM((RADIX, 2 * inner, LANES), jnp.float32),
                pltpu.VMEM((blocks, pairs, chunk, LANES), jnp.bfloat16),
            ],
        ),
        out_shape=[jax.ShapeDtypeStruct((pairs * chunk, LANES), jnp.bfloat16)] * blocks,
        compiler_params=pltpu.CompilerParams(vmem_limit_bytes=VMEM_BYTES),
        cost_estimate=pl.CostEstimate(
            flops=2 * RADIX * 2 * (2 * inner) * (2 * inner) * LANES * 2,
            bytes_accessed=RADIX * 2 * (2 * inner) ** 2 * 2,
            transcendentals=0,
        ),
        name=f"long_convolution_{chunk_id}",
    )(me, *slots, jnp.asarray(forward), jnp.asarray(backward))


def gate_kernel(blocks, joined, me_ref, *rest):
    slots = rest[:blocks]
    if joined:
        order_ref, gates_ref, values_ref, skip_ref, weight_ref, base_ref, out_ref, gated_ref, parts = rest[blocks:]
    else:
        order_ref, gates_ref, values_ref, skip_ref, weight_ref, out_ref, parts = rest[blocks:]
    me = me_ref[0]
    step = pl.program_id(0)

    @pl.when(step == 0)
    def _():
        for slot in range(blocks):
            parts[me ^ slot] = slots[slot][...]

    wide = gates_ref.shape[1]
    pairs = wide // LANES
    left = left_lanes(parts.shape[1])
    columns = []
    for pair in range(pairs):
        even = parts[2 * (step * pairs + pair)].astype(jnp.float32)
        odd = parts[2 * (step * pairs + pair) + 1].astype(jnp.float32)
        low = jnp.where(left, even, swap_halves(odd))
        high = jnp.where(left, swap_halves(even), odd)
        columns.append(jnp.concatenate([low, high], axis=0).astype(jnp.bfloat16))
    conv = jnp.dot(
        order_ref[...], jnp.concatenate(columns, axis=1), preferred_element_type=jnp.float32
    )
    direct = skip_ref[...] * values_ref[...].astype(jnp.float32)
    gated = (gates_ref[...].astype(jnp.float32) * (conv + direct)).astype(jnp.bfloat16)
    if joined:
        gated_ref[...] = gated
    term = jnp.dot(gated, weight_ref[...], preferred_element_type=jnp.float32)

    @pl.when(step == 0)
    def _():
        out_ref[...] = base_ref[...] + term if joined else term

    @pl.when(step > 0)
    def _():
        out_ref[...] += term


def gate_and_project(me, slots, gates, values, skip_gain, out_weight, chunk, base=None):
    blocks = len(slots)
    rows = gates.shape[0]
    features = out_weight.shape[1]
    steps = 4
    wide = blocks * HALF // steps
    joined = base is not None
    taken = features // 2 if joined else features
    in_specs = [pl.BlockSpec(slots[0].shape, lambda i, me: (0, 0))] * blocks + [
        pl.BlockSpec((rows, rows), lambda i, me: (0, 0)),
        pl.BlockSpec((rows, wide), lambda i, me: (0, chunk * steps + i)),
        pl.BlockSpec((rows, wide), lambda i, me: (0, chunk * steps + i)),
        pl.BlockSpec((1, wide), lambda i, me: (0, chunk * steps + i)),
    ]
    operands = [me, *slots, jnp.asarray(row_order(rows).T), gates, values, skip_gain[None, :], out_weight]
    out_specs = [pl.BlockSpec((rows, taken), lambda i, me: (0, 0))]
    out_shape = [jax.ShapeDtypeStruct((rows, taken), jnp.float32)]
    if joined:
        in_specs.append(pl.BlockSpec((wide, taken), lambda i, me: (chunk * steps + i, 1 - me[1])))
        in_specs.append(pl.BlockSpec((rows, taken), lambda i, me: (0, 1 - me[1])))
        operands.append(base)
        out_specs.append(pl.BlockSpec((rows, wide), lambda i, me: (0, i)))
        out_shape.append(jax.ShapeDtypeStruct((rows, steps * wide), jnp.bfloat16))
    else:
        in_specs.append(pl.BlockSpec((wide, taken), lambda i, me: (chunk * steps + i, 0)))
    return pl.pallas_call(
        functools.partial(gate_kernel, blocks, joined),
        grid_spec=pltpu.PrefetchScalarGridSpec(
            num_scalar_prefetch=1,
            grid=(steps,),
            in_specs=in_specs,
            out_specs=out_specs,
            scratch_shapes=[pltpu.VMEM((blocks, *slots[0].shape), jnp.bfloat16)],
        ),
        out_shape=out_shape,
        compiler_params=pltpu.CompilerParams(vmem_limit_bytes=SMALL_BYTES),
        cost_estimate=pl.CostEstimate(
            flops=2 * rows * steps * wide * taken,
            bytes_accessed=2 * steps * wide * taken + 12 * rows * steps * wide,
            transcendentals=0,
        ),
        name=f"gate_project_{chunk}",
    )(*operands)


def kept_kernel(me_ref, gated_ref, weight_ref, base_ref, out_ref):
    del me_ref
    step = pl.program_id(0)
    term = jnp.dot(gated_ref[...], weight_ref[...], preferred_element_type=jnp.float32)

    @pl.when(step == 0)
    def _():
        out_ref[...] = base_ref[...] + term

    @pl.when(step > 0)
    def _():
        out_ref[...] += term


def project_kept(me, gated, out_weight, base):
    rows, width = gated.shape
    features = out_weight.shape[1]
    steps = 2
    deep = width // steps
    return pl.pallas_call(
        kept_kernel,
        grid_spec=pltpu.PrefetchScalarGridSpec(
            num_scalar_prefetch=1,
            grid=(steps,),
            in_specs=[
                pl.BlockSpec((rows, deep), lambda i, me: (0, i)),
                pl.BlockSpec((deep, features // 2), lambda i, me: (steps + i, me[1])),
                pl.BlockSpec((rows, features // 2), lambda i, me: (0, me[1])),
            ],
            out_specs=pl.BlockSpec((rows, features // 2), lambda i, me: (0, 0)),
        ),
        out_shape=jax.ShapeDtypeStruct((rows, features // 2), jnp.float32),
        compiler_params=pltpu.CompilerParams(vmem_limit_bytes=SMALL_BYTES),
        cost_estimate=pl.CostEstimate(
            flops=rows * width * features, bytes_accessed=width * features + 8 * rows * width, transcendentals=0
        ),
        name="project_kept",
    )(me, gated, out_weight, base)


def join_kernel(kept_ref, came_ref, out_ref):
    out_ref[...] = (kept_ref[...] + came_ref[...]).astype(jnp.bfloat16).T


def join(kept, came):
    rows, features = kept.shape
    wide = features // 4
    return pl.pallas_call(
        join_kernel,
        grid=(4,),
        in_specs=[pl.BlockSpec((rows, wide), lambda i: (0, i))] * 2,
        out_specs=pl.BlockSpec((wide, rows), lambda i: (i, 0)),
        out_shape=jax.ShapeDtypeStruct((features, rows), jnp.bfloat16),
        compiler_params=pltpu.CompilerParams(vmem_limit_bytes=SMALL_BYTES),
        name="join_halves",
    )(kept, came)


def exchange(slots):
    blocks = len(slots)
    return [slots[0]] + [
        lax.ppermute(slots[slot], "seq", [(j, j ^ slot) for j in range(blocks)]) for slot in range(1, blocks)
    ]


def kernel_local(values, gates, filter_taps, skip_gain, out_weight):
    blocks = lax.axis_size("seq")
    me = jnp.stack([lax.axis_index("seq"), lax.axis_index("chan")]).astype(jnp.int32)
    came = [exchange(arrange(me, values, filter_taps, blocks, chunk)) for chunk in range(2)]
    back = [exchange(convolve(me, came[chunk], blocks, chunk)) for chunk in range(2)]
    (base,) = gate_and_project(me, back[0], gates, values, skip_gain, out_weight, 0)
    sent, gated = gate_and_project(me, back[1], gates, values, skip_gain, out_weight, 1, base)
    other = lax.ppermute(sent, "chan", [(0, 1), (1, 0)])
    kept = project_kept(me, gated, out_weight, base)
    return join(kept, other)


def takes_kernels(mesh, values, out_weight):
    blocks, halves = mesh.shape["seq"], mesh.shape["chan"]
    rows = values.shape[0] // blocks
    return (
        halves == 2
        and blocks == 16
        and rows == 256
        and values.shape[1] == halves * blocks * LANES
        and out_weight.shape[1] % (8 * LANES) == 0
    )


def solution(mesh):
    placed = (P("seq", "chan"), P("seq", "chan"), P("seq", "chan"), P("chan"), P("chan", None))

    def whole(values, gates, filter_taps, skip_gain, out_weight):
        local = kernel_local if takes_kernels(mesh, values, out_weight) else general_local
        return jax.shard_map(
            local, mesh=mesh, in_specs=placed, out_specs=P("chan", "seq"), check_vma=False
        )(values, gates, filter_taps, skip_gain, out_weight)

    return whole
```

time: 128 us -> 174 us (1.36)
  starting transfers between devices: 3.91 us -> 110 us
  blocking collectives: 57.3 us -> 0 us
  waiting for transfers between devices: 23.7 us -> 5.01 us
  local copies, waits for them, and re-layouts: 1.96 us -> 10.1 us
  Pallas kernels: 39.3 us -> 47.4 us
    ppermute x1 -> x61, starting transfers between devices: 0.01 us -> 110 us  [the longest x60 110 us: exchange(): lax.ppermute(slots[slot], 'seq', [(j, j ^ slot) for j in range(blocks)])]
    all_to_all x1 -> x0, blocking collectives: 57.3 us -> none  [kernel_local(): lax.all_to_all(streams, 'seq', split_axis=0, concat_axis=0, tiled=True)]
    all_to_all x1 -> x0, waiting for transfers between devices: 23.7 us -> none  [kernel_local(): conv = lax.all_to_all(conv, 'seq', split_axis=0, concat_axis=0, tiled=True)]
    pallas_call x3 -> x6, Pallas kernels: 30.4 us -> 43.7 us  [the longest x2 33.2 us: convolve(): pl.pallas_call(functools.partial(convolve_kernel, blocks, pairs), grid_sp...]
    unnamed x4 -> x22, local copies, waits for them, and re-layouts: 1.96 us -> 10.1 us
    ppermute x1 -> x61, waiting for transfers between devices: 0.01 us -> 5.01 us  [the longest x60 4.36 us: exchange(): lax.ppermute(slots[slot], 'seq', [(j, j ^ slot) for j in range(blocks)])]
    all_to_all x1 -> x0, starting transfers between devices: 3.91 us -> none  [kernel_local(): conv = lax.all_to_all(conv, 'seq', split_axis=0, concat_axis=0, tiled=True)]
    pallas_call x1, Pallas kernels: 5.31 us -> 1.98 us  [project_kept(): pl.pallas_call(kept_kernel, grid_spec=pltpu.PrefetchScalarGridSpec(num_sc...]
  transfers between devices with their start and end apart: 2 -> 61, of which waited for: 1 -> 4; matrix products, arithmetic and copies ran while one was open for 0% -> 0% of each run, Pallas kernels for 4% -> 24%
where the time goes in v1:
time: 174 us; the launch traced here: 173 us
  starting transfers between devices  110 us (63%)
  Pallas kernels  47.4 us (27%)
  local copies, waits for them, and re-layouts  10.1 us (6%)
  waiting for transfers between devices  5.01 us (3%)
    ppermute x60, starting transfers between devices, exchange(): lax.ppermute(slots[slot], 'seq', [(j, j ^ slot) for j in range(blocks)])  110 us
    pallas_call x2, Pallas kernels, convolve(): pl.pallas_call(functools.partial(convolve_kernel, blocks, pairs), grid_sp...  33.2 us
    unnamed x22, local copies, waits for them, and re-layouts  10.1 us
    pallas_call x2, Pallas kernels, gate_and_project(): pl.pallas_call(functools.partial(gate_kernel, blocks, joined), grid_spec=...  8.17 us
    ppermute x60, waiting for transfers between devices, exchange(): lax.ppermute(slots[slot], 'seq', [(j, j ^ slot) for j in range(blocks)])  4.36 us
  transfers between devices with their start and end apart: 61, of which 4 were waited for; matrix products, arithmetic and copies ran while one was open for 0% of the time, Pallas kernels for 24%

profile of v1, /device:TPU:0, one launch (start us, length us, event | category | flops | bytes accessed | tf_op | source)
XLA Modules:
  0.0 173.3 jit_solution(680633881547584177)
XLA Ops:
  4.6 3.0 %collective-permute-start.30 = (bf16[256,128]{1,0:T(8,128)(2,1)S(1)}, bf16[256,128]{1,0:T(8,128)(2,1)S(1)}, u32[]{:S(2)}, u32[]{:S(2)}) collective-permute-start(bf16[256,128]{1,0:T(8,128)(2,1)S(1)} %get-tuple-element.104), channel_id=1, source_target_pairs={{0,2},{2,0},{4,6},{6,4},{8,10},{10,8},{12,14},{14,12},{16,18},{18,... | collective-permute-start | bytes 196616 | tf_op jit(solution)/shard_map/ppermute | solution.py:500
  15.2 2.9 %collective-permute-start.37 = (bf16[256,128]{1,0:T(8,128)(2,1)S(1)}, bf16[256,128]{1,0:T(8,128)(2,1)S(1)}, u32[]{:S(2)}, u32[]{:S(2)}) collective-permute-start(bf16[256,128]{1,0:T(8,128)(2,1)S(1)} %get-tuple-element.111), channel_id=1, source_target_pairs={{0,16},{2,18},{4,20},{6,22},{8,24},{10,26},{12,28},{14,30},{16,0},... | collective-permute-start | bytes 196616 | tf_op jit(solution)/shard_map/ppermute | solution.py:500
  19.4 3.5 %collective-permute-start.39 = (bf16[256,128]{1,0:T(8,128)(2,1)S(1)}, bf16[256,128]{1,0:T(8,128)(2,1)S(1)}, u32[]{:S(2)}, u32[]{:S(2)}) collective-permute-start(bf16[256,128]{1,0:T(8,128)(2,1)S(1)} %get-tuple-element.113), channel_id=1, source_target_pairs={{0,20},{2,22},{4,16},{6,18},{8,28},{10,30},{12,24},{14,26},{16,4},... | collective-permute-start | bytes 196616 | tf_op jit(solution)/shard_map/ppermute | solution.py:500
  23.0 3.8 %collective-permute-start.41 = (bf16[256,128]{1,0:T(8,128)(2,1)S(1)}, bf16[256,128]{1,0:T(8,128)(2,1)S(1)}, u32[]{:S(2)}, u32[]{:S(2)}) collective-permute-start(bf16[256,128]{1,0:T(8,128)(2,1)S(1)} %get-tuple-element.115), channel_id=1, source_target_pairs={{0,24},{2,26},{4,28},{6,30},{8,16},{10,18},{12,20},{14,22},{16,8},... | collective-permute-start | bytes 196616 | tf_op jit(solution)/shard_map/ppermute | solution.py:500
  26.8 4.6 %collective-permute-start.42 = (bf16[256,128]{1,0:T(8,128)(2,1)S(1)}, bf16[256,128]{1,0:T(8,128)(2,1)S(1)}, u32[]{:S(2)}, u32[]{:S(2)}) collective-permute-start(bf16[256,128]{1,0:T(8,128)(2,1)S(1)} %get-tuple-element.116), channel_id=1, source_target_pairs={{0,26},{2,24},{4,30},{6,28},{8,18},{10,16},{12,22},{14,20},{16,10}... | collective-permute-start | bytes 196616 | tf_op jit(solution)/shard_map/ppermute | solution.py:500
  33.8 3.4 %collective-permute-start.44 = (bf16[256,128]{1,0:T(8,128)(2,1)S(1)}, bf16[256,128]{1,0:T(8,128)(2,1)S(1)}, u32[]{:S(2)}, u32[]{:S(2)}) collective-permute-start(bf16[256,128]{1,0:T(8,128)(2,1)S(1)} %get-tuple-element.118), channel_id=1, source_target_pairs={{0,30},{2,28},{4,26},{6,24},{8,22},{10,20},{12,18},{14,16},{16,14}... | collective-permute-start | bytes 196616 | tf_op jit(solution)/shard_map/ppermute | solution.py:500
  45.0 2.8 %collective-permute-start.6 = (bf16[256,128]{1,0:T(8,128)(2,1)S(1)}, bf16[256,128]{1,0:T(8,128)(2,1)S(1)}, u32[]{:S(2)}, u32[]{:S(2)}) collective-permute-start(bf16[256,128]{1,0:T(8,128)(2,1)S(1)} %get-tuple-element.78), channel_id=1, source_target_pairs={{0,14},{2,12},{4,10},{6,8},{8,6},{10,4},{12,2},{14,0},{16,30},{18,... | collective-permute-start | bytes 196616 | tf_op jit(solution)/shard_map/ppermute | solution.py:500
  64.2 3.2 %collective-permute-start.14 = (bf16[256,128]{1,0:T(8,128)(2,1)S(1)}, bf16[256,128]{1,0:T(8,128)(2,1)S(1)}, u32[]{:S(2)}, u32[]{:S(2)}) collective-permute-start(bf16[256,128]{1,0:T(8,128)(2,1)S(1)} %get-tuple-element.86), channel_id=1, source_target_pairs={{0,30},{2,28},{4,26},{6,24},{8,22},{10,20},{12,18},{14,16},{16,14}... | collective-permute-start | bytes 196616 | tf_op jit(solution)/shard_map/ppermute | solution.py:500
  67.5 3.4 %copy-done = bf16[8,2,512,512]{3,2,1,0:T(8,128)(2,1)S(1)} copy-done((bf16[8,2,512,512]{3,2,1,0:T(8,128)(2,1)S(1)}, bf16[8,2,512,512]{3,2,1,0:T(8,128)(2,1)}, u32[]{:S(2)}) %copy-start) | copy-done | bytes 8388632
  70.8 16.5 %long_convolution_0.1 = (bf16[128,128]{1,0:T(8,128)(2,1)S(1)}, bf16[128,128]{1,0:T(8,128)(2,1)S(1)}, bf16[128,128]{1,0:T(8,128)(2,1)S(1)}, bf16[128,128]{1,0:T(8...) custom-call(s32[2]{0:T(128)S(1)} %pad_add_fusion.me_ref, ...), custom_call_target="tpu_custom_call" | custom-call | flops 4294967296 | bytes 16777216 | tf_op jit(solution)/shard_map/long_convolution_0/pallas_call | solution.py:324
  91.0 3.0 %collective-permute-start.49 = (bf16[128,128]{1,0:T(8,128)(2,1)S(1)}, bf16[128,128]{1,0:T(8,128)(2,1)S(1)}, u32[]{:S(2)}, u32[]{:S(2)}) collective-permute-start(bf16[128,128]{1,0:T(8,128)(2,1)S(1)} %get-tuple-element.124), channel_id=1, source_target_pairs={{0,10},{2,8},{4,14},{6,12},{8,2},{10,0},{12,6},{14,4},{16,26},{18,... | collective-permute-start | bytes 98312 | tf_op jit(solution)/shard_map/ppermute | solution.py:500
  97.4 3.3 %collective-permute-start.53 = (bf16[128,128]{1,0:T(8,128)(2,1)S(1)}, bf16[128,128]{1,0:T(8,128)(2,1)S(1)}, u32[]{:S(2)}, u32[]{:S(2)}) collective-permute-start(bf16[128,128]{1,0:T(8,128)(2,1)S(1)} %get-tuple-element.128), channel_id=1, source_target_pairs={{0,18},{2,16},{4,22},{6,20},{8,26},{10,24},{12,30},{14,28},{16,2},... | collective-permute-start | bytes 98312 | tf_op jit(solution)/shard_map/ppermute | solution.py:500
  101.3 3.2 %collective-permute-start.55 = (bf16[128,128]{1,0:T(8,128)(2,1)S(1)}, bf16[128,128]{1,0:T(8,128)(2,1)S(1)}, u32[]{:S(2)}, u32[]{:S(2)}) collective-permute-start(bf16[128,128]{1,0:T(8,128)(2,1)S(1)} %get-tuple-element.130), channel_id=1, source_target_pairs={{0,22},{2,20},{4,18},{6,16},{8,30},{10,28},{12,26},{14,24},{16,6},... | collective-permute-start | bytes 98312 | tf_op jit(solution)/shard_map/ppermute | solution.py:500
  106.5 2.8 %collective-permute-start.57 = (bf16[128,128]{1,0:T(8,128)(2,1)S(1)}, bf16[128,128]{1,0:T(8,128)(2,1)S(1)}, u32[]{:S(2)}, u32[]{:S(2)}) collective-permute-start(bf16[128,128]{1,0:T(8,128)(2,1)S(1)} %get-tuple-element.132), channel_id=1, source_target_pairs={{0,26},{2,24},{4,30},{6,28},{8,18},{10,16},{12,22},{14,20},{16,10}... | collective-permute-start | bytes 98312 | tf_op jit(solution)/shard_map/ppermute | solution.py:500
  110.7 3.2 %collective-permute-start.59 = (bf16[128,128]{1,0:T(8,128)(2,1)S(1)}, bf16[128,128]{1,0:T(8,128)(2,1)S(1)}, u32[]{:S(2)}, u32[]{:S(2)}) collective-permute-start(bf16[128,128]{1,0:T(8,128)(2,1)S(1)} %get-tuple-element.134), channel_id=1, source_target_pairs={{0,30},{2,28},{4,26},{6,24},{8,22},{10,20},{12,18},{14,16},{16,14}... | collective-permute-start | bytes 98312 | tf_op jit(solution)/shard_map/ppermute | solution.py:500
  114.0 3.4 %copy-done.1 = bf16[8,2,512,512]{3,2,1,0:T(8,128)(2,1)S(1)} copy-done((bf16[8,2,512,512]{3,2,1,0:T(8,128)(2,1)S(1)}, bf16[8,2,512,512]{3,2,1,0:T(8,128)(2,1)}, u32[]{:S(2)}) %copy-start.1) | copy-done | bytes 8388632
  117.4 16.6 %long_convolution_1.1 = (bf16[128,128]{1,0:T(8,128)(2,1)S(1)}, bf16[128,128]{1,0:T(8,128)(2,1)S(1)}, bf16[128,128]{1,0:T(8,128)(2,1)S(1)}, bf16[128,128]{1,0:T(8...) custom-call(s32[2]{0:T(128)S(1)} %pad_add_fusion.me_ref, ...), custom_call_target="tpu_custom_call" | custom-call | flops 4294967296 | bytes 16777216 | tf_op jit(solution)/shard_map/long_convolution_1/pallas_call | solution.py:324
  137.6 3.0 %collective-permute-start.19 = (bf16[128,128]{1,0:T(8,128)(2,1)S(1)}, bf16[128,128]{1,0:T(8,128)(2,1)S(1)}, u32[]{:S(2)}, u32[]{:S(2)}) collective-permute-start(bf16[128,128]{1,0:T(8,128)(2,1)S(1)} %get-tuple-element.92), channel_id=1, source_target_pairs={{0,10},{2,8},{4,14},{6,12},{8,2},{10,0},{12,6},{14,4},{16,26},{18,... | collective-permute-start | bytes 98312 | tf_op jit(solution)/shard_map/ppermute | solution.py:500
  144.0 3.3 %collective-permute-start.23 = (bf16[128,128]{1,0:T(8,128)(2,1)S(1)}, bf16[128,128]{1,0:T(8,128)(2,1)S(1)}, u32[]{:S(2)}, u32[]{:S(2)}) collective-permute-start(bf16[128,128]{1,0:T(8,128)(2,1)S(1)} %get-tuple-element.96), channel_id=1, source_target_pairs={{0,18},{2,16},{4,22},{6,20},{8,26},{10,24},{12,30},{14,28},{16,2},... | collective-permute-start | bytes 98312 | tf_op jit(solution)/shard_map/ppermute | solution.py:500
  147.9 3.2 %collective-permute-start.25 = (bf16[128,128]{1,0:T(8,128)(2,1)S(1)}, bf16[128,128]{1,0:T(8,128)(2,1)S(1)}, u32[]{:S(2)}, u32[]{:S(2)}) collective-permute-start(bf16[128,128]{1,0:T(8,128)(2,1)S(1)} %get-tuple-element.98), channel_id=1, source_target_pairs={{0,22},{2,20},{4,18},{6,16},{8,30},{10,28},{12,26},{14,24},{16,6},... | collective-permute-start | bytes 98312 | tf_op jit(solution)/shard_map/ppermute | solution.py:500
  153.1 2.8 %collective-permute-start.27 = (bf16[128,128]{1,0:T(8,128)(2,1)S(1)}, bf16[128,128]{1,0:T(8,128)(2,1)S(1)}, u32[]{:S(2)}, u32[]{:S(2)}) collective-permute-start(bf16[128,128]{1,0:T(8,128)(2,1)S(1)} %get-tuple-element.100), channel_id=1, source_target_pairs={{0,26},{2,24},{4,30},{6,28},{8,18},{10,16},{12,22},{14,20},{16,10}... | collective-permute-start | bytes 98312 | tf_op jit(solution)/shard_map/ppermute | solution.py:500
  157.3 3.2 %collective-permute-start.29 = (bf16[128,128]{1,0:T(8,128)(2,1)S(1)}, bf16[128,128]{1,0:T(8,128)(2,1)S(1)}, u32[]{:S(2)}, u32[]{:S(2)}) collective-permute-start(bf16[128,128]{1,0:T(8,128)(2,1)S(1)} %get-tuple-element.102), channel_id=1, source_target_pairs={{0,30},{2,28},{4,26},{6,24},{8,22},{10,20},{12,18},{14,16},{16,14}... | collective-permute-start | bytes 98312 | tf_op jit(solution)/shard_map/ppermute | solution.py:500
  160.6 4.4 %gate_project_0.1.rest_21_.base_ref = f32[256,2048]{1,0:T(8,128)S(1)} custom-call(s32[2]{0:T(128)S(1)} %pad_add_fusion.me_ref, bf16[128,128]{1,0:T(8,128)(2,1)S(1)} %get-tuple-element.119.rest_0_, bf16[128,128]{1,0:T(8,128)(2,1)S(1)} %collective-permute-done.45.rest_1_, bf16[128,128]{1,0:T(8,128)(2,1)S(1)} %collective-permute-done.46.rest_2_, ...), custom_call_target="tpu_custom_call" | custom-call | flops 1073741824 | bytes 7340032 | tf_op jit(solution)/shard_map/gate_project_0/pallas_call | solution.py:419
  165.1 3.8 %gate_project_1.1 = (f32[256,1024]{1,0:T(8,128)S(1)}, bf16[256,1024]{1,0:T(8,128)(2,1)S(1)}) custom-call(s32[2]{0:T(128)S(1)} %pad_add_fusion.me_ref, bf16[128,128]{1,0:T(8,128)(2,1)S(1)} %get-tuple-element.87.rest_0_, bf16[128,128]{1,0:T(8,128)(2,1)S(1)} %collective-permute-done.15.rest_1_, bf16[128,128]{1,0:T(8,128)(2,1)S(1)} %collective-permute-done.16.rest_2_, ...), custom_call_target="tpu_custom_call" | custom-call | flops 536870912 | bytes 5242880 | tf_op jit(solution)/shard_map/gate_project_1/pallas_call | solution.py:419
  (130 shorter events, 66.5 us)
Async XLA Ops:
  15.2 11.6 %collective-permute-start.37 = (bf16[256,128]{1,0:T(8,128)(2,1)S(1)}, bf16[256,128]{1,0:T(8,128)(2,1)S(1)}, u32[]{:S(2)}, u32[]{:S(2)}) collective-permute-start(bf16[256,128]{1,0:T(8,128)(2,1)S(1)} %get-tuple-element.111), channel_id=1, source_target_pairs={{0,16},{2,18},{4,20},{6,22},{8,24},{10,26},{12,28},{14,30},{16,0},... | collective-permute-start | bytes 196616 | tf_op jit(solution)/shard_map/ppermute | solution.py:500
  18.1 13.4 %collective-permute-start.38 = (bf16[256,128]{1,0:T(8,128)(2,1)S(1)}, bf16[256,128]{1,0:T(8,128)(2,1)S(1)}, u32[]{:S(2)}, u32[]{:S(2)}) collective-permute-start(bf16[256,128]{1,0:T(8,128)(2,1)S(1)} %get-tuple-element.112), channel_id=1, source_target_pairs={{0,18},{2,16},{4,22},{6,20},{8,26},{10,24},{12,30},{14,28},{16,2},... | collective-permute-start | bytes 196616 | tf_op jit(solution)/shard_map/ppermute | solution.py:500
  19.4 14.5 %collective-permute-start.39 = (bf16[256,128]{1,0:T(8,128)(2,1)S(1)}, bf16[256,128]{1,0:T(8,128)(2,1)S(1)}, u32[]{:S(2)}, u32[]{:S(2)}) collective-permute-start(bf16[256,128]{1,0:T(8,128)(2,1)S(1)} %get-tuple-element.113), channel_id=1, source_target_pairs={{0,20},{2,22},{4,16},{6,18},{8,28},{10,30},{12,24},{14,26},{16,4},... | collective-permute-start | bytes 196616 | tf_op jit(solution)/shard_map/ppermute | solution.py:500
  22.9 15.5 %collective-permute-start.40 = (bf16[256,128]{1,0:T(8,128)(2,1)S(1)}, bf16[256,128]{1,0:T(8,128)(2,1)S(1)}, u32[]{:S(2)}, u32[]{:S(2)}) collective-permute-start(bf16[256,128]{1,0:T(8,128)(2,1)S(1)} %get-tuple-element.114), channel_id=1, source_target_pairs={{0,22},{2,20},{4,18},{6,16},{8,30},{10,28},{12,26},{14,24},{16,6},... | collective-permute-start | bytes 196616 | tf_op jit(solution)/shard_map/ppermute | solution.py:500
  23.0 16.0 %collective-permute-start.41 = (bf16[256,128]{1,0:T(8,128)(2,1)S(1)}, bf16[256,128]{1,0:T(8,128)(2,1)S(1)}, u32[]{:S(2)}, u32[]{:S(2)}) collective-permute-start(bf16[256,128]{1,0:T(8,128)(2,1)S(1)} %get-tuple-element.115), channel_id=1, source_target_pairs={{0,24},{2,26},{4,28},{6,30},{8,16},{10,18},{12,20},{14,22},{16,8},... | collective-permute-start | bytes 196616 | tf_op jit(solution)/shard_map/ppermute | solution.py:500
  26.8 13.8 %collective-permute-start.42 = (bf16[256,128]{1,0:T(8,128)(2,1)S(1)}, bf16[256,128]{1,0:T(8,128)(2,1)S(1)}, u32[]{:S(2)}, u32[]{:S(2)}) collective-permute-start(bf16[256,128]{1,0:T(8,128)(2,1)S(1)} %get-tuple-element.116), channel_id=1, source_target_pairs={{0,26},{2,24},{4,30},{6,28},{8,18},{10,16},{12,22},{14,20},{16,10}... | collective-permute-start | bytes 196616 | tf_op jit(solution)/shard_map/ppermute | solution.py:500
  45.0 10.5 %collective-permute-start.6 = (bf16[256,128]{1,0:T(8,128)(2,1)S(1)}, bf16[256,128]{1,0:T(8,128)(2,1)S(1)}, u32[]{:S(2)}, u32[]{:S(2)}) collective-permute-start(bf16[256,128]{1,0:T(8,128)(2,1)S(1)} %get-tuple-element.78), channel_id=1, source_target_pairs={{0,14},{2,12},{4,10},{6,8},{8,6},{10,4},{12,2},{14,0},{16,30},{18,... | collective-permute-start | bytes 196616 | tf_op jit(solution)/shard_map/ppermute | solution.py:500
  48.8 13.1 %collective-permute-start.8 = (bf16[256,128]{1,0:T(8,128)(2,1)S(1)}, bf16[256,128]{1,0:T(8,128)(2,1)S(1)}, u32[]{:S(2)}, u32[]{:S(2)}) collective-permute-start(bf16[256,128]{1,0:T(8,128)(2,1)S(1)} %get-tuple-element.80), channel_id=1, source_target_pairs={{0,18},{2,16},{4,22},{6,20},{8,26},{10,24},{12,30},{14,28},{16,2},... | collective-permute-start | bytes 196616 | tf_op jit(solution)/shard_map/ppermute | solution.py:500
  50.7 13.5 %collective-permute-start.9 = (bf16[256,128]{1,0:T(8,128)(2,1)S(1)}, bf16[256,128]{1,0:T(8,128)(2,1)S(1)}, u32[]{:S(2)}, u32[]{:S(2)}) collective-permute-start(bf16[256,128]{1,0:T(8,128)(2,1)S(1)} %get-tuple-element.81), channel_id=1, source_target_pairs={{0,20},{2,22},{4,16},{6,18},{8,28},{10,30},{12,24},{14,26},{16,4},... | collective-permute-start | bytes 196616 | tf_op jit(solution)/shard_map/ppermute | solution.py:500
  52.7 34.7 %collective-permute-start.10 = (bf16[256,128]{1,0:T(8,128)(2,1)S(1)}, bf16[256,128]{1,0:T(8,128)(2,1)S(1)}, u32[]{:S(2)}, u32[]{:S(2)}) collective-permute-start(bf16[256,128]{1,0:T(8,128)(2,1)S(1)} %get-tuple-element.82), channel_id=1, source_target_pairs={{0,22},{2,20},{4,18},{6,16},{8,30},{10,28},{12,26},{14,24},{16,6},... | collective-permute-start | bytes 196616 | tf_op jit(solution)/shard_map/ppermute | solution.py:500
  55.5 33.5 %collective-permute-start.11 = (bf16[256,128]{1,0:T(8,128)(2,1)S(1)}, bf16[256,128]{1,0:T(8,128)(2,1)S(1)}, u32[]{:S(2)}, u32[]{:S(2)}) collective-permute-start(bf16[256,128]{1,0:T(8,128)(2,1)S(1)} %get-tuple-element.83), channel_id=1, source_target_pairs={{0,24},{2,26},{4,28},{6,30},{8,16},{10,18},{12,20},{14,22},{16,8},... | collective-permute-start | bytes 196616 | tf_op jit(solution)/shard_map/ppermute | solution.py:500
  58.3 31.4 %collective-permute-start.12 = (bf16[256,128]{1,0:T(8,128)(2,1)S(1)}, bf16[256,128]{1,0:T(8,128)(2,1)S(1)}, u32[]{:S(2)}, u32[]{:S(2)}) collective-permute-start(bf16[256,128]{1,0:T(8,128)(2,1)S(1)} %get-tuple-element.84), channel_id=1, source_target_pairs={{0,26},{2,24},{4,30},{6,28},{8,18},{10,16},{12,22},{14,20},{16,10}... | collective-permute-start | bytes 196616 | tf_op jit(solution)/shard_map/ppermute | solution.py:500
  61.9 29.1 %collective-permute-start.13 = (bf16[256,128]{1,0:T(8,128)(2,1)S(1)}, bf16[256,128]{1,0:T(8,128)(2,1)S(1)}, u32[]{:S(2)}, u32[]{:S(2)}) collective-permute-start(bf16[256,128]{1,0:T(8,128)(2,1)S(1)} %get-tuple-element.85), channel_id=1, source_target_pairs={{0,28},{2,30},{4,24},{6,26},{8,20},{10,22},{12,16},{14,18},{16,12}... | collective-permute-start | bytes 196616 | tf_op jit(solution)/shard_map/ppermute | solution.py:500
  64.2 26.7 %collective-permute-start.14 = (bf16[256,128]{1,0:T(8,128)(2,1)S(1)}, bf16[256,128]{1,0:T(8,128)(2,1)S(1)}, u32[]{:S(2)}, u32[]{:S(2)}) collective-permute-start(bf16[256,128]{1,0:T(8,128)(2,1)S(1)} %get-tuple-element.86), channel_id=1, source_target_pairs={{0,30},{2,28},{4,26},{6,24},{8,22},{10,20},{12,18},{14,16},{16,14}... | collective-permute-start | bytes 196616 | tf_op jit(solution)/shard_map/ppermute | solution.py:500
  97.4 11.9 %collective-permute-start.53 = (bf16[128,128]{1,0:T(8,128)(2,1)S(1)}, bf16[128,128]{1,0:T(8,128)(2,1)S(1)}, u32[]{:S(2)}, u32[]{:S(2)}) collective-permute-start(bf16[128,128]{1,0:T(8,128)(2,1)S(1)} %get-tuple-element.128), channel_id=1, source_target_pairs={{0,18},{2,16},{4,22},{6,20},{8,26},{10,24},{12,30},{14,28},{16,2},... | collective-permute-start | bytes 98312 | tf_op jit(solution)/shard_map/ppermute | solution.py:500
  101.3 32.7 %collective-permute-start.55 = (bf16[128,128]{1,0:T(8,128)(2,1)S(1)}, bf16[128,128]{1,0:T(8,128)(2,1)S(1)}, u32[]{:S(2)}, u32[]{:S(2)}) collective-permute-start(bf16[128,128]{1,0:T(8,128)(2,1)S(1)} %get-tuple-element.130), channel_id=1, source_target_pairs={{0,22},{2,20},{4,18},{6,16},{8,30},{10,28},{12,26},{14,24},{16,6},... | collective-permute-start | bytes 98312 | tf_op jit(solution)/shard_map/ppermute | solution.py:500
  104.5 31.1 %collective-permute-start.56 = (bf16[128,128]{1,0:T(8,128)(2,1)S(1)}, bf16[128,128]{1,0:T(8,128)(2,1)S(1)}, u32[]{:S(2)}, u32[]{:S(2)}) collective-permute-start(bf16[128,128]{1,0:T(8,128)(2,1)S(1)} %get-tuple-element.131), channel_id=1, source_target_pairs={{0,24},{2,26},{4,28},{6,30},{8,16},{10,18},{12,20},{14,22},{16,8},... | collective-permute-start | bytes 98312 | tf_op jit(solution)/shard_map/ppermute | solution.py:500
  106.5 29.8 %collective-permute-start.57 = (bf16[128,128]{1,0:T(8,128)(2,1)S(1)}, bf16[128,128]{1,0:T(8,128)(2,1)S(1)}, u32[]{:S(2)}, u32[]{:S(2)}) collective-permute-start(bf16[128,128]{1,0:T(8,128)(2,1)S(1)} %get-tuple-element.132), channel_id=1, source_target_pairs={{0,26},{2,24},{4,30},{6,28},{8,18},{10,16},{12,22},{14,20},{16,10}... | collective-permute-start | bytes 98312 | tf_op jit(solution)/shard_map/ppermute | solution.py:500
  109.3 28.3 %collective-permute-start.58 = (bf16[128,128]{1,0:T(8,128)(2,1)S(1)}, bf16[128,128]{1,0:T(8,128)(2,1)S(1)}, u32[]{:S(2)}, u32[]{:S(2)}) collective-permute-start(bf16[128,128]{1,0:T(8,128)(2,1)S(1)} %get-tuple-element.133), channel_id=1, source_target_pairs={{0,28},{2,30},{4,24},{6,26},{8,20},{10,22},{12,16},{14,18},{16,12}... | collective-permute-start | bytes 98312 | tf_op jit(solution)/shard_map/ppermute | solution.py:500
  110.7 26.8 %collective-permute-start.59 = (bf16[128,128]{1,0:T(8,128)(2,1)S(1)}, bf16[128,128]{1,0:T(8,128)(2,1)S(1)}, u32[]{:S(2)}, u32[]{:S(2)}) collective-permute-start(bf16[128,128]{1,0:T(8,128)(2,1)S(1)} %get-tuple-element.134), channel_id=1, source_target_pairs={{0,30},{2,28},{4,26},{6,24},{8,22},{10,20},{12,18},{14,16},{16,14}... | collective-permute-start | bytes 98312 | tf_op jit(solution)/shard_map/ppermute | solution.py:500
  144.0 11.9 %collective-permute-start.23 = (bf16[128,128]{1,0:T(8,128)(2,1)S(1)}, bf16[128,128]{1,0:T(8,128)(2,1)S(1)}, u32[]{:S(2)}, u32[]{:S(2)}) collective-permute-start(bf16[128,128]{1,0:T(8,128)(2,1)S(1)} %get-tuple-element.96), channel_id=1, source_target_pairs={{0,18},{2,16},{4,22},{6,20},{8,26},{10,24},{12,30},{14,28},{16,2},... | collective-permute-start | bytes 98312 | tf_op jit(solution)/shard_map/ppermute | solution.py:500
  147.9 17.1 %collective-permute-start.25 = (bf16[128,128]{1,0:T(8,128)(2,1)S(1)}, bf16[128,128]{1,0:T(8,128)(2,1)S(1)}, u32[]{:S(2)}, u32[]{:S(2)}) collective-permute-start(bf16[128,128]{1,0:T(8,128)(2,1)S(1)} %get-tuple-element.98), channel_id=1, source_target_pairs={{0,22},{2,20},{4,18},{6,16},{8,30},{10,28},{12,26},{14,24},{16,6},... | collective-permute-start | bytes 98312 | tf_op jit(solution)/shard_map/ppermute | solution.py:500
  151.1 13.9 %collective-permute-start.26 = (bf16[128,128]{1,0:T(8,128)(2,1)S(1)}, bf16[128,128]{1,0:T(8,128)(2,1)S(1)}, u32[]{:S(2)}, u32[]{:S(2)}) collective-permute-start(bf16[128,128]{1,0:T(8,128)(2,1)S(1)} %get-tuple-element.99), channel_id=1, source_target_pairs={{0,24},{2,26},{4,28},{6,30},{8,16},{10,18},{12,20},{14,22},{16,8},... | collective-permute-start | bytes 98312 | tf_op jit(solution)/shard_map/ppermute | solution.py:500
  153.1 12.0 %collective-permute-start.27 = (bf16[128,128]{1,0:T(8,128)(2,1)S(1)}, bf16[128,128]{1,0:T(8,128)(2,1)S(1)}, u32[]{:S(2)}, u32[]{:S(2)}) collective-permute-start(bf16[128,128]{1,0:T(8,128)(2,1)S(1)} %get-tuple-element.100), channel_id=1, source_target_pairs={{0,26},{2,24},{4,30},{6,28},{8,18},{10,16},{12,22},{14,20},{16,10}... | collective-permute-start | bytes 98312 | tf_op jit(solution)/shard_map/ppermute | solution.py:500
  (48 other events, 609.3 us)

commit v2 on v1

--- a/solution.py
+++ b/solution.py
@@ -114,18 +114,16 @@
 @functools.lru_cache(maxsize=None)
 def transform_tables(length):
     inner = length // RADIX
-    q = np.arange(RADIX)[:, None, None]
-    k = np.arange(inner)[None, :, None]
-    m = np.arange(inner)[None, None, :]
-    phase = ((RADIX * m + q) * (4 * k + 1)) % (4 * length)
-    angles = phase * (TWO_PI / (4 * length))
-    table = np.concatenate([np.cos(angles), -np.sin(angles)], axis=1)
-    forward = np.concatenate(split_table(table), axis=2)
-    backward = np.concatenate(split_table(table.transpose(0, 2, 1) / length), axis=1)
-    return tuple(
-        np.ascontiguousarray(part.reshape(2, RADIX // 2, *part.shape[1:]).swapaxes(0, 1))
-        for part in (forward, backward)
-    )
+    k = np.arange(inner)[:, None]
+    m = np.arange(inner)[None, :]
+    angles = (RADIX * m * (4 * k + 1)) % (4 * length) * (TWO_PI / (4 * length))
+    table = np.concatenate([np.cos(angles), -np.sin(angles)], axis=0)
+    forward = np.concatenate(split_table(table), axis=1)
+    backward = np.concatenate(split_table(table.T / length), axis=0)
+    turns = (np.arange(RADIX)[None, :] * (4 * k + 1)) % (4 * length) * (TWO_PI / (4 * length))
+    turns = np.concatenate([np.cos(turns), np.sin(turns)], axis=1)
+    turns = np.pad(turns, ((0, 0), (0, LANES - 2 * RADIX))).astype(np.float32)
+    return forward, backward, turns
 
 
 @functools.lru_cache(maxsize=None)
@@ -196,172 +194,217 @@
     return pltpu.roll(block, HALF, 1)
 
 
-def arrange_kernel(blocks, me_ref, order_ref, values_ref, taps_ref, *rest):
-    outs, packed = rest[:blocks], rest[blocks]
-    me = me_ref[0]
-    order = order_ref[...]
-    left = left_lanes(order.shape[0])
-    for pair in range(blocks // 2):
-        lanes = pl.ds(pair * LANES, LANES)
-        both = jnp.concatenate([values_ref[:, lanes], taps_ref[:, lanes]], axis=1)
-        moved = jnp.dot(order, both, preferred_element_type=jnp.float32)
-        value, taps = moved[:, :LANES], moved[:, LANES:]
-        packed[2 * pair] = jnp.where(left, value, swap_halves(taps)).astype(jnp.bfloat16)
-        packed[2 * pair + 1] = jnp.where(left, swap_halves(value), taps).astype(jnp.bfloat16)
-    for slot in range(blocks):
-        outs[slot][...] = packed[me ^ slot]
-
-
-def arrange(me, values, taps, blocks, chunk):
+def arrange_kernel(blocks, pieces, slotted, chunk, me_ref, order_hbm, values_hbm, taps_hbm, *rest):
+    outs = rest[: blocks if slotted else 1]
+    order_ref, values_ref, taps_ref, packed, sems = rest[len(outs) :]
+    wide = values_ref.shape[1]
+    piece = wide // pieces
+    loads = [pltpu.make_async_copy(order_hbm, order_ref, sems.at[2 * pieces])]
+    for part in range(pieces):
+        lanes = pl.ds(chunk * wide + part * piece, piece)
+        to = pl.ds(part * piece, piece)
+        loads.append(pltpu.make_async_copy(values_hbm.at[:, lanes], values_ref.at[:, to], sems.at[2 * part]))
+        loads.append(pltpu.make_async_copy(taps_hbm.at[:, lanes], taps_ref.at[:, to], sems.at[2 * part + 1]))
+    for load in loads:
+        load.start()
+    loads[0].wait()
+    left = left_lanes(order_ref.shape[0])
+    target = packed if slotted else outs[0]
+    for part in range(pieces):
+        loads[2 * part + 1].wait()
+        loads[2 * part + 2].wait()
+        for pair in range(part * piece // LANES, (part + 1) * piece // LANES):
+            lanes = pl.ds(pair * LANES, LANES)
+            both = jnp.concatenate([values_ref[:, lanes], taps_ref[:, lanes]], axis=1)
+            moved = jnp.dot(order_ref[...], both, preferred_element_type=jnp.float32)
+            value, taps = moved[:, :LANES], moved[:, LANES:]
+            target[2 * pair] = jnp.where(left, value, swap_halves(taps)).astype(jnp.bfloat16)
+            target[2 * pair + 1] = jnp.where(left, swap_halves(value), taps).astype(jnp.bfloat16)
+    if slotted:
+        me = me_ref[0]
+        for slot in range(blocks):
+            outs[slot][...] = packed[me ^ slot]
+
+
+def arrange(me, values, taps, blocks, chunk, slotted):
     rows = values.shape[0]
     wide = blocks * HALF
+    pieces = 4
+    if slotted:
+        out_shape = [jax.ShapeDtypeStruct((rows, LANES), jnp.bfloat16)] * blocks
+    else:
+        out_shape = [jax.ShapeDtypeStruct((blocks, rows, LANES), jnp.bfloat16)]
     return pl.pallas_call(
-        functools.partial(arrange_kernel, blocks),
-        grid_spec=pltpu.PrefetchScalarGridSpec(
-            num_scalar_prefetch=1,
-            grid=(1,),
-            in_specs=[
-                pl.BlockSpec((rows, rows), lambda i, me: (0, 0)),
-                pl.BlockSpec((rows, wide), lambda i, me: (0, chunk)),
-                pl.BlockSpec((rows, wide), lambda i, me: (0, chunk)),
-            ],
-            out_specs=[pl.BlockSpec((rows, LANES), lambda i, me: (0, 0))] * blocks,
-            scratch_shapes=[pltpu.VMEM((blocks, rows, LANES), jnp.bfloat16)],
-        ),
-        out_shape=[jax.ShapeDtypeStruct((rows, LANES), jnp.bfloat16)] * blocks,
+        functools.partial(arrange_kernel, blocks, pieces, slotted, chunk),
+        in_specs=[pl.BlockSpec(memory_space=pltpu.SMEM)] + [pl.BlockSpec(memory_space=pltpu.HBM)] * 3,
+        out_specs=[pl.BlockSpec(memory_space=pltpu.VMEM)] * len(out_shape),
+        out_shape=out_shape,
+        scratch_shapes=[
+            pltpu.VMEM((rows, rows), jnp.bfloat16),
+            pltpu.VMEM((rows, wide), jnp.bfloat16),
+            pltpu.VMEM((rows, wide), jnp.bfloat16),
+            pltpu.VMEM((blocks, rows, LANES) if slotted else (16, LANES), jnp.bfloat16),
+            pltpu.SemaphoreType.DMA((2 * pieces + 1,)),
+        ],
         compiler_params=pltpu.CompilerParams(vmem_limit_bytes=VMEM_BYTES),
         name=f"arrange_{chunk}",
     )(me, jnp.asarray(row_order(rows)), values, taps)
 
 
-def convolve_kernel(blocks, pairs, me_ref, *rest):
-    slots = rest[:blocks]
-    forward_ref, backward_ref = rest[blocks : blocks + 2]
-    outs = rest[blocks + 2 : 2 * blocks + 2]
-    streams, spectra, signals = rest[2 * blocks + 2 :]
+def turned(point, turns, q, sign):
+    if q == 0:
+        return point
+    re, im = point
+    cos, sin = turns[0][q], turns[1][q]
+    if sign < 0:
+        return (re * cos + im * sin, im * cos - re * sin)
+    return (re * cos - im * sin, im * cos + re * sin)
+
+
+def spread(turns_ref, rows):
+    block = turns_ref[rows]
+    columns = [jnp.broadcast_to(block[:, i : i + 1], block.shape) for i in range(2 * RADIX)]
+    return columns[:RADIX], columns[RADIX:]
+
+
+def convolve_kernel(blocks, slots_in, slots_out, me_ref, *rest):
+    count_in = blocks if slots_in else 1
+    count_out = blocks if slots_out else 1
+    slots = rest[:count_in]
+    forward_ref, backward_ref, turns_ref = rest[count_in : count_in + 3]
+    outs = rest[count_in + 3 : count_in + 3 + count_out]
+    streams, spectra, signals = rest[count_in + 3 + count_out :]
     me = me_ref[0]
-    phase, step = pl.program_id(0), pl.program_id(1)
     chunk = streams.shape[2]
     inner = blocks * chunk
     part_rows = inner // 2
-
-    @pl.when((phase == 0) & (step == 0))
-    def _():
+    pairs = RADIX // 2
+    if slots_in:
         for slot in range(blocks):
             streams[me ^ slot] = slots[slot][...].reshape(RADIX, chunk, LANES)
 
-    @pl.when(phase == 0)
-    def _():
-        for part in range(2):
-            q = step + part * pairs
-            stream = streams[:, pl.ds(q, 1)].reshape(inner, LANES)
-            spectra[q] = jnp.dot(
-                forward_ref[0, part],
-                jnp.concatenate([stream, stream], axis=0),
-                preferred_element_type=jnp.float32,
-            )
-
-    @pl.when((phase == 0) & (step == pairs - 1))
-    def _():
-        left = left_lanes(8)
-
-        def rows_step(index, carry):
-            starts = [pl.multiple_of(base + index * 8, 8) for base in range(0, 2 * inner, part_rows)]
-            first_re, second_re, first_im, second_im = [pl.ds(start, 8) for start in starts]
-            first = sixteen_points([(spectra[q, first_re], spectra[q, first_im]) for q in range(RADIX)], -1)
-            second = sixteen_points([(spectra[q, second_re], spectra[q, second_im]) for q in range(RADIX)], -1)
-            product = []
-            for one, two in zip(first, second):
-                a = [jnp.where(left, x, y) for x, y in zip(one, two)]
-                b = [swap_halves(jnp.where(left, y, x)) for x, y in zip(one, two)]
-                product.append((a[0] * b[0] - a[1] * b[1], a[0] * b[1] + a[1] * b[0]))
-            back = sixteen_points(product, 1)
-            for q in range(RADIX):
-                spectra[q, first_re] = back[q][0]
-                spectra[q, first_im] = back[q][1]
-            return carry
-
-        lax.fori_loop(0, part_rows // 8, rows_step, 0)
-
-    @pl.when(phase == 1)
-    def _():
-        left = left_lanes(part_rows)
-        sides = []
-        for part in range(2):
-            q = step + part * pairs
+    def stream_of(q):
+        if slots_in:
+            return streams[:, pl.ds(q, 1)].reshape(inner, LANES)
+        return slots[0][:, pl.ds(pl.multiple_of(q * chunk, chunk), chunk)].reshape(inner, LANES)
+
+    def forward_step(pair, carry):
+        both = jnp.concatenate([stream_of(2 * pair), stream_of(2 * pair + 1)], axis=1)
+        result = jnp.dot(
+            forward_ref[...], jnp.concatenate([both, both], axis=0), preferred_element_type=jnp.float32
+        )
+        spectra[2 * pair] = result[:, :LANES]
+        spectra[2 * pair + 1] = result[:, LANES:]
+        return carry
+
+    lax.fori_loop(0, pairs, forward_step, 0)
+    left = left_lanes(8)
+
+    def rows_step(index, carry):
+        starts = [pl.multiple_of(base + index * 8, 8) for base in range(0, 2 * inner, part_rows)]
+        first_re, second_re, first_im, second_im = [pl.ds(start, 8) for start in starts]
+        first_turns = spread(turns_ref, first_re)
+        second_turns = spread(turns_ref, second_re)
+        first = sixteen_points(
+            [turned((spectra[q, first_re], spectra[q, first_im]), first_turns, q, -1) for q in range(RADIX)], -1
+        )
+        second = sixteen_points(
+            [turned((spectra[q, second_re], spectra[q, second_im]), second_turns, q, -1) for q in range(RADIX)], -1
+        )
+        product = []
+        for one, two in zip(first, second):
+            a = [jnp.where(left, x, y) for x, y in zip(one, two)]
+            b = [swap_halves(jnp.where(left, y, x)) for x, y in zip(one, two)]
+            product.append((a[0] * b[0] - a[1] * b[1], a[0] * b[1] + a[1] * b[0]))
+        back = sixteen_points(product, 1)
+        mixed = [
+            [jnp.where(left, x, y) for x, y in zip(one, two)] for one, two in zip(first_turns, second_turns)
+        ]
+        for q in range(RADIX):
+            spectra[q, first_re], spectra[q, first_im] = turned(back[q], mixed, q, 1)
+        return carry
+
+    lax.fori_loop(0, part_rows // 8, rows_step, 0)
+    left_part = left_lanes(part_rows)
+    left_inner = left_lanes(inner)
+
+    def backward_step(pair, carry):
+        columns = []
+        for q in (pair, pair + pairs):
             pieces = []
             for base in (0, inner):
                 points = spectra[q, pl.ds(base, part_rows)]
                 high = points.astype(jnp.bfloat16).astype(jnp.float32)
                 low = points - high
-                pieces.append(jnp.where(left, high, swap_halves(low)).astype(jnp.bfloat16))
-                pieces.append(jnp.where(left, swap_halves(high), low).astype(jnp.bfloat16))
-            terms = jnp.dot(
-                backward_ref[0, part],
-                jnp.concatenate(pieces, axis=0),
-                preferred_element_type=jnp.float32,
-            )
-            total = terms[:inner] + terms[inner:]
-            sides.append(total + swap_halves(total))
-        signal = jnp.where(left_lanes(inner), sides[0], sides[1]).astype(jnp.bfloat16)
-        signals[:, pl.ds(step, 1)] = signal.reshape(blocks, 1, chunk, LANES)
-
-    @pl.when((phase == 1) & (step == pairs - 1))
-    def _():
+                pieces.append(jnp.where(left_part, high, swap_halves(low)).astype(jnp.bfloat16))
+                pieces.append(jnp.where(left_part, swap_halves(high), low).astype(jnp.bfloat16))
+            columns.append(jnp.concatenate(pieces, axis=0))
+        terms = jnp.dot(
+            backward_ref[...], jnp.concatenate(columns, axis=1), preferred_element_type=jnp.float32
+        )
+        total = terms[:inner] + terms[inner:]
+        sides = [part + swap_halves(part) for part in (total[:, :LANES], total[:, LANES:])]
+        signal = jnp.where(left_inner, *sides).astype(jnp.bfloat16).reshape(blocks, chunk, LANES)
+        if slots_out:
+            signals[:, pl.ds(pair, 1)] = signal[:, None]
+        else:
+            outs[0][:, pl.ds(pl.multiple_of(pair * chunk, chunk), chunk)] = signal
+        return carry
+
+    lax.fori_loop(0, pairs, backward_step, 0)
+    if slots_out:
         for slot in range(blocks):
             outs[slot][...] = signals[me ^ slot].reshape(pairs * chunk, LANES)
 
 
-def convolve(me, slots, blocks, chunk_id):
-    rows = slots[0].shape[0]
+def convolve(me, slots, blocks, chunk_id, slots_out):
+    slots_in = len(slots) > 1
+    rows = slots[0].shape[-2]
     length = blocks * rows
     chunk = rows // RADIX
     inner = length // RADIX
     pairs = RADIX // 2
-    forward, backward = transform_tables(length)
-    whole = lambda p, i, me: (0, 0)
-    table = (1, 2, 2 * inner, 2 * inner)
+    if slots_out:
+        out_shape = [jax.ShapeDtypeStruct((pairs * chunk, LANES), jnp.bfloat16)] * blocks
+    else:
+        out_shape = [jax.ShapeDtypeStruct((blocks, pairs * chunk, LANES), jnp.bfloat16)]
     return pl.pallas_call(
-        functools.partial(convolve_kernel, blocks, pairs),
-        grid_spec=pltpu.PrefetchScalarGridSpec(
-            num_scalar_prefetch=1,
-            grid=(2, pairs),
-            in_specs=[pl.BlockSpec((rows, LANES), whole)] * blocks
-            + [
-                pl.BlockSpec(table, lambda p, i, me: (i * (1 - p) + (pairs - 1) * p, 0, 0, 0)),
-                pl.BlockSpec(table, lambda p, i, me: (i * p, 0, 0, 0)),
-            ],
-            out_specs=[pl.BlockSpec((pairs * chunk, LANES), whole)] * blocks,
-            scratch_shapes=[
-                pltpu.VMEM((blocks, RADIX, chunk, LANES), jnp.bfloat16),
-                pltpu.VMEM((RADIX, 2 * inner, LANES), jnp.float32),
-                pltpu.VMEM((blocks, pairs, chunk, LANES), jnp.bfloat16),
-            ],
-        ),
-        out_shape=[jax.ShapeDtypeStruct((pairs * chunk, LANES), jnp.bfloat16)] * blocks,
-        compiler_params=pltpu.CompilerParams(vmem_limit_bytes=VMEM_BYTES),
+        functools.partial(convolve_kernel, blocks, slots_in, slots_out),
+        in_specs=[pl.BlockSpec(memory_space=pltpu.SMEM)]
+        + [pl.BlockSpec(memory_space=pltpu.VMEM)] * (len(slots) + 3),
+        out_specs=[pl.BlockSpec(memory_space=pltpu.VMEM)] * len(out_shape),
+        out_shape=out_shape,
+        scratch_shapes=[
+            pltpu.VMEM((blocks, RADIX, chunk, LANES) if slots_in else (1, 1, chunk, LANES), jnp.bfloat16),
+            pltpu.VMEM((RADIX, 2 * inner, LANES), jnp.float32),
+            pltpu.VMEM((blocks, pairs, chunk, LANES) if slots_out else (1, 1, chunk, LANES), jnp.bfloat16),
+        ],
+        compiler_params=pltpu.CompilerParams(vmem_limit_bytes=SMALL_BYTES),
         cost_estimate=pl.CostEstimate(
-            flops=2 * RADIX * 2 * (2 * inner) * (2 * inner) * LANES * 2,
-            bytes_accessed=RADIX * 2 * (2 * inner) ** 2 * 2,
-            transcendentals=0,
+            flops=3 * 10**9, bytes_accessed=24 * 10**6, transcendentals=0
         ),
         name=f"long_convolution_{chunk_id}",
-    )(me, *slots, jnp.asarray(forward), jnp.asarray(backward))
-
-
-def gate_kernel(blocks, joined, me_ref, *rest):
-    slots = rest[:blocks]
+    )(me, *slots, *(jnp.asarray(table) for table in transform_tables(length)))
+
+
+def gate_kernel(count, joined, me_ref, *rest):
+    slots, rest = rest[:count], rest[count:]
     if joined:
-        order_ref, gates_ref, values_ref, skip_ref, weight_ref, base_ref, out_ref, gated_ref, parts = rest[blocks:]
+        order_ref, gates_ref, values_ref, skip_ref, weight_ref, base_ref, out_ref, gated_ref, parts = rest
     else:
-        order_ref, gates_ref, values_ref, skip_ref, weight_ref, out_ref, parts = rest[blocks:]
+        order_ref, gates_ref, values_ref, skip_ref, weight_ref, out_ref, parts = rest
     me = me_ref[0]
     step = pl.program_id(0)
 
-    @pl.when(step == 0)
-    def _():
-        for slot in range(blocks):
-            parts[me ^ slot] = slots[slot][...]
+    if count > 1:
+
+        @pl.when(step == 0)
+        def _():
+            for slot in range(count):
+                parts[me ^ slot] = slots[slot][...]
+
+    else:
+        parts = slots[0]
 
     wide = gates_ref.shape[1]
     pairs = wide // LANES
@@ -392,14 +435,16 @@
 
 
 def gate_and_project(me, slots, gates, values, skip_gain, out_weight, chunk, base=None):
-    blocks = len(slots)
+    count = len(slots)
+    blocks = lax.axis_size("seq")
+    block_shape = slots[0].shape[-2:]
     rows = gates.shape[0]
     features = out_weight.shape[1]
     steps = 4
     wide = blocks * HALF // steps
     joined = base is not None
     taken = features // 2 if joined else features
-    in_specs = [pl.BlockSpec(slots[0].shape, lambda i, me: (0, 0))] * blocks + [
+    in_specs = [pl.BlockSpec(slot.shape, lambda i, me, rank=slot.ndim: (0,) * rank) for slot in slots] + [
         pl.BlockSpec((rows, rows), lambda i, me: (0, 0)),
         pl.BlockSpec((rows, wide), lambda i, me: (0, chunk * steps + i)),
         pl.BlockSpec((rows, wide), lambda i, me: (0, chunk * steps + i)),
@@ -417,13 +462,13 @@
     else:
         in_specs.append(pl.BlockSpec((wide, taken), lambda i, me: (chunk * steps + i, 0)))
     return pl.pallas_call(
-        functools.partial(gate_kernel, blocks, joined),
+        functools.partial(gate_kernel, count, joined),
         grid_spec=pltpu.PrefetchScalarGridSpec(
             num_scalar_prefetch=1,
             grid=(steps,),
             in_specs=in_specs,
             out_specs=out_specs,
-            scratch_shapes=[pltpu.VMEM((blocks, *slots[0].shape), jnp.bfloat16)],
+            scratch_shapes=[pltpu.VMEM((blocks if count > 1 else 1, *block_shape), jnp.bfloat16)],
         ),
         out_shape=out_shape,
         compiler_params=pltpu.CompilerParams(vmem_limit_bytes=SMALL_BYTES),
@@ -496,18 +541,27 @@
 
 def exchange(slots):
     blocks = len(slots)
-    return [slots[0]] + [
-        lax.ppermute(slots[slot], "seq", [(j, j ^ slot) for j in range(blocks)]) for slot in range(1, blocks)
-    ]
+    upper, lower = list(range(blocks // 2, blocks)), list(range(1, blocks // 2))
+    order = [slot for pair in zip(upper, lower + [0]) for slot in pair if slot]
+    came = {0: slots[0]}
+    for slot in order:
+        came[slot] = lax.ppermute(slots[slot], "seq", [(j, j ^ slot) for j in range(blocks)])
+    return [came[slot] for slot in range(blocks)]
+
+
+def swap_blocks(array):
+    return [lax.all_to_all(array, "seq", split_axis=0, concat_axis=0, tiled=True)]
 
 
 def kernel_local(values, gates, filter_taps, skip_gain, out_weight):
     blocks = lax.axis_size("seq")
     me = jnp.stack([lax.axis_index("seq"), lax.axis_index("chan")]).astype(jnp.int32)
-    came = [exchange(arrange(me, values, filter_taps, blocks, chunk)) for chunk in range(2)]
-    back = [exchange(convolve(me, came[chunk], blocks, chunk)) for chunk in range(2)]
-    (base,) = gate_and_project(me, back[0], gates, values, skip_gain, out_weight, 0)
-    sent, gated = gate_and_project(me, back[1], gates, values, skip_gain, out_weight, 1, base)
+    first = exchange(arrange(me, values, filter_taps, blocks, 0, True))
+    second = swap_blocks(*arrange(me, values, filter_taps, blocks, 1, False))
+    first = swap_blocks(*convolve(me, first, blocks, 0, False))
+    second = exchange(convolve(me, second, blocks, 1, True))
+    (base,) = gate_and_project(me, first, gates, values, skip_gain, out_weight, 0)
+    sent, gated = gate_and_project(me, second, gates, values, skip_gain, out_weight, 1, base)
     other = lax.ppermute(sent, "chan", [(0, 1), (1, 0)])
     kept = project_kept(me, gated, out_weight, base)
     return join(kept, other)

time: 174 us -> 147 us (0.84)
  starting transfers between devices: 110 us -> 67.9 us
  local copies, waits for them, and re-layouts: 10.1 us -> 22.5 us
  waiting for transfers between devices: 5.01 us -> 15.3 us
  Pallas kernels: 47.4 us -> 40.6 us
    ppermute x60 -> x30, starting transfers between devices: 110 us -> 55.9 us  [exchange(): lax.ppermute(slots[slot], 'seq', [(j, j ^ slot) for j in range(blocks)])]
    unnamed x22 -> x46, local copies, waits for them, and re-layouts: 10.1 us -> 22.5 us
    all_to_all x0 -> x2, starting transfers between devices: none -> 11.9 us  [swap_blocks(): lax.all_to_all(array, 'seq', split_axis=0, concat_axis=0, tiled=True)]
    ppermute x60 -> x30, waiting for transfers between devices: 4.36 us -> 14.6 us  [exchange(): lax.ppermute(slots[slot], 'seq', [(j, j ^ slot) for j in range(blocks)])]
    pallas_call x6, Pallas kernels: 43.7 us -> 36.9 us  [the longest x2 23.6 us: convolve(): pl.pallas_call(functools.partial(convolve_kernel, blocks, slots_in, slots...]
  transfers between devices with their start and end apart: 61 -> 33, of which waited for: 4 -> 7; matrix products, arithmetic and copies ran while one was open for 0% -> 0% of each run, Pallas kernels for 24% -> 22%
where the time goes in v2:
time: 147 us
  starting transfers between devices  67.9 us (46%)
  Pallas kernels  40.6 us (28%)
  local copies, waits for them, and re-layouts  22.5 us (15%)
  waiting for transfers between devices  15.3 us (10%)
    ppermute x30, starting transfers between devices, exchange(): lax.ppermute(slots[slot], 'seq', [(j, j ^ slot) for j in range(blocks)])  55.9 us
    pallas_call x2, Pallas kernels, convolve(): pl.pallas_call(functools.partial(convolve_kernel, blocks, slots_in, slots...  23.6 us
    unnamed x46, local copies, waits for them, and re-layouts  22.5 us
    ppermute x30, waiting for transfers between devices, exchange(): lax.ppermute(slots[slot], 'seq', [(j, j ^ slot) for j in range(blocks)])  14.6 us
    all_to_all x2, starting transfers between devices, swap_blocks(): lax.all_to_all(array, 'seq', split_axis=0, concat_axis=0, tiled=True)  11.9 us
    pallas_call x2, Pallas kernels, gate_and_project(): pl.pallas_call(functools.partial(gate_kernel, count, joined), grid_spec=p...  7.7 us
    pallas_call x2, Pallas kernels, arrange(): pl.pallas_call(functools.partial(arrange_kernel, blocks, pieces, slotted,...  5.57 us
  transfers between devices with their start and end apart: 33, of which 7 were waited for; matrix products, arithmetic and copies ran while one was open for 0% of the time, Pallas kernels for 22%

profile of v2, /device:TPU:0, one launch (start us, length us, event | category | flops | bytes accessed | tf_op | source)
XLA Modules:
  0.0 146.6 jit_solution(8407979398097753634)
XLA Ops:
  3.4 3.3 %arrange_1.1 = bf16[16,256,128]{2,1,0:T(8,128)(2,1)} custom-call(s32[2]{0:T(128)S(1)} %pad_add_fusion.me_ref, bf16[256,256]{1,0:T(8,128)(2,1)S(1)} %copy-done.8, bf16[256,2048]{1,0:T(8,128)(2,1)S(1)} %copy-done.2, bf16[256,2048]{1,0:T(8,128)(2,1)S(1)} %copy-done.6), custom_call_target="tpu_custom_call" | custom-call | tf_op jit(solution)/shard_map/arrange_1/pallas_call | solution.py:237
  6.7 8.3 %all-to-all-start = ((bf16[16,256,128]{2,1,0:T(8,128)(2,1)}), bf16[16,256,128]{2,1,0:T(8,128)(2,1)S(1)}, u32[]{:S(2)}, u32[]{:S(2)}) async-start(bf16[16,256,128]{2,1,0:T(8,128)(2,1)} %arrange_1.1), calls=%async_computation | async-start | bytes 2097152 | tf_op jit(solution)/shard_map/all_to_all | solution.py:553
  18.4 2.3 %arrange_0.1 = (bf16[256,128]{1,0:T(8,128)(2,1)S(1)}, bf16[256,128]{1,0:T(8,128)(2,1)S(1)}, bf16[256,128]{1,0:T(8,128)(2,1)S(1)}, bf16[256,128]{1,0:T(8,128)(2,1...) custom-call(s32[2]{0:T(128)S(1)} %pad_add_fusion.me_ref, ...), custom_call_target="tpu_custom_call" | custom-call | tf_op jit(solution)/shard_map/arrange_0/pallas_call | solution.py:237
  20.7 2.0 %collective-permute-start.15 = (bf16[256,128]{1,0:T(8,128)(2,1)S(1)}, bf16[256,128]{1,0:T(8,128)(2,1)S(1)}, u32[]{:S(2)}, u32[]{:S(2)}) collective-permute-start(bf16[256,128]{1,0:T(8,128)(2,1)S(1)} %get-tuple-element.56), channel_id=1, source_target_pairs={{0,2},{2,0},{4,6},{6,4},{8,10},{10,8},{12,14},{14,12},{16,18},{18,... | collective-permute-start | bytes 196616 | tf_op jit(solution)/shard_map/ppermute | solution.py:548
  27.7 2.4 %collective-permute-start.20 = (bf16[256,128]{1,0:T(8,128)(2,1)S(1)}, bf16[256,128]{1,0:T(8,128)(2,1)S(1)}, u32[]{:S(2)}, u32[]{:S(2)}) collective-permute-start(bf16[256,128]{1,0:T(8,128)(2,1)S(1)} %get-tuple-element.61), channel_id=1, source_target_pairs={{0,12},{2,14},{4,8},{6,10},{8,4},{10,6},{12,0},{14,2},{16,28},{18,... | collective-permute-start | bytes 196616 | tf_op jit(solution)/shard_map/ppermute | solution.py:548
  34.6 5.7 %collective-permute-start.23 = (bf16[256,128]{1,0:T(8,128)(2,1)S(1)}, bf16[256,128]{1,0:T(8,128)(2,1)S(1)}, u32[]{:S(2)}, u32[]{:S(2)}) collective-permute-start(bf16[256,128]{1,0:T(8,128)(2,1)S(1)} %get-tuple-element.64), channel_id=1, source_target_pairs={{0,18},{2,16},{4,22},{6,20},{8,26},{10,24},{12,30},{14,28},{16,2},... | collective-permute-start | bytes 196616 | tf_op jit(solution)/shard_map/ppermute | solution.py:548
  40.3 2.4 %collective-permute-start.24 = (bf16[256,128]{1,0:T(8,128)(2,1)S(1)}, bf16[256,128]{1,0:T(8,128)(2,1)S(1)}, u32[]{:S(2)}, u32[]{:S(2)}) collective-permute-start(bf16[256,128]{1,0:T(8,128)(2,1)S(1)} %get-tuple-element.65), channel_id=1, source_target_pairs={{0,20},{2,22},{4,16},{6,18},{8,28},{10,30},{12,24},{14,26},{16,4},... | collective-permute-start | bytes 196616 | tf_op jit(solution)/shard_map/ppermute | solution.py:548
  45.1 6.0 %collective-permute-done.22.rest_8_ = bf16[256,128]{1,0:T(8,128)(2,1)S(1)} collective-permute-done((bf16[256,128]{1,0:T(8,128)(2,1)S(1)}, bf16[256,128]{1,0:T(8,128)(2,1)S(1)}, u32[]{:S(2)}, u32[]{:S(2)}) %collective-permute-start.22) | collective-permute-done | bytes 65568 | tf_op jit(solution)/shard_map/ppermute | solution.py:548
  51.0 2.6 %collective-permute-start.27 = (bf16[256,128]{1,0:T(8,128)(2,1)S(1)}, bf16[256,128]{1,0:T(8,128)(2,1)S(1)}, u32[]{:S(2)}, u32[]{:S(2)}) collective-permute-start(bf16[256,128]{1,0:T(8,128)(2,1)S(1)} %get-tuple-element.68), channel_id=1, source_target_pairs={{0,26},{2,24},{4,30},{6,28},{8,18},{10,16},{12,22},{14,20},{16,10}... | collective-permute-start | bytes 196616 | tf_op jit(solution)/shard_map/ppermute | solution.py:548
  53.6 3.2 %collective-permute-start.28 = (bf16[256,128]{1,0:T(8,128)(2,1)S(1)}, bf16[256,128]{1,0:T(8,128)(2,1)S(1)}, u32[]{:S(2)}, u32[]{:S(2)}) collective-permute-start(bf16[256,128]{1,0:T(8,128)(2,1)S(1)} %get-tuple-element.69), channel_id=1, source_target_pairs={{0,28},{2,30},{4,24},{6,26},{8,20},{10,22},{12,16},{14,18},{16,12}... | collective-permute-start | bytes 196616 | tf_op jit(solution)/shard_map/ppermute | solution.py:548
  58.7 2.1 %collective-permute-done.28.rest_14_ = bf16[256,128]{1,0:T(8,128)(2,1)S(1)} collective-permute-done((bf16[256,128]{1,0:T(8,128)(2,1)S(1)}, bf16[256,128]{1,0:T(8,128)(2,1)S(1)}, u32[]{:S(2)}, u32[]{:S(2)}) %collective-permute-start.28) | collective-permute-done | bytes 65568 | tf_op jit(solution)/shard_map/ppermute | solution.py:548
  60.8 3.9 %collective-permute-done.29.rest_15_ = bf16[256,128]{1,0:T(8,128)(2,1)S(1)} collective-permute-done((bf16[256,128]{1,0:T(8,128)(2,1)S(1)}, bf16[256,128]{1,0:T(8,128)(2,1)S(1)}, u32[]{:S(2)}, u32[]{:S(2)}) %collective-permute-start.29) | collective-permute-done | bytes 65568 | tf_op jit(solution)/shard_map/ppermute | solution.py:548
  67.7 11.8 %long_convolution_0.1 = bf16[16,128,128]{2,1,0:T(8,128)(2,1)S(1)} custom-call(s32[2]{0:T(128)S(1)} %pad_add_fusion.me_ref, bf16[256,128]{1,0:T(8,128)(2,1)S(1)} %get-tuple-element.55.rest_0_, bf16[256,128]{1,0:T(8,128)(2,1)S(1)} %collective-permute-done.15.rest_1_, bf16[256,128]{1,0:T(8,128)(2,1)S(1)} %collective-permute-done.16.rest_2_, ...), custom_call_target="tpu_custom_call" | custom-call | flops 3000000000 | bytes 24000000 | tf_op jit(solution)/shard_map/long_convolution_0/pallas_call | solution.py:371
  81.4 3.6 %all-to-all-start.1 = ((bf16[16,128,128]{2,1,0:T(8,128)(2,1)}), bf16[16,128,128]{2,1,0:T(8,128)(2,1)S(1)}, u32[]{:S(2)}, u32[]{:S(2)}) async-start(bf16[16,128,128]{2,1,0:T(8,128)(2,1)} %copy-done.13), calls=%async_computation.1 | async-start | bytes 1048576 | tf_op jit(solution)/shard_map/all_to_all | solution.py:553
  89.2 11.8 %long_convolution_1.1 = (bf16[128,128]{1,0:T(8,128)(2,1)S(1)}, bf16[128,128]{1,0:T(8,128)(2,1)S(1)}, bf16[128,128]{1,0:T(8,128)(2,1)S(1)}, bf16[128,128]{1,0:T(8...) custom-call(s32[2]{0:T(128)S(1)} %pad_add_fusion.me_ref, ...), custom_call_target="tpu_custom_call" | custom-call | flops 3000000000 | bytes 24000000 | tf_op jit(solution)/shard_map/long_convolution_1/pallas_call | solution.py:371
  107.8 2.4 %collective-permute-start.5 = (bf16[128,128]{1,0:T(8,128)(2,1)S(1)}, bf16[128,128]{1,0:T(8,128)(2,1)S(1)}, u32[]{:S(2)}, u32[]{:S(2)}) collective-permute-start(bf16[128,128]{1,0:T(8,128)(2,1)S(1)} %get-tuple-element.45), channel_id=1, source_target_pairs={{0,12},{2,14},{4,8},{6,10},{8,4},{10,6},{12,0},{14,2},{16,28},{18,... | collective-permute-start | bytes 98312 | tf_op jit(solution)/shard_map/ppermute | solution.py:548
  110.4 2.8 %collective-permute-start.7 = (bf16[128,128]{1,0:T(8,128)(2,1)S(1)}, bf16[128,128]{1,0:T(8,128)(2,1)S(1)}, u32[]{:S(2)}, u32[]{:S(2)}) collective-permute-start(bf16[128,128]{1,0:T(8,128)(2,1)S(1)} %get-tuple-element.47), channel_id=1, source_target_pairs={{0,16},{2,18},{4,20},{6,22},{8,24},{10,26},{12,28},{14,30},{16,0},... | collective-permute-start | bytes 98312 | tf_op jit(solution)/shard_map/ppermute | solution.py:548
  114.6 3.3 %collective-permute-start.9 = (bf16[128,128]{1,0:T(8,128)(2,1)S(1)}, bf16[128,128]{1,0:T(8,128)(2,1)S(1)}, u32[]{:S(2)}, u32[]{:S(2)}) collective-permute-start(bf16[128,128]{1,0:T(8,128)(2,1)S(1)} %get-tuple-element.49), channel_id=1, source_target_pairs={{0,20},{2,22},{4,16},{6,18},{8,28},{10,30},{12,24},{14,26},{16,4},... | collective-permute-start | bytes 98312 | tf_op jit(solution)/shard_map/ppermute | solution.py:548
  118.1 3.7 %collective-permute-start.11 = (bf16[128,128]{1,0:T(8,128)(2,1)S(1)}, bf16[128,128]{1,0:T(8,128)(2,1)S(1)}, u32[]{:S(2)}, u32[]{:S(2)}) collective-permute-start(bf16[128,128]{1,0:T(8,128)(2,1)S(1)} %get-tuple-element.51), channel_id=1, source_target_pairs={{0,24},{2,26},{4,28},{6,30},{8,16},{10,18},{12,20},{14,22},{16,8},... | collective-permute-start | bytes 98312 | tf_op jit(solution)/shard_map/ppermute | solution.py:548
  123.2 4.3 %collective-permute-start.13 = (bf16[128,128]{1,0:T(8,128)(2,1)S(1)}, bf16[128,128]{1,0:T(8,128)(2,1)S(1)}, u32[]{:S(2)}, u32[]{:S(2)}) collective-permute-start(bf16[128,128]{1,0:T(8,128)(2,1)S(1)} %get-tuple-element.53), channel_id=1, source_target_pairs={{0,28},{2,30},{4,24},{6,26},{8,20},{10,22},{12,16},{14,18},{16,12}... | collective-permute-start | bytes 98312 | tf_op jit(solution)/shard_map/ppermute | solution.py:548
  127.6 3.4 %copy-done = bf16[2048,2048]{1,0:T(8,128)(2,1)S(1)} copy-done((bf16[2048,2048]{1,0:T(8,128)(2,1)S(1)}, bf16[2048,2048]{1,0:T(8,128)(2,1)}, u32[]{:S(2)}) %copy-start) | copy-done | bytes 8388632
  131.0 4.0 %gate_project_0.1.rest_21_.base_ref = f32[256,2048]{1,0:T(8,128)S(1)} custom-call(s32[2]{0:T(128)S(1)} %pad_add_fusion.me_ref, bf16[16,128,128]{2,1,0:T(8,128)(2,1)S(1)} %all-to-all-done.1.rest_0_, bf16[256,256]{1,0:T(8,128)(2,1)S(1)} %copy-done.10, bf16[256,2048]{1,0:T(8,128)(2,1)S(1)} %copy-done.5, bf16[256,2048]{1,0:T(8,128)(2,1)S(1)} %copy-done.4, ...), custom_call_target="tpu_custom_call" | custom-call | flops 1073741824 | bytes 7340032 | tf_op jit(solution)/shard_map/gate_project_0/pallas_call | solution.py:464
  135.1 3.4 %copy-done.1 = bf16[2048,2048]{1,0:T(8,128)(2,1)S(1)} copy-done((bf16[2048,2048]{1,0:T(8,128)(2,1)S(1)}, bf16[2048,2048]{1,0:T(8,128)(2,1)}, u32[]{:S(2)}) %copy-start.1) | copy-done | bytes 8388632
  138.4 3.7 %gate_project_1.1 = (f32[256,1024]{1,0:T(8,128)S(1)}, bf16[256,1024]{1,0:T(8,128)(2,1)S(1)}) custom-call(s32[2]{0:T(128)S(1)} %pad_add_fusion.me_ref, bf16[128,128]{1,0:T(8,128)(2,1)S(1)} %get-tuple-element.39.rest_0_, bf16[128,128]{1,0:T(8,128)(2,1)S(1)} %collective-permute-done.rest_1_, bf16[128,128]{1,0:T(8,128)(2,1)S(1)} %collective-permute-done.1.rest_2_, ...), custom_call_target="tpu_custom_call" | custom-call | flops 536870912 | bytes 5242880 | tf_op jit(solution)/shard_map/gate_project_1/pallas_call | solution.py:464
  (98 shorter events, 44.1 us)
Async XLA Ops:
  6.7 73.7 %all-to-all-start = ((bf16[16,256,128]{2,1,0:T(8,128)(2,1)}), bf16[16,256,128]{2,1,0:T(8,128)(2,1)S(1)}, u32[]{:S(2)}, u32[]{:S(2)}) async-start(bf16[16,256,128]{2,1,0:T(8,128)(2,1)} %arrange_1.1), calls=%async_computation | async-start | bytes 2097152 | tf_op jit(solution)/shard_map/all_to_all | solution.py:553
  24.2 8.9 %collective-permute-start.17 = (bf16[256,128]{1,0:T(8,128)(2,1)S(1)}, bf16[256,128]{1,0:T(8,128)(2,1)S(1)}, u32[]{:S(2)}, u32[]{:S(2)}) collective-permute-start(bf16[256,128]{1,0:T(8,128)(2,1)S(1)} %get-tuple-element.58), channel_id=1, source_target_pairs={{0,6},{2,4},{4,2},{6,0},{8,14},{10,12},{12,10},{14,8},{16,22},{18,... | collective-permute-start | bytes 196616 | tf_op jit(solution)/shard_map/ppermute | solution.py:548
  24.3 10.3 %collective-permute-start.18 = (bf16[256,128]{1,0:T(8,128)(2,1)S(1)}, bf16[256,128]{1,0:T(8,128)(2,1)S(1)}, u32[]{:S(2)}, u32[]{:S(2)}) collective-permute-start(bf16[256,128]{1,0:T(8,128)(2,1)S(1)} %get-tuple-element.59), channel_id=1, source_target_pairs={{0,8},{2,10},{4,12},{6,14},{8,0},{10,2},{12,4},{14,6},{16,24},{18,... | collective-permute-start | bytes 196616 | tf_op jit(solution)/shard_map/ppermute | solution.py:548
  26.2 14.1 %collective-permute-start.19 = (bf16[256,128]{1,0:T(8,128)(2,1)S(1)}, bf16[256,128]{1,0:T(8,128)(2,1)S(1)}, u32[]{:S(2)}, u32[]{:S(2)}) collective-permute-start(bf16[256,128]{1,0:T(8,128)(2,1)S(1)} %get-tuple-element.60), channel_id=1, source_target_pairs={{0,10},{2,8},{4,14},{6,12},{8,2},{10,0},{12,6},{14,4},{16,26},{18,... | collective-permute-start | bytes 196616 | tf_op jit(solution)/shard_map/ppermute | solution.py:548
  27.7 15.0 %collective-permute-start.20 = (bf16[256,128]{1,0:T(8,128)(2,1)S(1)}, bf16[256,128]{1,0:T(8,128)(2,1)S(1)}, u32[]{:S(2)}, u32[]{:S(2)}) collective-permute-start(bf16[256,128]{1,0:T(8,128)(2,1)S(1)} %get-tuple-element.61), channel_id=1, source_target_pairs={{0,12},{2,14},{4,8},{6,10},{8,4},{10,6},{12,0},{14,2},{16,28},{18,... | collective-permute-start | bytes 196616 | tf_op jit(solution)/shard_map/ppermute | solution.py:548
  30.0 14.2 %collective-permute-start.21 = (bf16[256,128]{1,0:T(8,128)(2,1)S(1)}, bf16[256,128]{1,0:T(8,128)(2,1)S(1)}, u32[]{:S(2)}, u32[]{:S(2)}) collective-permute-start(bf16[256,128]{1,0:T(8,128)(2,1)S(1)} %get-tuple-element.62), channel_id=1, source_target_pairs={{0,14},{2,12},{4,10},{6,8},{8,6},{10,4},{12,2},{14,0},{16,30},{18,... | collective-permute-start | bytes 196616 | tf_op jit(solution)/shard_map/ppermute | solution.py:548
  33.1 17.9 %collective-permute-start.22 = (bf16[256,128]{1,0:T(8,128)(2,1)S(1)}, bf16[256,128]{1,0:T(8,128)(2,1)S(1)}, u32[]{:S(2)}, u32[]{:S(2)}) collective-permute-start(bf16[256,128]{1,0:T(8,128)(2,1)S(1)} %get-tuple-element.63), channel_id=1, source_target_pairs={{0,16},{2,18},{4,20},{6,22},{8,24},{10,26},{12,28},{14,30},{16,0},... | collective-permute-start | bytes 196616 | tf_op jit(solution)/shard_map/ppermute | solution.py:548
  34.6 19.0 %collective-permute-start.23 = (bf16[256,128]{1,0:T(8,128)(2,1)S(1)}, bf16[256,128]{1,0:T(8,128)(2,1)S(1)}, u32[]{:S(2)}, u32[]{:S(2)}) collective-permute-start(bf16[256,128]{1,0:T(8,128)(2,1)S(1)} %get-tuple-element.64), channel_id=1, source_target_pairs={{0,18},{2,16},{4,22},{6,20},{8,26},{10,24},{12,30},{14,28},{16,2},... | collective-permute-start | bytes 196616 | tf_op jit(solution)/shard_map/ppermute | solution.py:548
  40.3 16.5 %collective-permute-start.24 = (bf16[256,128]{1,0:T(8,128)(2,1)S(1)}, bf16[256,128]{1,0:T(8,128)(2,1)S(1)}, u32[]{:S(2)}, u32[]{:S(2)}) collective-permute-start(bf16[256,128]{1,0:T(8,128)(2,1)S(1)} %get-tuple-element.65), channel_id=1, source_target_pairs={{0,20},{2,22},{4,16},{6,18},{8,28},{10,30},{12,24},{14,26},{16,4},... | collective-permute-start | bytes 196616 | tf_op jit(solution)/shard_map/ppermute | solution.py:548
  42.7 15.6 %collective-permute-start.25 = (bf16[256,128]{1,0:T(8,128)(2,1)S(1)}, bf16[256,128]{1,0:T(8,128)(2,1)S(1)}, u32[]{:S(2)}, u32[]{:S(2)}) collective-permute-start(bf16[256,128]{1,0:T(8,128)(2,1)S(1)} %get-tuple-element.66), channel_id=1, source_target_pairs={{0,22},{2,20},{4,18},{6,16},{8,30},{10,28},{12,26},{14,24},{16,6},... | collective-permute-start | bytes 196616 | tf_op jit(solution)/shard_map/ppermute | solution.py:548
  44.2 14.1 %collective-permute-start.26 = (bf16[256,128]{1,0:T(8,128)(2,1)S(1)}, bf16[256,128]{1,0:T(8,128)(2,1)S(1)}, u32[]{:S(2)}, u32[]{:S(2)}) collective-permute-start(bf16[256,128]{1,0:T(8,128)(2,1)S(1)} %get-tuple-element.67), channel_id=1, source_target_pairs={{0,24},{2,26},{4,28},{6,30},{8,16},{10,18},{12,20},{14,22},{16,8},... | collective-permute-start | bytes 196616 | tf_op jit(solution)/shard_map/ppermute | solution.py:548
  56.8 8.0 %collective-permute-start.29 = (bf16[256,128]{1,0:T(8,128)(2,1)S(1)}, bf16[256,128]{1,0:T(8,128)(2,1)S(1)}, u32[]{:S(2)}, u32[]{:S(2)}) collective-permute-start(bf16[256,128]{1,0:T(8,128)(2,1)S(1)} %get-tuple-element.70), channel_id=1, source_target_pairs={{0,30},{2,28},{4,26},{6,24},{8,22},{10,20},{12,18},{14,16},{16,14}... | collective-permute-start | bytes 196616 | tf_op jit(solution)/shard_map/ppermute | solution.py:548
  81.4 46.2 %all-to-all-start.1 = ((bf16[16,128,128]{2,1,0:T(8,128)(2,1)}), bf16[16,128,128]{2,1,0:T(8,128)(2,1)S(1)}, u32[]{:S(2)}, u32[]{:S(2)}) async-start(bf16[16,128,128]{2,1,0:T(8,128)(2,1)} %copy-done.13), calls=%async_computation.1 | async-start | bytes 1048576 | tf_op jit(solution)/shard_map/all_to_all | solution.py:553
  104.6 8.6 %collective-permute-start.3 = (bf16[128,128]{1,0:T(8,128)(2,1)S(1)}, bf16[128,128]{1,0:T(8,128)(2,1)S(1)}, u32[]{:S(2)}, u32[]{:S(2)}) collective-permute-start(bf16[128,128]{1,0:T(8,128)(2,1)S(1)} %get-tuple-element.43), channel_id=1, source_target_pairs={{0,8},{2,10},{4,12},{6,14},{8,0},{10,2},{12,4},{14,6},{16,24},{18,... | collective-permute-start | bytes 98312 | tf_op jit(solution)/shard_map/ppermute | solution.py:548
  106.4 8.2 %collective-permute-start.4 = (bf16[128,128]{1,0:T(8,128)(2,1)S(1)}, bf16[128,128]{1,0:T(8,128)(2,1)S(1)}, u32[]{:S(2)}, u32[]{:S(2)}) collective-permute-start(bf16[128,128]{1,0:T(8,128)(2,1)S(1)} %get-tuple-element.44), channel_id=1, source_target_pairs={{0,10},{2,8},{4,14},{6,12},{8,2},{10,0},{12,6},{14,4},{16,26},{18,... | collective-permute-start | bytes 98312 | tf_op jit(solution)/shard_map/ppermute | solution.py:548
  107.8 10.1 %collective-permute-start.5 = (bf16[128,128]{1,0:T(8,128)(2,1)S(1)}, bf16[128,128]{1,0:T(8,128)(2,1)S(1)}, u32[]{:S(2)}, u32[]{:S(2)}) collective-permute-start(bf16[128,128]{1,0:T(8,128)(2,1)S(1)} %get-tuple-element.45), channel_id=1, source_target_pairs={{0,12},{2,14},{4,8},{6,10},{8,4},{10,6},{12,0},{14,2},{16,28},{18,... | collective-permute-start | bytes 98312 | tf_op jit(solution)/shard_map/ppermute | solution.py:548
  110.2 7.8 %collective-permute-start.6 = (bf16[128,128]{1,0:T(8,128)(2,1)S(1)}, bf16[128,128]{1,0:T(8,128)(2,1)S(1)}, u32[]{:S(2)}, u32[]{:S(2)}) collective-permute-start(bf16[128,128]{1,0:T(8,128)(2,1)S(1)} %get-tuple-element.46), channel_id=1, source_target_pairs={{0,14},{2,12},{4,10},{6,8},{8,6},{10,4},{12,2},{14,0},{16,30},{18,... | collective-permute-start | bytes 98312 | tf_op jit(solution)/shard_map/ppermute | solution.py:548
  110.4 11.4 %collective-permute-start.7 = (bf16[128,128]{1,0:T(8,128)(2,1)S(1)}, bf16[128,128]{1,0:T(8,128)(2,1)S(1)}, u32[]{:S(2)}, u32[]{:S(2)}) collective-permute-start(bf16[128,128]{1,0:T(8,128)(2,1)S(1)} %get-tuple-element.47), channel_id=1, source_target_pairs={{0,16},{2,18},{4,20},{6,22},{8,24},{10,26},{12,28},{14,30},{16,0},... | collective-permute-start | bytes 98312 | tf_op jit(solution)/shard_map/ppermute | solution.py:548
  113.2 10.0 %collective-permute-start.8 = (bf16[128,128]{1,0:T(8,128)(2,1)S(1)}, bf16[128,128]{1,0:T(8,128)(2,1)S(1)}, u32[]{:S(2)}, u32[]{:S(2)}) collective-permute-start(bf16[128,128]{1,0:T(8,128)(2,1)S(1)} %get-tuple-element.48), channel_id=1, source_target_pairs={{0,18},{2,16},{4,22},{6,20},{8,26},{10,24},{12,30},{14,28},{16,2},... | collective-permute-start | bytes 98312 | tf_op jit(solution)/shard_map/ppermute | solution.py:548
  114.6 12.8 %collective-permute-start.9 = (bf16[128,128]{1,0:T(8,128)(2,1)S(1)}, bf16[128,128]{1,0:T(8,128)(2,1)S(1)}, u32[]{:S(2)}, u32[]{:S(2)}) collective-permute-start(bf16[128,128]{1,0:T(8,128)(2,1)S(1)} %get-tuple-element.49), channel_id=1, source_target_pairs={{0,20},{2,22},{4,16},{6,18},{8,28},{10,30},{12,24},{14,26},{16,4},... | collective-permute-start | bytes 98312 | tf_op jit(solution)/shard_map/ppermute | solution.py:548
  117.9 17.1 %collective-permute-start.10 = (bf16[128,128]{1,0:T(8,128)(2,1)S(1)}, bf16[128,128]{1,0:T(8,128)(2,1)S(1)}, u32[]{:S(2)}, u32[]{:S(2)}) collective-permute-start(bf16[128,128]{1,0:T(8,128)(2,1)S(1)} %get-tuple-element.50), channel_id=1, source_target_pairs={{0,22},{2,20},{4,18},{6,16},{8,30},{10,28},{12,26},{14,24},{16,6},... | collective-permute-start | bytes 98312 | tf_op jit(solution)/shard_map/ppermute | solution.py:548
  118.1 16.9 %collective-permute-start.11 = (bf16[128,128]{1,0:T(8,128)(2,1)S(1)}, bf16[128,128]{1,0:T(8,128)(2,1)S(1)}, u32[]{:S(2)}, u32[]{:S(2)}) collective-permute-start(bf16[128,128]{1,0:T(8,128)(2,1)S(1)} %get-tuple-element.51), channel_id=1, source_target_pairs={{0,24},{2,26},{4,28},{6,30},{8,16},{10,18},{12,20},{14,22},{16,8},... | collective-permute-start | bytes 98312 | tf_op jit(solution)/shard_map/ppermute | solution.py:548
  121.8 13.3 %collective-permute-start.12 = (bf16[128,128]{1,0:T(8,128)(2,1)S(1)}, bf16[128,128]{1,0:T(8,128)(2,1)S(1)}, u32[]{:S(2)}, u32[]{:S(2)}) collective-permute-start(bf16[128,128]{1,0:T(8,128)(2,1)S(1)} %get-tuple-element.52), channel_id=1, source_target_pairs={{0,26},{2,24},{4,30},{6,28},{8,18},{10,16},{12,22},{14,20},{16,10}... | collective-permute-start | bytes 98312 | tf_op jit(solution)/shard_map/ppermute | solution.py:548
  123.2 11.9 %collective-permute-start.13 = (bf16[128,128]{1,0:T(8,128)(2,1)S(1)}, bf16[128,128]{1,0:T(8,128)(2,1)S(1)}, u32[]{:S(2)}, u32[]{:S(2)}) collective-permute-start(bf16[128,128]{1,0:T(8,128)(2,1)S(1)} %get-tuple-element.53), channel_id=1, source_target_pairs={{0,28},{2,30},{4,24},{6,26},{8,20},{10,22},{12,16},{14,18},{16,12}... | collective-permute-start | bytes 98312 | tf_op jit(solution)/shard_map/ppermute | solution.py:548
  (32 other events, 298.7 us)

commit v3 on v2

--- a/solution.py
+++ b/solution.py
@@ -15,8 +15,7 @@
 RADIX = 16
 LANES = 128
 HALF = 64
-VMEM_BYTES = 40 * 1024 * 1024
-SMALL_BYTES = 24 * 1024 * 1024
+VMEM_BYTES = 60 * 1024 * 1024
 
 
 def angle_table(first, second, period):
@@ -126,6 +125,11 @@
     return forward, backward, turns
 
 
+def tables_in_order(length):
+    forward, backward, turns = transform_tables(length)
+    return forward, turns, backward
+
+
 @functools.lru_cache(maxsize=None)
 def row_order(rows):
     chunk = rows // RADIX
@@ -194,22 +198,22 @@
     return pltpu.roll(block, HALF, 1)
 
 
-def arrange_kernel(blocks, pieces, slotted, chunk, me_ref, order_hbm, values_hbm, taps_hbm, *rest):
-    outs = rest[: blocks if slotted else 1]
-    order_ref, values_ref, taps_ref, packed, sems = rest[len(outs) :]
+def arrange_kernel(pieces, chunk, order_hbm, values_hbm, taps_hbm, out_hbm, order_ref, values_ref, taps_ref, packed, sems):
     wide = values_ref.shape[1]
     piece = wide // pieces
-    loads = [pltpu.make_async_copy(order_hbm, order_ref, sems.at[2 * pieces])]
+    loads = [pltpu.make_async_copy(order_hbm, order_ref, sems.at[3 * pieces])]
+    stores = []
     for part in range(pieces):
         lanes = pl.ds(chunk * wide + part * piece, piece)
         to = pl.ds(part * piece, piece)
-        loads.append(pltpu.make_async_copy(values_hbm.at[:, lanes], values_ref.at[:, to], sems.at[2 * part]))
-        loads.append(pltpu.make_async_copy(taps_hbm.at[:, lanes], taps_ref.at[:, to], sems.at[2 * part + 1]))
+        loads.append(pltpu.make_async_copy(values_hbm.at[:, lanes], values_ref.at[:, to], sems.at[3 * part]))
+        loads.append(pltpu.make_async_copy(taps_hbm.at[:, lanes], taps_ref.at[:, to], sems.at[3 * part + 1]))
+        taken = pl.ds(part * piece // HALF, piece // HALF)
+        stores.append(pltpu.make_async_copy(packed.at[taken], out_hbm.at[taken], sems.at[3 * part + 2]))
     for load in loads:
         load.start()
     loads[0].wait()
     left = left_lanes(order_ref.shape[0])
-    target = packed if slotted else outs[0]
     for part in range(pieces):
         loads[2 * part + 1].wait()
         loads[2 * part + 2].wait()
@@ -218,37 +222,35 @@
             both = jnp.concatenate([values_ref[:, lanes], taps_ref[:, lanes]], axis=1)
             moved = jnp.dot(order_ref[...], both, preferred_element_type=jnp.float32)
             value, taps = moved[:, :LANES], moved[:, LANES:]
-            target[2 * pair] = jnp.where(left, value, swap_halves(taps)).astype(jnp.bfloat16)
-            target[2 * pair + 1] = jnp.where(left, swap_halves(value), taps).astype(jnp.bfloat16)
-    if slotted:
-        me = me_ref[0]
-        for slot in range(blocks):
-            outs[slot][...] = packed[me ^ slot]
-
-
-def arrange(me, values, taps, blocks, chunk, slotted):
+            packed[2 * pair] = jnp.where(left, value, swap_halves(taps)).astype(jnp.bfloat16)
+            packed[2 * pair + 1] = jnp.where(left, swap_halves(value), taps).astype(jnp.bfloat16)
+        stores[part].start()
+    for store in stores:
+        store.wait()
+
+
+def arrange(values, taps, blocks, chunk):
     rows = values.shape[0]
     wide = blocks * HALF
     pieces = 4
-    if slotted:
-        out_shape = [jax.ShapeDtypeStruct((rows, LANES), jnp.bfloat16)] * blocks
-    else:
-        out_shape = [jax.ShapeDtypeStruct((blocks, rows, LANES), jnp.bfloat16)]
     return pl.pallas_call(
-        functools.partial(arrange_kernel, blocks, pieces, slotted, chunk),
-        in_specs=[pl.BlockSpec(memory_space=pltpu.SMEM)] + [pl.BlockSpec(memory_space=pltpu.HBM)] * 3,
-        out_specs=[pl.BlockSpec(memory_space=pltpu.VMEM)] * len(out_shape),
-        out_shape=out_shape,
+        functools.partial(arrange_kernel, pieces, chunk),
+        in_specs=[pl.BlockSpec(memory_space=pl.ANY)] * 3,
+        out_specs=pl.BlockSpec(memory_space=pl.ANY),
+        out_shape=jax.ShapeDtypeStruct((blocks, rows, LANES), jnp.bfloat16),
         scratch_shapes=[
             pltpu.VMEM((rows, rows), jnp.bfloat16),
             pltpu.VMEM((rows, wide), jnp.bfloat16),
             pltpu.VMEM((rows, wide), jnp.bfloat16),
-            pltpu.VMEM((blocks, rows, LANES) if slotted else (16, LANES), jnp.bfloat16),
-            pltpu.SemaphoreType.DMA((2 * pieces + 1,)),
+            pltpu.VMEM((blocks, rows, LANES), jnp.bfloat16),
+            pltpu.SemaphoreType.DMA((3 * pieces + 1,)),
         ],
         compiler_params=pltpu.CompilerParams(vmem_limit_bytes=VMEM_BYTES),
+        cost_estimate=pl.CostEstimate(
+            flops=4 * rows * rows * wide, bytes_accessed=8 * rows * wide, transcendentals=0
+        ),
         name=f"arrange_{chunk}",
-    )(me, jnp.asarray(row_order(rows)), values, taps)
+    )(jnp.asarray(row_order(rows)), values, taps)
 
 
 def turned(point, turns, q, sign):
@@ -267,26 +269,29 @@
     return columns[:RADIX], columns[RADIX:]
 
 
-def convolve_kernel(blocks, slots_in, slots_out, me_ref, *rest):
-    count_in = blocks if slots_in else 1
-    count_out = blocks if slots_out else 1
-    slots = rest[:count_in]
-    forward_ref, backward_ref, turns_ref = rest[count_in : count_in + 3]
-    outs = rest[count_in + 3 : count_in + 3 + count_out]
-    streams, spectra, signals = rest[count_in + 3 + count_out :]
-    me = me_ref[0]
-    chunk = streams.shape[2]
+def convolve_kernel(
+    streams_hbm, forward_hbm, turns_hbm, backward_hbm, out_hbm,
+    streams, forward_ref, turns_ref, backward_ref, spectra, signals, sems,
+):
+    blocks, rows, _ = streams.shape
+    chunk = rows // RADIX
     inner = blocks * chunk
     part_rows = inner // 2
     pairs = RADIX // 2
-    if slots_in:
-        for slot in range(blocks):
-            streams[me ^ slot] = slots[slot][...].reshape(RADIX, chunk, LANES)
+    pieces = 4
+    piece = rows // pieces
+    loads = [pltpu.make_async_copy(forward_hbm, forward_ref, sems.at[0])]
+    for part in range(pieces):
+        taken = pl.ds(part * piece, piece)
+        loads.append(pltpu.make_async_copy(streams_hbm.at[:, taken], streams.at[:, taken], sems.at[1 + part]))
+    loads.append(pltpu.make_async_copy(turns_hbm, turns_ref, sems.at[1 + pieces]))
+    loads.append(pltpu.make_async_copy(backward_hbm, backward_ref, sems.at[2 + pieces]))
+    for load in loads:
+        load.start()
+    loads[0].wait()
 
     def stream_of(q):
-        if slots_in:
-            return streams[:, pl.ds(q, 1)].reshape(inner, LANES)
-        return slots[0][:, pl.ds(pl.multiple_of(q * chunk, chunk), chunk)].reshape(inner, LANES)
+        return streams[:, pl.ds(pl.multiple_of(q * chunk, chunk), chunk)].reshape(inner, LANES)
 
     def forward_step(pair, carry):
         both = jnp.concatenate([stream_of(2 * pair), stream_of(2 * pair + 1)], axis=1)
@@ -297,7 +302,10 @@
         spectra[2 * pair + 1] = result[:, LANES:]
         return carry
 
-    lax.fori_loop(0, pairs, forward_step, 0)
+    for part in range(pieces):
+        loads[1 + part].wait()
+        lax.fori_loop(part * pairs // pieces, (part + 1) * pairs // pieces, forward_step, 0)
+    loads[1 + pieces].wait()
     left = left_lanes(8)
 
     def rows_step(index, carry):
@@ -325,6 +333,7 @@
         return carry
 
     lax.fori_loop(0, part_rows // 8, rows_step, 0)
+    loads[2 + pieces].wait()
     left_part = left_lanes(part_rows)
     left_inner = left_lanes(inner)
 
@@ -345,67 +354,51 @@
         total = terms[:inner] + terms[inner:]
         sides = [part + swap_halves(part) for part in (total[:, :LANES], total[:, LANES:])]
         signal = jnp.where(left_inner, *sides).astype(jnp.bfloat16).reshape(blocks, chunk, LANES)
-        if slots_out:
-            signals[:, pl.ds(pair, 1)] = signal[:, None]
-        else:
-            outs[0][:, pl.ds(pl.multiple_of(pair * chunk, chunk), chunk)] = signal
+        signals[:, pl.ds(pl.multiple_of(pair * chunk, chunk), chunk)] = signal
         return carry
 
-    lax.fori_loop(0, pairs, backward_step, 0)
-    if slots_out:
-        for slot in range(blocks):
-            outs[slot][...] = signals[me ^ slot].reshape(pairs * chunk, LANES)
-
-
-def convolve(me, slots, blocks, chunk_id, slots_out):
-    slots_in = len(slots) > 1
-    rows = slots[0].shape[-2]
+    stores = []
+    half = pairs * chunk // 2
+    for part in range(2):
+        lax.fori_loop(part * pairs // 2, (part + 1) * pairs // 2, backward_step, 0)
+        taken = pl.ds(part * half, half)
+        stores.append(pltpu.make_async_copy(signals.at[:, taken], out_hbm.at[:, taken], sems.at[3 + pieces + part]))
+        stores[part].start()
+    for store in stores:
+        store.wait()
+
+
+def convolve(streams, chunk_id):
+    blocks, rows, _ = streams.shape
     length = blocks * rows
-    chunk = rows // RADIX
     inner = length // RADIX
-    pairs = RADIX // 2
-    if slots_out:
-        out_shape = [jax.ShapeDtypeStruct((pairs * chunk, LANES), jnp.bfloat16)] * blocks
+    return pl.pallas_call(
+        convolve_kernel,
+        in_specs=[pl.BlockSpec(memory_space=pl.ANY)] * 4,
+        out_specs=pl.BlockSpec(memory_space=pl.ANY),
+        out_shape=jax.ShapeDtypeStruct((blocks, rows // 2, LANES), jnp.bfloat16),
+        scratch_shapes=[
+            pltpu.VMEM((blocks, rows, LANES), jnp.bfloat16),
+            pltpu.VMEM((2 * inner, 2 * inner), jnp.bfloat16),
+            pltpu.VMEM((inner, LANES), jnp.float32),
+            pltpu.VMEM((2 * inner, 2 * inner), jnp.bfloat16),
+            pltpu.VMEM((RADIX, 2 * inner, LANES), jnp.float32),
+            pltpu.VMEM((blocks, rows // 2, LANES), jnp.bfloat16),
+            pltpu.SemaphoreType.DMA((9,)),
+        ],
+        compiler_params=pltpu.CompilerParams(vmem_limit_bytes=VMEM_BYTES),
+        cost_estimate=pl.CostEstimate(flops=6 * 10**9, bytes_accessed=24 * 10**6, transcendentals=0),
+        name=f"long_convolution_{chunk_id}",
+    )(streams, *(jnp.asarray(table) for table in tables_in_order(length)))
+
+
+def gate_kernel(joined, me_ref, parts, *rest):
+    if joined:
+        order_ref, gates_ref, values_ref, skip_ref, weight_ref, base_ref, out_ref, gated_ref = rest
     else:
-        out_shape = [jax.ShapeDtypeStruct((blocks, pairs * chunk, LANES), jnp.bfloat16)]
-    return pl.pallas_call(
-        functools.partial(convolve_kernel, blocks, slots_in, slots_out),
-        in_specs=[pl.BlockSpec(memory_space=pltpu.SMEM)]
-        + [pl.BlockSpec(memory_space=pltpu.VMEM)] * (len(slots) + 3),
-        out_specs=[pl.BlockSpec(memory_space=pltpu.VMEM)] * len(out_shape),
-        out_shape=out_shape,
-        scratch_shapes=[
-            pltpu.VMEM((blocks, RADIX, chunk, LANES) if slots_in else (1, 1, chunk, LANES), jnp.bfloat16),
-            pltpu.VMEM((RADIX, 2 * inner, LANES), jnp.float32),
-            pltpu.VMEM((blocks, pairs, chunk, LANES) if slots_out else (1, 1, chunk, LANES), jnp.bfloat16),
-        ],
-        compiler_params=pltpu.CompilerParams(vmem_limit_bytes=SMALL_BYTES),
-        cost_estimate=pl.CostEstimate(
-            flops=3 * 10**9, bytes_accessed=24 * 10**6, transcendentals=0
-        ),
-        name=f"long_convolution_{chunk_id}",
-    )(me, *slots, *(jnp.asarray(table) for table in transform_tables(length)))
-
-
-def gate_kernel(count, joined, me_ref, *rest):
-    slots, rest = rest[:count], rest[count:]
-    if joined:
-        order_ref, gates_ref, values_ref, skip_ref, weight_ref, base_ref, out_ref, gated_ref, parts = rest
-    else:
-        order_ref, gates_ref, values_ref, skip_ref, weight_ref, out_ref, parts = rest
-    me = me_ref[0]
+        order_ref, gates_ref, values_ref, skip_ref, weight_ref, out_ref = rest
+    del me_ref
     step = pl.program_id(0)
-
-    if count > 1:
-
-        @pl.when(step == 0)
-        def _():
-            for slot in range(count):
-                parts[me ^ slot] = slots[slot][...]
-
-    else:
-        parts = slots[0]
-
     wide = gates_ref.shape[1]
     pairs = wide // LANES
     left = left_lanes(parts.shape[1])
@@ -434,23 +427,22 @@
         out_ref[...] += term
 
 
-def gate_and_project(me, slots, gates, values, skip_gain, out_weight, chunk, base=None):
-    count = len(slots)
-    blocks = lax.axis_size("seq")
-    block_shape = slots[0].shape[-2:]
+def gate_and_project(me, parts, gates, values, skip_gain, out_weight, chunk, base=None):
+    blocks = parts.shape[0]
     rows = gates.shape[0]
     features = out_weight.shape[1]
     steps = 4
     wide = blocks * HALF // steps
     joined = base is not None
     taken = features // 2 if joined else features
-    in_specs = [pl.BlockSpec(slot.shape, lambda i, me, rank=slot.ndim: (0,) * rank) for slot in slots] + [
+    in_specs = [
+        pl.BlockSpec(parts.shape, lambda i, me: (0, 0, 0)),
         pl.BlockSpec((rows, rows), lambda i, me: (0, 0)),
         pl.BlockSpec((rows, wide), lambda i, me: (0, chunk * steps + i)),
         pl.BlockSpec((rows, wide), lambda i, me: (0, chunk * steps + i)),
         pl.BlockSpec((1, wide), lambda i, me: (0, chunk * steps + i)),
     ]
-    operands = [me, *slots, jnp.asarray(row_order(rows).T), gates, values, skip_gain[None, :], out_weight]
+    operands = [me, parts, jnp.asarray(row_order(rows).T), gates, values, skip_gain[None, :], out_weight]
     out_specs = [pl.BlockSpec((rows, taken), lambda i, me: (0, 0))]
     out_shape = [jax.ShapeDtypeStruct((rows, taken), jnp.float32)]
     if joined:
@@ -462,16 +454,15 @@
     else:
         in_specs.append(pl.BlockSpec((wide, taken), lambda i, me: (chunk * steps + i, 0)))
     return pl.pallas_call(
-        functools.partial(gate_kernel, count, joined),
+        functools.partial(gate_kernel, joined),
         grid_spec=pltpu.PrefetchScalarGridSpec(
             num_scalar_prefetch=1,
             grid=(steps,),
             in_specs=in_specs,
             out_specs=out_specs,
-            scratch_shapes=[pltpu.VMEM((blocks if count > 1 else 1, *block_shape), jnp.bfloat16)],
         ),
         out_shape=out_shape,
-        compiler_params=pltpu.CompilerParams(vmem_limit_bytes=SMALL_BYTES),
+        compiler_params=pltpu.CompilerParams(vmem_limit_bytes=VMEM_BYTES),
         cost_estimate=pl.CostEstimate(
             flops=2 * rows * steps * wide * taken,
             bytes_accessed=2 * steps * wide * taken + 12 * rows * steps * wide,
@@ -513,7 +504,7 @@
             out_specs=pl.BlockSpec((rows, features // 2), lambda i, me: (0, 0)),
         ),
         out_shape=jax.ShapeDtypeStruct((rows, features // 2), jnp.float32),
-        compiler_params=pltpu.CompilerParams(vmem_limit_bytes=SMALL_BYTES),
+        compiler_params=pltpu.CompilerParams(vmem_limit_bytes=VMEM_BYTES),
         cost_estimate=pl.CostEstimate(
             flops=rows * width * features, bytes_accessed=width * features + 8 * rows * width, transcendentals=0
         ),
@@ -534,34 +525,22 @@
         in_specs=[pl.BlockSpec((rows, wide), lambda i: (0, i))] * 2,
         out_specs=pl.BlockSpec((wide, rows), lambda i: (i, 0)),
         out_shape=jax.ShapeDtypeStruct((features, rows), jnp.bfloat16),
-        compiler_params=pltpu.CompilerParams(vmem_limit_bytes=SMALL_BYTES),
+        compiler_params=pltpu.CompilerParams(vmem_limit_bytes=VMEM_BYTES),
         name="join_halves",
     )(kept, came)
 
 
-def exchange(slots):
-    blocks = len(slots)
-    upper, lower = list(range(blocks // 2, blocks)), list(range(1, blocks // 2))
-    order = [slot for pair in zip(upper, lower + [0]) for slot in pair if slot]
-    came = {0: slots[0]}
-    for slot in order:
-        came[slot] = lax.ppermute(slots[slot], "seq", [(j, j ^ slot) for j in range(blocks)])
-    return [came[slot] for slot in range(blocks)]
-
-
 def swap_blocks(array):
-    return [lax.all_to_all(array, "seq", split_axis=0, concat_axis=0, tiled=True)]
+    return lax.all_to_all(array, "seq", split_axis=0, concat_axis=0, tiled=True)
 
 
 def kernel_local(values, gates, filter_taps, skip_gain, out_weight):
     blocks = lax.axis_size("seq")
     me = jnp.stack([lax.axis_index("seq"), lax.axis_index("chan")]).astype(jnp.int32)
-    first = exchange(arrange(me, values, filter_taps, blocks, 0, True))
-    second = swap_blocks(*arrange(me, values, filter_taps, blocks, 1, False))
-    first = swap_blocks(*convolve(me, first, blocks, 0, False))
-    second = exchange(convolve(me, second, blocks, 1, True))
-    (base,) = gate_and_project(me, first, gates, values, skip_gain, out_weight, 0)
-    sent, gated = gate_and_project(me, second, gates, values, skip_gain, out_weight, 1, base)
+    streams = [swap_blocks(arrange(values, filter_taps, blocks, chunk)) for chunk in range(2)]
+    conv = [swap_blocks(convolve(streams[chunk], chunk)) for chunk in range(2)]
+    (base,) = gate_and_project(me, conv[0], gates, values, skip_gain, out_weight, 0)
+    sent, gated = gate_and_project(me, conv[1], gates, values, skip_gain, out_weight, 1, base)
     other = lax.ppermute(sent, "chan", [(0, 1), (1, 0)])
     kept = project_kept(me, gated, out_weight, base)
     return join(kept, other)

time: 147 us -> 121 us (0.82)
  starting transfers between devices: 67.9 us -> 26.6 us
  waiting for transfers between devices: 15.3 us -> 36.6 us
  local copies, waits for them, and re-layouts: 22.5 us -> 1.79 us
  Pallas kernels: 40.6 us -> 54.6 us
    ppermute x30 -> x0, starting transfers between devices: 55.9 us -> none  [exchange(): lax.ppermute(slots[slot], 'seq', [(j, j ^ slot) for j in range(blocks)])]
    all_to_all x2 -> x4, waiting for transfers between devices: 0.01 us -> 36.6 us  [swap_blocks(): return lax.all_to_all(array, 'seq', split_axis=0, concat_axis=0, tiled=True)]
    unnamed x46 -> x10, local copies, waits for them, and re-layouts: 22.5 us -> 1.79 us
    all_to_all x2 -> x4, starting transfers between devices: 11.9 us -> 26.6 us  [swap_blocks(): return lax.all_to_all(array, 'seq', split_axis=0, concat_axis=0, tiled=True)]
    ppermute x30 -> x0, waiting for transfers between devices: 14.6 us -> none  [exchange(): lax.ppermute(slots[slot], 'seq', [(j, j ^ slot) for j in range(blocks)])]
    pallas_call x6, Pallas kernels: 36.9 us -> 46.6 us  [the longest x2 26.2 us: convolve(): pl.pallas_call(convolve_kernel, in_specs=[pl.BlockSpec(memory_space=pl.AN...]
    pallas_call x1, Pallas kernels: 1.96 us -> 4.39 us  [project_kept(): pl.pallas_call(kept_kernel, grid_spec=pltpu.PrefetchScalarGridSpec(num_sc...]
    pallas_call x1, Pallas kernels: 1.73 us -> 3.59 us  [join(): pl.pallas_call(join_kernel, grid=(4,), in_specs=[pl.BlockSpec((rows, wide...]
  transfers between devices with their start and end apart: 33 -> 5, of which waited for: 7 -> 4; matrix products, arithmetic and copies ran while one was open for 0% -> 1% of each run, Pallas kernels for 22% -> 34%
where the time goes in v3:
time: 121 us; the launch traced here: 120 us
  Pallas kernels  54.6 us (45%)
  waiting for transfers between devices  36.6 us (30%)
  starting transfers between devices  26.6 us (22%)
  local copies, waits for them, and re-layouts  1.79 us (1%)
    all_to_all x4, waiting for transfers between devices, swap_blocks(): return lax.all_to_all(array, 'seq', split_axis=0, concat_axis=0, tiled=True)  36.6 us
    all_to_all x4, starting transfers between devices, swap_blocks(): return lax.all_to_all(array, 'seq', split_axis=0, concat_axis=0, tiled=True)  26.6 us
    pallas_call x2, Pallas kernels, convolve(): pl.pallas_call(convolve_kernel, in_specs=[pl.BlockSpec(memory_space=pl.AN...  26.2 us
    pallas_call x2, Pallas kernels, gate_and_project(): pl.pallas_call(functools.partial(gate_kernel, joined), grid_spec=pltpu.Pr...  14.2 us
    pallas_call x2, Pallas kernels, arrange(): pl.pallas_call(functools.partial(arrange_kernel, pieces, chunk), in_specs...  6.2 us
    pallas_call x1, Pallas kernels, project_kept(): pl.pallas_call(kept_kernel, grid_spec=pltpu.PrefetchScalarGridSpec(num_sc...  4.39 us
    pallas_call x1, Pallas kernels, join(): pl.pallas_call(join_kernel, grid=(4,), in_specs=[pl.BlockSpec((rows, wide...  3.59 us
  transfers between devices with their start and end apart: 5, of which 4 were waited for; matrix products, arithmetic and copies ran while one was open for 1% of the time, Pallas kernels for 34%

profile of v3, /device:TPU:0, one launch (start us, length us, event | category | flops | bytes accessed | tf_op | source)
XLA Modules:
  0.0 120.2 jit_solution(16094304862841409372)
XLA Ops:
  0.0 3.1 %arrange_0.1 = bf16[16,256,128]{2,1,0:T(8,128)(2,1)} custom-call(bf16[256,256]{1,0:T(8,128)(2,1)} %constant.16.clone.order_hbm.rest_0_, bf16[256,2048]{1,0:T(8,128)(2,1)} %rest_2_.3, bf16[256,2048]{1,0:T(8,128)(2,1)} %taps_hbm.3), custom_call_target="tpu_custom_call" | custom-call | flops 268435456 | bytes 2097152 | tf_op jit(solution)/shard_map/arrange_0/pallas_call | solution.py:236
  3.1 8.3 %all-to-all-start.2 = ((bf16[16,256,128]{2,1,0:T(8,128)(2,1)}), bf16[16,256,128]{2,1,0:T(8,128)(2,1)S(1)}, u32[]{:S(2)}, u32[]{:S(2)}) async-start(bf16[16,256,128]{2,1,0:T(8,128)(2,1)} %arrange_0.1), calls=%async_computation.2 | async-start | bytes 2097152 | tf_op jit(solution)/shard_map/all_to_all | solution.py:534
  11.4 3.1 %arrange_1.1 = bf16[16,256,128]{2,1,0:T(8,128)(2,1)} custom-call(bf16[256,256]{1,0:T(8,128)(2,1)} %constant.16.clone.order_hbm.rest_0_, bf16[256,2048]{1,0:T(8,128)(2,1)} %rest_2_.3, bf16[256,2048]{1,0:T(8,128)(2,1)} %taps_hbm.3), custom_call_target="tpu_custom_call" | custom-call | flops 268435456 | bytes 2097152 | tf_op jit(solution)/shard_map/arrange_1/pallas_call | solution.py:236
  14.6 21.3 %all-to-all-done.2.streams_hbm = bf16[16,256,128]{2,1,0:T(8,128)(2,1)S(1)} async-done(((bf16[16,256,128]{2,1,0:T(8,128)(2,1)}), bf16[16,256,128]{2,1,0:T(8,128)(2,1)S(1)}, u32[]{:S(2)}, u32[]{:S(2)}) %all-to-all-start.2) | async-done | bytes 1048608 | tf_op jit(solution)/shard_map/all_to_all | solution.py:534
  35.9 5.8 %all-to-all-start = ((bf16[16,256,128]{2,1,0:T(8,128)(2,1)}), bf16[16,256,128]{2,1,0:T(8,128)(2,1)S(1)}, u32[]{:S(2)}, u32[]{:S(2)}) async-start(bf16[16,256,128]{2,1,0:T(8,128)(2,1)} %arrange_1.1), calls=%async_computation | async-start | bytes 2097152 | tf_op jit(solution)/shard_map/all_to_all | solution.py:534
  41.7 0.0 copy-done.3
  41.7 13.1 %long_convolution_0.1 = bf16[16,128,128]{2,1,0:T(8,128)(2,1)} custom-call(bf16[16,256,128]{2,1,0:T(8,128)(2,1)} %copy-done.3, bf16[512,512]{1,0:T(8,128)(2,1)} %constant.17.clone.forward_hbm, f32[256,128]{1,0:T(8,128)} %constant.18.clone.turns_hbm, bf16[512,512]{1,0:T(8,128)(2,1)} %constant.19.clone.backward_hbm), custom_call_target="tpu_custom_call" | custom-call | flops 6000000000 | bytes 24000000 | tf_op jit(solution)/shard_map/long_convolution_0/pallas_call | solution.py:375
  54.8 9.8 %all-to-all-done.streams_hbm = bf16[16,256,128]{2,1,0:T(8,128)(2,1)S(1)} async-done(((bf16[16,256,128]{2,1,0:T(8,128)(2,1)}), bf16[16,256,128]{2,1,0:T(8,128)(2,1)S(1)}, u32[]{:S(2)}, u32[]{:S(2)}) %all-to-all-start) | async-done | bytes 1048608 | tf_op jit(solution)/shard_map/all_to_all | solution.py:534
  64.7 6.0 %all-to-all-start.3 = ((bf16[16,128,128]{2,1,0:T(8,128)(2,1)}), bf16[16,128,128]{2,1,0:T(8,128)(2,1)S(1)}, u32[]{:S(2)}, u32[]{:S(2)}) async-start(bf16[16,128,128]{2,1,0:T(8,128)(2,1)} %long_convolution_0.1), calls=%async_computation.3 | async-start | bytes 1048576 | tf_op jit(solution)/shard_map/all_to_all | solution.py:534
  70.7 0.0 copy-done.2
  70.7 13.1 %long_convolution_1.1 = bf16[16,128,128]{2,1,0:T(8,128)(2,1)} custom-call(bf16[16,256,128]{2,1,0:T(8,128)(2,1)} %copy-done.2, bf16[512,512]{1,0:T(8,128)(2,1)} %constant.17.clone.forward_hbm, f32[256,128]{1,0:T(8,128)} %constant.18.clone.turns_hbm, bf16[512,512]{1,0:T(8,128)(2,1)} %constant.19.clone.backward_hbm), custom_call_target="tpu_custom_call" | custom-call | flops 6000000000 | bytes 24000000 | tf_op jit(solution)/shard_map/long_convolution_1/pallas_call | solution.py:375
  83.8 0.5 all-to-all-done.3.parts
  84.3 6.4 %all-to-all-start.1 = ((bf16[16,128,128]{2,1,0:T(8,128)(2,1)}), bf16[16,128,128]{2,1,0:T(8,128)(2,1)S(1)}, u32[]{:S(2)}, u32[]{:S(2)}) async-start(bf16[16,128,128]{2,1,0:T(8,128)(2,1)} %long_convolution_1.1), calls=%async_computation.1 | async-start | bytes 1048576 | tf_op jit(solution)/shard_map/all_to_all | solution.py:534
  90.7 0.7 pad_add_fusion.me_ref
  91.4 0.0 copy-done
  91.4 7.5 %gate_project_0.1.rest_5_.base_ref = f32[256,2048]{1,0:T(8,128)} custom-call(s32[2]{0:T(128)} %pad_add_fusion.me_ref, bf16[16,128,128]{2,1,0:T(8,128)(2,1)} %copy-done, bf16[256,256]{1,0:T(8,128)(2,1)} %constant.16.clone.order_hbm.rest_0_, bf16[256,2048]{1,0:T(8,128)(2,1)} %rest_1_.3, bf16[256,2048]{1,0:T(8,128)(2,1)} %rest_2_.3, f32[1,2048]{1,0:T(1,128)} %bitcast.3, ...), custom_call_target="tpu_custom_call" | custom-call | flops 1073741824 | bytes 7340032 | tf_op jit(solution)/shard_map/gate_project_0/pallas_call | solution.py:456
  98.9 4.9 %all-to-all-done.1.parts = bf16[16,128,128]{2,1,0:T(8,128)(2,1)S(1)} async-done(((bf16[16,128,128]{2,1,0:T(8,128)(2,1)}), bf16[16,128,128]{2,1,0:T(8,128)(2,1)S(1)}, u32[]{:S(2)}, u32[]{:S(2)}) %all-to-all-start.1) | async-done | bytes 524320 | tf_op jit(solution)/shard_map/all_to_all | solution.py:534
  103.8 0.8 copy-done.1
  104.6 6.7 %gate_project_1.1 = (f32[256,1024]{1,0:T(8,128)}, bf16[256,1024]{1,0:T(8,128)(2,1)}) custom-call(s32[2]{0:T(128)} %pad_add_fusion.me_ref, bf16[16,128,128]{2,1,0:T(8,128)(2,1)} %copy-done.1, bf16[256,256]{1,0:T(8,128)(2,1)} %constant.16.clone.order_hbm.rest_0_, bf16[256,2048]{1,0:T(8,128)(2,1)} %rest_1_.3, bf16[256,2048]{1,0:T(8,128)(2,1)} %rest_2_.3, ...), custom_call_target="tpu_custom_call" | custom-call | flops 536870912 | bytes 5242880 | tf_op jit(solution)/shard_map/gate_project_1/pallas_call | solution.py:456
  111.2 0.0 collective-permute-start
  111.2 4.4 %project_kept.1.kept_ref = f32[256,1024]{1,0:T(8,128)} custom-call(s32[2]{0:T(128)} %pad_add_fusion.me_ref, bf16[256,1024]{1,0:T(8,128)(2,1)} %get-tuple-element.7.gated_ref, bf16[2048,2048]{1,0:T(8,128)(2,1)} %weight_ref.1, f32[256,2048]{1,0:T(8,128)} %gate_project_0.1.rest_5_.base_ref), custom_call_target="tpu_custom_call" | custom-call | flops 536870912 | bytes 4194304 | tf_op jit(solution)/shard_map/project_kept/pallas_call | solution.py:494
  115.6 0.0 collective-permute-done.came_ref
  115.6 1.0 copy-done.4
  116.6 3.6 %join_halves.1 = bf16[1024,256]{1,0:T(8,128)(2,1)} custom-call(f32[256,1024]{1,0:T(8,128)} %project_kept.1.kept_ref, f32[256,1024]{1,0:T(8,128)} %copy-done.4), custom_call_target="tpu_custom_call" | custom-call | tf_op jit(solution)/shard_map/join_halves/pallas_call | solution.py:522
  (5 shorter events, 0.0 us)
Async XLA Ops:
  3.1 32.8 %all-to-all-start.2 = ((bf16[16,256,128]{2,1,0:T(8,128)(2,1)}), bf16[16,256,128]{2,1,0:T(8,128)(2,1)S(1)}, u32[]{:S(2)}, u32[]{:S(2)}) async-start(bf16[16,256,128]{2,1,0:T(8,128)(2,1)} %arrange_0.1), calls=%async_computation.2 | async-start | bytes 2097152 | tf_op jit(solution)/shard_map/all_to_all | solution.py:534
  35.9 5.8 %copy-start.3 = (bf16[16,256,128]{2,1,0:T(8,128)(2,1)}, bf16[16,256,128]{2,1,0:T(8,128)(2,1)S(1)}, u32[]{:S(2)}) copy-start(bf16[16,256,128]{2,1,0:T(8,128)(2,1)S(1)} %all-to-all-done.2.streams_hbm) | copy-start | bytes 3145732
  35.9 28.8 %all-to-all-start = ((bf16[16,256,128]{2,1,0:T(8,128)(2,1)}), bf16[16,256,128]{2,1,0:T(8,128)(2,1)S(1)}, u32[]{:S(2)}, u32[]{:S(2)}) async-start(bf16[16,256,128]{2,1,0:T(8,128)(2,1)} %arrange_1.1), calls=%async_computation | async-start | bytes 2097152 | tf_op jit(solution)/shard_map/all_to_all | solution.py:534
  64.7 6.0 %copy-start.2 = (bf16[16,256,128]{2,1,0:T(8,128)(2,1)}, bf16[16,256,128]{2,1,0:T(8,128)(2,1)S(1)}, u32[]{:S(2)}) copy-start(bf16[16,256,128]{2,1,0:T(8,128)(2,1)S(1)} %all-to-all-done.streams_hbm) | copy-start | bytes 3145732
  64.7 19.6 %all-to-all-start.3 = ((bf16[16,128,128]{2,1,0:T(8,128)(2,1)}), bf16[16,128,128]{2,1,0:T(8,128)(2,1)S(1)}, u32[]{:S(2)}, u32[]{:S(2)}) async-start(bf16[16,128,128]{2,1,0:T(8,128)(2,1)} %long_convolution_0.1), calls=%async_computation.3 | async-start | bytes 1048576 | tf_op jit(solution)/shard_map/all_to_all | solution.py:534
  84.3 7.1 %copy-start = (bf16[16,128,128]{2,1,0:T(8,128)(2,1)}, bf16[16,128,128]{2,1,0:T(8,128)(2,1)S(1)}, u32[]{:S(2)}) copy-start(bf16[16,128,128]{2,1,0:T(8,128)(2,1)S(1)} %all-to-all-done.3.parts) | copy-start | bytes 1572868
  84.3 19.5 %all-to-all-start.1 = ((bf16[16,128,128]{2,1,0:T(8,128)(2,1)}), bf16[16,128,128]{2,1,0:T(8,128)(2,1)S(1)}, u32[]{:S(2)}, u32[]{:S(2)}) async-start(bf16[16,128,128]{2,1,0:T(8,128)(2,1)} %long_convolution_1.1), calls=%async_computation.1 | async-start | bytes 1048576 | tf_op jit(solution)/shard_map/all_to_all | solution.py:534
  103.8 0.8 copy-start.1
  111.2 4.4 %collective-permute-start = (f32[256,1024]{1,0:T(8,128)}, f32[256,1024]{1,0:T(8,128)S(1)}, u32[]{:S(2)}, u32[]{:S(2)}) collective-permute-start(f32[256,1024]{1,0:T(8,128)} %get-tuple-element.8), channel_id=1, source_target_pairs={{0,1},{1,0},{2,3},{3,2},{4,5},{5,4},{6,7},{7,6},{8,9},{9,8},{10,11... | collective-permute-start | bytes 3145736 | tf_op jit(solution)/shard_map/ppermute | solution.py:544
  115.6 1.0 copy-start.4

commit v4 on v0

--- a/solution.py
+++ b/solution.py
@@ -14,7 +14,8 @@
 HIGH = lax.Precision.HIGHEST
 RADIX = 16
 LANES = 128
-VMEM_BYTES = 56 * 1024 * 1024
+Q_ORDER = [low + 4 * high for low in range(4) for high in range(4)]
+VMEM_BYTES = 60 * 1024 * 1024
 
 
 def angle_table(first, second, period):
@@ -112,24 +113,25 @@
 @functools.lru_cache(maxsize=None)
 def transform_tables(length):
     inner = length // RADIX
-    q = np.arange(RADIX)[:, None, None]
-    k = np.arange(inner)[None, :, None]
-    m = np.arange(inner)[None, None, :]
-    phase = ((RADIX * m + q) * (4 * k + 1)) % (4 * length)
-    angles = phase * (TWO_PI / (4 * length))
-    table = np.concatenate([np.cos(angles), -np.sin(angles)], axis=1)
-    forward = np.stack(split_table(table), axis=1)
-    backward = np.stack(split_table(table.transpose(0, 2, 1) / length), axis=1)
-    return forward, backward
+    k = np.arange(inner)[:, None]
+    m = np.arange(inner)[None, :]
+    angles = (RADIX * m * (4 * k + 1)) % (4 * length) * (TWO_PI / (4 * length))
+    table = np.concatenate([np.cos(angles), -np.sin(angles)], axis=0)
+    forward = np.concatenate(split_table(table), axis=1)
+    backward = np.concatenate(split_table(table.T / length), axis=0)
+    turns = (np.array(Q_ORDER)[:, None] * (4 * k.T + 1)) % (4 * length) * (TWO_PI / (4 * length))
+    turns = np.stack([np.cos(turns), np.sin(turns)], axis=1).astype(np.float32)
+    turns = np.ascontiguousarray(np.broadcast_to(turns[..., None], (*turns.shape, LANES)))
+    return forward, turns, backward
 
 
 @functools.lru_cache(maxsize=None)
 def row_order(rows):
     chunk = rows // RADIX
     order = np.zeros((rows, rows), np.float32)
-    for q in range(RADIX):
+    for i, q in enumerate(Q_ORDER):
         for j in range(chunk):
-            order[q * chunk + j, RADIX * j + q] = 1.0
+            order[i * chunk + j, RADIX * j + q] = 1.0
     return order.astype(ml_dtypes.bfloat16)
 
 
@@ -170,133 +172,235 @@
     )
 
 
-def sixteen_points(points, sign):
-    out = [None] * 16
-    columns = []
-    for low in range(4):
-        column = four_points([points[low + 4 * high] for high in range(4)], sign)
-        columns.append([turn(column[k], low * k, sign) for k in range(4)])
-    for k in range(4):
-        row = four_points([columns[low][k] for low in range(4)], sign)
-        for high in range(4):
-            out[k + 4 * high] = row[high]
-    return out
-
-
-def arrange_kernel(group, order_ref, values_ref, taps_ref, out_ref):
-    order = order_ref[...]
-    for index, source in enumerate((values_ref, taps_ref)):
-        moved = jnp.dot(order, source[...], preferred_element_type=jnp.float32).astype(jnp.bfloat16)
-        for part in range(group):
-            out_ref[part, index] = moved[:, part * LANES : (part + 1) * LANES]
+def turned(point, cos, sin, sign):
+    re, im = point
+    if sign < 0:
+        return (re * cos + im * sin, im * cos - re * sin)
+    return (re * cos - im * sin, im * cos + re * sin)
+
+
+def arrange_kernel(pieces, order_hbm, values_hbm, taps_hbm, out_hbm, order_ref, values_ref, taps_ref, packed, sems):
+    piece = values_ref.shape[1] // pieces
+    loads = [pltpu.make_async_copy(order_hbm, order_ref, sems.at[3 * pieces])]
+    stores = []
+    for part in range(pieces):
+        lanes = pl.ds(part * piece, piece)
+        loads.append(pltpu.make_async_copy(values_hbm.at[:, lanes], values_ref.at[:, lanes], sems.at[3 * part]))
+        loads.append(pltpu.make_async_copy(taps_hbm.at[:, lanes], taps_ref.at[:, lanes], sems.at[3 * part + 1]))
+        taken = pl.ds(part * piece // LANES, piece // LANES)
+        stores.append(pltpu.make_async_copy(packed.at[taken], out_hbm.at[taken], sems.at[3 * part + 2]))
+    for load in loads:
+        load.start()
+    loads[0].wait()
+    for part in range(pieces):
+        for side, source in enumerate((values_ref, taps_ref)):
+            loads[2 * part + 1 + side].wait()
+            lanes = pl.ds(part * piece, piece)
+            moved = jnp.dot(order_ref[...], source[:, lanes], preferred_element_type=jnp.float32).astype(jnp.bfloat16)
+            for block in range(piece // LANES):
+                packed[part * piece // LANES + block, :, pl.ds(side * LANES, LANES)] = moved[
+                    :, block * LANES : (block + 1) * LANES
+                ]
+        stores[part].start()
+    for store in stores:
+        store.wait()
 
 
 def arrange(values, taps, blocks):
-    rows, width = values.shape
-    group = 4
+    rows, wide = values.shape
+    pieces = 8
     return pl.pallas_call(
-        functools.partial(arrange_kernel, group),
-        grid=(blocks // group,),
-        out_shape=jax.ShapeDtypeStruct((blocks, 2, rows, LANES), jnp.bfloat16),
-        in_specs=[
-            pl.BlockSpec((rows, rows), lambda i: (0, 0)),
-            pl.BlockSpec((rows, group * LANES), lambda i: (0, i)),
-            pl.BlockSpec((rows, group * LANES), lambda i: (0, i)),
+        functools.partial(arrange_kernel, pieces),
+        in_specs=[pl.BlockSpec(memory_space=pl.ANY)] * 3,
+        out_specs=pl.BlockSpec(memory_space=pl.ANY),
+        out_shape=jax.ShapeDtypeStruct((blocks, rows, 2 * LANES), jnp.bfloat16),
+        scratch_shapes=[
+            pltpu.VMEM((rows, rows), jnp.bfloat16),
+            pltpu.VMEM((rows, wide), jnp.bfloat16),
+            pltpu.VMEM((rows, wide), jnp.bfloat16),
+            pltpu.VMEM((blocks, rows, 2 * LANES), jnp.bfloat16),
+            pltpu.SemaphoreType.DMA((3 * pieces + 1,)),
         ],
-        out_specs=pl.BlockSpec((group, 2, rows, LANES), lambda i: (i, 0, 0, 0)),
         compiler_params=pltpu.CompilerParams(vmem_limit_bytes=VMEM_BYTES),
+        cost_estimate=pl.CostEstimate(
+            flops=4 * rows * rows * wide, bytes_accessed=8 * rows * wide, transcendentals=0
+        ),
         name="arrange_rows",
     )(jnp.asarray(row_order(rows)), values, taps)
 
 
-def convolve_kernel(step_q, steps, streams_ref, forward_ref, backward_ref, out_ref, spectra):
-    phase, step = pl.program_id(0), pl.program_id(1)
-    blocks, _, _, chunk, lanes = streams_ref.shape
+def convolve_kernel(
+    streams_hbm, forward_hbm, turns_hbm, backward_hbm, out_hbm,
+    streams, forward_ref, turns_ref, backward_ref,
+    raw_even, raw_odd, columns, mixed, halves_even, halves_odd, signals, sems,
+):
+    blocks, rows, _ = streams.shape
+    chunk = rows // RADIX
     inner = blocks * chunk
-    half = inner
-
-    @pl.when(phase == 0)
-    def _():
-        for part in range(step_q):
-            q = step * step_q + part
-            value = streams_ref[:, 0, pl.ds(q, 1), :, :].reshape(inner, lanes)
-            taps = streams_ref[:, 1, pl.ds(q, 1), :, :].reshape(inner, lanes)
-            pair = jnp.concatenate([value, taps], axis=1)
-            spectra[q] = jnp.dot(
-                forward_ref[part, 0], pair, preferred_element_type=jnp.float32
-            ) + jnp.dot(forward_ref[part, 1], pair, preferred_element_type=jnp.float32)
-
-    @pl.when((phase == 0) & (step == steps - 1))
-    def _():
-        def rows_step(index, carry):
-            upper = pl.ds(pl.multiple_of(index * 8, 8), 8)
-            lower = pl.ds(pl.multiple_of(half + index * 8, 8), 8)
-            left, right = pl.ds(0, lanes), pl.ds(lanes, lanes)
-            value = sixteen_points(
-                [(spectra[q, upper, left], spectra[q, lower, left]) for q in range(RADIX)], -1
-            )
-            taps = sixteen_points(
-                [(spectra[q, upper, right], spectra[q, lower, right]) for q in range(RADIX)], -1
-            )
+    group = rows // 4
+    raws = (raw_even, raw_odd)
+    halves = (halves_even, halves_odd)
+    load_forward = pltpu.make_async_copy(forward_hbm, forward_ref, sems.at[0])
+    load_backward = pltpu.make_async_copy(backward_hbm, backward_ref, sems.at[1])
+    load_streams, load_turns, stores = [], [], []
+    for low in range(4):
+        taken = pl.ds(low * group, group)
+        load_streams.append(pltpu.make_async_copy(streams_hbm.at[:, taken], streams.at[:, taken], sems.at[2 + low]))
+        four = pl.ds(4 * low, 4)
+        load_turns.append(pltpu.make_async_copy(turns_hbm.at[four], turns_ref.at[four], sems.at[6 + low]))
+        stores.append(pltpu.make_async_copy(signals.at[:, taken], out_hbm.at[:, taken], sems.at[10 + low]))
+    load_forward.start()
+    load_streams[0].start()
+    load_streams[1].start()
+    load_turns[0].start()
+    load_streams[2].start()
+    load_turns[1].start()
+    load_streams[3].start()
+    load_turns[2].start()
+    load_turns[3].start()
+    load_backward.start()
+
+    def transform(low, high):
+        taken = pl.ds(pl.multiple_of(low * group + high * chunk, chunk), chunk)
+        stream = streams[:, taken].reshape(inner, 2 * LANES)
+        raws[low % 2][high] = jnp.dot(
+            forward_ref[...], jnp.concatenate([stream, stream], axis=0), preferred_element_type=jnp.float32
+        )
+
+    def first_pass(low, start):
+        raw = raws[low % 2]
+        upper, lower = pl.ds(start, 8), pl.ds(inner + start, 8)
+        for side in range(2):
+            lanes = pl.ds(side * LANES, LANES)
+            points = []
+            for high in range(4):
+                point = (raw[high, upper, lanes], raw[high, lower, lanes])
+                if low + high:
+                    turns = [turns_ref[4 * low + high, part, upper] for part in range(2)]
+                    point = turned(point, *turns, -1)
+                points.append(point)
+            for k, point in enumerate(four_points(points, -1)):
+                point = turn(point, low * k, -1)
+                columns[4 * low + k, upper, lanes] = point[0]
+                columns[4 * low + k, lower, lanes] = point[1]
+
+    def first_rows(low, start, count):
+        for part in range(count):
+            first_pass(low, pl.multiple_of(start + 8 * part, 8))
+
+    steps = inner // 4
+
+    load_forward.wait()
+    load_streams[0].wait()
+
+    def alone(high, carry):
+        transform(0, high)
+        return carry
+
+    lax.fori_loop(0, 4, alone, 0)
+    for low in range(1, 4):
+        load_streams[low].wait()
+        load_turns[low - 1].wait()
+
+        def beside(high, carry, low=low):
+            transform(low, high)
+            first_rows(low - 1, high * steps, steps // 8)
+            return carry
+
+        lax.fori_loop(0, 4, beside, 0)
+    load_turns[3].wait()
+
+    def middle(index, carry):
+        start = pl.multiple_of(index * 8, 8)
+        first_pass(3, start)
+        upper, lower = pl.ds(start, 8), pl.ds(inner + start, 8)
+        for k in range(4):
+            sides = []
+            for side in range(2):
+                lanes = pl.ds(side * LANES, LANES)
+                points = [(columns[4 * low + k, upper, lanes], columns[4 * low + k, lower, lanes]) for low in range(4)]
+                sides.append(four_points(points, -1))
             product = [
-                (a[0] * b[0] - a[1] * b[1], a[0] * b[1] + a[1] * b[0]) for a, b in zip(value, taps)
+                (a[0] * b[0] - a[1] * b[1], a[0] * b[1] + a[1] * b[0]) for a, b in zip(*sides)
             ]
-            back = sixteen_points(product, 1)
-            for q in range(RADIX):
-                spectra[q, upper, left] = back[q][0]
-                spectra[q, lower, left] = back[q][1]
+            for part, point in enumerate(four_points(product, 1)):
+                point = turn(point, k * part, 1)
+                mixed[4 * part + k, upper] = point[0]
+                mixed[4 * part + k, lower] = point[1]
+        return carry
+
+    lax.fori_loop(0, inner // 8, middle, 0)
+
+    def last_pass(low, start):
+        target = halves[low % 2]
+        upper, lower = pl.ds(start, 16), pl.ds(inner + start, 16)
+        points = [(mixed[4 * low + k, upper], mixed[4 * low + k, lower]) for k in range(4)]
+        for high, point in enumerate(four_points(points, 1)):
+            if low + high:
+                turns = [turns_ref[4 * low + high, part, upper] for part in range(2)]
+                point = turned(point, *turns, 1)
+            for part, taken in zip(point, (upper, lower)):
+                rounded = part.astype(jnp.bfloat16)
+                target[high, taken, pl.ds(0, LANES)] = rounded
+                target[high, taken, pl.ds(LANES, LANES)] = (part - rounded.astype(jnp.float32)).astype(jnp.bfloat16)
+
+    def last_rows(low, start, count):
+        for part in range(count):
+            last_pass(low, pl.multiple_of(start + 16 * part, 16))
+
+    def restore(low, high):
+        terms = jnp.dot(backward_ref[...], halves[low % 2][high], preferred_element_type=jnp.float32)
+        signal = terms[:inner, :LANES] + terms[:inner, LANES:] + terms[inner:, :LANES]
+        taken = pl.ds(pl.multiple_of(low * group + high * chunk, chunk), chunk)
+        signals[:, taken] = signal.astype(jnp.bfloat16).reshape(blocks, chunk, LANES)
+
+    def prepare(index, carry):
+        last_rows(0, index * steps, steps // 16)
+        return carry
+
+    lax.fori_loop(0, 4, prepare, 0)
+    load_backward.wait()
+    for low in range(4):
+
+        def back(high, carry, low=low):
+            restore(low, high)
+            if low < 3:
+                last_rows(low + 1, high * steps, steps // 16)
             return carry
 
-        lax.fori_loop(0, half // 8, rows_step, 0)
-
-    @pl.when(phase == 1)
-    def _():
-        for part in range(step_q):
-            q = step * step_q + part
-            points = spectra[q, :, pl.ds(0, lanes)]
-            high = points.astype(jnp.bfloat16)
-            low = (points - high.astype(jnp.float32)).astype(jnp.bfloat16)
-            both = jnp.dot(
-                backward_ref[part, 0],
-                jnp.concatenate([high, low], axis=1),
-                preferred_element_type=jnp.float32,
-            )
-            signal = (
-                both[:, :lanes]
-                + both[:, lanes:]
-                + jnp.dot(backward_ref[part, 1], high, preferred_element_type=jnp.float32)
-            )
-            out_ref[:, part] = signal.astype(jnp.bfloat16).reshape(blocks, chunk, lanes)
-
-
-def convolve(streams, blocks, rows):
+        lax.fori_loop(0, 4, back, 0)
+        stores[low].start()
+    for store in stores:
+        store.wait()
+
+
+def convolve(streams):
+    blocks, rows, lanes = streams.shape
     length = blocks * rows
-    chunk = rows // RADIX
     inner = length // RADIX
-    forward, backward = transform_tables(length)
-    step_q = 2
-    steps = RADIX // step_q
     return pl.pallas_call(
-        functools.partial(convolve_kernel, step_q, steps),
-        grid=(2, steps),
-        out_shape=jax.ShapeDtypeStruct((blocks, RADIX, chunk, LANES), jnp.bfloat16),
-        in_specs=[
-            pl.BlockSpec((blocks, 2, RADIX, chunk, LANES), lambda p, i: (0, 0, 0, 0, 0)),
-            pl.BlockSpec(
-                (step_q, 2, 2 * inner, inner),
-                lambda p, i: (i * (1 - p) + (steps - 1) * p, 0, 0, 0),
-            ),
-            pl.BlockSpec((step_q, 2, inner, 2 * inner), lambda p, i: (i * p, 0, 0, 0)),
+        convolve_kernel,
+        in_specs=[pl.BlockSpec(memory_space=pl.ANY)] * 4,
+        out_specs=pl.BlockSpec(memory_space=pl.ANY),
+        out_shape=jax.ShapeDtypeStruct((blocks, rows, LANES), jnp.bfloat16),
+        scratch_shapes=[
+            pltpu.VMEM(streams.shape, jnp.bfloat16),
+            pltpu.VMEM((2 * inner, 2 * inner), jnp.bfloat16),
+            pltpu.VMEM((RADIX, 2, inner, LANES), jnp.float32),
+            pltpu.VMEM((2 * inner, 2 * inner), jnp.bfloat16),
+            pltpu.VMEM((4, 2 * inner, lanes), jnp.float32),
+            pltpu.VMEM((4, 2 * inner, lanes), jnp.float32),
+            pltpu.VMEM((RADIX, 2 * inner, lanes), jnp.float32),
+            pltpu.VMEM((RADIX, 2 * inner, LANES), jnp.float32),
+            pltpu.VMEM((4, 2 * inner, lanes), jnp.bfloat16),
+            pltpu.VMEM((4, 2 * inner, lanes), jnp.bfloat16),
+            pltpu.VMEM((blocks, rows, LANES), jnp.bfloat16),
+            pltpu.SemaphoreType.DMA((14,)),
         ],
-        out_specs=pl.BlockSpec((blocks, step_q, chunk, LANES), lambda p, i: (0, i * p, 0, 0)),
-        scratch_shapes=[pltpu.VMEM((RADIX, 2 * inner, 2 * LANES), jnp.float32)],
         compiler_params=pltpu.CompilerParams(vmem_limit_bytes=VMEM_BYTES),
+        cost_estimate=pl.CostEstimate(flops=9 * 10**9, bytes_accessed=9 * 10**6, transcendentals=0),
         name="long_convolution",
-    )(
-        streams.reshape(blocks, 2, RADIX, chunk, LANES),
-        jnp.asarray(forward),
-        jnp.asarray(backward),
-    )
+    )(streams, *(jnp.asarray(table) for table in transform_tables(length)))
 
 
 def gate_kernel(group, half_ref, order_ref, conv_ref, gates_ref, values_ref, skip_ref, weight_ref, gated_ref, out_ref):
@@ -392,7 +496,7 @@
 
 
 def join_kernel(kept_ref, came_ref, out_ref):
-    out_ref[...] = (kept_ref[...] + came_ref[...]).T.astype(jnp.bfloat16)
+    out_ref[...] = (kept_ref[...] + came_ref[...]).astype(jnp.bfloat16).T
 
 
 def join(kept, came):
@@ -409,18 +513,18 @@
     )(kept, came)
 
 
+def swap_blocks(array):
+    return lax.all_to_all(array, "seq", split_axis=0, concat_axis=0, tiled=True)
+
+
 def kernel_local(values, gates, filter_taps, skip_gain, out_weight):
-    rows, _ = values.shape
     blocks = lax.axis_size("seq")
-    streams = arrange(values, filter_taps, blocks)
-    streams = lax.all_to_all(streams, "seq", split_axis=0, concat_axis=0, tiled=True)
-    conv = convolve(streams, blocks, rows).reshape(blocks, rows, LANES)
-    conv = lax.all_to_all(conv, "seq", split_axis=0, concat_axis=0, tiled=True)
+    conv = swap_blocks(convolve(swap_blocks(arrange(values, filter_taps, blocks))))
     half = lax.axis_index("chan").astype(jnp.int32)[None]
     gated, sent = gate_and_project(half, conv, gates, values, skip_gain, out_weight)
-    came = lax.ppermute(sent, "chan", [(0, 1), (1, 0)])
+    other = lax.ppermute(sent, "chan", [(0, 1), (1, 0)])
     kept = project_kept(half, gated, out_weight)
-    return join(kept, came)
+    return join(kept, other)
 
 
 def takes_kernels(mesh, values, out_weight):
@@ -428,9 +532,8 @@
     rows = values.shape[0] // blocks
     return (
         halves == 2
-        and blocks % 4 == 0
+        and blocks == 16
         and rows == 256
-        and blocks * rows == 4096
         and values.shape[1] == halves * blocks * LANES
         and out_weight.shape[1] % (8 * LANES) == 0
     )

time: 128 us -> 124 us (0.969)
  Pallas kernels: 39.3 us -> 35.7 us
    pallas_call x2, Pallas kernels: 23.9 us -> 20.3 us  [the longest x1 14.9 us: convolve(): pl.pallas_call(convolve_kernel, in_specs=[pl.BlockSpec(memory_space=pl.AN...]
where the time goes in v4:
time: 124 us; the launch traced here: 123 us
  blocking collectives  57.3 us (46%)
  Pallas kernels  35.7 us (29%)
  waiting for transfers between devices  23.7 us (19%)
  starting transfers between devices  3.92 us (3%)
  local copies, waits for them, and re-layouts  1.96 us (2%)
    all_to_all x1, blocking collectives, swap_blocks(): return lax.all_to_all(array, 'seq', split_axis=0, concat_axis=0, tiled=True)  57.3 us
    all_to_all x1, waiting for transfers between devices, swap_blocks(): return lax.all_to_all(array, 'seq', split_axis=0, concat_axis=0, tiled=True)  23.7 us
    pallas_call x1, Pallas kernels, convolve(): pl.pallas_call(convolve_kernel, in_specs=[pl.BlockSpec(memory_space=pl.AN...  14.9 us
    pallas_call x1, Pallas kernels, gate_and_project(): pl.pallas_call(functools.partial(gate_kernel, group), grid_spec=pltpu.Pre...  6.5 us
    pallas_call x1, Pallas kernels, arrange(): pl.pallas_call(functools.partial(arrange_kernel, pieces), in_specs=[pl.Bl...  5.39 us
    pallas_call x1, Pallas kernels, project_kept(): pl.pallas_call(kept_kernel, grid_spec=pltpu.PrefetchScalarGridSpec(num_sc...  5.31 us
    all_to_all x1, starting transfers between devices, swap_blocks(): return lax.all_to_all(array, 'seq', split_axis=0, concat_axis=0, tiled=True)  3.91 us
    pallas_call x1, Pallas kernels, join(): pl.pallas_call(join_kernel, grid=(4,), in_specs=[pl.BlockSpec((rows, wide...  3.59 us
  transfers between devices with their start and end apart: 2, of which 1 were waited for; matrix products, arithmetic and copies ran while one was open for 0% of the time, Pallas kernels for 4%

profile of v4, /device:TPU:0, one launch (start us, length us, event | category | flops | bytes accessed | tf_op | source)
XLA Modules:
  0.0 122.6 jit_solution(11339542860299408972)
XLA Ops:
  0.0 5.4 %arrange_rows.1 = bf16[16,256,256]{2,1,0:T(8,128)(2,1)} custom-call(bf16[256,256]{1,0:T(8,128)(2,1)} %constant.14.clone.order_hbm, bf16[256,2048]{1,0:T(8,128)(2,1)} %values_ref.1, bf16[256,2048]{1,0:T(8,128)(2,1)} %taps_hbm.1), custom_call_target="tpu_custom_call" | custom-call | flops 536870912 | bytes 4194304 | tf_op jit(solution)/shard_map/arrange_rows/pallas_call | solution.py:212
  5.4 57.3 %all_to_all.10.streams_hbm = bf16[16,256,256]{2,1,0:T(8,128)(2,1)} all-to-all(bf16[16,256,256]{2,1,0:T(8,128)(2,1)} %arrange_rows.1), channel_id=1, replica_groups=mesh['seq'=16,'chan'=2] {'seq'}, dimensions={0} | all-to-all | bytes 4194304 | tf_op jit(solution)/shard_map/all_to_all | solution.py:517
  62.7 14.9 %long_convolution.1 = bf16[16,256,128]{2,1,0:T(8,128)(2,1)} custom-call(bf16[16,256,256]{2,1,0:T(8,128)(2,1)} %all_to_all.10.streams_hbm, bf16[512,512]{1,0:T(8,128)(2,1)} %constant.15.clone.forward_hbm, f32[16,2,256,128]{3,2,1,0:T(8,128)} %constant.16.clone.turns_hbm, bf16[512,512]{1,0:T(8,128)(2,1)} %constant.17.clone.backward_hbm), custom_call_target="tpu_custom_call" | custom-call | flops 8999999488 | bytes 9000000 | tf_op jit(solution)/shard_map/long_convolution/pallas_call | solution.py:381
  77.6 3.9 %all-to-all-start.1 = ((bf16[16,256,128]{2,1,0:T(8,128)(2,1)}), bf16[16,256,128]{2,1,0:T(8,128)(2,1)S(1)}, u32[]{:S(2)}, u32[]{:S(2)}) async-start(bf16[16,256,128]{2,1,0:T(8,128)(2,1)} %long_convolution.1), calls=%async_computation.1 | async-start | bytes 2097152 | tf_op jit(solution)/shard_map/all_to_all | solution.py:517
  81.5 23.7 %all-to-all-done.1.conv_ref = bf16[16,256,128]{2,1,0:T(8,128)(2,1)S(1)} async-done(((bf16[16,256,128]{2,1,0:T(8,128)(2,1)}), bf16[16,256,128]{2,1,0:T(8,128)(2,1)S(1)}, u32[]{:S(2)}, u32[]{:S(2)}) %all-to-all-start.1) | async-done | bytes 1048608 | tf_op jit(solution)/shard_map/all_to_all | solution.py:517
  105.2 0.0 copy-start
  105.2 1.0 copy-done
  106.2 6.5 %gate_project_sent.1 = (bf16[256,2048]{1,0:T(8,128)(2,1)}, f32[256,1024]{1,0:T(8,128)}) custom-call(s32[1]{0:T(128)} %bitcast.half_ref, bf16[256,256]{1,0:T(8,128)(2,1)} %constant.18.clone.order_ref, bf16[16,256,128]{2,1,0:T(8,128)(2,1)} %copy-done, bf16[256,2048]{1,0:T(8,128)(2,1)} %gates_ref.1, bf16[256,2048]{1,0:T(8,128)(2,1)} %values_ref.1, ...), custom_call_target="tpu_custom_call" | custom-call | flops 1073741824 | bytes 8388608 | tf_op jit(solution)/shard_map/gate_project_sent/pallas_call | solution.py:430
  112.7 0.0 collective-permute-start
  112.7 5.3 %project_kept.1.kept_ref = f32[256,1024]{1,0:T(8,128)} custom-call(s32[1]{0:T(128)} %bitcast.half_ref, bf16[256,2048]{1,0:T(8,128)(2,1)} %get-tuple-element.7.gated_ref, bf16[2048,2048]{1,0:T(8,128)(2,1)} %weight_ref.3), custom_call_target="tpu_custom_call" | custom-call | flops 1073741824 | bytes 6291456 | tf_op jit(solution)/shard_map/project_kept/pallas_call | solution.py:478
  118.0 0.0 collective-permute-done.came_ref
  118.0 0.0 copy-start.1
  118.0 1.0 copy-done.1
  119.0 3.6 %join_halves.1 = bf16[1024,256]{1,0:T(8,128)(2,1)} custom-call(f32[256,1024]{1,0:T(8,128)} %project_kept.1.kept_ref, f32[256,1024]{1,0:T(8,128)} %copy-done.1), custom_call_target="tpu_custom_call" | custom-call | tf_op jit(solution)/shard_map/join_halves/pallas_call | solution.py:505
Async XLA Ops:
  77.6 27.6 %all-to-all-start.1 = ((bf16[16,256,128]{2,1,0:T(8,128)(2,1)}), bf16[16,256,128]{2,1,0:T(8,128)(2,1)S(1)}, u32[]{:S(2)}, u32[]{:S(2)}) async-start(bf16[16,256,128]{2,1,0:T(8,128)(2,1)} %long_convolution.1), calls=%async_computation.1 | async-start | bytes 2097152 | tf_op jit(solution)/shard_map/all_to_all | solution.py:517
  105.2 1.0 copy-start
  112.7 5.3 %collective-permute-start = (f32[256,1024]{1,0:T(8,128)}, f32[256,1024]{1,0:T(8,128)S(1)}, u32[]{:S(2)}, u32[]{:S(2)}) collective-permute-start(f32[256,1024]{1,0:T(8,128)} %get-tuple-element.8), channel_id=1, source_target_pairs={{0,1},{1,0},{2,3},{3,2},{4,5},{5,4},{6,7},{7,6},{8,9},{9,8},{10,11... | collective-permute-start | bytes 3145736 | tf_op jit(solution)/shard_map/ppermute | solution.py:525
  118.0 1.0 copy-start.1

commit v5 on v4

--- a/solution.py
+++ b/solution.py
@@ -16,6 +16,8 @@
 LANES = 128
 Q_ORDER = [low + 4 * high for low in range(4) for high in range(4)]
 VMEM_BYTES = 60 * 1024 * 1024
+STAGE_BYTES = 52 * 1024 * 1024
+TAIL_BYTES = 16 * 1024 * 1024
 
 
 def angle_table(first, second, period):
@@ -193,14 +195,15 @@
         load.start()
     loads[0].wait()
     for part in range(pieces):
-        for side, source in enumerate((values_ref, taps_ref)):
-            loads[2 * part + 1 + side].wait()
-            lanes = pl.ds(part * piece, piece)
-            moved = jnp.dot(order_ref[...], source[:, lanes], preferred_element_type=jnp.float32).astype(jnp.bfloat16)
-            for block in range(piece // LANES):
-                packed[part * piece // LANES + block, :, pl.ds(side * LANES, LANES)] = moved[
-                    :, block * LANES : (block + 1) * LANES
-                ]
+        loads[2 * part + 1].wait()
+        loads[2 * part + 2].wait()
+        lanes = pl.ds(part * piece, piece)
+        both = jnp.concatenate([values_ref[:, lanes], taps_ref[:, lanes]], axis=1)
+        moved = jnp.dot(order_ref[...], both, preferred_element_type=jnp.float32).astype(jnp.bfloat16)
+        for block in range(piece // LANES):
+            for side in range(2):
+                start = side * piece + block * LANES
+                packed[part * piece // LANES + block, :, pl.ds(side * LANES, LANES)] = moved[:, start : start + LANES]
         stores[part].start()
     for store in stores:
         store.wait()
@@ -208,7 +211,7 @@
 
 def arrange(values, taps, blocks):
     rows, wide = values.shape
-    pieces = 8
+    pieces = 4
     return pl.pallas_call(
         functools.partial(arrange_kernel, pieces),
         in_specs=[pl.BlockSpec(memory_space=pl.ANY)] * 3,
@@ -260,12 +263,17 @@
     load_turns[3].start()
     load_backward.start()
 
-    def transform(low, high):
-        taken = pl.ds(pl.multiple_of(low * group + high * chunk, chunk), chunk)
-        stream = streams[:, taken].reshape(inner, 2 * LANES)
-        raws[low % 2][high] = jnp.dot(
-            forward_ref[...], jnp.concatenate([stream, stream], axis=0), preferred_element_type=jnp.float32
+    def transform(low, pair):
+        streams_of = []
+        for part in range(2):
+            taken = pl.ds(pl.multiple_of(low * group + (2 * pair + part) * chunk, chunk), chunk)
+            streams_of.append(streams[:, taken].reshape(inner, 2 * LANES))
+        both = jnp.concatenate(streams_of, axis=1)
+        result = jnp.dot(
+            forward_ref[...], jnp.concatenate([both, both], axis=0), preferred_element_type=jnp.float32
         )
+        raws[low % 2][2 * pair] = result[:, : 2 * LANES]
+        raws[low % 2][2 * pair + 1] = result[:, 2 * LANES :]
 
     def first_pass(low, start):
         raw = raws[low % 2]
@@ -288,26 +296,26 @@
         for part in range(count):
             first_pass(low, pl.multiple_of(start + 8 * part, 8))
 
-    steps = inner // 4
+    steps = inner // 2
 
     load_forward.wait()
     load_streams[0].wait()
 
-    def alone(high, carry):
-        transform(0, high)
+    def alone(pair, carry):
+        transform(0, pair)
         return carry
 
-    lax.fori_loop(0, 4, alone, 0)
+    lax.fori_loop(0, 2, alone, 0)
     for low in range(1, 4):
         load_streams[low].wait()
         load_turns[low - 1].wait()
 
-        def beside(high, carry, low=low):
-            transform(low, high)
-            first_rows(low - 1, high * steps, steps // 8)
+        def beside(pair, carry, low=low):
+            transform(low, pair)
+            first_rows(low - 1, pair * steps, steps // 8)
             return carry
 
-        lax.fori_loop(0, 4, beside, 0)
+        lax.fori_loop(0, 2, beside, 0)
     load_turns[3].wait()
 
     def middle(index, carry):
@@ -348,27 +356,30 @@
         for part in range(count):
             last_pass(low, pl.multiple_of(start + 16 * part, 16))
 
-    def restore(low, high):
-        terms = jnp.dot(backward_ref[...], halves[low % 2][high], preferred_element_type=jnp.float32)
-        signal = terms[:inner, :LANES] + terms[:inner, LANES:] + terms[inner:, :LANES]
-        taken = pl.ds(pl.multiple_of(low * group + high * chunk, chunk), chunk)
-        signals[:, taken] = signal.astype(jnp.bfloat16).reshape(blocks, chunk, LANES)
+    def restore(low, pair):
+        both = jnp.concatenate([halves[low % 2][2 * pair], halves[low % 2][2 * pair + 1]], axis=1)
+        terms = jnp.dot(backward_ref[...], both, preferred_element_type=jnp.float32)
+        for part in range(2):
+            first, second = [slice((2 * part + i) * LANES, (2 * part + i + 1) * LANES) for i in range(2)]
+            signal = terms[:inner, first] + terms[:inner, second] + terms[inner:, first]
+            taken = pl.ds(pl.multiple_of(low * group + (2 * pair + part) * chunk, chunk), chunk)
+            signals[:, taken] = signal.astype(jnp.bfloat16).reshape(blocks, chunk, LANES)
 
     def prepare(index, carry):
         last_rows(0, index * steps, steps // 16)
         return carry
 
-    lax.fori_loop(0, 4, prepare, 0)
+    lax.fori_loop(0, 2, prepare, 0)
     load_backward.wait()
     for low in range(4):
 
-        def back(high, carry, low=low):
-            restore(low, high)
+        def back(pair, carry, low=low):
+            restore(low, pair)
             if low < 3:
-                last_rows(low + 1, high * steps, steps // 16)
+                last_rows(low + 1, pair * steps, steps // 16)
             return carry
 
-        lax.fori_loop(0, 4, back, 0)
+        lax.fori_loop(0, 2, back, 0)
         stores[low].start()
     for store in stores:
         store.wait()
@@ -403,96 +414,89 @@
     )(streams, *(jnp.asarray(table) for table in transform_tables(length)))
 
 
-def gate_kernel(group, half_ref, order_ref, conv_ref, gates_ref, values_ref, skip_ref, weight_ref, gated_ref, out_ref):
-    del half_ref
-    step = pl.program_id(0)
-    conv = jnp.concatenate([conv_ref[part] for part in range(group)], axis=1)
-    conv = jnp.dot(order_ref[...], conv, preferred_element_type=jnp.float32)
-    direct = skip_ref[...] * values_ref[...].astype(jnp.float32)
-    gated = (gates_ref[...].astype(jnp.float32) * (conv + direct)).astype(jnp.bfloat16)
-    gated_ref[...] = gated
-    term = jnp.dot(gated, weight_ref[...], preferred_element_type=jnp.float32)
-
-    @pl.when(step == 0)
-    def _():
-        out_ref[...] = term
-
-    @pl.when(step > 0)
-    def _():
-        out_ref[...] += term
-
-
-def gate_and_project(half, conv, gates, values, skip_gain, out_weight):
-    blocks, rows, lanes = conv.shape
+def stage_kernel(half_ref, after_ref, weight_hbm, gates_hbm, values_hbm, sent_ref, kept_ref, gates_ref, values_ref, sems):
+    del after_ref
+    features = sent_ref.shape[1]
+    half = half_ref[0]
+    sides = [pl.ds(pl.multiple_of(side * features, features), features) for side in (1 - half, half)]
+    copies = [
+        pltpu.make_async_copy(weight_hbm.at[:, sides[0]], sent_ref, sems.at[0]),
+        pltpu.make_async_copy(weight_hbm.at[:, sides[1]], kept_ref, sems.at[1]),
+        pltpu.make_async_copy(gates_hbm, gates_ref, sems.at[2]),
+        pltpu.make_async_copy(values_hbm, values_ref, sems.at[3]),
+    ]
+    for copy in copies:
+        copy.start()
+    for copy in copies:
+        copy.wait()
+
+
+def stage(half, after, out_weight, gates, values):
     width, features = out_weight.shape
-    group = 4
-    wide = group * lanes
+    share = jax.ShapeDtypeStruct((width, features // 2), out_weight.dtype)
+    stream = jax.ShapeDtypeStruct(gates.shape, gates.dtype)
     return pl.pallas_call(
-        functools.partial(gate_kernel, group),
-        grid_spec=pltpu.PrefetchScalarGridSpec(
-            num_scalar_prefetch=1,
-            grid=(blocks // group,),
-            in_specs=[
-                pl.BlockSpec((rows, rows), lambda i, h: (0, 0)),
-                pl.BlockSpec((group, rows, lanes), lambda i, h: (i, 0, 0)),
-                pl.BlockSpec((rows, wide), lambda i, h: (0, i)),
-                pl.BlockSpec((rows, wide), lambda i, h: (0, i)),
-                pl.BlockSpec((1, wide), lambda i, h: (0, i)),
-                pl.BlockSpec((wide, features // 2), lambda i, h: (i, 1 - h[0])),
-            ],
-            out_specs=[
-                pl.BlockSpec((rows, wide), lambda i, h: (0, i)),
-                pl.BlockSpec((rows, features // 2), lambda i, h: (0, 0)),
-            ],
+        stage_kernel,
+        in_specs=[pl.BlockSpec(memory_space=pltpu.SMEM)] + [pl.BlockSpec(memory_space=pl.ANY)] * 4,
+        out_specs=[pl.BlockSpec(memory_space=pl.ANY)] * 4,
+        out_shape=[share, share, stream, stream],
+        scratch_shapes=[pltpu.SemaphoreType.DMA((4,))],
+        compiler_params=pltpu.CompilerParams(vmem_limit_bytes=STAGE_BYTES),
+        cost_estimate=pl.CostEstimate(
+            flops=0, bytes_accessed=4 * width * features + 8 * gates.size, transcendentals=0
         ),
+        name="stage_tail",
+    )(half, after, out_weight, gates, values)
+
+
+def gate_kernel(group, order_ref, conv_ref, gates_ref, values_ref, skip_ref, weight_ref, gated_ref, out_ref):
+    blocks, _, lanes = conv_ref.shape
+    for step in range(blocks // group):
+        taken = pl.ds(step * group * lanes, group * lanes)
+        conv = jnp.concatenate([conv_ref[step * group + part] for part in range(group)], axis=1)
+        conv = jnp.dot(order_ref[...], conv, preferred_element_type=jnp.float32)
+        direct = skip_ref[:, taken] * values_ref[:, taken].astype(jnp.float32)
+        gated_ref[:, taken] = (gates_ref[:, taken].astype(jnp.float32) * (conv + direct)).astype(jnp.bfloat16)
+    out_ref[...] = jnp.dot(gated_ref[...], weight_ref[...], preferred_element_type=jnp.float32)
+
+
+def gate_and_project(conv, gates, values, skip_gain, weight):
+    rows, width = gates.shape
+    features = weight.shape[1]
+    return pl.pallas_call(
+        functools.partial(gate_kernel, 4),
+        in_specs=[pl.BlockSpec(memory_space=pltpu.VMEM)] * 6,
+        out_specs=[pl.BlockSpec(memory_space=pltpu.VMEM)] * 2,
         out_shape=[
             jax.ShapeDtypeStruct((rows, width), jnp.bfloat16),
-            jax.ShapeDtypeStruct((rows, features // 2), jnp.float32),
+            jax.ShapeDtypeStruct((rows, features), jnp.float32),
         ],
-        compiler_params=pltpu.CompilerParams(vmem_limit_bytes=VMEM_BYTES),
+        compiler_params=pltpu.CompilerParams(vmem_limit_bytes=TAIL_BYTES),
         cost_estimate=pl.CostEstimate(
-            flops=rows * width * features, bytes_accessed=width * features + 8 * rows * width, transcendentals=0
+            flops=2 * rows * width * features, bytes_accessed=2 * width * features, transcendentals=0
         ),
         name="gate_project_sent",
-    )(half, jnp.asarray(row_order(rows).T), conv, gates, values, skip_gain[None, :], out_weight)
-
-
-def kept_kernel(half_ref, gated_ref, weight_ref, out_ref):
-    del half_ref
-    step = pl.program_id(0)
-    term = jnp.dot(gated_ref[...], weight_ref[...], preferred_element_type=jnp.float32)
-
-    @pl.when(step == 0)
-    def _():
-        out_ref[...] = term
-
-    @pl.when(step > 0)
-    def _():
-        out_ref[...] += term
-
-
-def project_kept(half, gated, out_weight):
+    )(jnp.asarray(row_order(rows).T), conv, gates, values, skip_gain[None, :], weight)
+
+
+def kept_kernel(gated_ref, weight_ref, out_ref):
+    out_ref[...] = jnp.dot(gated_ref[...], weight_ref[...], preferred_element_type=jnp.float32)
+
+
+def project_kept(gated, weight):
     rows, width = gated.shape
-    features = out_weight.shape[1]
-    deep = width // 4
+    features = weight.shape[1]
     return pl.pallas_call(
         kept_kernel,
-        grid_spec=pltpu.PrefetchScalarGridSpec(
-            num_scalar_prefetch=1,
-            grid=(4,),
-            in_specs=[
-                pl.BlockSpec((rows, deep), lambda i, h: (0, i)),
-                pl.BlockSpec((deep, features // 2), lambda i, h: (i, h[0])),
-            ],
-            out_specs=pl.BlockSpec((rows, features // 2), lambda i, h: (0, 0)),
-        ),
-        out_shape=jax.ShapeDtypeStruct((rows, features // 2), jnp.float32),
-        compiler_params=pltpu.CompilerParams(vmem_limit_bytes=VMEM_BYTES),
+        in_specs=[pl.BlockSpec(memory_space=pltpu.VMEM)] * 2,
+        out_specs=pl.BlockSpec(memory_space=pltpu.VMEM),
+        out_shape=jax.ShapeDtypeStruct((rows, features), jnp.float32),
+        compiler_params=pltpu.CompilerParams(vmem_limit_bytes=TAIL_BYTES),
         cost_estimate=pl.CostEstimate(
-            flops=rows * width * features, bytes_accessed=width * features + 4 * rows * width, transcendentals=0
+            flops=2 * rows * width * features, bytes_accessed=2 * width * features, transcendentals=0
         ),
         name="project_kept",
-    )(half, gated, out_weight)
+    )(gated, weight)
 
 
 def join_kernel(kept_ref, came_ref, out_ref):
@@ -508,7 +512,7 @@
         in_specs=[pl.BlockSpec((rows, wide), lambda i: (0, i))] * 2,
         out_specs=pl.BlockSpec((wide, rows), lambda i: (i, 0)),
         out_shape=jax.ShapeDtypeStruct((features, rows), jnp.bfloat16),
-        compiler_params=pltpu.CompilerParams(vmem_limit_bytes=VMEM_BYTES),
+        compiler_params=pltpu.CompilerParams(vmem_limit_bytes=TAIL_BYTES),
         name="join_halves",
     )(kept, came)
 
@@ -519,11 +523,12 @@
 
 def kernel_local(values, gates, filter_taps, skip_gain, out_weight):
     blocks = lax.axis_size("seq")
-    conv = swap_blocks(convolve(swap_blocks(arrange(values, filter_taps, blocks))))
+    conv = convolve(swap_blocks(arrange(values, filter_taps, blocks)))
     half = lax.axis_index("chan").astype(jnp.int32)[None]
-    gated, sent = gate_and_project(half, conv, gates, values, skip_gain, out_weight)
+    weight_sent, weight_kept, gates, values = stage(half, conv, out_weight, gates, values)
+    gated, sent = gate_and_project(swap_blocks(conv), gates, values, skip_gain, weight_sent)
     other = lax.ppermute(sent, "chan", [(0, 1), (1, 0)])
-    kept = project_kept(half, gated, out_weight)
+    kept = project_kept(gated, weight_kept)
     return join(kept, other)
 
 

time: 124 us -> 374 us (3.02)
  Pallas kernels: 35.7 us -> 307 us
  waiting for transfers between devices: 23.7 us -> 1.39 us
    pallas_call x2 -> x3, Pallas kernels: 11.8 us -> 290 us  [the longest x1 287 us: stage(): pl.pallas_call(stage_kernel, in_specs=[pl.BlockSpec(memory_space=pltpu.SM...]
    all_to_all x1, waiting for transfers between devices: 23.7 us -> 0.01 us  [swap_blocks(): return lax.all_to_all(array, 'seq', split_axis=0, concat_axis=0, tiled=True)]
  transfers between devices with their start and end apart: 2 -> 2, of which waited for: 1 -> 1; matrix products, arithmetic and copies ran while one was open for 0% -> 0% of each run, Pallas kernels for 4% -> 77%
where the time goes in v5:
time: 374 us
  Pallas kernels  307 us (82%)
  blocking collectives  57.3 us (15%)
  starting transfers between devices  3.98 us (1%)
    pallas_call x1, Pallas kernels, stage(): pl.pallas_call(stage_kernel, in_specs=[pl.BlockSpec(memory_space=pltpu.SM...  287 us
    all_to_all x1, blocking collectives, swap_blocks(): return lax.all_to_all(array, 'seq', split_axis=0, concat_axis=0, tiled=True)  57.3 us
    pallas_call x1, Pallas kernels, convolve(): pl.pallas_call(convolve_kernel, in_specs=[pl.BlockSpec(memory_space=pl.AN...  12.5 us
  transfers between devices with their start and end apart: 2, of which 1 were waited for; matrix products, arithmetic and copies ran while one was open for 0% of the time, Pallas kernels for 77%

profile of v5, /device:TPU:0, one launch (start us, length us, event | category | flops | bytes accessed | tf_op | source)
XLA Modules:
  0.0 373.8 jit_solution(9487351950030237607)
XLA Ops:
  0.0 3.2 arrange_rows.1
  3.2 57.3 %all_to_all.10.streams_hbm = bf16[16,256,256]{2,1,0:T(8,128)(2,1)} all-to-all(bf16[16,256,256]{2,1,0:T(8,128)(2,1)} %arrange_rows.1), channel_id=1, replica_groups=mesh['seq'=16,'chan'=2] {'seq'}, dimensions={0} | all-to-all | bytes 4194304 | tf_op jit(solution)/shard_map/all_to_all | solution.py:521
  60.5 12.5 %long_convolution.1.after_ref = bf16[16,256,128]{2,1,0:T(8,128)(2,1)} custom-call(bf16[16,256,256]{2,1,0:T(8,128)(2,1)} %all_to_all.10.streams_hbm, bf16[512,512]{1,0:T(8,128)(2,1)} %constant.15.clone.forward_hbm, f32[16,2,256,128]{3,2,1,0:T(8,128)} %constant.16.clone.turns_hbm, bf16[512,512]{1,0:T(8,128)(2,1)} %constant.17.clone.backward_hbm), custom_call_target="tpu_custom_call" | custom-call | flops 8999999488 | bytes 9000000 | tf_op jit(solution)/shard_map/long_convolution/pallas_call | solution.py:392
  73.0 3.9 %all-to-all-start.1 = ((bf16[16,256,128]{2,1,0:T(8,128)(2,1)}), bf16[16,256,128]{2,1,0:T(8,128)(2,1)S(1)}, u32[]{:S(2)}, u32[]{:S(2)}) async-start(bf16[16,256,128]{2,1,0:T(8,128)(2,1)} %long_convolution.1.after_ref), calls=%async_computation.1 | async-start | bytes 2097152 | tf_op jit(solution)/shard_map/all_to_all | solution.py:521
  76.9 0.0 copy-start.3
  76.9 0.0 copy-start.4
  76.9 287.0 %stage_tail.1 = (bf16[2048,1024]{1,0:T(8,128)(2,1)}, bf16[2048,1024]{1,0:T(8,128)(2,1)}, bf16[256,2048]{1,0:T(8,128)(2,1)S(1)}, bf16[256,2048]{1,0:T(8,128)(2,1)}) custom-call(s32[1]{0:T(128)} %bitcast.half_ref, bf16[16,256,128]{2,1,0:T(8,128)(2,1)} %long_convolution.1.after_ref, bf16[2048,2048]{1,0:T(8,128)(2,1)} %weight_hbm.1, ...), custom_call_target="tpu_custom_call" | custom-call | bytes 20971520 | tf_op jit(solution)/shard_map/stage_tail/pallas_call | solution.py:438
  364.0 0.0 all-to-all-done.1.conv_ref
  364.0 0.0 copy-start
  364.0 0.0 copy-done.3
  364.0 0.0 copy-done.4
  364.0 0.0 copy-start.1
  364.0 2.3 copy-done.1
  366.3 0.0 copy-start.2
  366.3 1.4 copy-done.2
  367.7 1.7 gate_project_sent.1
  369.4 0.1 collective-permute-start
  369.5 0.0 copy-done
  369.5 1.2 project_kept.1.kept_ref
  370.7 1.4 collective-permute-done.came_ref
  372.1 1.7 join_halves.1
Async XLA Ops:
  73.0 291.0 %all-to-all-start.1 = ((bf16[16,256,128]{2,1,0:T(8,128)(2,1)}), bf16[16,256,128]{2,1,0:T(8,128)(2,1)S(1)}, u32[]{:S(2)}, u32[]{:S(2)}) async-start(bf16[16,256,128]{2,1,0:T(8,128)(2,1)} %long_convolution.1.after_ref), calls=%async_computation.1 | async-start | bytes 2097152 | tf_op jit(solution)/shard_map/all_to_all | solution.py:521
  76.9 287.1 %copy-start.3 = (bf16[256,256]{1,0:T(8,128)(2,1)S(1)}, bf16[256,256]{1,0:T(8,128)(2,1)}, u32[]{:S(2)}) copy-start(bf16[256,256]{1,0:T(8,128)(2,1)} %constant.18.clone.order_ref) | copy-start | bytes 393220
  76.9 287.1 %copy-start.4 = (f32[2048]{0:T(1024)S(1)}, f32[2048]{0:T(1024)}, u32[]{:S(2)}) copy-start(f32[2048]{0:T(1024)} %param.13) | copy-start | bytes 24580
  364.0 5.5 %copy-start = (bf16[2048,1024]{1,0:T(8,128)(2,1)S(1)}, bf16[2048,1024]{1,0:T(8,128)(2,1)}, u32[]{:S(2)}) copy-start(bf16[2048,1024]{1,0:T(8,128)(2,1)} %get-tuple-element.15.weight_ref) | copy-start | bytes 12582916
  364.0 2.3 copy-start.1
  366.3 1.4 copy-start.2
  369.4 2.7 collective-permute-start

commit v6 on v5

--- a/solution.py
+++ b/solution.py
@@ -16,7 +16,7 @@
 LANES = 128
 Q_ORDER = [low + 4 * high for low in range(4) for high in range(4)]
 VMEM_BYTES = 60 * 1024 * 1024
-STAGE_BYTES = 52 * 1024 * 1024
+CONV_BYTES = 49 * 1024 * 1024
 TAIL_BYTES = 16 * 1024 * 1024
 
 
@@ -181,16 +181,22 @@
     return (re * cos - im * sin, im * cos + re * sin)
 
 
-def arrange_kernel(pieces, order_hbm, values_hbm, taps_hbm, out_hbm, order_ref, values_ref, taps_ref, packed, sems):
+def slot_order(blocks):
+    half = blocks // 2
+    across = [half + (i // 2 if i % 2 == 0 else half // 2 + i // 2) for i in range(half)]
+    near = list(range(1, half)) + [0]
+    return [slot for pair in zip(across, near) for slot in pair]
+
+
+def arrange_kernel(pieces, blocks, me_ref, order_hbm, values_hbm, taps_hbm, *rest):
+    outs = rest[:blocks]
+    order_ref, values_ref, taps_ref, packed, sems = rest[blocks:]
     piece = values_ref.shape[1] // pieces
-    loads = [pltpu.make_async_copy(order_hbm, order_ref, sems.at[3 * pieces])]
-    stores = []
+    loads = [pltpu.make_async_copy(order_hbm, order_ref, sems.at[2 * pieces])]
     for part in range(pieces):
         lanes = pl.ds(part * piece, piece)
-        loads.append(pltpu.make_async_copy(values_hbm.at[:, lanes], values_ref.at[:, lanes], sems.at[3 * part]))
-        loads.append(pltpu.make_async_copy(taps_hbm.at[:, lanes], taps_ref.at[:, lanes], sems.at[3 * part + 1]))
-        taken = pl.ds(part * piece // LANES, piece // LANES)
-        stores.append(pltpu.make_async_copy(packed.at[taken], out_hbm.at[taken], sems.at[3 * part + 2]))
+        loads.append(pltpu.make_async_copy(values_hbm.at[:, lanes], values_ref.at[:, lanes], sems.at[2 * part]))
+        loads.append(pltpu.make_async_copy(taps_hbm.at[:, lanes], taps_ref.at[:, lanes], sems.at[2 * part + 1]))
     for load in loads:
         load.start()
     loads[0].wait()
@@ -204,36 +210,40 @@
             for side in range(2):
                 start = side * piece + block * LANES
                 packed[part * piece // LANES + block, :, pl.ds(side * LANES, LANES)] = moved[:, start : start + LANES]
-        stores[part].start()
-    for store in stores:
-        store.wait()
-
-
-def arrange(values, taps, blocks):
+    for out, slot in zip(outs, slot_order(blocks)):
+        out[...] = packed[me_ref[0] ^ slot]
+
+
+def arrange(me, values, taps, blocks):
     rows, wide = values.shape
     pieces = 4
     return pl.pallas_call(
-        functools.partial(arrange_kernel, pieces),
-        in_specs=[pl.BlockSpec(memory_space=pl.ANY)] * 3,
-        out_specs=pl.BlockSpec(memory_space=pl.ANY),
-        out_shape=jax.ShapeDtypeStruct((blocks, rows, 2 * LANES), jnp.bfloat16),
+        functools.partial(arrange_kernel, pieces, blocks),
+        in_specs=[pl.BlockSpec(memory_space=pltpu.SMEM)] + [pl.BlockSpec(memory_space=pl.ANY)] * 3,
+        out_specs=[pl.BlockSpec(memory_space=pltpu.VMEM)] * blocks,
+        out_shape=[jax.ShapeDtypeStruct((rows, 2 * LANES), jnp.bfloat16)] * blocks,
         scratch_shapes=[
             pltpu.VMEM((rows, rows), jnp.bfloat16),
             pltpu.VMEM((rows, wide), jnp.bfloat16),
             pltpu.VMEM((rows, wide), jnp.bfloat16),
             pltpu.VMEM((blocks, rows, 2 * LANES), jnp.bfloat16),
-            pltpu.SemaphoreType.DMA((3 * pieces + 1,)),
+            pltpu.SemaphoreType.DMA((2 * pieces + 1,)),
         ],
         compiler_params=pltpu.CompilerParams(vmem_limit_bytes=VMEM_BYTES),
         cost_estimate=pl.CostEstimate(
             flops=4 * rows * rows * wide, bytes_accessed=8 * rows * wide, transcendentals=0
         ),
         name="arrange_rows",
-    )(jnp.asarray(row_order(rows)), values, taps)
-
-
-def convolve_kernel(
-    streams_hbm, forward_hbm, turns_hbm, backward_hbm, out_hbm,
+    )(me, jnp.asarray(row_order(rows)), values, taps)
+
+
+def convolve_kernel(blocks, me_ref, *rest):
+    slots = rest[:blocks]
+    convolve_blocks(me_ref, slots, *rest[blocks:])
+
+
+def convolve_blocks(
+    me_ref, slots, forward_hbm, turns_hbm, backward_hbm, out_hbm,
     streams, forward_ref, turns_ref, backward_ref,
     raw_even, raw_odd, columns, mixed, halves_even, halves_odd, signals, sems,
 ):
@@ -245,23 +255,18 @@
     halves = (halves_even, halves_odd)
     load_forward = pltpu.make_async_copy(forward_hbm, forward_ref, sems.at[0])
     load_backward = pltpu.make_async_copy(backward_hbm, backward_ref, sems.at[1])
-    load_streams, load_turns, stores = [], [], []
+    load_turns, stores = [], []
     for low in range(4):
         taken = pl.ds(low * group, group)
-        load_streams.append(pltpu.make_async_copy(streams_hbm.at[:, taken], streams.at[:, taken], sems.at[2 + low]))
         four = pl.ds(4 * low, 4)
         load_turns.append(pltpu.make_async_copy(turns_hbm.at[four], turns_ref.at[four], sems.at[6 + low]))
         stores.append(pltpu.make_async_copy(signals.at[:, taken], out_hbm.at[:, taken], sems.at[10 + low]))
     load_forward.start()
-    load_streams[0].start()
-    load_streams[1].start()
-    load_turns[0].start()
-    load_streams[2].start()
-    load_turns[1].start()
-    load_streams[3].start()
-    load_turns[2].start()
-    load_turns[3].start()
+    for load in load_turns:
+        load.start()
     load_backward.start()
+    for slot, source in zip(slot_order(blocks), slots):
+        streams[me_ref[0] ^ slot] = source[...]
 
     def transform(low, pair):
         streams_of = []
@@ -299,7 +304,6 @@
     steps = inner // 2
 
     load_forward.wait()
-    load_streams[0].wait()
 
     def alone(pair, carry):
         transform(0, pair)
@@ -307,7 +311,6 @@
 
     lax.fori_loop(0, 2, alone, 0)
     for low in range(1, 4):
-        load_streams[low].wait()
         load_turns[low - 1].wait()
 
         def beside(pair, carry, low=low):
@@ -385,17 +388,20 @@
         store.wait()
 
 
-def convolve(streams):
-    blocks, rows, lanes = streams.shape
+def convolve(me, slots):
+    blocks = len(slots)
+    rows, lanes = slots[0].shape
     length = blocks * rows
     inner = length // RADIX
     return pl.pallas_call(
-        convolve_kernel,
-        in_specs=[pl.BlockSpec(memory_space=pl.ANY)] * 4,
+        functools.partial(convolve_kernel, blocks),
+        in_specs=[pl.BlockSpec(memory_space=pltpu.SMEM)]
+        + [pl.BlockSpec(memory_space=pltpu.VMEM)] * blocks
+        + [pl.BlockSpec(memory_space=pl.ANY)] * 3,
         out_specs=pl.BlockSpec(memory_space=pl.ANY),
         out_shape=jax.ShapeDtypeStruct((blocks, rows, LANES), jnp.bfloat16),
         scratch_shapes=[
-            pltpu.VMEM(streams.shape, jnp.bfloat16),
+            pltpu.VMEM((blocks, rows, lanes), jnp.bfloat16),
             pltpu.VMEM((2 * inner, 2 * inner), jnp.bfloat16),
             pltpu.VMEM((RADIX, 2, inner, LANES), jnp.float32),
             pltpu.VMEM((2 * inner, 2 * inner), jnp.bfloat16),
@@ -408,10 +414,10 @@
             pltpu.VMEM((blocks, rows, LANES), jnp.bfloat16),
             pltpu.SemaphoreType.DMA((14,)),
         ],
-        compiler_params=pltpu.CompilerParams(vmem_limit_bytes=VMEM_BYTES),
+        compiler_params=pltpu.CompilerParams(vmem_limit_bytes=CONV_BYTES),
         cost_estimate=pl.CostEstimate(flops=9 * 10**9, bytes_accessed=9 * 10**6, transcendentals=0),
         name="long_convolution",
-    )(streams, *(jnp.asarray(table) for table in transform_tables(length)))
+    )(me, *slots, *(jnp.asarray(table) for table in transform_tables(length)))
 
 
 def stage_kernel(half_ref, after_ref, weight_hbm, gates_hbm, values_hbm, sent_ref, kept_ref, gates_ref, values_ref, sems):
@@ -438,10 +444,10 @@
     return pl.pallas_call(
         stage_kernel,
         in_specs=[pl.BlockSpec(memory_space=pltpu.SMEM)] + [pl.BlockSpec(memory_space=pl.ANY)] * 4,
-        out_specs=[pl.BlockSpec(memory_space=pl.ANY)] * 4,
+        out_specs=[pl.BlockSpec(memory_space=pltpu.VMEM)] * 4,
         out_shape=[share, share, stream, stream],
         scratch_shapes=[pltpu.SemaphoreType.DMA((4,))],
-        compiler_params=pltpu.CompilerParams(vmem_limit_bytes=STAGE_BYTES),
+        compiler_params=pltpu.CompilerParams(vmem_limit_bytes=TAIL_BYTES),
         cost_estimate=pl.CostEstimate(
             flops=0, bytes_accessed=4 * width * features + 8 * gates.size, transcendentals=0
         ),
@@ -521,10 +527,19 @@
     return lax.all_to_all(array, "seq", split_axis=0, concat_axis=0, tiled=True)
 
 
+def exchange(slots):
+    blocks = len(slots)
+    return [
+        lax.ppermute(source, "seq", [(j, j ^ slot) for j in range(blocks)]) if slot else source
+        for slot, source in zip(slot_order(blocks), slots)
+    ]
+
+
 def kernel_local(values, gates, filter_taps, skip_gain, out_weight):
     blocks = lax.axis_size("seq")
-    conv = convolve(swap_blocks(arrange(values, filter_taps, blocks)))
+    me = lax.axis_index("seq").astype(jnp.int32)[None]
     half = lax.axis_index("chan").astype(jnp.int32)[None]
+    conv = convolve(me, exchange(arrange(me, values, filter_taps, blocks)))
     weight_sent, weight_kept, gates, values = stage(half, conv, out_weight, gates, values)
     gated, sent = gate_and_project(swap_blocks(conv), gates, values, skip_gain, weight_sent)
     other = lax.ppermute(sent, "chan", [(0, 1), (1, 0)])

time: 374 us -> 112 us (0.30)
  Pallas kernels: 307 us -> 21.9 us
  blocking collectives: 57.3 us -> 0 us
  waiting for transfers between devices: 1.39 us -> 36.7 us
  starting transfers between devices: 3.98 us -> 34.7 us
  local copies, waits for them, and re-layouts: 3.73 us -> 17.3 us
    pallas_call x1, Pallas kernels: 287 us -> 1.78 us  [stage(): pl.pallas_call(stage_kernel, in_specs=[pl.BlockSpec(memory_space=pltpu.SM...]
    all_to_all x1 -> x0, blocking collectives: 57.3 us -> none  [swap_blocks(): return lax.all_to_all(array, 'seq', split_axis=0, concat_axis=0, tiled=True)]
    ppermute x0 -> x15, starting transfers between devices: none -> 28.3 us  [exchange(): lax.ppermute(source, 'seq', [(j, j ^ slot) for j in range(blocks)])]
    ppermute x0 -> x15, waiting for transfers between devices: none -> 22 us  [exchange(): lax.ppermute(source, 'seq', [(j, j ^ slot) for j in range(blocks)])]
    unnamed x10 -> x32, local copies, waits for them, and re-layouts: 3.73 us -> 17.3 us
    all_to_all x1, waiting for transfers between devices: 0.01 us -> 13.4 us  [swap_blocks(): return lax.all_to_all(array, 'seq', split_axis=0, concat_axis=0, tiled=True)]
  transfers between devices with their start and end apart: 2 -> 17, of which waited for: 1 -> 10; matrix products, arithmetic and copies ran while one was open for 0% -> 0% of each run, Pallas kernels for 77% -> 3%
where the time goes in v6:
time: 112 us; the launch traced here: 111 us
  waiting for transfers between devices  36.7 us (33%)
  starting transfers between devices  34.7 us (31%)
  Pallas kernels  21.9 us (20%)
  local copies, waits for them, and re-layouts  17.3 us (15%)
    ppermute x15, starting transfers between devices, exchange(): lax.ppermute(source, 'seq', [(j, j ^ slot) for j in range(blocks)])  28.3 us
    ppermute x15, waiting for transfers between devices, exchange(): lax.ppermute(source, 'seq', [(j, j ^ slot) for j in range(blocks)])  22 us
    unnamed x32, local copies, waits for them, and re-layouts  17.3 us
    all_to_all x1, waiting for transfers between devices, swap_blocks(): return lax.all_to_all(array, 'seq', split_axis=0, concat_axis=0, tiled=True)  13.4 us
    pallas_call x1, Pallas kernels, convolve(): pl.pallas_call(functools.partial(convolve_kernel, blocks), in_specs=[pl.B...  11.8 us
    all_to_all x1, starting transfers between devices, swap_blocks(): return lax.all_to_all(array, 'seq', split_axis=0, concat_axis=0, tiled=True)  6.34 us
    pallas_call x1, Pallas kernels, arrange(): pl.pallas_call(functools.partial(arrange_kernel, pieces, blocks), in_spec...  3.71 us
  transfers between devices with their start and end apart: 17, of which 10 were waited for; matrix products, arithmetic and copies ran while one was open for 0% of the time, Pallas kernels for 3%

profile of v6, /device:TPU:0, one launch (start us, length us, event | category | flops | bytes accessed | tf_op | source)
XLA Modules:
  0.0 110.8 jit_solution(15102210506092586538)
XLA Ops:
  0.0 3.7 %arrange_rows.1 = (bf16[256,256]{1,0:T(8,128)(2,1)}, bf16[256,256]{1,0:T(8,128)(2,1)}, bf16[256,256]{1,0:T(8,128)(2,1)}, bf16[256,256]{1,0:T(8,128)(2,1)}, bf16[...) custom-call(s32[1]{0:T(128)} %bitcast.me_ref, ...), custom_call_target="tpu_custom_call" | custom-call | flops 536870912 | bytes 4194304 | tf_op jit(solution)/shard_map/arrange_rows/pallas_call | solution.py:220
  3.7 4.1 %collective-permute-start = (bf16[256,256]{1,0:T(8,128)(2,1)}, bf16[256,256]{1,0:T(8,128)(2,1)S(1)}, u32[]{:S(2)}, u32[]{:S(2)}) collective-permute-start(bf16[256,256]{1,0:T(8,128)(2,1)} %get-tuple-element.27), channel_id=1, source_target_pairs={{0,16},{2,18},{4,20},{6,22},{8,24},{10,26},{12,28},{14,30},{16,0},... | collective-permute-start | bytes 393224 | tf_op jit(solution)/shard_map/ppermute | solution.py:533
  10.7 1.5 %collective-permute-start.3 = (bf16[256,256]{1,0:T(8,128)(2,1)}, bf16[256,256]{1,0:T(8,128)(2,1)S(1)}, u32[]{:S(2)}, u32[]{:S(2)}) collective-permute-start(bf16[256,256]{1,0:T(8,128)(2,1)} %get-tuple-element.30), channel_id=1, source_target_pairs={{0,4},{2,6},{4,0},{6,2},{8,12},{10,14},{12,8},{14,10},{16,20},{18,... | collective-permute-start | bytes 393224 | tf_op jit(solution)/shard_map/ppermute | solution.py:533
  12.2 1.7 %collective-permute-start.4 = (bf16[256,256]{1,0:T(8,128)(2,1)}, bf16[256,256]{1,0:T(8,128)(2,1)S(1)}, u32[]{:S(2)}, u32[]{:S(2)}) collective-permute-start(bf16[256,256]{1,0:T(8,128)(2,1)} %get-tuple-element.31), channel_id=1, source_target_pairs={{0,18},{2,16},{4,22},{6,20},{8,26},{10,24},{12,30},{14,28},{16,2},... | collective-permute-start | bytes 393224 | tf_op jit(solution)/shard_map/ppermute | solution.py:533
  13.8 6.9 %collective-permute-done.rest_0_ = bf16[256,256]{1,0:T(8,128)(2,1)S(1)} collective-permute-done((bf16[256,256]{1,0:T(8,128)(2,1)}, bf16[256,256]{1,0:T(8,128)(2,1)S(1)}, u32[]{:S(2)}, u32[]{:S(2)}) %collective-permute-start) | collective-permute-done | bytes 131104 | tf_op jit(solution)/shard_map/ppermute | solution.py:533
  20.8 2.8 %collective-permute-start.5 = (bf16[256,256]{1,0:T(8,128)(2,1)}, bf16[256,256]{1,0:T(8,128)(2,1)S(1)}, u32[]{:S(2)}, u32[]{:S(2)}) collective-permute-start(bf16[256,256]{1,0:T(8,128)(2,1)} %get-tuple-element.32), channel_id=1, source_target_pairs={{0,6},{2,4},{4,2},{6,0},{8,14},{10,12},{12,10},{14,8},{16,22},{18,... | collective-permute-start | bytes 393224 | tf_op jit(solution)/shard_map/ppermute | solution.py:533
  23.6 2.4 %collective-permute-start.6 = (bf16[256,256]{1,0:T(8,128)(2,1)}, bf16[256,256]{1,0:T(8,128)(2,1)S(1)}, u32[]{:S(2)}, u32[]{:S(2)}) collective-permute-start(bf16[256,256]{1,0:T(8,128)(2,1)} %get-tuple-element.33), channel_id=1, source_target_pairs={{0,26},{2,24},{4,30},{6,28},{8,18},{10,16},{12,22},{14,20},{16,10}... | collective-permute-start | bytes 393224 | tf_op jit(solution)/shard_map/ppermute | solution.py:533
  26.0 1.5 %collective-permute-start.8 = (bf16[256,256]{1,0:T(8,128)(2,1)}, bf16[256,256]{1,0:T(8,128)(2,1)S(1)}, u32[]{:S(2)}, u32[]{:S(2)}) collective-permute-start(bf16[256,256]{1,0:T(8,128)(2,1)} %get-tuple-element.35), channel_id=1, source_target_pairs={{0,20},{2,22},{4,16},{6,18},{8,28},{10,30},{12,24},{14,26},{16,4},... | collective-permute-start | bytes 393224 | tf_op jit(solution)/shard_map/ppermute | solution.py:533
  30.2 7.3 %collective-permute-start.10 = (bf16[256,256]{1,0:T(8,128)(2,1)}, bf16[256,256]{1,0:T(8,128)(2,1)S(1)}, u32[]{:S(2)}, u32[]{:S(2)}) collective-permute-start(bf16[256,256]{1,0:T(8,128)(2,1)} %get-tuple-element.37), channel_id=1, source_target_pairs={{0,28},{2,30},{4,24},{6,26},{8,20},{10,22},{12,16},{14,18},{16,12}... | collective-permute-start | bytes 393224 | tf_op jit(solution)/shard_map/ppermute | solution.py:533
  38.1 3.3 %collective-permute-done.8.rest_8_ = bf16[256,256]{1,0:T(8,128)(2,1)S(1)} collective-permute-done((bf16[256,256]{1,0:T(8,128)(2,1)}, bf16[256,256]{1,0:T(8,128)(2,1)S(1)}, u32[]{:S(2)}, u32[]{:S(2)}) %collective-permute-start.8) | collective-permute-done | bytes 131104 | tf_op jit(solution)/shard_map/ppermute | solution.py:533
  41.9 2.3 %collective-permute-start.14 = (bf16[256,256]{1,0:T(8,128)(2,1)}, bf16[256,256]{1,0:T(8,128)(2,1)S(1)}, u32[]{:S(2)}, u32[]{:S(2)}) collective-permute-start(bf16[256,256]{1,0:T(8,128)(2,1)} %get-tuple-element.41), channel_id=1, source_target_pairs={{0,30},{2,28},{4,26},{6,24},{8,22},{10,20},{12,18},{14,16},{16,14}... | collective-permute-start | bytes 393224 | tf_op jit(solution)/shard_map/ppermute | solution.py:533
  44.3 1.7 %collective-permute-done.11.rest_11_ = bf16[256,256]{1,0:T(8,128)(2,1)S(1)} collective-permute-done((bf16[256,256]{1,0:T(8,128)(2,1)}, bf16[256,256]{1,0:T(8,128)(2,1)S(1)}, u32[]{:S(2)}, u32[]{:S(2)}) %collective-permute-start.11) | collective-permute-done | bytes 131104 | tf_op jit(solution)/shard_map/ppermute | solution.py:533
  46.0 6.1 %collective-permute-done.12.rest_12_ = bf16[256,256]{1,0:T(8,128)(2,1)S(1)} collective-permute-done((bf16[256,256]{1,0:T(8,128)(2,1)}, bf16[256,256]{1,0:T(8,128)(2,1)S(1)}, u32[]{:S(2)}, u32[]{:S(2)}) %collective-permute-start.12) | collective-permute-done | bytes 131104 | tf_op jit(solution)/shard_map/ppermute | solution.py:533
  52.1 1.9 %collective-permute-done.14.rest_14_ = bf16[256,256]{1,0:T(8,128)(2,1)S(1)} collective-permute-done((bf16[256,256]{1,0:T(8,128)(2,1)}, bf16[256,256]{1,0:T(8,128)(2,1)S(1)}, u32[]{:S(2)}, u32[]{:S(2)}) %collective-permute-start.14) | collective-permute-done | bytes 131104 | tf_op jit(solution)/shard_map/ppermute | solution.py:533
  56.9 11.8 %long_convolution.1.after_ref = bf16[16,256,128]{2,1,0:T(8,128)(2,1)} custom-call(s32[1]{0:T(128)} %bitcast.me_ref, bf16[256,256]{1,0:T(8,128)(2,1)S(1)} %collective-permute-done.rest_0_, bf16[256,256]{1,0:T(8,128)(2,1)S(1)} %collective-permute-done.1.rest_1_, bf16[256,256]{1,0:T(8,128)(2,1)S(1)} %collective-permute-done.2.rest_2_, ...), custom_call_target="tpu_custom_call" | custom-call | flops 8999999488 | bytes 9000000 | tf_op jit(solution)/shard_map/long_convolution/pallas_call | solution.py:396
  68.8 6.3 %all-to-all-start = ((bf16[16,256,128]{2,1,0:T(8,128)(2,1)}), bf16[16,256,128]{2,1,0:T(8,128)(2,1)S(1)}, u32[]{:S(2)}, u32[]{:S(2)}) async-start(bf16[16,256,128]{2,1,0:T(8,128)(2,1)} %long_convolution.1.after_ref), calls=%async_computation | async-start | bytes 2097152 | tf_op jit(solution)/shard_map/all_to_all | solution.py:527
  75.1 3.4 %copy-done = bf16[2048,2048]{1,0:T(8,128)(2,1)S(1)} copy-done((bf16[2048,2048]{1,0:T(8,128)(2,1)S(1)}, bf16[2048,2048]{1,0:T(8,128)(2,1)}, u32[]{:S(2)}) %copy-start) | copy-done | bytes 8388632
  78.5 1.8 %stage_tail.1 = (bf16[2048,1024]{1,0:T(8,128)(2,1)S(1)}, bf16[2048,1024]{1,0:T(8,128)(2,1)S(1)}, bf16[256,2048]{1,0:T(8,128)(2,1)S(1)}, bf16[256,2048]{1,0:T(8,128)(2,1)S(1)}) custom-call(s32[1]{0:T(128)} %bitcast.1.half_ref, bf16[16,256,128]{2,1,0:T(8,128)(2,1)} %long_convolution.1.after_ref, bf16[2048,2048]{1,0:T(8,128)(2,1)S(1)} %copy-done, ...), custom_call_target="tpu_custom_call" | custom-call | bytes 20971520 | tf_op jit(solution)/shard_map/stage_tail/pallas_call | solution.py:444
  80.3 2.0 %copy-done.2 = bf16[2048,1024]{1,0:T(8,128)(2,1)} copy-done((bf16[2048,1024]{1,0:T(8,128)(2,1)}, bf16[2048,1024]{1,0:T(8,128)(2,1)S(1)}, u32[]{:S(2)}) %copy-start.2) | copy-done | bytes 4194328
  82.3 2.0 %copy-done.4 = bf16[2048,1024]{1,0:T(8,128)(2,1)} copy-done((bf16[2048,1024]{1,0:T(8,128)(2,1)}, bf16[2048,1024]{1,0:T(8,128)(2,1)S(1)}, u32[]{:S(2)}) %copy-start.4) | copy-done | bytes 4194328
  86.3 13.4 %all-to-all-done.conv_ref = bf16[16,256,128]{2,1,0:T(8,128)(2,1)S(1)} async-done(((bf16[16,256,128]{2,1,0:T(8,128)(2,1)}), bf16[16,256,128]{2,1,0:T(8,128)(2,1)S(1)}, u32[]{:S(2)}, u32[]{:S(2)}) %all-to-all-start) | async-done | bytes 1048608 | tf_op jit(solution)/shard_map/all_to_all | solution.py:527
  99.7 2.3 %copy-done.5 = bf16[2048,1024]{1,0:T(8,128)(2,1)S(1)} copy-done((bf16[2048,1024]{1,0:T(8,128)(2,1)S(1)}, bf16[2048,1024]{1,0:T(8,128)(2,1)}, u32[]{:S(2)}) %copy-start.5) | copy-done | bytes 4194328
  104.7 1.7 %gate_project_sent.1 = (bf16[256,2048]{1,0:T(8,128)(2,1)S(1)}, f32[256,1024]{1,0:T(8,128)S(1)}) custom-call(bf16[256,256]{1,0:T(8,128)(2,1)S(1)} %copy-done.11, bf16[16,256,128]{2,1,0:T(8,128)(2,1)S(1)} %all-to-all-done.conv_ref, bf16[256,2048]{1,0:T(8,128)(2,1)S(1)} %copy-done.8, bf16[256,2048]{1,0:T(8,128)(2,1)S(1)} %copy-done.10, f32[1,2048]{1,0:T(1,128)S(1)} %bitcast.3, ...), custom_call_target="tpu_custom_call" | custom-call | flops 1073741824 | bytes 4194304 | tf_op jit(solution)/shard_map/gate_project_sent/pallas_call | solution.py:472
  109.0 1.7 %join_halves.1 = bf16[1024,256]{1,0:T(8,128)(2,1)} custom-call(f32[256,1024]{1,0:T(8,128)S(1)} %project_kept.1.kept_ref, f32[256,1024]{1,0:T(8,128)S(1)} %collective-permute-done.15.came_ref), custom_call_target="tpu_custom_call" | custom-call | tf_op jit(solution)/shard_map/join_halves/pallas_call | solution.py:515
  (48 shorter events, 16.9 us)
Async XLA Ops:
  3.7 17.1 %collective-permute-start = (bf16[256,256]{1,0:T(8,128)(2,1)}, bf16[256,256]{1,0:T(8,128)(2,1)S(1)}, u32[]{:S(2)}, u32[]{:S(2)}) collective-permute-start(bf16[256,256]{1,0:T(8,128)(2,1)} %get-tuple-element.27), channel_id=1, source_target_pairs={{0,16},{2,18},{4,20},{6,22},{8,24},{10,26},{12,28},{14,30},{16,0},... | collective-permute-start | bytes 393224 | tf_op jit(solution)/shard_map/ppermute | solution.py:533
  7.8 15.8 %collective-permute-start.1 = (bf16[256,256]{1,0:T(8,128)(2,1)}, bf16[256,256]{1,0:T(8,128)(2,1)S(1)}, u32[]{:S(2)}, u32[]{:S(2)}) collective-permute-start(bf16[256,256]{1,0:T(8,128)(2,1)} %get-tuple-element.28), channel_id=1, source_target_pairs={{0,2},{2,0},{4,6},{6,4},{8,10},{10,8},{12,14},{14,12},{16,18},{18,... | collective-permute-start | bytes 393224 | tf_op jit(solution)/shard_map/ppermute | solution.py:533
  9.3 16.7 %collective-permute-start.2 = (bf16[256,256]{1,0:T(8,128)(2,1)}, bf16[256,256]{1,0:T(8,128)(2,1)S(1)}, u32[]{:S(2)}, u32[]{:S(2)}) collective-permute-start(bf16[256,256]{1,0:T(8,128)(2,1)} %get-tuple-element.29), channel_id=1, source_target_pairs={{0,24},{2,26},{4,28},{6,30},{8,16},{10,18},{12,20},{14,22},{16,8},... | collective-permute-start | bytes 393224 | tf_op jit(solution)/shard_map/ppermute | solution.py:533
  10.7 15.4 %collective-permute-start.3 = (bf16[256,256]{1,0:T(8,128)(2,1)}, bf16[256,256]{1,0:T(8,128)(2,1)S(1)}, u32[]{:S(2)}, u32[]{:S(2)}) collective-permute-start(bf16[256,256]{1,0:T(8,128)(2,1)} %get-tuple-element.30), channel_id=1, source_target_pairs={{0,4},{2,6},{4,0},{6,2},{8,12},{10,14},{12,8},{14,10},{16,20},{18,... | collective-permute-start | bytes 393224 | tf_op jit(solution)/shard_map/ppermute | solution.py:533
  12.2 16.1 %collective-permute-start.4 = (bf16[256,256]{1,0:T(8,128)(2,1)}, bf16[256,256]{1,0:T(8,128)(2,1)S(1)}, u32[]{:S(2)}, u32[]{:S(2)}) collective-permute-start(bf16[256,256]{1,0:T(8,128)(2,1)} %get-tuple-element.31), channel_id=1, source_target_pairs={{0,18},{2,16},{4,22},{6,20},{8,26},{10,24},{12,30},{14,28},{16,2},... | collective-permute-start | bytes 393224 | tf_op jit(solution)/shard_map/ppermute | solution.py:533
  20.8 9.4 %collective-permute-start.5 = (bf16[256,256]{1,0:T(8,128)(2,1)}, bf16[256,256]{1,0:T(8,128)(2,1)S(1)}, u32[]{:S(2)}, u32[]{:S(2)}) collective-permute-start(bf16[256,256]{1,0:T(8,128)(2,1)} %get-tuple-element.32), channel_id=1, source_target_pairs={{0,6},{2,4},{4,2},{6,0},{8,14},{10,12},{12,10},{14,8},{16,22},{18,... | collective-permute-start | bytes 393224 | tf_op jit(solution)/shard_map/ppermute | solution.py:533
  23.6 13.9 %collective-permute-start.6 = (bf16[256,256]{1,0:T(8,128)(2,1)}, bf16[256,256]{1,0:T(8,128)(2,1)S(1)}, u32[]{:S(2)}, u32[]{:S(2)}) collective-permute-start(bf16[256,256]{1,0:T(8,128)(2,1)} %get-tuple-element.33), channel_id=1, source_target_pairs={{0,26},{2,24},{4,30},{6,28},{8,18},{10,16},{12,22},{14,20},{16,10}... | collective-permute-start | bytes 393224 | tf_op jit(solution)/shard_map/ppermute | solution.py:533
  26.0 11.4 %collective-permute-start.7 = (bf16[256,256]{1,0:T(8,128)(2,1)}, bf16[256,256]{1,0:T(8,128)(2,1)S(1)}, u32[]{:S(2)}, u32[]{:S(2)}) collective-permute-start(bf16[256,256]{1,0:T(8,128)(2,1)} %get-tuple-element.34), channel_id=1, source_target_pairs={{0,8},{2,10},{4,12},{6,14},{8,0},{10,2},{12,4},{14,6},{16,24},{18,... | collective-permute-start | bytes 393224 | tf_op jit(solution)/shard_map/ppermute | solution.py:533
  26.0 15.4 %collective-permute-start.8 = (bf16[256,256]{1,0:T(8,128)(2,1)}, bf16[256,256]{1,0:T(8,128)(2,1)S(1)}, u32[]{:S(2)}, u32[]{:S(2)}) collective-permute-start(bf16[256,256]{1,0:T(8,128)(2,1)} %get-tuple-element.35), channel_id=1, source_target_pairs={{0,20},{2,22},{4,16},{6,18},{8,28},{10,30},{12,24},{14,26},{16,4},... | collective-permute-start | bytes 393224 | tf_op jit(solution)/shard_map/ppermute | solution.py:533
  28.3 13.6 %collective-permute-start.9 = (bf16[256,256]{1,0:T(8,128)(2,1)}, bf16[256,256]{1,0:T(8,128)(2,1)S(1)}, u32[]{:S(2)}, u32[]{:S(2)}) collective-permute-start(bf16[256,256]{1,0:T(8,128)(2,1)} %get-tuple-element.36), channel_id=1, source_target_pairs={{0,10},{2,8},{4,14},{6,12},{8,2},{10,0},{12,6},{14,4},{16,26},{18,... | collective-permute-start | bytes 393224 | tf_op jit(solution)/shard_map/ppermute | solution.py:533
  30.2 14.1 %collective-permute-start.10 = (bf16[256,256]{1,0:T(8,128)(2,1)}, bf16[256,256]{1,0:T(8,128)(2,1)S(1)}, u32[]{:S(2)}, u32[]{:S(2)}) collective-permute-start(bf16[256,256]{1,0:T(8,128)(2,1)} %get-tuple-element.37), channel_id=1, source_target_pairs={{0,28},{2,30},{4,24},{6,26},{8,20},{10,22},{12,16},{14,18},{16,12}... | collective-permute-start | bytes 393224 | tf_op jit(solution)/shard_map/ppermute | solution.py:533
  37.4 8.6 %collective-permute-start.11 = (bf16[256,256]{1,0:T(8,128)(2,1)}, bf16[256,256]{1,0:T(8,128)(2,1)S(1)}, u32[]{:S(2)}, u32[]{:S(2)}) collective-permute-start(bf16[256,256]{1,0:T(8,128)(2,1)} %get-tuple-element.38), channel_id=1, source_target_pairs={{0,12},{2,14},{4,8},{6,10},{8,4},{10,6},{12,0},{14,2},{16,28},{18,... | collective-permute-start | bytes 393224 | tf_op jit(solution)/shard_map/ppermute | solution.py:533
  37.5 14.6 %collective-permute-start.12 = (bf16[256,256]{1,0:T(8,128)(2,1)}, bf16[256,256]{1,0:T(8,128)(2,1)S(1)}, u32[]{:S(2)}, u32[]{:S(2)}) collective-permute-start(bf16[256,256]{1,0:T(8,128)(2,1)} %get-tuple-element.39), channel_id=1, source_target_pairs={{0,22},{2,20},{4,18},{6,16},{8,30},{10,28},{12,26},{14,24},{16,6},... | collective-permute-start | bytes 393224 | tf_op jit(solution)/shard_map/ppermute | solution.py:533
  41.4 10.6 %collective-permute-start.13 = (bf16[256,256]{1,0:T(8,128)(2,1)}, bf16[256,256]{1,0:T(8,128)(2,1)S(1)}, u32[]{:S(2)}, u32[]{:S(2)}) collective-permute-start(bf16[256,256]{1,0:T(8,128)(2,1)} %get-tuple-element.40), channel_id=1, source_target_pairs={{0,14},{2,12},{4,10},{6,8},{8,6},{10,4},{12,2},{14,0},{16,30},{18,... | collective-permute-start | bytes 393224 | tf_op jit(solution)/shard_map/ppermute | solution.py:533
  41.9 12.0 %collective-permute-start.14 = (bf16[256,256]{1,0:T(8,128)(2,1)}, bf16[256,256]{1,0:T(8,128)(2,1)S(1)}, u32[]{:S(2)}, u32[]{:S(2)}) collective-permute-start(bf16[256,256]{1,0:T(8,128)(2,1)} %get-tuple-element.41), channel_id=1, source_target_pairs={{0,30},{2,28},{4,26},{6,24},{8,22},{10,20},{12,18},{14,16},{16,14}... | collective-permute-start | bytes 393224 | tf_op jit(solution)/shard_map/ppermute | solution.py:533
  56.9 18.2 %copy-start.1 = (bf16[256,2048]{1,0:T(8,128)(2,1)S(1)}, bf16[256,2048]{1,0:T(8,128)(2,1)}, u32[]{:S(2)}) copy-start(bf16[256,2048]{1,0:T(8,128)(2,1)} %values_hbm.3) | copy-start | bytes 3145732
  56.9 18.2 %copy-start.6 = (bf16[256,2048]{1,0:T(8,128)(2,1)S(1)}, bf16[256,2048]{1,0:T(8,128)(2,1)}, u32[]{:S(2)}) copy-start(bf16[256,2048]{1,0:T(8,128)(2,1)} %gates_hbm.1) | copy-start | bytes 3145732
  68.8 30.9 %all-to-all-start = ((bf16[16,256,128]{2,1,0:T(8,128)(2,1)}), bf16[16,256,128]{2,1,0:T(8,128)(2,1)S(1)}, u32[]{:S(2)}, u32[]{:S(2)}) async-start(bf16[16,256,128]{2,1,0:T(8,128)(2,1)} %long_convolution.1.after_ref), calls=%async_computation | async-start | bytes 2097152 | tf_op jit(solution)/shard_map/all_to_all | solution.py:527
  75.1 3.4 %copy-start = (bf16[2048,2048]{1,0:T(8,128)(2,1)S(1)}, bf16[2048,2048]{1,0:T(8,128)(2,1)}, u32[]{:S(2)}) copy-start(bf16[2048,2048]{1,0:T(8,128)(2,1)} %weight_hbm.1) | copy-start | bytes 25165828
  78.5 21.2 %copy-start.11 = (bf16[256,256]{1,0:T(8,128)(2,1)S(1)}, bf16[256,256]{1,0:T(8,128)(2,1)}, u32[]{:S(2)}) copy-start(bf16[256,256]{1,0:T(8,128)(2,1)} %constant.22.clone.order_ref) | copy-start | bytes 393220
  78.5 21.2 %copy-start.12 = (f32[2048]{0:T(1024)S(1)}, f32[2048]{0:T(1024)}, u32[]{:S(2)}) copy-start(f32[2048]{0:T(1024)} %param.13) | copy-start | bytes 24580
  99.7 6.7 %copy-start.3 = (bf16[2048,1024]{1,0:T(8,128)(2,1)S(1)}, bf16[2048,1024]{1,0:T(8,128)(2,1)}, u32[]{:S(2)}) copy-start(bf16[2048,1024]{1,0:T(8,128)(2,1)} %copy-done.2) | copy-start | bytes 12582916
  99.7 2.3 %copy-start.5 = (bf16[2048,1024]{1,0:T(8,128)(2,1)S(1)}, bf16[2048,1024]{1,0:T(8,128)(2,1)}, u32[]{:S(2)}) copy-start(bf16[2048,1024]{1,0:T(8,128)(2,1)} %copy-done.4) | copy-start | bytes 12582916
  106.3 2.7 %collective-permute-start.15 = (f32[256,1024]{1,0:T(8,128)S(1)}, f32[256,1024]{1,0:T(8,128)S(1)}, u32[]{:S(2)}, u32[]{:S(2)}) collective-permute-start(f32[256,1024]{1,0:T(8,128)S(1)} %get-tuple-element.48), channel_id=1, source_target_pairs={{0,1},{1,0},{2,3},{3,2},{4,5},{5,4},{6,7},{7,6},{8,9},{9,8},{10,11... | collective-permute-start | bytes 3145736 | tf_op jit(solution)/shard_map/ppermute | solution.py:545
  (9 other events, 11.6 us)

commit v7 on v6

--- a/solution.py
+++ b/solution.py
@@ -17,7 +17,7 @@
 Q_ORDER = [low + 4 * high for low in range(4) for high in range(4)]
 VMEM_BYTES = 60 * 1024 * 1024
 CONV_BYTES = 49 * 1024 * 1024
-TAIL_BYTES = 16 * 1024 * 1024
+TAIL_BYTES = 49 * 1024 * 1024
 
 
 def angle_table(first, second, period):
@@ -116,15 +116,20 @@
 def transform_tables(length):
     inner = length // RADIX
     k = np.arange(inner)[:, None]
-    m = np.arange(inner)[None, :]
-    angles = (RADIX * m * (4 * k + 1)) % (4 * length) * (TWO_PI / (4 * length))
-    table = np.concatenate([np.cos(angles), -np.sin(angles)], axis=0)
-    forward = np.concatenate(split_table(table), axis=1)
-    backward = np.concatenate(split_table(table.T / length), axis=0)
-    turns = (np.array(Q_ORDER)[:, None] * (4 * k.T + 1)) % (4 * length) * (TWO_PI / (4 * length))
-    turns = np.stack([np.cos(turns), np.sin(turns)], axis=1).astype(np.float32)
-    turns = np.ascontiguousarray(np.broadcast_to(turns[..., None], (*turns.shape, LANES)))
-    return forward, turns, backward
+    unit = TWO_PI / (4 * length)
+    turns = (np.array(Q_ORDER)[:, None] * (4 * k.T + 1)) % (4 * length) * unit
+    turns = np.stack([np.cos(turns), np.sin(turns)], axis=1).reshape(2 * RADIX, inner, 1)
+    blocks = [np.broadcast_to(turns, (2 * RADIX, inner, LANES))]
+    forward, backward = [], []
+    for odd in range(2):
+        m = 2 * np.arange(inner // 2)[None, :] + odd
+        angles = (RADIX * m * (4 * k[: inner // 2] + 1)) % (4 * length) * unit
+        table = np.concatenate([np.cos(angles), -np.sin(angles)], axis=0)
+        forward.append(np.concatenate(split_table(table), axis=1))
+        backward.append(np.concatenate(split_table(table.T / length), axis=0))
+    for table in forward + backward:
+        blocks.append(table.astype(np.float32).reshape(inner, -1, LANES).swapaxes(0, 1))
+    return np.concatenate(blocks, axis=0).astype(np.float32)
 
 
 @functools.lru_cache(maxsize=None)
@@ -132,8 +137,9 @@
     chunk = rows // RADIX
     order = np.zeros((rows, rows), np.float32)
     for i, q in enumerate(Q_ORDER):
-        for j in range(chunk):
-            order[i * chunk + j, RADIX * j + q] = 1.0
+        for odd in range(2):
+            for j in range(chunk // 2):
+                order[i * chunk + odd * (chunk // 2) + j, RADIX * (2 * j + odd) + q] = 1.0
     return order.astype(ml_dtypes.bfloat16)
 
 
@@ -185,7 +191,9 @@
     half = blocks // 2
     across = [half + (i // 2 if i % 2 == 0 else half // 2 + i // 2) for i in range(half)]
     near = list(range(1, half)) + [0]
-    return [slot for pair in zip(across, near) for slot in pair]
+    lead = 2
+    mixed = [slot for pair in zip(across[lead:], near) for slot in pair]
+    return across[:lead] + mixed + near[half - lead :]
 
 
 def arrange_kernel(pieces, blocks, me_ref, order_hbm, values_hbm, taps_hbm, *rest):
@@ -243,67 +251,77 @@
 
 
 def convolve_blocks(
-    me_ref, slots, forward_hbm, turns_hbm, backward_hbm, out_hbm,
-    streams, forward_ref, turns_ref, backward_ref,
-    raw_even, raw_odd, columns, mixed, halves_even, halves_odd, signals, sems,
+    me_ref, slots, tables_hbm, out_hbm,
+    streams, turns_ref, fixed, stages, raw_even, raw_odd, columns, mixed, halves_even, halves_odd, signals, sems,
 ):
     blocks, rows, _ = streams.shape
     chunk = rows // RADIX
     inner = blocks * chunk
+    part_rows = inner // 2
     group = rows // 4
     raws = (raw_even, raw_odd)
     halves = (halves_even, halves_odd)
-    load_forward = pltpu.make_async_copy(forward_hbm, forward_ref, sems.at[0])
-    load_backward = pltpu.make_async_copy(backward_hbm, backward_ref, sems.at[1])
+    count = fixed.shape[0]
+    load_fixed = pltpu.make_async_copy(tables_hbm.at[pl.ds(2 * RADIX, count)], fixed, sems.at[0])
     load_turns, stores = [], []
     for low in range(4):
         taken = pl.ds(low * group, group)
-        four = pl.ds(4 * low, 4)
-        load_turns.append(pltpu.make_async_copy(turns_hbm.at[four], turns_ref.at[four], sems.at[6 + low]))
-        stores.append(pltpu.make_async_copy(signals.at[:, taken], out_hbm.at[:, taken], sems.at[10 + low]))
-    load_forward.start()
+        eight = pl.ds(8 * low, 8)
+        load_turns.append(pltpu.make_async_copy(tables_hbm.at[eight], turns_ref.at[eight], sems.at[1 + low]))
+        stores.append(pltpu.make_async_copy(signals.at[:, taken], out_hbm.at[:, taken], sems.at[5 + low]))
+    load_fixed.start()
     for load in load_turns:
         load.start()
-    load_backward.start()
     for slot, source in zip(slot_order(blocks), slots):
         streams[me_ref[0] ^ slot] = source[...]
+    load_fixed.wait()
+    width = inner // LANES
+    for table in range(4):
+        for block in range(width):
+            stages[table, :, pl.ds(block * LANES, LANES)] = fixed[table * width + block].astype(jnp.bfloat16)
 
     def transform(low, pair):
-        streams_of = []
+        sides = [[], []]
         for part in range(2):
             taken = pl.ds(pl.multiple_of(low * group + (2 * pair + part) * chunk, chunk), chunk)
-            streams_of.append(streams[:, taken].reshape(inner, 2 * LANES))
-        both = jnp.concatenate(streams_of, axis=1)
-        result = jnp.dot(
-            forward_ref[...], jnp.concatenate([both, both], axis=0), preferred_element_type=jnp.float32
-        )
-        raws[low % 2][2 * pair] = result[:, : 2 * LANES]
-        raws[low % 2][2 * pair + 1] = result[:, 2 * LANES :]
+            stream = streams[:, taken].astype(jnp.float32).reshape(blocks, 2, chunk // 2, 2 * LANES)
+            for odd in range(2):
+                sides[odd].append(stream[:, odd].reshape(part_rows, 2 * LANES).astype(jnp.bfloat16))
+        for odd in range(2):
+            both = jnp.concatenate(sides[odd], axis=1)
+            result = jnp.dot(
+                stages[odd], jnp.concatenate([both, both], axis=0), preferred_element_type=jnp.float32
+            )
+            for part in range(2):
+                raws[low % 2][2 * pair + part, odd] = result[:, 2 * part * LANES : 2 * (part + 1) * LANES]
 
     def first_pass(low, start):
         raw = raws[low % 2]
-        upper, lower = pl.ds(start, 8), pl.ds(inner + start, 8)
+        real, imaginary = pl.ds(start, 8), pl.ds(part_rows + start, 8)
         for side in range(2):
             lanes = pl.ds(side * LANES, LANES)
-            points = []
+            points = [[], []]
             for high in range(4):
-                point = (raw[high, upper, lanes], raw[high, lower, lanes])
-                if low + high:
-                    turns = [turns_ref[4 * low + high, part, upper] for part in range(2)]
-                    point = turned(point, *turns, -1)
-                points.append(point)
-            for k, point in enumerate(four_points(points, -1)):
-                point = turn(point, low * k, -1)
-                columns[4 * low + k, upper, lanes] = point[0]
-                columns[4 * low + k, lower, lanes] = point[1]
+                even = (raw[high, 0, real, lanes], raw[high, 0, imaginary, lanes])
+                odd = (raw[high, 1, real, lanes], raw[high, 1, imaginary, lanes])
+                points[0].append((even[0] + odd[0], even[1] + odd[1]))
+                points[1].append((even[0] - odd[0], even[1] - odd[1]))
+            for part in range(2):
+                upper, lower = pl.ds(part * part_rows + start, 8), pl.ds(inner + part * part_rows + start, 8)
+                for high in range(4):
+                    if low + high:
+                        turns = [turns_ref[2 * (4 * low + high) + i, upper] for i in range(2)]
+                        points[part][high] = turned(points[part][high], *turns, -1)
+                for k, point in enumerate(four_points(points[part], -1)):
+                    point = turn(point, low * k, -1)
+                    columns[4 * low + k, upper, lanes] = point[0]
+                    columns[4 * low + k, lower, lanes] = point[1]
 
     def first_rows(low, start, count):
         for part in range(count):
             first_pass(low, pl.multiple_of(start + 8 * part, 8))
 
-    steps = inner // 2
-
-    load_forward.wait()
+    steps = part_rows // 2
 
     def alone(pair, carry):
         transform(0, pair)
@@ -324,56 +342,74 @@
     def middle(index, carry):
         start = pl.multiple_of(index * 8, 8)
         first_pass(3, start)
-        upper, lower = pl.ds(start, 8), pl.ds(inner + start, 8)
-        for k in range(4):
-            sides = []
-            for side in range(2):
-                lanes = pl.ds(side * LANES, LANES)
-                points = [(columns[4 * low + k, upper, lanes], columns[4 * low + k, lower, lanes]) for low in range(4)]
-                sides.append(four_points(points, -1))
-            product = [
-                (a[0] * b[0] - a[1] * b[1], a[0] * b[1] + a[1] * b[0]) for a, b in zip(*sides)
-            ]
-            for part, point in enumerate(four_points(product, 1)):
-                point = turn(point, k * part, 1)
-                mixed[4 * part + k, upper] = point[0]
-                mixed[4 * part + k, lower] = point[1]
+        for part in range(2):
+            upper, lower = pl.ds(part * part_rows + start, 8), pl.ds(inner + part * part_rows + start, 8)
+            for k in range(4):
+                sides = []
+                for side in range(2):
+                    lanes = pl.ds(side * LANES, LANES)
+                    points = [
+                        (columns[4 * low + k, upper, lanes], columns[4 * low + k, lower, lanes]) for low in range(4)
+                    ]
+                    sides.append(four_points(points, -1))
+                product = [
+                    (a[0] * b[0] - a[1] * b[1], a[0] * b[1] + a[1] * b[0]) for a, b in zip(*sides)
+                ]
+                for high, point in enumerate(four_points(product, 1)):
+                    point = turn(point, k * high, 1)
+                    mixed[4 * high + k, upper] = point[0]
+                    mixed[4 * high + k, lower] = point[1]
         return carry
 
-    lax.fori_loop(0, inner // 8, middle, 0)
+    lax.fori_loop(0, part_rows // 8, middle, 0)
 
     def last_pass(low, start):
         target = halves[low % 2]
-        upper, lower = pl.ds(start, 16), pl.ds(inner + start, 16)
-        points = [(mixed[4 * low + k, upper], mixed[4 * low + k, lower]) for k in range(4)]
-        for high, point in enumerate(four_points(points, 1)):
-            if low + high:
-                turns = [turns_ref[4 * low + high, part, upper] for part in range(2)]
-                point = turned(point, *turns, 1)
-            for part, taken in zip(point, (upper, lower)):
-                rounded = part.astype(jnp.bfloat16)
-                target[high, taken, pl.ds(0, LANES)] = rounded
-                target[high, taken, pl.ds(LANES, LANES)] = (part - rounded.astype(jnp.float32)).astype(jnp.bfloat16)
+        found = []
+        for part in range(2):
+            upper, lower = pl.ds(part * part_rows + start, 16), pl.ds(inner + part * part_rows + start, 16)
+            points = list(four_points([(mixed[4 * low + k, upper], mixed[4 * low + k, lower]) for k in range(4)], 1))
+            for high in range(4):
+                if low + high:
+                    turns = [turns_ref[2 * (4 * low + high) + i, upper] for i in range(2)]
+                    points[high] = turned(points[high], *turns, 1)
+            found.append(points)
+        for high in range(4):
+            for i in range(2):
+                taken = pl.ds(i * part_rows + start, 16)
+                first, second = found[0][high][i], found[1][high][i]
+                for odd, value in enumerate((first + second, first - second)):
+                    rounded = value.astype(jnp.bfloat16)
+                    target[high, odd, taken, pl.ds(0, LANES)] = rounded
+                    target[high, odd, taken, pl.ds(LANES, LANES)] = (value - rounded.astype(jnp.float32)).astype(
+                        jnp.bfloat16
+                    )
 
     def last_rows(low, start, count):
         for part in range(count):
             last_pass(low, pl.multiple_of(start + 16 * part, 16))
 
     def restore(low, pair):
-        both = jnp.concatenate([halves[low % 2][2 * pair], halves[low % 2][2 * pair + 1]], axis=1)
-        terms = jnp.dot(backward_ref[...], both, preferred_element_type=jnp.float32)
+        sides = []
+        for odd in range(2):
+            both = jnp.concatenate([halves[low % 2][2 * pair + part, odd] for part in range(2)], axis=1)
+            terms = jnp.dot(stages[2 + odd], both, preferred_element_type=jnp.float32)
+            found = []
+            for part in range(2):
+                first, second = [slice((2 * part + i) * LANES, (2 * part + i + 1) * LANES) for i in range(2)]
+                signal = terms[:part_rows, first] + terms[:part_rows, second] + terms[part_rows:, first]
+                found.append(signal.reshape(blocks, 1, chunk // 2, LANES))
+            sides.append(found)
         for part in range(2):
-            first, second = [slice((2 * part + i) * LANES, (2 * part + i + 1) * LANES) for i in range(2)]
-            signal = terms[:inner, first] + terms[:inner, second] + terms[inner:, first]
+            signal = jnp.concatenate([sides[0][part], sides[1][part]], axis=1).reshape(blocks, chunk, LANES)
             taken = pl.ds(pl.multiple_of(low * group + (2 * pair + part) * chunk, chunk), chunk)
-            signals[:, taken] = signal.astype(jnp.bfloat16).reshape(blocks, chunk, LANES)
+            signals[:, taken] = signal.astype(jnp.bfloat16)
 
     def prepare(index, carry):
         last_rows(0, index * steps, steps // 16)
         return carry
 
     lax.fori_loop(0, 2, prepare, 0)
-    load_backward.wait()
     for low in range(4):
 
         def back(pair, carry, low=low):
@@ -393,116 +429,124 @@
     rows, lanes = slots[0].shape
     length = blocks * rows
     inner = length // RADIX
+    tables = transform_tables(length)
     return pl.pallas_call(
         functools.partial(convolve_kernel, blocks),
         in_specs=[pl.BlockSpec(memory_space=pltpu.SMEM)]
         + [pl.BlockSpec(memory_space=pltpu.VMEM)] * blocks
-        + [pl.BlockSpec(memory_space=pl.ANY)] * 3,
+        + [pl.BlockSpec(memory_space=pl.ANY)],
         out_specs=pl.BlockSpec(memory_space=pl.ANY),
         out_shape=jax.ShapeDtypeStruct((blocks, rows, LANES), jnp.bfloat16),
         scratch_shapes=[
             pltpu.VMEM((blocks, rows, lanes), jnp.bfloat16),
-            pltpu.VMEM((2 * inner, 2 * inner), jnp.bfloat16),
-            pltpu.VMEM((RADIX, 2, inner, LANES), jnp.float32),
-            pltpu.VMEM((2 * inner, 2 * inner), jnp.bfloat16),
-            pltpu.VMEM((4, 2 * inner, lanes), jnp.float32),
-            pltpu.VMEM((4, 2 * inner, lanes), jnp.float32),
+            pltpu.VMEM((2 * RADIX, inner, LANES), jnp.float32),
+            pltpu.VMEM((tables.shape[0] - 2 * RADIX, inner, LANES), jnp.float32),
+            pltpu.VMEM((4, inner, inner), jnp.bfloat16),
+            pltpu.VMEM((4, 2, inner, lanes), jnp.float32),
+            pltpu.VMEM((4, 2, inner, lanes), jnp.float32),
             pltpu.VMEM((RADIX, 2 * inner, lanes), jnp.float32),
             pltpu.VMEM((RADIX, 2 * inner, LANES), jnp.float32),
-            pltpu.VMEM((4, 2 * inner, lanes), jnp.bfloat16),
-            pltpu.VMEM((4, 2 * inner, lanes), jnp.bfloat16),
+            pltpu.VMEM((4, 2, inner, lanes), jnp.bfloat16),
+            pltpu.VMEM((4, 2, inner, lanes), jnp.bfloat16),
             pltpu.VMEM((blocks, rows, LANES), jnp.bfloat16),
-            pltpu.SemaphoreType.DMA((14,)),
+            pltpu.SemaphoreType.DMA((9,)),
         ],
         compiler_params=pltpu.CompilerParams(vmem_limit_bytes=CONV_BYTES),
-        cost_estimate=pl.CostEstimate(flops=9 * 10**9, bytes_accessed=9 * 10**6, transcendentals=0),
+        cost_estimate=pl.CostEstimate(flops=5 * 10**9, bytes_accessed=9 * 10**6, transcendentals=0),
         name="long_convolution",
-    )(me, *slots, *(jnp.asarray(table) for table in transform_tables(length)))
-
-
-def stage_kernel(half_ref, after_ref, weight_hbm, gates_hbm, values_hbm, sent_ref, kept_ref, gates_ref, values_ref, sems):
-    del after_ref
-    features = sent_ref.shape[1]
-    half = half_ref[0]
-    sides = [pl.ds(pl.multiple_of(side * features, features), features) for side in (1 - half, half)]
-    copies = [
-        pltpu.make_async_copy(weight_hbm.at[:, sides[0]], sent_ref, sems.at[0]),
-        pltpu.make_async_copy(weight_hbm.at[:, sides[1]], kept_ref, sems.at[1]),
-        pltpu.make_async_copy(gates_hbm, gates_ref, sems.at[2]),
-        pltpu.make_async_copy(values_hbm, values_ref, sems.at[3]),
+    )(me, *slots, jnp.asarray(tables))
+
+
+def gate_kernel(
+    group, half_ref, order_hbm, conv_ref, gates_hbm, values_hbm, skip_ref, weight_hbm, gated_ref, out_ref,
+    order_ref, gates_ref, values_ref, weight_ref, sems,
+):
+    blocks, _, lanes = conv_ref.shape
+    width, features = weight_ref.shape
+    columns = pl.ds(pl.multiple_of((1 - half_ref[0]) * features, features), features)
+    loads = [
+        pltpu.make_async_copy(order_hbm, order_ref, sems.at[0]),
+        pltpu.make_async_copy(gates_hbm, gates_ref, sems.at[1]),
+        pltpu.make_async_copy(values_hbm, values_ref, sems.at[2]),
     ]
-    for copy in copies:
-        copy.start()
-    for copy in copies:
-        copy.wait()
-
-
-def stage(half, after, out_weight, gates, values):
-    width, features = out_weight.shape
-    share = jax.ShapeDtypeStruct((width, features // 2), out_weight.dtype)
-    stream = jax.ShapeDtypeStruct(gates.shape, gates.dtype)
-    return pl.pallas_call(
-        stage_kernel,
-        in_specs=[pl.BlockSpec(memory_space=pltpu.SMEM)] + [pl.BlockSpec(memory_space=pl.ANY)] * 4,
-        out_specs=[pl.BlockSpec(memory_space=pltpu.VMEM)] * 4,
-        out_shape=[share, share, stream, stream],
-        scratch_shapes=[pltpu.SemaphoreType.DMA((4,))],
-        compiler_params=pltpu.CompilerParams(vmem_limit_bytes=TAIL_BYTES),
-        cost_estimate=pl.CostEstimate(
-            flops=0, bytes_accessed=4 * width * features + 8 * gates.size, transcendentals=0
-        ),
-        name="stage_tail",
-    )(half, after, out_weight, gates, values)
-
-
-def gate_kernel(group, order_ref, conv_ref, gates_ref, values_ref, skip_ref, weight_ref, gated_ref, out_ref):
-    blocks, _, lanes = conv_ref.shape
+    deep = width // 2
+    for part in range(2):
+        rows = pl.ds(part * deep, deep)
+        loads.append(pltpu.make_async_copy(weight_hbm.at[rows, columns], weight_ref.at[rows], sems.at[3 + part]))
+    for load in loads:
+        load.start()
+    for load in loads[:3]:
+        load.wait()
     for step in range(blocks // group):
         taken = pl.ds(step * group * lanes, group * lanes)
         conv = jnp.concatenate([conv_ref[step * group + part] for part in range(group)], axis=1)
         conv = jnp.dot(order_ref[...], conv, preferred_element_type=jnp.float32)
         direct = skip_ref[:, taken] * values_ref[:, taken].astype(jnp.float32)
         gated_ref[:, taken] = (gates_ref[:, taken].astype(jnp.float32) * (conv + direct)).astype(jnp.bfloat16)
-    out_ref[...] = jnp.dot(gated_ref[...], weight_ref[...], preferred_element_type=jnp.float32)
-
-
-def gate_and_project(conv, gates, values, skip_gain, weight):
+    loads[3].wait()
+    first = jnp.dot(gated_ref[:, :deep], weight_ref[:deep], preferred_element_type=jnp.float32)
+    loads[4].wait()
+    out_ref[...] = first + jnp.dot(gated_ref[:, deep:], weight_ref[deep:], preferred_element_type=jnp.float32)
+
+
+def gate_and_project(half, conv, gates, values, skip_gain, weight):
     rows, width = gates.shape
-    features = weight.shape[1]
+    features = weight.shape[1] // 2
+    anywhere, inside = pl.BlockSpec(memory_space=pl.ANY), pl.BlockSpec(memory_space=pltpu.VMEM)
     return pl.pallas_call(
         functools.partial(gate_kernel, 4),
-        in_specs=[pl.BlockSpec(memory_space=pltpu.VMEM)] * 6,
-        out_specs=[pl.BlockSpec(memory_space=pltpu.VMEM)] * 2,
+        in_specs=[pl.BlockSpec(memory_space=pltpu.SMEM), anywhere, inside, anywhere, anywhere, inside, anywhere],
+        out_specs=[inside] * 2,
         out_shape=[
             jax.ShapeDtypeStruct((rows, width), jnp.bfloat16),
             jax.ShapeDtypeStruct((rows, features), jnp.float32),
+        ],
+        scratch_shapes=[
+            pltpu.VMEM((rows, rows), jnp.bfloat16),
+            pltpu.VMEM((rows, width), jnp.bfloat16),
+            pltpu.VMEM((rows, width), jnp.bfloat16),
+            pltpu.VMEM((width, features), jnp.bfloat16),
+            pltpu.SemaphoreType.DMA((5,)),
         ],
         compiler_params=pltpu.CompilerParams(vmem_limit_bytes=TAIL_BYTES),
         cost_estimate=pl.CostEstimate(
             flops=2 * rows * width * features, bytes_accessed=2 * width * features, transcendentals=0
         ),
         name="gate_project_sent",
-    )(jnp.asarray(row_order(rows).T), conv, gates, values, skip_gain[None, :], weight)
-
-
-def kept_kernel(gated_ref, weight_ref, out_ref):
-    out_ref[...] = jnp.dot(gated_ref[...], weight_ref[...], preferred_element_type=jnp.float32)
-
-
-def project_kept(gated, weight):
+    )(half, jnp.asarray(row_order(rows).T), conv, gates, values, skip_gain[None, :], weight)
+
+
+def kept_kernel(half_ref, gated_ref, weight_hbm, out_ref, weight_ref, sems):
+    width, features = weight_ref.shape
+    columns = pl.ds(pl.multiple_of(half_ref[0] * features, features), features)
+    deep = width // 2
+    loads = []
+    for part in range(2):
+        rows = pl.ds(part * deep, deep)
+        loads.append(pltpu.make_async_copy(weight_hbm.at[rows, columns], weight_ref.at[rows], sems.at[part]))
+        loads[part].start()
+    loads[0].wait()
+    first = jnp.dot(gated_ref[:, :deep], weight_ref[:deep], preferred_element_type=jnp.float32)
+    loads[1].wait()
+    out_ref[...] = first + jnp.dot(gated_ref[:, deep:], weight_ref[deep:], preferred_element_type=jnp.float32)
+
+
+def project_kept(half, gated, weight):
     rows, width = gated.shape
-    features = weight.shape[1]
+    features = weight.shape[1] // 2
+    anywhere, inside = pl.BlockSpec(memory_space=pl.ANY), pl.BlockSpec(memory_space=pltpu.VMEM)
     return pl.pallas_call(
         kept_kernel,
-        in_specs=[pl.BlockSpec(memory_space=pltpu.VMEM)] * 2,
-        out_specs=pl.BlockSpec(memory_space=pltpu.VMEM),
+        in_specs=[pl.BlockSpec(memory_space=pltpu.SMEM), inside, anywhere],
+        out_specs=inside,
         out_shape=jax.ShapeDtypeStruct((rows, features), jnp.float32),
+        scratch_shapes=[pltpu.VMEM((width, features), jnp.bfloat16), pltpu.SemaphoreType.DMA((2,))],
         compiler_params=pltpu.CompilerParams(vmem_limit_bytes=TAIL_BYTES),
         cost_estimate=pl.CostEstimate(
             flops=2 * rows * width * features, bytes_accessed=2 * width * features, transcendentals=0
         ),
         name="project_kept",
-    )(gated, weight)
+    )(half, gated, weight)
 
 
 def join_kernel(kept_ref, came_ref, out_ref):
@@ -540,10 +584,9 @@
     me = lax.axis_index("seq").astype(jnp.int32)[None]
     half = lax.axis_index("chan").astype(jnp.int32)[None]
     conv = convolve(me, exchange(arrange(me, values, filter_taps, blocks)))
-    weight_sent, weight_kept, gates, values = stage(half, conv, out_weight, gates, values)
-    gated, sent = gate_and_project(swap_blocks(conv), gates, values, skip_gain, weight_sent)
+    gated, sent = gate_and_project(half, swap_blocks(conv), gates, values, skip_gain, out_weight)
     other = lax.ppermute(sent, "chan", [(0, 1), (1, 0)])
-    kept = project_kept(gated, weight_kept)
+    kept = project_kept(half, gated, out_weight)
     return join(kept, other)
 
 

time: 112 us -> 113 us (level)
  local copies, waits for them, and re-layouts: 17.3 us -> 0.92 us
  waiting for transfers between devices: 36.7 us -> 47.1 us
  starting transfers between devices: 34.7 us -> 40.5 us
  Pallas kernels: 21.9 us -> 23.6 us
    unnamed x32 -> x8, local copies, waits for them, and re-layouts: 17.3 us -> 0.92 us
    all_to_all x1, waiting for transfers between devices: 13.4 us -> 24.6 us  [swap_blocks(): return lax.all_to_all(array, 'seq', split_axis=0, concat_axis=0, tiled=True)]
    ppermute x15, starting transfers between devices: 28.3 us -> 34.3 us  [exchange(): lax.ppermute(source, 'seq', [(j, j ^ slot) for j in range(blocks)])]
    pallas_call x1, Pallas kernels: 1.66 us -> 4.09 us  [gate_and_project(): pl.pallas_call(functools.partial(gate_kernel, 4), in_specs=[pl.BlockSpec(...]
    ppermute x1, waiting for transfers between devices: 1.37 us -> 0.01 us  [kernel_local(): other = lax.ppermute(sent, 'chan', [(0, 1), (1, 0)])]
    pallas_call x1, Pallas kernels: 11.8 us -> 10.5 us  [convolve(): pl.pallas_call(functools.partial(convolve_kernel, blocks), in_specs=[pl.B...]
    pallas_call x2 -> x1, Pallas kernels: 3.04 us -> 3.5 us  [project_kept(): pl.pallas_call(kept_kernel, in_specs=[pl.BlockSpec(memory_space=pltpu.SME...]
  transfers between devices with their start and end apart: 17 -> 17, of which waited for: 10 -> 7; matrix products, arithmetic and copies ran while one was open for 0% -> 0% of each run, Pallas kernels for 3% -> 3%
where the time goes in v7:
time: 113 us; the launch traced here: 112 us
  waiting for transfers between devices  47.1 us (42%)
  starting transfers between devices  40.5 us (36%)
  Pallas kernels  23.6 us (21%)
    ppermute x15, starting transfers between devices, exchange(): lax.ppermute(source, 'seq', [(j, j ^ slot) for j in range(blocks)])  34.3 us
    all_to_all x1, waiting for transfers between devices, swap_blocks(): return lax.all_to_all(array, 'seq', split_axis=0, concat_axis=0, tiled=True)  24.6 us
    ppermute x15, waiting for transfers between devices, exchange(): lax.ppermute(source, 'seq', [(j, j ^ slot) for j in range(blocks)])  22.5 us
    pallas_call x1, Pallas kernels, convolve(): pl.pallas_call(functools.partial(convolve_kernel, blocks), in_specs=[pl.B...  10.5 us
    all_to_all x1, starting transfers between devices, swap_blocks(): return lax.all_to_all(array, 'seq', split_axis=0, concat_axis=0, tiled=True)  6.15 us
    pallas_call x1, Pallas kernels, gate_and_project(): pl.pallas_call(functools.partial(gate_kernel, 4), in_specs=[pl.BlockSpec(...  4.09 us
    pallas_call x1, Pallas kernels, arrange(): pl.pallas_call(functools.partial(arrange_kernel, pieces, blocks), in_spec...  3.7 us
    pallas_call x1, Pallas kernels, project_kept(): pl.pallas_call(kept_kernel, in_specs=[pl.BlockSpec(memory_space=pltpu.SME...  3.5 us
  transfers between devices with their start and end apart: 17, of which 7 were waited for; matrix products, arithmetic and copies ran while one was open for 0% of the time, Pallas kernels for 3%

profile of v7, /device:TPU:0, one launch (start us, length us, event | category | flops | bytes accessed | tf_op | source)
XLA Modules:
  0.0 112.1 jit_solution(932125804311764094)
XLA Ops:
  0.0 3.7 %arrange_rows.1 = (bf16[256,256]{1,0:T(8,128)(2,1)}, bf16[256,256]{1,0:T(8,128)(2,1)}, bf16[256,256]{1,0:T(8,128)(2,1)}, bf16[256,256]{1,0:T(8,128)(2,1)}, bf16[...) custom-call(s32[1]{0:T(128)} %bitcast.1.me_ref, ...), custom_call_target="tpu_custom_call" | custom-call | flops 536870912 | bytes 4194304 | tf_op jit(solution)/shard_map/arrange_rows/pallas_call | solution.py:228
  3.7 4.1 %collective-permute-start = (bf16[256,256]{1,0:T(8,128)(2,1)}, bf16[256,256]{1,0:T(8,128)(2,1)S(1)}, u32[]{:S(2)}, u32[]{:S(2)}) collective-permute-start(bf16[256,256]{1,0:T(8,128)(2,1)} %get-tuple-element.23), channel_id=1, source_target_pairs={{0,16},{2,18},{4,20},{6,22},{8,24},{10,26},{12,28},{14,30},{16,0},... | collective-permute-start | bytes 393224 | tf_op jit(solution)/shard_map/ppermute | solution.py:577
  9.2 2.6 %collective-permute-start.2 = (bf16[256,256]{1,0:T(8,128)(2,1)}, bf16[256,256]{1,0:T(8,128)(2,1)S(1)}, u32[]{:S(2)}, u32[]{:S(2)}) collective-permute-start(bf16[256,256]{1,0:T(8,128)(2,1)} %get-tuple-element.25), channel_id=1, source_target_pairs={{0,18},{2,16},{4,22},{6,20},{8,26},{10,24},{12,30},{14,28},{16,2},... | collective-permute-start | bytes 393224 | tf_op jit(solution)/shard_map/ppermute | solution.py:577
  12.3 1.8 %collective-permute-start.4 = (bf16[256,256]{1,0:T(8,128)(2,1)}, bf16[256,256]{1,0:T(8,128)(2,1)S(1)}, u32[]{:S(2)}, u32[]{:S(2)}) collective-permute-start(bf16[256,256]{1,0:T(8,128)(2,1)} %get-tuple-element.27), channel_id=1, source_target_pairs={{0,26},{2,24},{4,30},{6,28},{8,18},{10,16},{12,22},{14,20},{16,10}... | collective-permute-start | bytes 393224 | tf_op jit(solution)/shard_map/ppermute | solution.py:577
  14.1 9.4 %collective-permute-done.rest_0_ = bf16[256,256]{1,0:T(8,128)(2,1)S(1)} collective-permute-done((bf16[256,256]{1,0:T(8,128)(2,1)}, bf16[256,256]{1,0:T(8,128)(2,1)S(1)}, u32[]{:S(2)}, u32[]{:S(2)}) %collective-permute-start) | collective-permute-done | bytes 131104 | tf_op jit(solution)/shard_map/ppermute | solution.py:577
  23.6 1.9 %collective-permute-start.5 = (bf16[256,256]{1,0:T(8,128)(2,1)}, bf16[256,256]{1,0:T(8,128)(2,1)S(1)}, u32[]{:S(2)}, u32[]{:S(2)}) collective-permute-start(bf16[256,256]{1,0:T(8,128)(2,1)} %get-tuple-element.28), channel_id=1, source_target_pairs={{0,4},{2,6},{4,0},{6,2},{8,12},{10,14},{12,8},{14,10},{16,20},{18,... | collective-permute-start | bytes 393224 | tf_op jit(solution)/shard_map/ppermute | solution.py:577
  25.5 3.8 %collective-permute-start.6 = (bf16[256,256]{1,0:T(8,128)(2,1)}, bf16[256,256]{1,0:T(8,128)(2,1)S(1)}, u32[]{:S(2)}, u32[]{:S(2)}) collective-permute-start(bf16[256,256]{1,0:T(8,128)(2,1)} %get-tuple-element.29), channel_id=1, source_target_pairs={{0,20},{2,22},{4,16},{6,18},{8,28},{10,30},{12,24},{14,26},{16,4},... | collective-permute-start | bytes 393224 | tf_op jit(solution)/shard_map/ppermute | solution.py:577
  30.5 1.5 %collective-permute-start.7 = (bf16[256,256]{1,0:T(8,128)(2,1)}, bf16[256,256]{1,0:T(8,128)(2,1)S(1)}, u32[]{:S(2)}, u32[]{:S(2)}) collective-permute-start(bf16[256,256]{1,0:T(8,128)(2,1)} %get-tuple-element.30), channel_id=1, source_target_pairs={{0,6},{2,4},{4,2},{6,0},{8,14},{10,12},{12,10},{14,8},{16,22},{18,... | collective-permute-start | bytes 393224 | tf_op jit(solution)/shard_map/ppermute | solution.py:577
  32.0 2.4 %collective-permute-start.8 = (bf16[256,256]{1,0:T(8,128)(2,1)}, bf16[256,256]{1,0:T(8,128)(2,1)S(1)}, u32[]{:S(2)}, u32[]{:S(2)}) collective-permute-start(bf16[256,256]{1,0:T(8,128)(2,1)} %get-tuple-element.31), channel_id=1, source_target_pairs={{0,28},{2,30},{4,24},{6,26},{8,20},{10,22},{12,16},{14,18},{16,12}... | collective-permute-start | bytes 393224 | tf_op jit(solution)/shard_map/ppermute | solution.py:577
  34.4 2.3 %collective-permute-start.9 = (bf16[256,256]{1,0:T(8,128)(2,1)}, bf16[256,256]{1,0:T(8,128)(2,1)S(1)}, u32[]{:S(2)}, u32[]{:S(2)}) collective-permute-start(bf16[256,256]{1,0:T(8,128)(2,1)} %get-tuple-element.32), channel_id=1, source_target_pairs={{0,8},{2,10},{4,12},{6,14},{8,0},{10,2},{12,4},{14,6},{16,24},{18,... | collective-permute-start | bytes 393224 | tf_op jit(solution)/shard_map/ppermute | solution.py:577
  36.7 1.9 %collective-permute-start.10 = (bf16[256,256]{1,0:T(8,128)(2,1)}, bf16[256,256]{1,0:T(8,128)(2,1)S(1)}, u32[]{:S(2)}, u32[]{:S(2)}) collective-permute-start(bf16[256,256]{1,0:T(8,128)(2,1)} %get-tuple-element.33), channel_id=1, source_target_pairs={{0,22},{2,20},{4,18},{6,16},{8,30},{10,28},{12,26},{14,24},{16,6},... | collective-permute-start | bytes 393224 | tf_op jit(solution)/shard_map/ppermute | solution.py:577
  38.6 3.8 %collective-permute-done.6.rest_6_ = bf16[256,256]{1,0:T(8,128)(2,1)S(1)} collective-permute-done((bf16[256,256]{1,0:T(8,128)(2,1)}, bf16[256,256]{1,0:T(8,128)(2,1)S(1)}, u32[]{:S(2)}, u32[]{:S(2)}) %collective-permute-start.6) | collective-permute-done | bytes 131104 | tf_op jit(solution)/shard_map/ppermute | solution.py:577
  42.9 3.9 %collective-permute-start.12 = (bf16[256,256]{1,0:T(8,128)(2,1)}, bf16[256,256]{1,0:T(8,128)(2,1)S(1)}, u32[]{:S(2)}, u32[]{:S(2)}) collective-permute-start(bf16[256,256]{1,0:T(8,128)(2,1)} %get-tuple-element.35), channel_id=1, source_target_pairs={{0,30},{2,28},{4,26},{6,24},{8,22},{10,20},{12,18},{14,16},{16,14}... | collective-permute-start | bytes 393224 | tf_op jit(solution)/shard_map/ppermute | solution.py:577
  46.8 2.6 %collective-permute-start.13 = (bf16[256,256]{1,0:T(8,128)(2,1)}, bf16[256,256]{1,0:T(8,128)(2,1)S(1)}, u32[]{:S(2)}, u32[]{:S(2)}) collective-permute-start(bf16[256,256]{1,0:T(8,128)(2,1)} %get-tuple-element.36), channel_id=1, source_target_pairs={{0,12},{2,14},{4,8},{6,10},{8,4},{10,6},{12,0},{14,2},{16,28},{18,... | collective-permute-start | bytes 393224 | tf_op jit(solution)/shard_map/ppermute | solution.py:577
  49.4 3.0 %collective-permute-start.14 = (bf16[256,256]{1,0:T(8,128)(2,1)}, bf16[256,256]{1,0:T(8,128)(2,1)S(1)}, u32[]{:S(2)}, u32[]{:S(2)}) collective-permute-start(bf16[256,256]{1,0:T(8,128)(2,1)} %get-tuple-element.37), channel_id=1, source_target_pairs={{0,14},{2,12},{4,10},{6,8},{8,6},{10,4},{12,2},{14,0},{16,30},{18,... | collective-permute-start | bytes 393224 | tf_op jit(solution)/shard_map/ppermute | solution.py:577
  52.5 2.3 %collective-permute-done.10.rest_10_ = bf16[256,256]{1,0:T(8,128)(2,1)S(1)} collective-permute-done((bf16[256,256]{1,0:T(8,128)(2,1)}, bf16[256,256]{1,0:T(8,128)(2,1)S(1)}, u32[]{:S(2)}, u32[]{:S(2)}) %collective-permute-start.10) | collective-permute-done | bytes 131104 | tf_op jit(solution)/shard_map/ppermute | solution.py:577
  54.8 2.4 %collective-permute-done.13.rest_13_ = bf16[256,256]{1,0:T(8,128)(2,1)S(1)} collective-permute-done((bf16[256,256]{1,0:T(8,128)(2,1)}, bf16[256,256]{1,0:T(8,128)(2,1)S(1)}, u32[]{:S(2)}, u32[]{:S(2)}) %collective-permute-start.13) | collective-permute-done | bytes 131104 | tf_op jit(solution)/shard_map/ppermute | solution.py:577
  57.2 3.3 %collective-permute-done.14.rest_14_ = bf16[256,256]{1,0:T(8,128)(2,1)S(1)} collective-permute-done((bf16[256,256]{1,0:T(8,128)(2,1)}, bf16[256,256]{1,0:T(8,128)(2,1)S(1)}, u32[]{:S(2)}, u32[]{:S(2)}) %collective-permute-start.14) | collective-permute-done | bytes 131104 | tf_op jit(solution)/shard_map/ppermute | solution.py:577
  61.4 10.5 %long_convolution.1 = bf16[16,256,128]{2,1,0:T(8,128)(2,1)} custom-call(s32[1]{0:T(128)} %bitcast.1.me_ref, bf16[256,256]{1,0:T(8,128)(2,1)S(1)} %collective-permute-done.rest_0_, bf16[256,256]{1,0:T(8,128)(2,1)S(1)} %collective-permute-done.1.rest_1_, bf16[256,256]{1,0:T(8,128)(2,1)S(1)} %collective-permute-done.2.rest_2_, ...), custom_call_target="tpu_custom_call" | custom-call | flops 5000000000 | bytes 9000000 | tf_op jit(solution)/shard_map/long_convolution/pallas_call | solution.py:433
  71.9 6.2 %all-to-all-start = ((bf16[16,256,128]{2,1,0:T(8,128)(2,1)}), bf16[16,256,128]{2,1,0:T(8,128)(2,1)S(1)}, u32[]{:S(2)}, u32[]{:S(2)}) async-start(bf16[16,256,128]{2,1,0:T(8,128)(2,1)} %long_convolution.1), calls=%async_computation | async-start | bytes 2097152 | tf_op jit(solution)/shard_map/all_to_all | solution.py:571
  78.1 24.6 %all-to-all-done.conv_ref = bf16[16,256,128]{2,1,0:T(8,128)(2,1)S(1)} async-done(((bf16[16,256,128]{2,1,0:T(8,128)(2,1)}), bf16[16,256,128]{2,1,0:T(8,128)(2,1)S(1)}, u32[]{:S(2)}, u32[]{:S(2)}) %all-to-all-start) | async-done | bytes 1048608 | tf_op jit(solution)/shard_map/all_to_all | solution.py:571
  102.7 4.1 %gate_project_sent.1 = (bf16[256,2048]{1,0:T(8,128)(2,1)S(1)}, f32[256,1024]{1,0:T(8,128)S(1)}) custom-call(s32[1]{0:T(128)} %bitcast.half_ref, bf16[256,256]{1,0:T(8,128)(2,1)S(1)} %copy-done.1, bf16[16,256,128]{2,1,0:T(8,128)(2,1)S(1)} %all-to-all-done.conv_ref, bf16[256,2048]{1,0:T(8,128)(2,1)S(1)} %copy-done, bf16[256,2048]{1,0:T(8,128)(2,1)} %values_hbm.3, ...), custom_call_target="tpu_custom_call" | custom-call | flops 1073741824 | bytes 4194304 | tf_op jit(solution)/shard_map/gate_project_sent/pallas_call | solution.py:496
  106.9 3.5 %project_kept.1.kept_ref = f32[256,1024]{1,0:T(8,128)S(1)} custom-call(s32[1]{0:T(128)} %bitcast.half_ref, bf16[256,2048]{1,0:T(8,128)(2,1)S(1)} %get-tuple-element.39.gated_ref, bf16[2048,2048]{1,0:T(8,128)(2,1)} %weight_hbm.3), custom_call_target="tpu_custom_call" | custom-call | flops 1073741824 | bytes 4194304 | tf_op jit(solution)/shard_map/project_kept/pallas_call | solution.py:538
  110.4 1.7 %join_halves.1 = bf16[1024,256]{1,0:T(8,128)(2,1)} custom-call(f32[256,1024]{1,0:T(8,128)S(1)} %project_kept.1.kept_ref, f32[256,1024]{1,0:T(8,128)S(1)} %collective-permute-done.15.came_ref), custom_call_target="tpu_custom_call" | custom-call | tf_op jit(solution)/shard_map/join_halves/pallas_call | solution.py:559
  (23 shorter events, 4.6 us)
Async XLA Ops:
  3.7 19.9 %collective-permute-start = (bf16[256,256]{1,0:T(8,128)(2,1)}, bf16[256,256]{1,0:T(8,128)(2,1)S(1)}, u32[]{:S(2)}, u32[]{:S(2)}) collective-permute-start(bf16[256,256]{1,0:T(8,128)(2,1)} %get-tuple-element.23), channel_id=1, source_target_pairs={{0,16},{2,18},{4,20},{6,22},{8,24},{10,26},{12,28},{14,30},{16,0},... | collective-permute-start | bytes 393224 | tf_op jit(solution)/shard_map/ppermute | solution.py:577
  7.8 17.6 %collective-permute-start.1 = (bf16[256,256]{1,0:T(8,128)(2,1)}, bf16[256,256]{1,0:T(8,128)(2,1)S(1)}, u32[]{:S(2)}, u32[]{:S(2)}) collective-permute-start(bf16[256,256]{1,0:T(8,128)(2,1)} %get-tuple-element.24), channel_id=1, source_target_pairs={{0,24},{2,26},{4,28},{6,30},{8,16},{10,18},{12,20},{14,22},{16,8},... | collective-permute-start | bytes 393224 | tf_op jit(solution)/shard_map/ppermute | solution.py:577
  9.2 21.3 %collective-permute-start.2 = (bf16[256,256]{1,0:T(8,128)(2,1)}, bf16[256,256]{1,0:T(8,128)(2,1)S(1)}, u32[]{:S(2)}, u32[]{:S(2)}) collective-permute-start(bf16[256,256]{1,0:T(8,128)(2,1)} %get-tuple-element.25), channel_id=1, source_target_pairs={{0,18},{2,16},{4,22},{6,20},{8,26},{10,24},{12,30},{14,28},{16,2},... | collective-permute-start | bytes 393224 | tf_op jit(solution)/shard_map/ppermute | solution.py:577
  11.8 20.2 %collective-permute-start.3 = (bf16[256,256]{1,0:T(8,128)(2,1)}, bf16[256,256]{1,0:T(8,128)(2,1)S(1)}, u32[]{:S(2)}, u32[]{:S(2)}) collective-permute-start(bf16[256,256]{1,0:T(8,128)(2,1)} %get-tuple-element.26), channel_id=1, source_target_pairs={{0,2},{2,0},{4,6},{6,4},{8,10},{10,8},{12,14},{14,12},{16,18},{18,... | collective-permute-start | bytes 393224 | tf_op jit(solution)/shard_map/ppermute | solution.py:577
  12.3 22.1 %collective-permute-start.4 = (bf16[256,256]{1,0:T(8,128)(2,1)}, bf16[256,256]{1,0:T(8,128)(2,1)S(1)}, u32[]{:S(2)}, u32[]{:S(2)}) collective-permute-start(bf16[256,256]{1,0:T(8,128)(2,1)} %get-tuple-element.27), channel_id=1, source_target_pairs={{0,26},{2,24},{4,30},{6,28},{8,18},{10,16},{12,22},{14,20},{16,10}... | collective-permute-start | bytes 393224 | tf_op jit(solution)/shard_map/ppermute | solution.py:577
  23.6 13.1 %collective-permute-start.5 = (bf16[256,256]{1,0:T(8,128)(2,1)}, bf16[256,256]{1,0:T(8,128)(2,1)S(1)}, u32[]{:S(2)}, u32[]{:S(2)}) collective-permute-start(bf16[256,256]{1,0:T(8,128)(2,1)} %get-tuple-element.28), channel_id=1, source_target_pairs={{0,4},{2,6},{4,0},{6,2},{8,12},{10,14},{12,8},{14,10},{16,20},{18,... | collective-permute-start | bytes 393224 | tf_op jit(solution)/shard_map/ppermute | solution.py:577
  25.5 16.9 %collective-permute-start.6 = (bf16[256,256]{1,0:T(8,128)(2,1)}, bf16[256,256]{1,0:T(8,128)(2,1)S(1)}, u32[]{:S(2)}, u32[]{:S(2)}) collective-permute-start(bf16[256,256]{1,0:T(8,128)(2,1)} %get-tuple-element.29), channel_id=1, source_target_pairs={{0,20},{2,22},{4,16},{6,18},{8,28},{10,30},{12,24},{14,26},{16,4},... | collective-permute-start | bytes 393224 | tf_op jit(solution)/shard_map/ppermute | solution.py:577
  30.5 12.4 %collective-permute-start.7 = (bf16[256,256]{1,0:T(8,128)(2,1)}, bf16[256,256]{1,0:T(8,128)(2,1)S(1)}, u32[]{:S(2)}, u32[]{:S(2)}) collective-permute-start(bf16[256,256]{1,0:T(8,128)(2,1)} %get-tuple-element.30), channel_id=1, source_target_pairs={{0,6},{2,4},{4,2},{6,0},{8,14},{10,12},{12,10},{14,8},{16,22},{18,... | collective-permute-start | bytes 393224 | tf_op jit(solution)/shard_map/ppermute | solution.py:577
  32.0 14.8 %collective-permute-start.8 = (bf16[256,256]{1,0:T(8,128)(2,1)}, bf16[256,256]{1,0:T(8,128)(2,1)S(1)}, u32[]{:S(2)}, u32[]{:S(2)}) collective-permute-start(bf16[256,256]{1,0:T(8,128)(2,1)} %get-tuple-element.31), channel_id=1, source_target_pairs={{0,28},{2,30},{4,24},{6,26},{8,20},{10,22},{12,16},{14,18},{16,12}... | collective-permute-start | bytes 393224 | tf_op jit(solution)/shard_map/ppermute | solution.py:577
  34.4 15.0 %collective-permute-start.9 = (bf16[256,256]{1,0:T(8,128)(2,1)}, bf16[256,256]{1,0:T(8,128)(2,1)S(1)}, u32[]{:S(2)}, u32[]{:S(2)}) collective-permute-start(bf16[256,256]{1,0:T(8,128)(2,1)} %get-tuple-element.32), channel_id=1, source_target_pairs={{0,8},{2,10},{4,12},{6,14},{8,0},{10,2},{12,4},{14,6},{16,24},{18,... | collective-permute-start | bytes 393224 | tf_op jit(solution)/shard_map/ppermute | solution.py:577
  36.7 18.1 %collective-permute-start.10 = (bf16[256,256]{1,0:T(8,128)(2,1)}, bf16[256,256]{1,0:T(8,128)(2,1)S(1)}, u32[]{:S(2)}, u32[]{:S(2)}) collective-permute-start(bf16[256,256]{1,0:T(8,128)(2,1)} %get-tuple-element.33), channel_id=1, source_target_pairs={{0,22},{2,20},{4,18},{6,16},{8,30},{10,28},{12,26},{14,24},{16,6},... | collective-permute-start | bytes 393224 | tf_op jit(solution)/shard_map/ppermute | solution.py:577
  42.4 12.4 %collective-permute-start.11 = (bf16[256,256]{1,0:T(8,128)(2,1)}, bf16[256,256]{1,0:T(8,128)(2,1)S(1)}, u32[]{:S(2)}, u32[]{:S(2)}) collective-permute-start(bf16[256,256]{1,0:T(8,128)(2,1)} %get-tuple-element.34), channel_id=1, source_target_pairs={{0,10},{2,8},{4,14},{6,12},{8,2},{10,0},{12,6},{14,4},{16,26},{18,... | collective-permute-start | bytes 393224 | tf_op jit(solution)/shard_map/ppermute | solution.py:577
  42.9 11.9 %collective-permute-start.12 = (bf16[256,256]{1,0:T(8,128)(2,1)}, bf16[256,256]{1,0:T(8,128)(2,1)S(1)}, u32[]{:S(2)}, u32[]{:S(2)}) collective-permute-start(bf16[256,256]{1,0:T(8,128)(2,1)} %get-tuple-element.35), channel_id=1, source_target_pairs={{0,30},{2,28},{4,26},{6,24},{8,22},{10,20},{12,18},{14,16},{16,14}... | collective-permute-start | bytes 393224 | tf_op jit(solution)/shard_map/ppermute | solution.py:577
  46.8 10.4 %collective-permute-start.13 = (bf16[256,256]{1,0:T(8,128)(2,1)}, bf16[256,256]{1,0:T(8,128)(2,1)S(1)}, u32[]{:S(2)}, u32[]{:S(2)}) collective-permute-start(bf16[256,256]{1,0:T(8,128)(2,1)} %get-tuple-element.36), channel_id=1, source_target_pairs={{0,12},{2,14},{4,8},{6,10},{8,4},{10,6},{12,0},{14,2},{16,28},{18,... | collective-permute-start | bytes 393224 | tf_op jit(solution)/shard_map/ppermute | solution.py:577
  49.4 11.1 %collective-permute-start.14 = (bf16[256,256]{1,0:T(8,128)(2,1)}, bf16[256,256]{1,0:T(8,128)(2,1)S(1)}, u32[]{:S(2)}, u32[]{:S(2)}) collective-permute-start(bf16[256,256]{1,0:T(8,128)(2,1)} %get-tuple-element.37), channel_id=1, source_target_pairs={{0,14},{2,12},{4,10},{6,8},{8,6},{10,4},{12,2},{14,0},{16,30},{18,... | collective-permute-start | bytes 393224 | tf_op jit(solution)/shard_map/ppermute | solution.py:577
  60.5 0.9 copy-start.3
  61.4 41.3 %copy-start = (bf16[256,2048]{1,0:T(8,128)(2,1)S(1)}, bf16[256,2048]{1,0:T(8,128)(2,1)}, u32[]{:S(2)}) copy-start(bf16[256,2048]{1,0:T(8,128)(2,1)} %gates_hbm.1) | copy-start | bytes 3145732
  61.4 41.3 %copy-start.1 = (bf16[256,256]{1,0:T(8,128)(2,1)S(1)}, bf16[256,256]{1,0:T(8,128)(2,1)}, u32[]{:S(2)}) copy-start(bf16[256,256]{1,0:T(8,128)(2,1)} %constant.16.clone.order_hbm) | copy-start | bytes 393220
  61.4 41.3 %copy-start.2 = (f32[2048]{0:T(1024)S(1)}, f32[2048]{0:T(1024)}, u32[]{:S(2)}) copy-start(f32[2048]{0:T(1024)} %param.11) | copy-start | bytes 24580
  71.9 30.7 %all-to-all-start = ((bf16[16,256,128]{2,1,0:T(8,128)(2,1)}), bf16[16,256,128]{2,1,0:T(8,128)(2,1)S(1)}, u32[]{:S(2)}, u32[]{:S(2)}) async-start(bf16[16,256,128]{2,1,0:T(8,128)(2,1)} %long_convolution.1), calls=%async_computation | async-start | bytes 2097152 | tf_op jit(solution)/shard_map/all_to_all | solution.py:571
  106.8 3.6 %collective-permute-start.15 = (f32[256,1024]{1,0:T(8,128)S(1)}, f32[256,1024]{1,0:T(8,128)S(1)}, u32[]{:S(2)}, u32[]{:S(2)}) collective-permute-start(f32[256,1024]{1,0:T(8,128)S(1)} %get-tuple-element.40), channel_id=1, source_target_pairs={{0,1},{1,0},{2,3},{3,2},{4,5},{5,4},{6,7},{7,6},{8,9},{9,8},{10,11... | collective-permute-start | bytes 3145736 | tf_op jit(solution)/shard_map/ppermute | solution.py:588

commit v8 on v7

--- a/solution.py
+++ b/solution.py
@@ -15,9 +15,9 @@
 RADIX = 16
 LANES = 128
 Q_ORDER = [low + 4 * high for low in range(4) for high in range(4)]
-VMEM_BYTES = 60 * 1024 * 1024
-CONV_BYTES = 49 * 1024 * 1024
-TAIL_BYTES = 49 * 1024 * 1024
+ARRANGE_BYTES = 60 * 1024 * 1024
+CONV_BYTES = 50 * 1024 * 1024
+TAIL_BYTES = 16 * 1024 * 1024
 
 
 def angle_table(first, second, period):
@@ -132,15 +132,14 @@
     return np.concatenate(blocks, axis=0).astype(np.float32)
 
 
-@functools.lru_cache(maxsize=None)
-def row_order(rows):
+def row_order(rows, turned_over=False):
+    place = lax.broadcasted_iota(jnp.int32, (rows, rows), 1 if turned_over else 0)
+    source = lax.broadcasted_iota(jnp.int32, (rows, rows), 0 if turned_over else 1)
     chunk = rows // RADIX
-    order = np.zeros((rows, rows), np.float32)
-    for i, q in enumerate(Q_ORDER):
-        for odd in range(2):
-            for j in range(chunk // 2):
-                order[i * chunk + odd * (chunk // 2) + j, RADIX * (2 * j + odd) + q] = 1.0
-    return order.astype(ml_dtypes.bfloat16)
+    index, within = place // chunk, place % chunk
+    odd, j = within // (chunk // 2), within % (chunk // 2)
+    wanted = RADIX * (2 * j + odd) + index // 4 + 4 * (index % 4)
+    return jnp.where(source == wanted, 1.0, 0.0).astype(jnp.bfloat16)
 
 
 def turn(point, index, sign):
@@ -191,29 +190,27 @@
     half = blocks // 2
     across = [half + (i // 2 if i % 2 == 0 else half // 2 + i // 2) for i in range(half)]
     near = list(range(1, half)) + [0]
-    lead = 2
-    mixed = [slot for pair in zip(across[lead:], near) for slot in pair]
-    return across[:lead] + mixed + near[half - lead :]
-
-
-def arrange_kernel(pieces, blocks, me_ref, order_hbm, values_hbm, taps_hbm, *rest):
+    return [slot for pair in zip(across, near) for slot in pair]
+
+
+def arrange_kernel(pieces, blocks, me_ref, values_hbm, taps_hbm, *rest):
     outs = rest[:blocks]
-    order_ref, values_ref, taps_ref, packed, sems = rest[blocks:]
+    values_ref, taps_ref, packed, sems = rest[blocks:]
     piece = values_ref.shape[1] // pieces
-    loads = [pltpu.make_async_copy(order_hbm, order_ref, sems.at[2 * pieces])]
+    loads = []
     for part in range(pieces):
         lanes = pl.ds(part * piece, piece)
         loads.append(pltpu.make_async_copy(values_hbm.at[:, lanes], values_ref.at[:, lanes], sems.at[2 * part]))
         loads.append(pltpu.make_async_copy(taps_hbm.at[:, lanes], taps_ref.at[:, lanes], sems.at[2 * part + 1]))
     for load in loads:
         load.start()
-    loads[0].wait()
+    order = row_order(values_ref.shape[0])
     for part in range(pieces):
+        loads[2 * part].wait()
         loads[2 * part + 1].wait()
-        loads[2 * part + 2].wait()
         lanes = pl.ds(part * piece, piece)
         both = jnp.concatenate([values_ref[:, lanes], taps_ref[:, lanes]], axis=1)
-        moved = jnp.dot(order_ref[...], both, preferred_element_type=jnp.float32).astype(jnp.bfloat16)
+        moved = jnp.dot(order, both, preferred_element_type=jnp.float32).astype(jnp.bfloat16)
         for block in range(piece // LANES):
             for side in range(2):
                 start = side * piece + block * LANES
@@ -227,22 +224,21 @@
     pieces = 4
     return pl.pallas_call(
         functools.partial(arrange_kernel, pieces, blocks),
-        in_specs=[pl.BlockSpec(memory_space=pltpu.SMEM)] + [pl.BlockSpec(memory_space=pl.ANY)] * 3,
+        in_specs=[pl.BlockSpec(memory_space=pltpu.SMEM)] + [pl.BlockSpec(memory_space=pl.ANY)] * 2,
         out_specs=[pl.BlockSpec(memory_space=pltpu.VMEM)] * blocks,
         out_shape=[jax.ShapeDtypeStruct((rows, 2 * LANES), jnp.bfloat16)] * blocks,
         scratch_shapes=[
-            pltpu.VMEM((rows, rows), jnp.bfloat16),
             pltpu.VMEM((rows, wide), jnp.bfloat16),
             pltpu.VMEM((rows, wide), jnp.bfloat16),
             pltpu.VMEM((blocks, rows, 2 * LANES), jnp.bfloat16),
-            pltpu.SemaphoreType.DMA((2 * pieces + 1,)),
+            pltpu.SemaphoreType.DMA((2 * pieces,)),
         ],
-        compiler_params=pltpu.CompilerParams(vmem_limit_bytes=VMEM_BYTES),
+        compiler_params=pltpu.CompilerParams(vmem_limit_bytes=ARRANGE_BYTES),
         cost_estimate=pl.CostEstimate(
             flops=4 * rows * rows * wide, bytes_accessed=8 * rows * wide, transcendentals=0
         ),
         name="arrange_rows",
-    )(me, jnp.asarray(row_order(rows)), values, taps)
+    )(me, values, taps)
 
 
 def convolve_kernel(blocks, me_ref, *rest):
@@ -272,8 +268,11 @@
     load_fixed.start()
     for load in load_turns:
         load.start()
-    for slot, source in zip(slot_order(blocks), slots):
+    own = pltpu.make_async_copy(slots[-1], streams.at[me_ref[0]], sems.at[9])
+    own.start()
+    for slot, source in zip(slot_order(blocks)[:-1], slots[:-1]):
         streams[me_ref[0] ^ slot] = source[...]
+    own.wait()
     load_fixed.wait()
     width = inner // LANES
     for table in range(4):
@@ -433,8 +432,8 @@
     return pl.pallas_call(
         functools.partial(convolve_kernel, blocks),
         in_specs=[pl.BlockSpec(memory_space=pltpu.SMEM)]
-        + [pl.BlockSpec(memory_space=pltpu.VMEM)] * blocks
-        + [pl.BlockSpec(memory_space=pl.ANY)],
+        + [pl.BlockSpec(memory_space=pltpu.VMEM)] * (blocks - 1)
+        + [pl.BlockSpec(memory_space=pl.ANY)] * 2,
         out_specs=pl.BlockSpec(memory_space=pl.ANY),
         out_shape=jax.ShapeDtypeStruct((blocks, rows, LANES), jnp.bfloat16),
         scratch_shapes=[
@@ -449,7 +448,7 @@
             pltpu.VMEM((4, 2, inner, lanes), jnp.bfloat16),
             pltpu.VMEM((4, 2, inner, lanes), jnp.bfloat16),
             pltpu.VMEM((blocks, rows, LANES), jnp.bfloat16),
-            pltpu.SemaphoreType.DMA((9,)),
+            pltpu.SemaphoreType.DMA((10,)),
         ],
         compiler_params=pltpu.CompilerParams(vmem_limit_bytes=CONV_BYTES),
         cost_estimate=pl.CostEstimate(flops=5 * 10**9, bytes_accessed=9 * 10**6, transcendentals=0),
@@ -457,90 +456,53 @@
     )(me, *slots, jnp.asarray(tables))
 
 
-def gate_kernel(
-    group, half_ref, order_hbm, conv_ref, gates_hbm, values_hbm, skip_ref, weight_hbm, gated_ref, out_ref,
-    order_ref, gates_ref, values_ref, weight_ref, sems,
-):
-    blocks, _, lanes = conv_ref.shape
-    width, features = weight_ref.shape
-    columns = pl.ds(pl.multiple_of((1 - half_ref[0]) * features, features), features)
-    loads = [
-        pltpu.make_async_copy(order_hbm, order_ref, sems.at[0]),
-        pltpu.make_async_copy(gates_hbm, gates_ref, sems.at[1]),
-        pltpu.make_async_copy(values_hbm, values_ref, sems.at[2]),
-    ]
-    deep = width // 2
-    for part in range(2):
-        rows = pl.ds(part * deep, deep)
-        loads.append(pltpu.make_async_copy(weight_hbm.at[rows, columns], weight_ref.at[rows], sems.at[3 + part]))
-    for load in loads:
-        load.start()
-    for load in loads[:3]:
-        load.wait()
+def gate_kernel(group, half_ref, conv_ref, gates_ref, values_ref, skip_ref, weight_ref, gated_ref, out_ref):
+    blocks, rows, lanes = conv_ref.shape
+    features = out_ref.shape[1]
+    order = row_order(rows, True)
     for step in range(blocks // group):
         taken = pl.ds(step * group * lanes, group * lanes)
         conv = jnp.concatenate([conv_ref[step * group + part] for part in range(group)], axis=1)
-        conv = jnp.dot(order_ref[...], conv, preferred_element_type=jnp.float32)
+        conv = jnp.dot(order, conv, preferred_element_type=jnp.float32)
         direct = skip_ref[:, taken] * values_ref[:, taken].astype(jnp.float32)
         gated_ref[:, taken] = (gates_ref[:, taken].astype(jnp.float32) * (conv + direct)).astype(jnp.bfloat16)
-    loads[3].wait()
-    first = jnp.dot(gated_ref[:, :deep], weight_ref[:deep], preferred_element_type=jnp.float32)
-    loads[4].wait()
-    out_ref[...] = first + jnp.dot(gated_ref[:, deep:], weight_ref[deep:], preferred_element_type=jnp.float32)
+    columns = pl.ds(pl.multiple_of((1 - half_ref[0]) * features, features), features)
+    out_ref[...] = jnp.dot(gated_ref[...], weight_ref[:, columns], preferred_element_type=jnp.float32)
 
 
 def gate_and_project(half, conv, gates, values, skip_gain, weight):
     rows, width = gates.shape
     features = weight.shape[1] // 2
-    anywhere, inside = pl.BlockSpec(memory_space=pl.ANY), pl.BlockSpec(memory_space=pltpu.VMEM)
     return pl.pallas_call(
         functools.partial(gate_kernel, 4),
-        in_specs=[pl.BlockSpec(memory_space=pltpu.SMEM), anywhere, inside, anywhere, anywhere, inside, anywhere],
-        out_specs=[inside] * 2,
+        in_specs=[pl.BlockSpec(memory_space=pltpu.SMEM)] + [pl.BlockSpec(memory_space=pltpu.VMEM)] * 5,
+        out_specs=[pl.BlockSpec(memory_space=pltpu.VMEM)] * 2,
         out_shape=[
             jax.ShapeDtypeStruct((rows, width), jnp.bfloat16),
             jax.ShapeDtypeStruct((rows, features), jnp.float32),
-        ],
-        scratch_shapes=[
-            pltpu.VMEM((rows, rows), jnp.bfloat16),
-            pltpu.VMEM((rows, width), jnp.bfloat16),
-            pltpu.VMEM((rows, width), jnp.bfloat16),
-            pltpu.VMEM((width, features), jnp.bfloat16),
-            pltpu.SemaphoreType.DMA((5,)),
         ],
         compiler_params=pltpu.CompilerParams(vmem_limit_bytes=TAIL_BYTES),
         cost_estimate=pl.CostEstimate(
             flops=2 * rows * width * features, bytes_accessed=2 * width * features, transcendentals=0
         ),
         name="gate_project_sent",
-    )(half, jnp.asarray(row_order(rows).T), conv, gates, values, skip_gain[None, :], weight)
-
-
-def kept_kernel(half_ref, gated_ref, weight_hbm, out_ref, weight_ref, sems):
-    width, features = weight_ref.shape
+    )(half, conv, gates, values, skip_gain[None, :], weight)
+
+
+def kept_kernel(half_ref, gated_ref, weight_ref, out_ref):
+    features = out_ref.shape[1]
     columns = pl.ds(pl.multiple_of(half_ref[0] * features, features), features)
-    deep = width // 2
-    loads = []
-    for part in range(2):
-        rows = pl.ds(part * deep, deep)
-        loads.append(pltpu.make_async_copy(weight_hbm.at[rows, columns], weight_ref.at[rows], sems.at[part]))
-        loads[part].start()
-    loads[0].wait()
-    first = jnp.dot(gated_ref[:, :deep], weight_ref[:deep], preferred_element_type=jnp.float32)
-    loads[1].wait()
-    out_ref[...] = first + jnp.dot(gated_ref[:, deep:], weight_ref[deep:], preferred_element_type=jnp.float32)
+    out_ref[...] = jnp.dot(gated_ref[...], weight_ref[:, columns], preferred_element_type=jnp.float32)
 
 
 def project_kept(half, gated, weight):
     rows, width = gated.shape
     features = weight.shape[1] // 2
-    anywhere, inside = pl.BlockSpec(memory_space=pl.ANY), pl.BlockSpec(memory_space=pltpu.VMEM)
     return pl.pallas_call(
         kept_kernel,
-        in_specs=[pl.BlockSpec(memory_space=pltpu.SMEM), inside, anywhere],
-        out_specs=inside,
+        in_specs=[pl.BlockSpec(memory_space=pltpu.SMEM)] + [pl.BlockSpec(memory_space=pltpu.VMEM)] * 2,
+        out_specs=pl.BlockSpec(memory_space=pltpu.VMEM),
         out_shape=jax.ShapeDtypeStruct((rows, features), jnp.float32),
-        scratch_shapes=[pltpu.VMEM((width, features), jnp.bfloat16), pltpu.SemaphoreType.DMA((2,))],
         compiler_params=pltpu.CompilerParams(vmem_limit_bytes=TAIL_BYTES),
         cost_estimate=pl.CostEstimate(
             flops=2 * rows * width * features, bytes_accessed=2 * width * features, transcendentals=0

time: 113 us -> 109 us (0.965)
  local copies, waits for them, and re-layouts: 0.92 us -> 8.68 us
  starting transfers between devices: 40.5 us -> 34.6 us
  Pallas kernels: 23.6 us -> 18.2 us
    unnamed x8 -> x14, local copies, waits for them, and re-layouts: 0.92 us -> 8.68 us
    ppermute x15, starting transfers between devices: 34.3 us -> 28.2 us  [exchange(): lax.ppermute(source, 'seq', [(j, j ^ slot) for j in range(blocks)])]
    pallas_call x1, Pallas kernels: 4.09 us -> 1.69 us  [gate_and_project(): pl.pallas_call(functools.partial(gate_kernel, 4), in_specs=[pl.BlockSpec(...]
    pallas_call x1, Pallas kernels: 3.5 us -> 1.25 us  [project_kept(): pl.pallas_call(kept_kernel, in_specs=[pl.BlockSpec(memory_space=pltpu.SME...]
  transfers between devices with their start and end apart: 17 -> 17, of which waited for: 7 -> 9; matrix products, arithmetic and copies ran while one was open for 0% -> 0% of each run, Pallas kernels for 3% -> 1%
where the time goes in v8:
time: 109 us; the launch traced here: 108 us
  waiting for transfers between devices  46.6 us (43%)
  starting transfers between devices  34.6 us (32%)
  Pallas kernels  18.2 us (17%)
  local copies, waits for them, and re-layouts  8.68 us (8%)
    ppermute x15, starting transfers between devices, exchange(): lax.ppermute(source, 'seq', [(j, j ^ slot) for j in range(blocks)])  28.2 us
    all_to_all x1, waiting for transfers between devices, swap_blocks(): return lax.all_to_all(array, 'seq', split_axis=0, concat_axis=0, tiled=True)  24.6 us
    ppermute x15, waiting for transfers between devices, exchange(): lax.ppermute(source, 'seq', [(j, j ^ slot) for j in range(blocks)])  22 us
    pallas_call x1, Pallas kernels, convolve(): pl.pallas_call(functools.partial(convolve_kernel, blocks), in_specs=[pl.B...  9.92 us
    unnamed x14, local copies, waits for them, and re-layouts  8.68 us
    all_to_all x1, starting transfers between devices, swap_blocks(): return lax.all_to_all(array, 'seq', split_axis=0, concat_axis=0, tiled=True)  6.34 us
    pallas_call x1, Pallas kernels, arrange(): pl.pallas_call(functools.partial(arrange_kernel, pieces, blocks), in_spec...  3.63 us
  transfers between devices with their start and end apart: 17, of which 9 were waited for; matrix products, arithmetic and copies ran while one was open for 0% of the time, Pallas kernels for 1%

profile of v8, /device:TPU:0, one launch (start us, length us, event | category | flops | bytes accessed | tf_op | source)
XLA Modules:
  0.0 108.2 jit_solution(13483013123269024680)
XLA Ops:
  0.0 3.6 %arrange_rows.1 = (bf16[256,256]{1,0:T(8,128)(2,1)}, bf16[256,256]{1,0:T(8,128)(2,1)}, bf16[256,256]{1,0:T(8,128)(2,1)}, bf16[256,256]{1,0:T(8,128)(2,1)}, bf16[...) custom-call(s32[1]{0:T(128)} %bitcast.1.me_ref, ...), custom_call_target="tpu_custom_call" | custom-call | flops 536870912 | bytes 4194304 | tf_op jit(solution)/shard_map/arrange_rows/pallas_call | solution.py:225
  3.6 4.1 %collective-permute-start = (bf16[256,256]{1,0:T(8,128)(2,1)}, bf16[256,256]{1,0:T(8,128)(2,1)S(1)}, u32[]{:S(2)}, u32[]{:S(2)}) collective-permute-start(bf16[256,256]{1,0:T(8,128)(2,1)} %get-tuple-element.23), channel_id=1, source_target_pairs={{0,16},{2,18},{4,20},{6,22},{8,24},{10,26},{12,28},{14,30},{16,0},... | collective-permute-start | bytes 393224 | tf_op jit(solution)/shard_map/ppermute | solution.py:539
  7.7 1.5 %collective-permute-start.1 = (bf16[256,256]{1,0:T(8,128)(2,1)}, bf16[256,256]{1,0:T(8,128)(2,1)S(1)}, u32[]{:S(2)}, u32[]{:S(2)}) collective-permute-start(bf16[256,256]{1,0:T(8,128)(2,1)} %get-tuple-element.24), channel_id=1, source_target_pairs={{0,2},{2,0},{4,6},{6,4},{8,10},{10,8},{12,14},{14,12},{16,18},{18,... | collective-permute-start | bytes 393224 | tf_op jit(solution)/shard_map/ppermute | solution.py:539
  9.2 1.3 %collective-permute-start.2 = (bf16[256,256]{1,0:T(8,128)(2,1)}, bf16[256,256]{1,0:T(8,128)(2,1)S(1)}, u32[]{:S(2)}, u32[]{:S(2)}) collective-permute-start(bf16[256,256]{1,0:T(8,128)(2,1)} %get-tuple-element.25), channel_id=1, source_target_pairs={{0,24},{2,26},{4,28},{6,30},{8,16},{10,18},{12,20},{14,22},{16,8},... | collective-permute-start | bytes 393224 | tf_op jit(solution)/shard_map/ppermute | solution.py:539
  10.6 1.5 %collective-permute-start.3 = (bf16[256,256]{1,0:T(8,128)(2,1)}, bf16[256,256]{1,0:T(8,128)(2,1)S(1)}, u32[]{:S(2)}, u32[]{:S(2)}) collective-permute-start(bf16[256,256]{1,0:T(8,128)(2,1)} %get-tuple-element.26), channel_id=1, source_target_pairs={{0,4},{2,6},{4,0},{6,2},{8,12},{10,14},{12,8},{14,10},{16,20},{18,... | collective-permute-start | bytes 393224 | tf_op jit(solution)/shard_map/ppermute | solution.py:539
  12.1 1.7 %collective-permute-start.4 = (bf16[256,256]{1,0:T(8,128)(2,1)}, bf16[256,256]{1,0:T(8,128)(2,1)S(1)}, u32[]{:S(2)}, u32[]{:S(2)}) collective-permute-start(bf16[256,256]{1,0:T(8,128)(2,1)} %get-tuple-element.27), channel_id=1, source_target_pairs={{0,18},{2,16},{4,22},{6,20},{8,26},{10,24},{12,30},{14,28},{16,2},... | collective-permute-start | bytes 393224 | tf_op jit(solution)/shard_map/ppermute | solution.py:539
  13.8 6.9 %collective-permute-done.rest_0_ = bf16[256,256]{1,0:T(8,128)(2,1)S(1)} collective-permute-done((bf16[256,256]{1,0:T(8,128)(2,1)}, bf16[256,256]{1,0:T(8,128)(2,1)S(1)}, u32[]{:S(2)}, u32[]{:S(2)}) %collective-permute-start) | collective-permute-done | bytes 131104 | tf_op jit(solution)/shard_map/ppermute | solution.py:539
  20.7 2.8 %collective-permute-start.5 = (bf16[256,256]{1,0:T(8,128)(2,1)}, bf16[256,256]{1,0:T(8,128)(2,1)S(1)}, u32[]{:S(2)}, u32[]{:S(2)}) collective-permute-start(bf16[256,256]{1,0:T(8,128)(2,1)} %get-tuple-element.28), channel_id=1, source_target_pairs={{0,6},{2,4},{4,2},{6,0},{8,14},{10,12},{12,10},{14,8},{16,22},{18,... | collective-permute-start | bytes 393224 | tf_op jit(solution)/shard_map/ppermute | solution.py:539
  23.5 2.4 %collective-permute-start.6 = (bf16[256,256]{1,0:T(8,128)(2,1)}, bf16[256,256]{1,0:T(8,128)(2,1)S(1)}, u32[]{:S(2)}, u32[]{:S(2)}) collective-permute-start(bf16[256,256]{1,0:T(8,128)(2,1)} %get-tuple-element.29), channel_id=1, source_target_pairs={{0,26},{2,24},{4,30},{6,28},{8,18},{10,16},{12,22},{14,20},{16,10}... | collective-permute-start | bytes 393224 | tf_op jit(solution)/shard_map/ppermute | solution.py:539
  25.9 1.5 %collective-permute-start.8 = (bf16[256,256]{1,0:T(8,128)(2,1)}, bf16[256,256]{1,0:T(8,128)(2,1)S(1)}, u32[]{:S(2)}, u32[]{:S(2)}) collective-permute-start(bf16[256,256]{1,0:T(8,128)(2,1)} %get-tuple-element.31), channel_id=1, source_target_pairs={{0,20},{2,22},{4,16},{6,18},{8,28},{10,30},{12,24},{14,26},{16,4},... | collective-permute-start | bytes 393224 | tf_op jit(solution)/shard_map/ppermute | solution.py:539
  30.1 7.2 %collective-permute-start.10 = (bf16[256,256]{1,0:T(8,128)(2,1)}, bf16[256,256]{1,0:T(8,128)(2,1)S(1)}, u32[]{:S(2)}, u32[]{:S(2)}) collective-permute-start(bf16[256,256]{1,0:T(8,128)(2,1)} %get-tuple-element.33), channel_id=1, source_target_pairs={{0,28},{2,30},{4,24},{6,26},{8,20},{10,22},{12,16},{14,18},{16,12}... | collective-permute-start | bytes 393224 | tf_op jit(solution)/shard_map/ppermute | solution.py:539
  38.0 3.3 %collective-permute-done.8.rest_8_ = bf16[256,256]{1,0:T(8,128)(2,1)S(1)} collective-permute-done((bf16[256,256]{1,0:T(8,128)(2,1)}, bf16[256,256]{1,0:T(8,128)(2,1)S(1)}, u32[]{:S(2)}, u32[]{:S(2)}) %collective-permute-start.8) | collective-permute-done | bytes 131104 | tf_op jit(solution)/shard_map/ppermute | solution.py:539
  41.9 2.3 %collective-permute-start.14 = (bf16[256,256]{1,0:T(8,128)(2,1)}, bf16[256,256]{1,0:T(8,128)(2,1)S(1)}, u32[]{:S(2)}, u32[]{:S(2)}) collective-permute-start(bf16[256,256]{1,0:T(8,128)(2,1)} %get-tuple-element.37), channel_id=1, source_target_pairs={{0,30},{2,28},{4,26},{6,24},{8,22},{10,20},{12,18},{14,16},{16,14}... | collective-permute-start | bytes 393224 | tf_op jit(solution)/shard_map/ppermute | solution.py:539
  44.2 1.7 %collective-permute-done.11.rest_11_ = bf16[256,256]{1,0:T(8,128)(2,1)S(1)} collective-permute-done((bf16[256,256]{1,0:T(8,128)(2,1)}, bf16[256,256]{1,0:T(8,128)(2,1)S(1)}, u32[]{:S(2)}, u32[]{:S(2)}) %collective-permute-start.11) | collective-permute-done | bytes 131104 | tf_op jit(solution)/shard_map/ppermute | solution.py:539
  46.0 6.1 %collective-permute-done.12.rest_12_ = bf16[256,256]{1,0:T(8,128)(2,1)S(1)} collective-permute-done((bf16[256,256]{1,0:T(8,128)(2,1)}, bf16[256,256]{1,0:T(8,128)(2,1)S(1)}, u32[]{:S(2)}, u32[]{:S(2)}) %collective-permute-start.12) | collective-permute-done | bytes 131104 | tf_op jit(solution)/shard_map/ppermute | solution.py:539
  52.0 1.9 %collective-permute-done.14.rest_14_ = bf16[256,256]{1,0:T(8,128)(2,1)S(1)} collective-permute-done((bf16[256,256]{1,0:T(8,128)(2,1)}, bf16[256,256]{1,0:T(8,128)(2,1)S(1)}, u32[]{:S(2)}, u32[]{:S(2)}) %collective-permute-start.14) | collective-permute-done | bytes 131104 | tf_op jit(solution)/shard_map/ppermute | solution.py:539
  54.8 9.9 %long_convolution.1 = bf16[16,256,128]{2,1,0:T(8,128)(2,1)S(1)} custom-call(s32[1]{0:T(128)} %bitcast.1.me_ref, bf16[256,256]{1,0:T(8,128)(2,1)S(1)} %collective-permute-done.rest_0_, bf16[256,256]{1,0:T(8,128)(2,1)S(1)} %collective-permute-done.1.rest_1_, bf16[256,256]{1,0:T(8,128)(2,1)S(1)} %collective-permute-done.2.rest_2_, ...), custom_call_target="tpu_custom_call" | custom-call | flops 5000000000 | bytes 9000000 | tf_op jit(solution)/shard_map/long_convolution/pallas_call | solution.py:432
  65.7 6.3 %all-to-all-start = ((bf16[16,256,128]{2,1,0:T(8,128)(2,1)}), bf16[16,256,128]{2,1,0:T(8,128)(2,1)S(1)}, u32[]{:S(2)}, u32[]{:S(2)}) async-start(bf16[16,256,128]{2,1,0:T(8,128)(2,1)} %copy-done.4), calls=%async_computation | async-start | bytes 2097152 | tf_op jit(solution)/shard_map/all_to_all | solution.py:533
  72.1 24.6 %all-to-all-done.conv_ref = bf16[16,256,128]{2,1,0:T(8,128)(2,1)S(1)} async-done(((bf16[16,256,128]{2,1,0:T(8,128)(2,1)}), bf16[16,256,128]{2,1,0:T(8,128)(2,1)S(1)}, u32[]{:S(2)}, u32[]{:S(2)}) %all-to-all-start) | async-done | bytes 1048608 | tf_op jit(solution)/shard_map/all_to_all | solution.py:533
  96.7 3.4 %copy-done = bf16[2048,2048]{1,0:T(8,128)(2,1)S(1)} copy-done((bf16[2048,2048]{1,0:T(8,128)(2,1)S(1)}, bf16[2048,2048]{1,0:T(8,128)(2,1)}, u32[]{:S(2)}) %copy-start) | copy-done | bytes 8388632
  100.0 1.7 %gate_project_sent.1 = (bf16[256,2048]{1,0:T(8,128)(2,1)S(1)}, f32[256,1024]{1,0:T(8,128)S(1)}) custom-call(s32[1]{0:T(128)} %bitcast.half_ref, bf16[16,256,128]{2,1,0:T(8,128)(2,1)S(1)} %all-to-all-done.conv_ref, bf16[256,2048]{1,0:T(8,128)(2,1)S(1)} %copy-done.3, bf16[256,2048]{1,0:T(8,128)(2,1)S(1)} %copy-done.2, f32[1,2048]{1,0:T(1,128)S(1)} %bitcast.3, ...), custom_call_target="tpu_custom_call" | custom-call | flops 1073741824 | bytes 4194304 | tf_op jit(solution)/shard_map/gate_project_sent/pallas_call | solution.py:476
  101.8 3.4 %copy-done.1 = bf16[2048,2048]{1,0:T(8,128)(2,1)S(1)} copy-done((bf16[2048,2048]{1,0:T(8,128)(2,1)S(1)}, bf16[2048,2048]{1,0:T(8,128)(2,1)}, u32[]{:S(2)}) %copy-start.1) | copy-done | bytes 8388632
  105.2 1.2 %project_kept.1.kept_ref = f32[256,1024]{1,0:T(8,128)S(1)} custom-call(s32[1]{0:T(128)} %bitcast.half_ref, bf16[256,2048]{1,0:T(8,128)(2,1)S(1)} %get-tuple-element.39.gated_ref, bf16[2048,2048]{1,0:T(8,128)(2,1)S(1)} %copy-done.1), custom_call_target="tpu_custom_call" | custom-call | flops 1073741824 | bytes 4194304 | tf_op jit(solution)/shard_map/project_kept/pallas_call | solution.py:501
  106.5 1.7 %join_halves.1 = bf16[1024,256]{1,0:T(8,128)(2,1)} custom-call(f32[256,1024]{1,0:T(8,128)S(1)} %project_kept.1.kept_ref, f32[256,1024]{1,0:T(8,128)S(1)} %collective-permute-done.15.came_ref), custom_call_target="tpu_custom_call" | custom-call | tf_op jit(solution)/shard_map/join_halves/pallas_call | solution.py:521
  (29 shorter events, 5.8 us)
Async XLA Ops:
  3.6 17.1 %collective-permute-start = (bf16[256,256]{1,0:T(8,128)(2,1)}, bf16[256,256]{1,0:T(8,128)(2,1)S(1)}, u32[]{:S(2)}, u32[]{:S(2)}) collective-permute-start(bf16[256,256]{1,0:T(8,128)(2,1)} %get-tuple-element.23), channel_id=1, source_target_pairs={{0,16},{2,18},{4,20},{6,22},{8,24},{10,26},{12,28},{14,30},{16,0},... | collective-permute-start | bytes 393224 | tf_op jit(solution)/shard_map/ppermute | solution.py:539
  7.7 15.8 %collective-permute-start.1 = (bf16[256,256]{1,0:T(8,128)(2,1)}, bf16[256,256]{1,0:T(8,128)(2,1)S(1)}, u32[]{:S(2)}, u32[]{:S(2)}) collective-permute-start(bf16[256,256]{1,0:T(8,128)(2,1)} %get-tuple-element.24), channel_id=1, source_target_pairs={{0,2},{2,0},{4,6},{6,4},{8,10},{10,8},{12,14},{14,12},{16,18},{18,... | collective-permute-start | bytes 393224 | tf_op jit(solution)/shard_map/ppermute | solution.py:539
  9.2 16.7 %collective-permute-start.2 = (bf16[256,256]{1,0:T(8,128)(2,1)}, bf16[256,256]{1,0:T(8,128)(2,1)S(1)}, u32[]{:S(2)}, u32[]{:S(2)}) collective-permute-start(bf16[256,256]{1,0:T(8,128)(2,1)} %get-tuple-element.25), channel_id=1, source_target_pairs={{0,24},{2,26},{4,28},{6,30},{8,16},{10,18},{12,20},{14,22},{16,8},... | collective-permute-start | bytes 393224 | tf_op jit(solution)/shard_map/ppermute | solution.py:539
  10.6 15.4 %collective-permute-start.3 = (bf16[256,256]{1,0:T(8,128)(2,1)}, bf16[256,256]{1,0:T(8,128)(2,1)S(1)}, u32[]{:S(2)}, u32[]{:S(2)}) collective-permute-start(bf16[256,256]{1,0:T(8,128)(2,1)} %get-tuple-element.26), channel_id=1, source_target_pairs={{0,4},{2,6},{4,0},{6,2},{8,12},{10,14},{12,8},{14,10},{16,20},{18,... | collective-permute-start | bytes 393224 | tf_op jit(solution)/shard_map/ppermute | solution.py:539
  12.1 16.1 %collective-permute-start.4 = (bf16[256,256]{1,0:T(8,128)(2,1)}, bf16[256,256]{1,0:T(8,128)(2,1)S(1)}, u32[]{:S(2)}, u32[]{:S(2)}) collective-permute-start(bf16[256,256]{1,0:T(8,128)(2,1)} %get-tuple-element.27), channel_id=1, source_target_pairs={{0,18},{2,16},{4,22},{6,20},{8,26},{10,24},{12,30},{14,28},{16,2},... | collective-permute-start | bytes 393224 | tf_op jit(solution)/shard_map/ppermute | solution.py:539
  20.7 9.4 %collective-permute-start.5 = (bf16[256,256]{1,0:T(8,128)(2,1)}, bf16[256,256]{1,0:T(8,128)(2,1)S(1)}, u32[]{:S(2)}, u32[]{:S(2)}) collective-permute-start(bf16[256,256]{1,0:T(8,128)(2,1)} %get-tuple-element.28), channel_id=1, source_target_pairs={{0,6},{2,4},{4,2},{6,0},{8,14},{10,12},{12,10},{14,8},{16,22},{18,... | collective-permute-start | bytes 393224 | tf_op jit(solution)/shard_map/ppermute | solution.py:539
  23.5 13.9 %collective-permute-start.6 = (bf16[256,256]{1,0:T(8,128)(2,1)}, bf16[256,256]{1,0:T(8,128)(2,1)S(1)}, u32[]{:S(2)}, u32[]{:S(2)}) collective-permute-start(bf16[256,256]{1,0:T(8,128)(2,1)} %get-tuple-element.29), channel_id=1, source_target_pairs={{0,26},{2,24},{4,30},{6,28},{8,18},{10,16},{12,22},{14,20},{16,10}... | collective-permute-start | bytes 393224 | tf_op jit(solution)/shard_map/ppermute | solution.py:539
  25.9 11.4 %collective-permute-start.7 = (bf16[256,256]{1,0:T(8,128)(2,1)}, bf16[256,256]{1,0:T(8,128)(2,1)S(1)}, u32[]{:S(2)}, u32[]{:S(2)}) collective-permute-start(bf16[256,256]{1,0:T(8,128)(2,1)} %get-tuple-element.30), channel_id=1, source_target_pairs={{0,8},{2,10},{4,12},{6,14},{8,0},{10,2},{12,4},{14,6},{16,24},{18,... | collective-permute-start | bytes 393224 | tf_op jit(solution)/shard_map/ppermute | solution.py:539
  25.9 15.4 %collective-permute-start.8 = (bf16[256,256]{1,0:T(8,128)(2,1)}, bf16[256,256]{1,0:T(8,128)(2,1)S(1)}, u32[]{:S(2)}, u32[]{:S(2)}) collective-permute-start(bf16[256,256]{1,0:T(8,128)(2,1)} %get-tuple-element.31), channel_id=1, source_target_pairs={{0,20},{2,22},{4,16},{6,18},{8,28},{10,30},{12,24},{14,26},{16,4},... | collective-permute-start | bytes 393224 | tf_op jit(solution)/shard_map/ppermute | solution.py:539
  28.3 13.6 %collective-permute-start.9 = (bf16[256,256]{1,0:T(8,128)(2,1)}, bf16[256,256]{1,0:T(8,128)(2,1)S(1)}, u32[]{:S(2)}, u32[]{:S(2)}) collective-permute-start(bf16[256,256]{1,0:T(8,128)(2,1)} %get-tuple-element.32), channel_id=1, source_target_pairs={{0,10},{2,8},{4,14},{6,12},{8,2},{10,0},{12,6},{14,4},{16,26},{18,... | collective-permute-start | bytes 393224 | tf_op jit(solution)/shard_map/ppermute | solution.py:539
  30.1 14.1 %collective-permute-start.10 = (bf16[256,256]{1,0:T(8,128)(2,1)}, bf16[256,256]{1,0:T(8,128)(2,1)S(1)}, u32[]{:S(2)}, u32[]{:S(2)}) collective-permute-start(bf16[256,256]{1,0:T(8,128)(2,1)} %get-tuple-element.33), channel_id=1, source_target_pairs={{0,28},{2,30},{4,24},{6,26},{8,20},{10,22},{12,16},{14,18},{16,12}... | collective-permute-start | bytes 393224 | tf_op jit(solution)/shard_map/ppermute | solution.py:539
  37.4 8.6 %collective-permute-start.11 = (bf16[256,256]{1,0:T(8,128)(2,1)}, bf16[256,256]{1,0:T(8,128)(2,1)S(1)}, u32[]{:S(2)}, u32[]{:S(2)}) collective-permute-start(bf16[256,256]{1,0:T(8,128)(2,1)} %get-tuple-element.34), channel_id=1, source_target_pairs={{0,12},{2,14},{4,8},{6,10},{8,4},{10,6},{12,0},{14,2},{16,28},{18,... | collective-permute-start | bytes 393224 | tf_op jit(solution)/shard_map/ppermute | solution.py:539
  37.4 14.6 %collective-permute-start.12 = (bf16[256,256]{1,0:T(8,128)(2,1)}, bf16[256,256]{1,0:T(8,128)(2,1)S(1)}, u32[]{:S(2)}, u32[]{:S(2)}) collective-permute-start(bf16[256,256]{1,0:T(8,128)(2,1)} %get-tuple-element.35), channel_id=1, source_target_pairs={{0,22},{2,20},{4,18},{6,16},{8,30},{10,28},{12,26},{14,24},{16,6},... | collective-permute-start | bytes 393224 | tf_op jit(solution)/shard_map/ppermute | solution.py:539
  41.4 10.6 %collective-permute-start.13 = (bf16[256,256]{1,0:T(8,128)(2,1)}, bf16[256,256]{1,0:T(8,128)(2,1)S(1)}, u32[]{:S(2)}, u32[]{:S(2)}) collective-permute-start(bf16[256,256]{1,0:T(8,128)(2,1)} %get-tuple-element.36), channel_id=1, source_target_pairs={{0,14},{2,12},{4,10},{6,8},{8,6},{10,4},{12,2},{14,0},{16,30},{18,... | collective-permute-start | bytes 393224 | tf_op jit(solution)/shard_map/ppermute | solution.py:539
  41.9 12.0 %collective-permute-start.14 = (bf16[256,256]{1,0:T(8,128)(2,1)}, bf16[256,256]{1,0:T(8,128)(2,1)S(1)}, u32[]{:S(2)}, u32[]{:S(2)}) collective-permute-start(bf16[256,256]{1,0:T(8,128)(2,1)} %get-tuple-element.37), channel_id=1, source_target_pairs={{0,30},{2,28},{4,26},{6,24},{8,22},{10,20},{12,18},{14,16},{16,14}... | collective-permute-start | bytes 393224 | tf_op jit(solution)/shard_map/ppermute | solution.py:539
  53.9 0.9 copy-start.6
  54.8 41.9 %copy-start.2 = (bf16[256,2048]{1,0:T(8,128)(2,1)S(1)}, bf16[256,2048]{1,0:T(8,128)(2,1)}, u32[]{:S(2)}) copy-start(bf16[256,2048]{1,0:T(8,128)(2,1)} %values_ref.1) | copy-start | bytes 3145732
  54.8 41.9 %copy-start.3 = (bf16[256,2048]{1,0:T(8,128)(2,1)S(1)}, bf16[256,2048]{1,0:T(8,128)(2,1)}, u32[]{:S(2)}) copy-start(bf16[256,2048]{1,0:T(8,128)(2,1)} %gates_ref.1) | copy-start | bytes 3145732
  54.8 41.9 %copy-start.5 = (f32[2048]{0:T(1024)S(1)}, f32[2048]{0:T(1024)}, u32[]{:S(2)}) copy-start(f32[2048]{0:T(1024)} %param.9) | copy-start | bytes 24580
  64.7 1.0 copy-start.4
  65.7 30.9 %all-to-all-start = ((bf16[16,256,128]{2,1,0:T(8,128)(2,1)}), bf16[16,256,128]{2,1,0:T(8,128)(2,1)S(1)}, u32[]{:S(2)}, u32[]{:S(2)}) async-start(bf16[16,256,128]{2,1,0:T(8,128)(2,1)} %copy-done.4), calls=%async_computation | async-start | bytes 2097152 | tf_op jit(solution)/shard_map/all_to_all | solution.py:533
  96.7 3.4 %copy-start = (bf16[2048,2048]{1,0:T(8,128)(2,1)S(1)}, bf16[2048,2048]{1,0:T(8,128)(2,1)}, u32[]{:S(2)}) copy-start(bf16[2048,2048]{1,0:T(8,128)(2,1)} %weight_ref.3) | copy-start | bytes 25165828
  101.7 4.7 %collective-permute-start.15 = (f32[256,1024]{1,0:T(8,128)S(1)}, f32[256,1024]{1,0:T(8,128)S(1)}, u32[]{:S(2)}, u32[]{:S(2)}) collective-permute-start(f32[256,1024]{1,0:T(8,128)S(1)} %get-tuple-element.40), channel_id=1, source_target_pairs={{0,1},{1,0},{2,3},{3,2},{4,5},{5,4},{6,7},{7,6},{8,9},{9,8},{10,11... | collective-permute-start | bytes 3145736 | tf_op jit(solution)/shard_map/ppermute | solution.py:550
  101.8 3.4 %copy-start.1 = (bf16[2048,2048]{1,0:T(8,128)(2,1)S(1)}, bf16[2048,2048]{1,0:T(8,128)(2,1)}, u32[]{:S(2)}) copy-start(bf16[2048,2048]{1,0:T(8,128)(2,1)} %weight_ref.3) | copy-start | bytes 25165828

commit v9 on v8

--- a/solution.py
+++ b/solution.py
@@ -16,8 +16,8 @@
 LANES = 128
 Q_ORDER = [low + 4 * high for low in range(4) for high in range(4)]
 ARRANGE_BYTES = 60 * 1024 * 1024
-CONV_BYTES = 50 * 1024 * 1024
-TAIL_BYTES = 16 * 1024 * 1024
+CONV_BYTES = 49 * 1024 * 1024
+TAIL_BYTES = 49 * 1024 * 1024
 
 
 def angle_table(first, second, period):
@@ -456,30 +456,73 @@
     )(me, *slots, jnp.asarray(tables))
 
 
-def gate_kernel(group, half_ref, conv_ref, gates_ref, values_ref, skip_ref, weight_ref, gated_ref, out_ref):
+PIECES = 4
+
+
+def weight_loads(weight_hbm, weight_ref, side, sems):
+    width, features = weight_ref.shape
+    columns = pl.ds(pl.multiple_of(side * features, features), features)
+    deep = width // PIECES
+    loads = []
+    for part in range(PIECES):
+        rows = pl.ds(part * deep, deep)
+        loads.append(pltpu.make_async_copy(weight_hbm.at[rows, columns], weight_ref.at[rows], sems.at[part]))
+        loads[part].start()
+    return loads
+
+
+def gate_kernel(
+    half_ref, conv_ref, gates_hbm, values_hbm, skip_ref, weight_hbm, gated_ref, out_ref,
+    gates_ref, values_ref, weight_ref, sems,
+):
     blocks, rows, lanes = conv_ref.shape
-    features = out_ref.shape[1]
+    streams = [
+        pltpu.make_async_copy(gates_hbm, gates_ref, sems.at[PIECES]),
+        pltpu.make_async_copy(values_hbm, values_ref, sems.at[PIECES + 1]),
+    ]
+    for stream in streams:
+        stream.start()
+    loads = weight_loads(weight_hbm, weight_ref, 1 - half_ref[0], sems)
     order = row_order(rows, True)
-    for step in range(blocks // group):
-        taken = pl.ds(step * group * lanes, group * lanes)
-        conv = jnp.concatenate([conv_ref[step * group + part] for part in range(group)], axis=1)
+    for stream in streams:
+        stream.wait()
+    group = blocks // PIECES
+    wide = group * lanes
+    for part in range(PIECES):
+        taken = pl.ds(part * wide, wide)
+        conv = jnp.concatenate([conv_ref[part * group + block] for block in range(group)], axis=1)
         conv = jnp.dot(order, conv, preferred_element_type=jnp.float32)
         direct = skip_ref[:, taken] * values_ref[:, taken].astype(jnp.float32)
         gated_ref[:, taken] = (gates_ref[:, taken].astype(jnp.float32) * (conv + direct)).astype(jnp.bfloat16)
-    columns = pl.ds(pl.multiple_of((1 - half_ref[0]) * features, features), features)
-    out_ref[...] = jnp.dot(gated_ref[...], weight_ref[:, columns], preferred_element_type=jnp.float32)
+    multiply_pieces(loads, gated_ref, weight_ref, out_ref)
+
+
+def multiply_pieces(loads, gated_ref, weight_ref, out_ref):
+    deep = weight_ref.shape[0] // PIECES
+    for part in range(PIECES):
+        taken = pl.ds(part * deep, deep)
+        loads[part].wait()
+        term = jnp.dot(gated_ref[:, taken], weight_ref[taken], preferred_element_type=jnp.float32)
+        out_ref[...] = term if part == 0 else out_ref[...] + term
 
 
 def gate_and_project(half, conv, gates, values, skip_gain, weight):
     rows, width = gates.shape
     features = weight.shape[1] // 2
+    anywhere, inside = pl.BlockSpec(memory_space=pl.ANY), pl.BlockSpec(memory_space=pltpu.VMEM)
     return pl.pallas_call(
-        functools.partial(gate_kernel, 4),
-        in_specs=[pl.BlockSpec(memory_space=pltpu.SMEM)] + [pl.BlockSpec(memory_space=pltpu.VMEM)] * 5,
-        out_specs=[pl.BlockSpec(memory_space=pltpu.VMEM)] * 2,
+        gate_kernel,
+        in_specs=[pl.BlockSpec(memory_space=pltpu.SMEM), inside, anywhere, anywhere, inside, anywhere],
+        out_specs=[inside] * 2,
         out_shape=[
             jax.ShapeDtypeStruct((rows, width), jnp.bfloat16),
             jax.ShapeDtypeStruct((rows, features), jnp.float32),
+        ],
+        scratch_shapes=[
+            pltpu.VMEM((rows, width), jnp.bfloat16),
+            pltpu.VMEM((rows, width), jnp.bfloat16),
+            pltpu.VMEM((width, features), jnp.bfloat16),
+            pltpu.SemaphoreType.DMA((PIECES + 2,)),
         ],
         compiler_params=pltpu.CompilerParams(vmem_limit_bytes=TAIL_BYTES),
         cost_estimate=pl.CostEstimate(
@@ -489,20 +532,20 @@
     )(half, conv, gates, values, skip_gain[None, :], weight)
 
 
-def kept_kernel(half_ref, gated_ref, weight_ref, out_ref):
-    features = out_ref.shape[1]
-    columns = pl.ds(pl.multiple_of(half_ref[0] * features, features), features)
-    out_ref[...] = jnp.dot(gated_ref[...], weight_ref[:, columns], preferred_element_type=jnp.float32)
+def kept_kernel(half_ref, gated_ref, weight_hbm, out_ref, weight_ref, sems):
+    multiply_pieces(weight_loads(weight_hbm, weight_ref, half_ref[0], sems), gated_ref, weight_ref, out_ref)
 
 
 def project_kept(half, gated, weight):
     rows, width = gated.shape
     features = weight.shape[1] // 2
+    inside = pl.BlockSpec(memory_space=pltpu.VMEM)
     return pl.pallas_call(
         kept_kernel,
-        in_specs=[pl.BlockSpec(memory_space=pltpu.SMEM)] + [pl.BlockSpec(memory_space=pltpu.VMEM)] * 2,
-        out_specs=pl.BlockSpec(memory_space=pltpu.VMEM),
+        in_specs=[pl.BlockSpec(memory_space=pltpu.SMEM), inside, pl.BlockSpec(memory_space=pl.ANY)],
+        out_specs=inside,
         out_shape=jax.ShapeDtypeStruct((rows, features), jnp.float32),
+        scratch_shapes=[pltpu.VMEM((width, features), jnp.bfloat16), pltpu.SemaphoreType.DMA((PIECES,))],
         compiler_params=pltpu.CompilerParams(vmem_limit_bytes=TAIL_BYTES),
         cost_estimate=pl.CostEstimate(
             flops=2 * rows * width * features, bytes_accessed=2 * width * features, transcendentals=0
@@ -511,19 +554,26 @@
     )(half, gated, weight)
 
 
-def join_kernel(kept_ref, came_ref, out_ref):
-    out_ref[...] = (kept_ref[...] + came_ref[...]).astype(jnp.bfloat16).T
+def join_kernel(kept_ref, came_ref, out_hbm, out_ref, sems):
+    wide = out_ref.shape[0] // PIECES
+    stores = []
+    for part in range(PIECES):
+        taken = pl.ds(part * wide, wide)
+        out_ref[taken] = (kept_ref[:, taken] + came_ref[:, taken]).astype(jnp.bfloat16).T
+        stores.append(pltpu.make_async_copy(out_ref.at[taken], out_hbm.at[taken], sems.at[part]))
+        stores[part].start()
+    for store in stores:
+        store.wait()
 
 
 def join(kept, came):
     rows, features = kept.shape
-    wide = features // 4
     return pl.pallas_call(
         join_kernel,
-        grid=(4,),
-        in_specs=[pl.BlockSpec((rows, wide), lambda i: (0, i))] * 2,
-        out_specs=pl.BlockSpec((wide, rows), lambda i: (i, 0)),
+        in_specs=[pl.BlockSpec(memory_space=pltpu.VMEM)] * 2,
+        out_specs=pl.BlockSpec(memory_space=pl.ANY),
         out_shape=jax.ShapeDtypeStruct((features, rows), jnp.bfloat16),
+        scratch_shapes=[pltpu.VMEM((features, rows), jnp.bfloat16), pltpu.SemaphoreType.DMA((PIECES,))],
         compiler_params=pltpu.CompilerParams(vmem_limit_bytes=TAIL_BYTES),
         name="join_halves",
     )(kept, came)

time: 109 us -> 104 us (0.954)
  local copies, waits for them, and re-layouts: 8.68 us -> 0.91 us
  Pallas kernels: 18.2 us -> 21 us
    unnamed x14 -> x6, local copies, waits for them, and re-layouts: 8.68 us -> 0.91 us
    pallas_call x1, Pallas kernels: 1.25 us -> 2.69 us  [project_kept(): pl.pallas_call(kept_kernel, in_specs=[pl.BlockSpec(memory_space=pltpu.SME...]
  transfers between devices with their start and end apart: 17 -> 17, of which waited for: 9 -> 9; matrix products, arithmetic and copies ran while one was open for 0% -> 0% of each run, Pallas kernels for 1% -> 3%
where the time goes in v9:
time: 104 us; the launch traced here: 103 us
  waiting for transfers between devices  46.6 us (45%)
  starting transfers between devices  34.6 us (33%)
  Pallas kernels  21 us (20%)
    ppermute x15, starting transfers between devices, exchange(): lax.ppermute(source, 'seq', [(j, j ^ slot) for j in range(blocks)])  28.2 us
    all_to_all x1, waiting for transfers between devices, swap_blocks(): return lax.all_to_all(array, 'seq', split_axis=0, concat_axis=0, tiled=True)  24.6 us
    ppermute x15, waiting for transfers between devices, exchange(): lax.ppermute(source, 'seq', [(j, j ^ slot) for j in range(blocks)])  22 us
    pallas_call x1, Pallas kernels, convolve(): pl.pallas_call(functools.partial(convolve_kernel, blocks), in_specs=[pl.B...  10.5 us
    all_to_all x1, starting transfers between devices, swap_blocks(): return lax.all_to_all(array, 'seq', split_axis=0, concat_axis=0, tiled=True)  6.32 us
    pallas_call x1, Pallas kernels, arrange(): pl.pallas_call(functools.partial(arrange_kernel, pieces, blocks), in_spec...  3.63 us
    pallas_call x1, Pallas kernels, gate_and_project(): pl.pallas_call(gate_kernel, in_specs=[pl.BlockSpec(memory_space=pltpu.SME...  3.31 us
    pallas_call x1, Pallas kernels, project_kept(): pl.pallas_call(kept_kernel, in_specs=[pl.BlockSpec(memory_space=pltpu.SME...  2.69 us
  transfers between devices with their start and end apart: 17, of which 9 were waited for; matrix products, arithmetic and copies ran while one was open for 0% of the time, Pallas kernels for 3%

profile of v9, /device:TPU:0, one launch (start us, length us, event | category | flops | bytes accessed | tf_op | source)
XLA Modules:
  0.0 103.2 jit_solution(3652508234579058866)
XLA Ops:
  0.0 3.6 %arrange_rows.1 = (bf16[256,256]{1,0:T(8,128)(2,1)}, bf16[256,256]{1,0:T(8,128)(2,1)}, bf16[256,256]{1,0:T(8,128)(2,1)}, bf16[256,256]{1,0:T(8,128)(2,1)}, bf16[...) custom-call(s32[1]{0:T(128)} %bitcast.1.me_ref, ...), custom_call_target="tpu_custom_call" | custom-call | flops 536870912 | bytes 4194304 | tf_op jit(solution)/shard_map/arrange_rows/pallas_call | solution.py:225
  3.6 4.1 %collective-permute-start = (bf16[256,256]{1,0:T(8,128)(2,1)}, bf16[256,256]{1,0:T(8,128)(2,1)S(1)}, u32[]{:S(2)}, u32[]{:S(2)}) collective-permute-start(bf16[256,256]{1,0:T(8,128)(2,1)} %get-tuple-element.23), channel_id=1, source_target_pairs={{0,16},{2,18},{4,20},{6,22},{8,24},{10,26},{12,28},{14,30},{16,0},... | collective-permute-start | bytes 393224 | tf_op jit(solution)/shard_map/ppermute | solution.py:589
  7.7 1.5 %collective-permute-start.1 = (bf16[256,256]{1,0:T(8,128)(2,1)}, bf16[256,256]{1,0:T(8,128)(2,1)S(1)}, u32[]{:S(2)}, u32[]{:S(2)}) collective-permute-start(bf16[256,256]{1,0:T(8,128)(2,1)} %get-tuple-element.24), channel_id=1, source_target_pairs={{0,2},{2,0},{4,6},{6,4},{8,10},{10,8},{12,14},{14,12},{16,18},{18,... | collective-permute-start | bytes 393224 | tf_op jit(solution)/shard_map/ppermute | solution.py:589
  9.2 1.3 %collective-permute-start.2 = (bf16[256,256]{1,0:T(8,128)(2,1)}, bf16[256,256]{1,0:T(8,128)(2,1)S(1)}, u32[]{:S(2)}, u32[]{:S(2)}) collective-permute-start(bf16[256,256]{1,0:T(8,128)(2,1)} %get-tuple-element.25), channel_id=1, source_target_pairs={{0,24},{2,26},{4,28},{6,30},{8,16},{10,18},{12,20},{14,22},{16,8},... | collective-permute-start | bytes 393224 | tf_op jit(solution)/shard_map/ppermute | solution.py:589
  10.6 1.5 %collective-permute-start.3 = (bf16[256,256]{1,0:T(8,128)(2,1)}, bf16[256,256]{1,0:T(8,128)(2,1)S(1)}, u32[]{:S(2)}, u32[]{:S(2)}) collective-permute-start(bf16[256,256]{1,0:T(8,128)(2,1)} %get-tuple-element.26), channel_id=1, source_target_pairs={{0,4},{2,6},{4,0},{6,2},{8,12},{10,14},{12,8},{14,10},{16,20},{18,... | collective-permute-start | bytes 393224 | tf_op jit(solution)/shard_map/ppermute | solution.py:589
  12.1 1.7 %collective-permute-start.4 = (bf16[256,256]{1,0:T(8,128)(2,1)}, bf16[256,256]{1,0:T(8,128)(2,1)S(1)}, u32[]{:S(2)}, u32[]{:S(2)}) collective-permute-start(bf16[256,256]{1,0:T(8,128)(2,1)} %get-tuple-element.27), channel_id=1, source_target_pairs={{0,18},{2,16},{4,22},{6,20},{8,26},{10,24},{12,30},{14,28},{16,2},... | collective-permute-start | bytes 393224 | tf_op jit(solution)/shard_map/ppermute | solution.py:589
  13.8 6.9 %collective-permute-done.rest_0_ = bf16[256,256]{1,0:T(8,128)(2,1)S(1)} collective-permute-done((bf16[256,256]{1,0:T(8,128)(2,1)}, bf16[256,256]{1,0:T(8,128)(2,1)S(1)}, u32[]{:S(2)}, u32[]{:S(2)}) %collective-permute-start) | collective-permute-done | bytes 131104 | tf_op jit(solution)/shard_map/ppermute | solution.py:589
  20.7 2.8 %collective-permute-start.5 = (bf16[256,256]{1,0:T(8,128)(2,1)}, bf16[256,256]{1,0:T(8,128)(2,1)S(1)}, u32[]{:S(2)}, u32[]{:S(2)}) collective-permute-start(bf16[256,256]{1,0:T(8,128)(2,1)} %get-tuple-element.28), channel_id=1, source_target_pairs={{0,6},{2,4},{4,2},{6,0},{8,14},{10,12},{12,10},{14,8},{16,22},{18,... | collective-permute-start | bytes 393224 | tf_op jit(solution)/shard_map/ppermute | solution.py:589
  23.5 2.4 %collective-permute-start.6 = (bf16[256,256]{1,0:T(8,128)(2,1)}, bf16[256,256]{1,0:T(8,128)(2,1)S(1)}, u32[]{:S(2)}, u32[]{:S(2)}) collective-permute-start(bf16[256,256]{1,0:T(8,128)(2,1)} %get-tuple-element.29), channel_id=1, source_target_pairs={{0,26},{2,24},{4,30},{6,28},{8,18},{10,16},{12,22},{14,20},{16,10}... | collective-permute-start | bytes 393224 | tf_op jit(solution)/shard_map/ppermute | solution.py:589
  25.9 1.5 %collective-permute-start.8 = (bf16[256,256]{1,0:T(8,128)(2,1)}, bf16[256,256]{1,0:T(8,128)(2,1)S(1)}, u32[]{:S(2)}, u32[]{:S(2)}) collective-permute-start(bf16[256,256]{1,0:T(8,128)(2,1)} %get-tuple-element.31), channel_id=1, source_target_pairs={{0,20},{2,22},{4,16},{6,18},{8,28},{10,30},{12,24},{14,26},{16,4},... | collective-permute-start | bytes 393224 | tf_op jit(solution)/shard_map/ppermute | solution.py:589
  28.3 1.1 %collective-permute-start.9 = (bf16[256,256]{1,0:T(8,128)(2,1)}, bf16[256,256]{1,0:T(8,128)(2,1)S(1)}, u32[]{:S(2)}, u32[]{:S(2)}) collective-permute-start(bf16[256,256]{1,0:T(8,128)(2,1)} %get-tuple-element.32), channel_id=1, source_target_pairs={{0,10},{2,8},{4,14},{6,12},{8,2},{10,0},{12,6},{14,4},{16,26},{18,... | collective-permute-start | bytes 393224 | tf_op jit(solution)/shard_map/ppermute | solution.py:589
  30.1 7.2 %collective-permute-start.10 = (bf16[256,256]{1,0:T(8,128)(2,1)}, bf16[256,256]{1,0:T(8,128)(2,1)S(1)}, u32[]{:S(2)}, u32[]{:S(2)}) collective-permute-start(bf16[256,256]{1,0:T(8,128)(2,1)} %get-tuple-element.33), channel_id=1, source_target_pairs={{0,28},{2,30},{4,24},{6,26},{8,20},{10,22},{12,16},{14,18},{16,12}... | collective-permute-start | bytes 393224 | tf_op jit(solution)/shard_map/ppermute | solution.py:589
  38.0 3.3 %collective-permute-done.8.rest_8_ = bf16[256,256]{1,0:T(8,128)(2,1)S(1)} collective-permute-done((bf16[256,256]{1,0:T(8,128)(2,1)}, bf16[256,256]{1,0:T(8,128)(2,1)S(1)}, u32[]{:S(2)}, u32[]{:S(2)}) %collective-permute-start.8) | collective-permute-done | bytes 131104 | tf_op jit(solution)/shard_map/ppermute | solution.py:589
  41.9 2.3 %collective-permute-start.14 = (bf16[256,256]{1,0:T(8,128)(2,1)}, bf16[256,256]{1,0:T(8,128)(2,1)S(1)}, u32[]{:S(2)}, u32[]{:S(2)}) collective-permute-start(bf16[256,256]{1,0:T(8,128)(2,1)} %get-tuple-element.37), channel_id=1, source_target_pairs={{0,30},{2,28},{4,26},{6,24},{8,22},{10,20},{12,18},{14,16},{16,14}... | collective-permute-start | bytes 393224 | tf_op jit(solution)/shard_map/ppermute | solution.py:589
  44.2 1.7 %collective-permute-done.11.rest_11_ = bf16[256,256]{1,0:T(8,128)(2,1)S(1)} collective-permute-done((bf16[256,256]{1,0:T(8,128)(2,1)}, bf16[256,256]{1,0:T(8,128)(2,1)S(1)}, u32[]{:S(2)}, u32[]{:S(2)}) %collective-permute-start.11) | collective-permute-done | bytes 131104 | tf_op jit(solution)/shard_map/ppermute | solution.py:589
  46.0 6.1 %collective-permute-done.12.rest_12_ = bf16[256,256]{1,0:T(8,128)(2,1)S(1)} collective-permute-done((bf16[256,256]{1,0:T(8,128)(2,1)}, bf16[256,256]{1,0:T(8,128)(2,1)S(1)}, u32[]{:S(2)}, u32[]{:S(2)}) %collective-permute-start.12) | collective-permute-done | bytes 131104 | tf_op jit(solution)/shard_map/ppermute | solution.py:589
  52.0 1.9 %collective-permute-done.14.rest_14_ = bf16[256,256]{1,0:T(8,128)(2,1)S(1)} collective-permute-done((bf16[256,256]{1,0:T(8,128)(2,1)}, bf16[256,256]{1,0:T(8,128)(2,1)S(1)}, u32[]{:S(2)}, u32[]{:S(2)}) %collective-permute-start.14) | collective-permute-done | bytes 131104 | tf_op jit(solution)/shard_map/ppermute | solution.py:589
  53.9 0.9 copy-done.2
  54.8 10.5 %long_convolution.1 = bf16[16,256,128]{2,1,0:T(8,128)(2,1)} custom-call(s32[1]{0:T(128)} %bitcast.1.me_ref, bf16[256,256]{1,0:T(8,128)(2,1)S(1)} %collective-permute-done.rest_0_, bf16[256,256]{1,0:T(8,128)(2,1)S(1)} %collective-permute-done.1.rest_1_, bf16[256,256]{1,0:T(8,128)(2,1)S(1)} %collective-permute-done.2.rest_2_, ...), custom_call_target="tpu_custom_call" | custom-call | flops 5000000000 | bytes 9000000 | tf_op jit(solution)/shard_map/long_convolution/pallas_call | solution.py:432
  65.3 6.3 %all-to-all-start = ((bf16[16,256,128]{2,1,0:T(8,128)(2,1)}), bf16[16,256,128]{2,1,0:T(8,128)(2,1)S(1)}, u32[]{:S(2)}, u32[]{:S(2)}) async-start(bf16[16,256,128]{2,1,0:T(8,128)(2,1)} %long_convolution.1), calls=%async_computation | async-start | bytes 2097152 | tf_op jit(solution)/shard_map/all_to_all | solution.py:583
  71.6 24.6 %all-to-all-done.conv_ref = bf16[16,256,128]{2,1,0:T(8,128)(2,1)S(1)} async-done(((bf16[16,256,128]{2,1,0:T(8,128)(2,1)}), bf16[16,256,128]{2,1,0:T(8,128)(2,1)S(1)}, u32[]{:S(2)}, u32[]{:S(2)}) %all-to-all-start) | async-done | bytes 1048608 | tf_op jit(solution)/shard_map/all_to_all | solution.py:583
  96.2 3.3 %gate_project_sent.1 = (bf16[256,2048]{1,0:T(8,128)(2,1)S(1)}, f32[256,1024]{1,0:T(8,128)S(1)}) custom-call(s32[1]{0:T(128)} %bitcast.half_ref, bf16[16,256,128]{2,1,0:T(8,128)(2,1)S(1)} %all-to-all-done.conv_ref, bf16[256,2048]{1,0:T(8,128)(2,1)S(1)} %copy-done, bf16[256,2048]{1,0:T(8,128)(2,1)} %values_hbm.3, f32[1,2048]{1,0:T(1,128)S(1)} %bitcast.3, ...), custom_call_target="tpu_custom_call" | custom-call | flops 1073741824 | bytes 4194304 | tf_op jit(solution)/shard_map/gate_project_sent/pallas_call | solution.py:513
  99.6 2.7 %project_kept.1.kept_ref = f32[256,1024]{1,0:T(8,128)S(1)} custom-call(s32[1]{0:T(128)} %bitcast.half_ref, bf16[256,2048]{1,0:T(8,128)(2,1)S(1)} %get-tuple-element.39.gated_ref, bf16[2048,2048]{1,0:T(8,128)(2,1)} %weight_hbm.3), custom_call_target="tpu_custom_call" | custom-call | flops 1073741824 | bytes 4194304 | tf_op jit(solution)/shard_map/project_kept/pallas_call | solution.py:543
  102.3 0.9 join_halves.1
  (21 shorter events, 2.8 us)
Async XLA Ops:
  3.6 17.1 %collective-permute-start = (bf16[256,256]{1,0:T(8,128)(2,1)}, bf16[256,256]{1,0:T(8,128)(2,1)S(1)}, u32[]{:S(2)}, u32[]{:S(2)}) collective-permute-start(bf16[256,256]{1,0:T(8,128)(2,1)} %get-tuple-element.23), channel_id=1, source_target_pairs={{0,16},{2,18},{4,20},{6,22},{8,24},{10,26},{12,28},{14,30},{16,0},... | collective-permute-start | bytes 393224 | tf_op jit(solution)/shard_map/ppermute | solution.py:589
  7.7 15.8 %collective-permute-start.1 = (bf16[256,256]{1,0:T(8,128)(2,1)}, bf16[256,256]{1,0:T(8,128)(2,1)S(1)}, u32[]{:S(2)}, u32[]{:S(2)}) collective-permute-start(bf16[256,256]{1,0:T(8,128)(2,1)} %get-tuple-element.24), channel_id=1, source_target_pairs={{0,2},{2,0},{4,6},{6,4},{8,10},{10,8},{12,14},{14,12},{16,18},{18,... | collective-permute-start | bytes 393224 | tf_op jit(solution)/shard_map/ppermute | solution.py:589
  9.2 16.7 %collective-permute-start.2 = (bf16[256,256]{1,0:T(8,128)(2,1)}, bf16[256,256]{1,0:T(8,128)(2,1)S(1)}, u32[]{:S(2)}, u32[]{:S(2)}) collective-permute-start(bf16[256,256]{1,0:T(8,128)(2,1)} %get-tuple-element.25), channel_id=1, source_target_pairs={{0,24},{2,26},{4,28},{6,30},{8,16},{10,18},{12,20},{14,22},{16,8},... | collective-permute-start | bytes 393224 | tf_op jit(solution)/shard_map/ppermute | solution.py:589
  10.6 15.4 %collective-permute-start.3 = (bf16[256,256]{1,0:T(8,128)(2,1)}, bf16[256,256]{1,0:T(8,128)(2,1)S(1)}, u32[]{:S(2)}, u32[]{:S(2)}) collective-permute-start(bf16[256,256]{1,0:T(8,128)(2,1)} %get-tuple-element.26), channel_id=1, source_target_pairs={{0,4},{2,6},{4,0},{6,2},{8,12},{10,14},{12,8},{14,10},{16,20},{18,... | collective-permute-start | bytes 393224 | tf_op jit(solution)/shard_map/ppermute | solution.py:589
  12.1 16.1 %collective-permute-start.4 = (bf16[256,256]{1,0:T(8,128)(2,1)}, bf16[256,256]{1,0:T(8,128)(2,1)S(1)}, u32[]{:S(2)}, u32[]{:S(2)}) collective-permute-start(bf16[256,256]{1,0:T(8,128)(2,1)} %get-tuple-element.27), channel_id=1, source_target_pairs={{0,18},{2,16},{4,22},{6,20},{8,26},{10,24},{12,30},{14,28},{16,2},... | collective-permute-start | bytes 393224 | tf_op jit(solution)/shard_map/ppermute | solution.py:589
  20.7 9.4 %collective-permute-start.5 = (bf16[256,256]{1,0:T(8,128)(2,1)}, bf16[256,256]{1,0:T(8,128)(2,1)S(1)}, u32[]{:S(2)}, u32[]{:S(2)}) collective-permute-start(bf16[256,256]{1,0:T(8,128)(2,1)} %get-tuple-element.28), channel_id=1, source_target_pairs={{0,6},{2,4},{4,2},{6,0},{8,14},{10,12},{12,10},{14,8},{16,22},{18,... | collective-permute-start | bytes 393224 | tf_op jit(solution)/shard_map/ppermute | solution.py:589
  23.5 13.9 %collective-permute-start.6 = (bf16[256,256]{1,0:T(8,128)(2,1)}, bf16[256,256]{1,0:T(8,128)(2,1)S(1)}, u32[]{:S(2)}, u32[]{:S(2)}) collective-permute-start(bf16[256,256]{1,0:T(8,128)(2,1)} %get-tuple-element.29), channel_id=1, source_target_pairs={{0,26},{2,24},{4,30},{6,28},{8,18},{10,16},{12,22},{14,20},{16,10}... | collective-permute-start | bytes 393224 | tf_op jit(solution)/shard_map/ppermute | solution.py:589
  25.9 11.4 %collective-permute-start.7 = (bf16[256,256]{1,0:T(8,128)(2,1)}, bf16[256,256]{1,0:T(8,128)(2,1)S(1)}, u32[]{:S(2)}, u32[]{:S(2)}) collective-permute-start(bf16[256,256]{1,0:T(8,128)(2,1)} %get-tuple-element.30), channel_id=1, source_target_pairs={{0,8},{2,10},{4,12},{6,14},{8,0},{10,2},{12,4},{14,6},{16,24},{18,... | collective-permute-start | bytes 393224 | tf_op jit(solution)/shard_map/ppermute | solution.py:589
  25.9 15.4 %collective-permute-start.8 = (bf16[256,256]{1,0:T(8,128)(2,1)}, bf16[256,256]{1,0:T(8,128)(2,1)S(1)}, u32[]{:S(2)}, u32[]{:S(2)}) collective-permute-start(bf16[256,256]{1,0:T(8,128)(2,1)} %get-tuple-element.31), channel_id=1, source_target_pairs={{0,20},{2,22},{4,16},{6,18},{8,28},{10,30},{12,24},{14,26},{16,4},... | collective-permute-start | bytes 393224 | tf_op jit(solution)/shard_map/ppermute | solution.py:589
  28.3 13.6 %collective-permute-start.9 = (bf16[256,256]{1,0:T(8,128)(2,1)}, bf16[256,256]{1,0:T(8,128)(2,1)S(1)}, u32[]{:S(2)}, u32[]{:S(2)}) collective-permute-start(bf16[256,256]{1,0:T(8,128)(2,1)} %get-tuple-element.32), channel_id=1, source_target_pairs={{0,10},{2,8},{4,14},{6,12},{8,2},{10,0},{12,6},{14,4},{16,26},{18,... | collective-permute-start | bytes 393224 | tf_op jit(solution)/shard_map/ppermute | solution.py:589
  30.1 14.1 %collective-permute-start.10 = (bf16[256,256]{1,0:T(8,128)(2,1)}, bf16[256,256]{1,0:T(8,128)(2,1)S(1)}, u32[]{:S(2)}, u32[]{:S(2)}) collective-permute-start(bf16[256,256]{1,0:T(8,128)(2,1)} %get-tuple-element.33), channel_id=1, source_target_pairs={{0,28},{2,30},{4,24},{6,26},{8,20},{10,22},{12,16},{14,18},{16,12}... | collective-permute-start | bytes 393224 | tf_op jit(solution)/shard_map/ppermute | solution.py:589
  37.4 8.6 %collective-permute-start.11 = (bf16[256,256]{1,0:T(8,128)(2,1)}, bf16[256,256]{1,0:T(8,128)(2,1)S(1)}, u32[]{:S(2)}, u32[]{:S(2)}) collective-permute-start(bf16[256,256]{1,0:T(8,128)(2,1)} %get-tuple-element.34), channel_id=1, source_target_pairs={{0,12},{2,14},{4,8},{6,10},{8,4},{10,6},{12,0},{14,2},{16,28},{18,... | collective-permute-start | bytes 393224 | tf_op jit(solution)/shard_map/ppermute | solution.py:589
  37.4 14.6 %collective-permute-start.12 = (bf16[256,256]{1,0:T(8,128)(2,1)}, bf16[256,256]{1,0:T(8,128)(2,1)S(1)}, u32[]{:S(2)}, u32[]{:S(2)}) collective-permute-start(bf16[256,256]{1,0:T(8,128)(2,1)} %get-tuple-element.35), channel_id=1, source_target_pairs={{0,22},{2,20},{4,18},{6,16},{8,30},{10,28},{12,26},{14,24},{16,6},... | collective-permute-start | bytes 393224 | tf_op jit(solution)/shard_map/ppermute | solution.py:589
  41.4 10.6 %collective-permute-start.13 = (bf16[256,256]{1,0:T(8,128)(2,1)}, bf16[256,256]{1,0:T(8,128)(2,1)S(1)}, u32[]{:S(2)}, u32[]{:S(2)}) collective-permute-start(bf16[256,256]{1,0:T(8,128)(2,1)} %get-tuple-element.36), channel_id=1, source_target_pairs={{0,14},{2,12},{4,10},{6,8},{8,6},{10,4},{12,2},{14,0},{16,30},{18,... | collective-permute-start | bytes 393224 | tf_op jit(solution)/shard_map/ppermute | solution.py:589
  41.9 12.0 %collective-permute-start.14 = (bf16[256,256]{1,0:T(8,128)(2,1)}, bf16[256,256]{1,0:T(8,128)(2,1)S(1)}, u32[]{:S(2)}, u32[]{:S(2)}) collective-permute-start(bf16[256,256]{1,0:T(8,128)(2,1)} %get-tuple-element.37), channel_id=1, source_target_pairs={{0,30},{2,28},{4,26},{6,24},{8,22},{10,20},{12,18},{14,16},{16,14}... | collective-permute-start | bytes 393224 | tf_op jit(solution)/shard_map/ppermute | solution.py:589
  53.9 0.9 copy-start.2
  54.8 41.4 %copy-start = (bf16[256,2048]{1,0:T(8,128)(2,1)S(1)}, bf16[256,2048]{1,0:T(8,128)(2,1)}, u32[]{:S(2)}) copy-start(bf16[256,2048]{1,0:T(8,128)(2,1)} %gates_hbm.1) | copy-start | bytes 3145732
  54.8 41.4 %copy-start.1 = (f32[2048]{0:T(1024)S(1)}, f32[2048]{0:T(1024)}, u32[]{:S(2)}) copy-start(f32[2048]{0:T(1024)} %param.9) | copy-start | bytes 24580
  65.3 30.9 %all-to-all-start = ((bf16[16,256,128]{2,1,0:T(8,128)(2,1)}), bf16[16,256,128]{2,1,0:T(8,128)(2,1)S(1)}, u32[]{:S(2)}, u32[]{:S(2)}) async-start(bf16[16,256,128]{2,1,0:T(8,128)(2,1)} %long_convolution.1), calls=%async_computation | async-start | bytes 2097152 | tf_op jit(solution)/shard_map/all_to_all | solution.py:583
  99.5 2.8 %collective-permute-start.15 = (f32[256,1024]{1,0:T(8,128)S(1)}, f32[256,1024]{1,0:T(8,128)S(1)}, u32[]{:S(2)}, u32[]{:S(2)}) collective-permute-start(f32[256,1024]{1,0:T(8,128)S(1)} %get-tuple-element.40), channel_id=1, source_target_pairs={{0,1},{1,0},{2,3},{3,2},{4,5},{5,4},{6,7},{7,6},{8,9},{9,8},{10,11... | collective-permute-start | bytes 3145736 | tf_op jit(solution)/shard_map/ppermute | solution.py:600

commit v10 on v9

--- a/solution.py
+++ b/solution.py
@@ -186,16 +186,18 @@
     return (re * cos - im * sin, im * cos + re * sin)
 
 
-def slot_order(blocks):
+def partners_across(blocks):
     half = blocks // 2
-    across = [half + (i // 2 if i % 2 == 0 else half // 2 + i // 2) for i in range(half)]
-    near = list(range(1, half)) + [0]
-    return [slot for pair in zip(across, near) for slot in pair]
+    return [half + (i // 2 if i % 2 == 0 else half // 2 + i // 2) for i in range(half)]
+
+
+def first_near(me, blocks):
+    return me & (blocks // 2)
 
 
 def arrange_kernel(pieces, blocks, me_ref, values_hbm, taps_hbm, *rest):
-    outs = rest[:blocks]
-    values_ref, taps_ref, packed, sems = rest[blocks:]
+    near_hbm, outs = rest[0], rest[1 : 1 + blocks // 2]
+    values_ref, taps_ref, packed, sems = rest[1 + blocks // 2 :]
     piece = values_ref.shape[1] // pieces
     loads = []
     for part in range(pieces):
@@ -215,8 +217,18 @@
             for side in range(2):
                 start = side * piece + block * LANES
                 packed[part * piece // LANES + block, :, pl.ds(side * LANES, LANES)] = moved[:, start : start + LANES]
-    for out, slot in zip(outs, slot_order(blocks)):
-        out[...] = packed[me_ref[0] ^ slot]
+    me = me_ref[0]
+    stores = [
+        pltpu.make_async_copy(
+            packed.at[pl.ds(first_near(me, blocks), blocks // 2)], near_hbm, sems.at[2 * pieces]
+        )
+    ]
+    for i, (out, slot) in enumerate(zip(outs, partners_across(blocks))):
+        stores.append(pltpu.make_async_copy(packed.at[me ^ slot], out, sems.at[2 * pieces + 1 + i]))
+    for store in stores:
+        store.start()
+    for store in stores:
+        store.wait()
 
 
 def arrange(me, values, taps, blocks):
@@ -225,13 +237,14 @@
     return pl.pallas_call(
         functools.partial(arrange_kernel, pieces, blocks),
         in_specs=[pl.BlockSpec(memory_space=pltpu.SMEM)] + [pl.BlockSpec(memory_space=pl.ANY)] * 2,
-        out_specs=[pl.BlockSpec(memory_space=pltpu.VMEM)] * blocks,
-        out_shape=[jax.ShapeDtypeStruct((rows, 2 * LANES), jnp.bfloat16)] * blocks,
+        out_specs=[pl.BlockSpec(memory_space=pl.ANY)] * (1 + blocks // 2),
+        out_shape=[jax.ShapeDtypeStruct((blocks // 2, rows, 2 * LANES), jnp.bfloat16)]
+        + [jax.ShapeDtypeStruct((rows, 2 * LANES), jnp.bfloat16)] * (blocks // 2),
         scratch_shapes=[
             pltpu.VMEM((rows, wide), jnp.bfloat16),
             pltpu.VMEM((rows, wide), jnp.bfloat16),
             pltpu.VMEM((blocks, rows, 2 * LANES), jnp.bfloat16),
-            pltpu.SemaphoreType.DMA((2 * pieces,)),
+            pltpu.SemaphoreType.DMA((2 * pieces + 1 + blocks // 2,)),
         ],
         compiler_params=pltpu.CompilerParams(vmem_limit_bytes=ARRANGE_BYTES),
         cost_estimate=pl.CostEstimate(
@@ -241,13 +254,13 @@
     )(me, values, taps)
 
 
-def convolve_kernel(blocks, me_ref, *rest):
-    slots = rest[:blocks]
-    convolve_blocks(me_ref, slots, *rest[blocks:])
+def convolve_kernel(blocks, me_ref, near_ref, *rest):
+    half = blocks // 2
+    convolve_blocks(me_ref, near_ref, rest[:half], rest[half], rest[half + 1], rest[half + 2 : 2 * half + 2], *rest[2 * half + 2 :])
 
 
 def convolve_blocks(
-    me_ref, slots, tables_hbm, out_hbm,
+    me_ref, near_ref, slots, tables_hbm, near_hbm, outs,
     streams, turns_ref, fixed, stages, raw_even, raw_odd, columns, mixed, halves_even, halves_odd, signals, sems,
 ):
     blocks, rows, _ = streams.shape
@@ -259,20 +272,30 @@
     halves = (halves_even, halves_odd)
     count = fixed.shape[0]
     load_fixed = pltpu.make_async_copy(tables_hbm.at[pl.ds(2 * RADIX, count)], fixed, sems.at[0])
+    me = me_ref[0]
+    first, across = first_near(me, blocks), partners_across(blocks)
     load_turns, stores = [], []
     for low in range(4):
         taken = pl.ds(low * group, group)
         eight = pl.ds(8 * low, 8)
         load_turns.append(pltpu.make_async_copy(tables_hbm.at[eight], turns_ref.at[eight], sems.at[1 + low]))
-        stores.append(pltpu.make_async_copy(signals.at[:, taken], out_hbm.at[:, taken], sems.at[5 + low]))
+        stores.append(
+            [
+                pltpu.make_async_copy(
+                    signals.at[pl.ds(first, blocks // 2), taken], near_hbm.at[:, taken], sems.at[5 + low * (1 + len(outs))]
+                )
+            ]
+        )
+        for i, (out, slot) in enumerate(zip(outs, across)):
+            stores[low].append(
+                pltpu.make_async_copy(signals.at[me ^ slot, taken], out.at[taken], sems.at[6 + low * (1 + len(outs)) + i])
+            )
     load_fixed.start()
     for load in load_turns:
         load.start()
-    own = pltpu.make_async_copy(slots[-1], streams.at[me_ref[0]], sems.at[9])
-    own.start()
-    for slot, source in zip(slot_order(blocks)[:-1], slots[:-1]):
-        streams[me_ref[0] ^ slot] = source[...]
-    own.wait()
+    streams[pl.ds(first, blocks // 2)] = near_ref[...]
+    for slot, source in zip(across, slots):
+        streams[me ^ slot] = source[...]
     load_fixed.wait()
     width = inner // LANES
     for table in range(4):
@@ -418,24 +441,26 @@
             return carry
 
         lax.fori_loop(0, 2, back, 0)
-        stores[low].start()
-    for store in stores:
+        for store in stores[low]:
+            store.start()
+    for store in sum(stores, []):
         store.wait()
 
 
-def convolve(me, slots):
-    blocks = len(slots)
-    rows, lanes = slots[0].shape
+def convolve(me, near, slots):
+    half, rows, lanes = near.shape
+    blocks = 2 * half
     length = blocks * rows
     inner = length // RADIX
     tables = transform_tables(length)
     return pl.pallas_call(
         functools.partial(convolve_kernel, blocks),
         in_specs=[pl.BlockSpec(memory_space=pltpu.SMEM)]
-        + [pl.BlockSpec(memory_space=pltpu.VMEM)] * (blocks - 1)
-        + [pl.BlockSpec(memory_space=pl.ANY)] * 2,
-        out_specs=pl.BlockSpec(memory_space=pl.ANY),
-        out_shape=jax.ShapeDtypeStruct((blocks, rows, LANES), jnp.bfloat16),
+        + [pl.BlockSpec(memory_space=pltpu.VMEM)] * (1 + half)
+        + [pl.BlockSpec(memory_space=pl.ANY)],
+        out_specs=[pl.BlockSpec(memory_space=pl.ANY)] * (1 + half),
+        out_shape=[jax.ShapeDtypeStruct((half, rows, LANES), jnp.bfloat16)]
+        + [jax.ShapeDtypeStruct((rows, LANES), jnp.bfloat16)] * half,
         scratch_shapes=[
             pltpu.VMEM((blocks, rows, lanes), jnp.bfloat16),
             pltpu.VMEM((2 * RADIX, inner, LANES), jnp.float32),
@@ -448,12 +473,12 @@
             pltpu.VMEM((4, 2, inner, lanes), jnp.bfloat16),
             pltpu.VMEM((4, 2, inner, lanes), jnp.bfloat16),
             pltpu.VMEM((blocks, rows, LANES), jnp.bfloat16),
-            pltpu.SemaphoreType.DMA((10,)),
+            pltpu.SemaphoreType.DMA((5 + 4 * (1 + half),)),
         ],
         compiler_params=pltpu.CompilerParams(vmem_limit_bytes=CONV_BYTES),
         cost_estimate=pl.CostEstimate(flops=5 * 10**9, bytes_accessed=9 * 10**6, transcendentals=0),
         name="long_convolution",
-    )(me, *slots, jnp.asarray(tables))
+    )(me, near, *slots, jnp.asarray(tables))
 
 
 PIECES = 4
@@ -472,9 +497,10 @@
 
 
 def gate_kernel(
-    half_ref, conv_ref, gates_hbm, values_hbm, skip_ref, weight_hbm, gated_ref, out_ref,
-    gates_ref, values_ref, weight_ref, sems,
+    count, me_ref, half_ref, near_ref, gates_hbm, values_hbm, skip_ref, weight_hbm, *rest,
 ):
+    slots = rest[:count]
+    gated_ref, out_ref, conv_ref, gates_ref, values_ref, weight_ref, sems = rest[count:]
     blocks, rows, lanes = conv_ref.shape
     streams = [
         pltpu.make_async_copy(gates_hbm, gates_ref, sems.at[PIECES]),
@@ -484,6 +510,10 @@
         stream.start()
     loads = weight_loads(weight_hbm, weight_ref, 1 - half_ref[0], sems)
     order = row_order(rows, True)
+    me = me_ref[0]
+    conv_ref[pl.ds(first_near(me, blocks), blocks // 2)] = near_ref[...]
+    for slot, source in zip(partners_across(blocks), slots):
+        conv_ref[me ^ slot] = source[...]
     for stream in streams:
         stream.wait()
     group = blocks // PIECES
@@ -506,19 +536,22 @@
         out_ref[...] = term if part == 0 else out_ref[...] + term
 
 
-def gate_and_project(half, conv, gates, values, skip_gain, weight):
+def gate_and_project(me, half, near, slots, gates, values, skip_gain, weight):
     rows, width = gates.shape
     features = weight.shape[1] // 2
     anywhere, inside = pl.BlockSpec(memory_space=pl.ANY), pl.BlockSpec(memory_space=pltpu.VMEM)
     return pl.pallas_call(
-        gate_kernel,
-        in_specs=[pl.BlockSpec(memory_space=pltpu.SMEM), inside, anywhere, anywhere, inside, anywhere],
+        functools.partial(gate_kernel, len(slots)),
+        in_specs=[pl.BlockSpec(memory_space=pltpu.SMEM)] * 2
+        + [inside, anywhere, anywhere, inside, anywhere]
+        + [inside] * len(slots),
         out_specs=[inside] * 2,
         out_shape=[
             jax.ShapeDtypeStruct((rows, width), jnp.bfloat16),
             jax.ShapeDtypeStruct((rows, features), jnp.float32),
         ],
         scratch_shapes=[
+            pltpu.VMEM((2 * len(slots), rows, LANES), jnp.bfloat16),
             pltpu.VMEM((rows, width), jnp.bfloat16),
             pltpu.VMEM((rows, width), jnp.bfloat16),
             pltpu.VMEM((width, features), jnp.bfloat16),
@@ -529,7 +562,7 @@
             flops=2 * rows * width * features, bytes_accessed=2 * width * features, transcendentals=0
         ),
         name="gate_project_sent",
-    )(half, conv, gates, values, skip_gain[None, :], weight)
+    )(me, half, near, gates, values, skip_gain[None, :], weight, *slots)
 
 
 def kept_kernel(half_ref, gated_ref, weight_hbm, out_ref, weight_ref, sems):
@@ -579,24 +612,24 @@
     )(kept, came)
 
 
-def swap_blocks(array):
-    return lax.all_to_all(array, "seq", split_axis=0, concat_axis=0, tiled=True)
-
-
-def exchange(slots):
-    blocks = len(slots)
-    return [
-        lax.ppermute(source, "seq", [(j, j ^ slot) for j in range(blocks)]) if slot else source
-        for slot, source in zip(slot_order(blocks), slots)
+def exchange(near, across):
+    half = near.shape[0]
+    groups = [list(range(half)), list(range(half, 2 * half))]
+    near = lax.all_to_all(near, "seq", split_axis=0, concat_axis=0, axis_index_groups=groups, tiled=True)
+    came = [
+        lax.ppermute(source, "seq", [(j, j ^ slot) for j in range(2 * half)])
+        for slot, source in zip(partners_across(2 * half), across)
     ]
+    return near, came
 
 
 def kernel_local(values, gates, filter_taps, skip_gain, out_weight):
     blocks = lax.axis_size("seq")
     me = lax.axis_index("seq").astype(jnp.int32)[None]
     half = lax.axis_index("chan").astype(jnp.int32)[None]
-    conv = convolve(me, exchange(arrange(me, values, filter_taps, blocks)))
-    gated, sent = gate_and_project(half, swap_blocks(conv), gates, values, skip_gain, out_weight)
+    near, *across = arrange(me, values, filter_taps, blocks)
+    near, *across = convolve(me, *exchange(near, across))
+    gated, sent = gate_and_project(me, half, *exchange(near, across), gates, values, skip_gain, out_weight)
     other = lax.ppermute(sent, "chan", [(0, 1), (1, 0)])
     kept = project_kept(half, gated, out_weight)
     return join(kept, other)

time: 104 us -> 111 us (1.067)
  starting transfers between devices: 34.6 us -> 65.6 us
  waiting for transfers between devices: 46.6 us -> 22 us
    ppermute x15 -> x16, starting transfers between devices: 28.2 us -> 55.8 us  [exchange(): lax.ppermute(source, 'seq', [(j, j ^ slot) for j in range(2 * half)])]
    all_to_all x1 -> x2, waiting for transfers between devices: 24.6 us -> 0.01 us  [exchange(): lax.all_to_all(near, 'seq', split_axis=0, concat_axis=0, axis_index_group...]
    all_to_all x1 -> x2, starting transfers between devices: 6.32 us -> 9.69 us  [exchange(): lax.all_to_all(near, 'seq', split_axis=0, concat_axis=0, axis_index_group...]
    ppermute x15 -> x16, waiting for transfers between devices: 22 us -> 22 us  [exchange(): lax.ppermute(source, 'seq', [(j, j ^ slot) for j in range(2 * half)])]
  transfers between devices with their start and end apart: 17 -> 19, of which waited for: 9 -> 8; matrix products, arithmetic and copies ran while one was open for 0% -> 0% of each run, Pallas kernels for 3% -> 2%
where the time goes in v10:
time: 111 us
  starting transfers between devices  65.6 us (59%)
  waiting for transfers between devices  22 us (20%)
  Pallas kernels  21.9 us (20%)
  local copies, waits for them, and re-layouts  1.24 us (1%)
    ppermute x16, starting transfers between devices, exchange(): lax.ppermute(source, 'seq', [(j, j ^ slot) for j in range(2 * half)])  55.8 us
    ppermute x16, waiting for transfers between devices, exchange(): lax.ppermute(source, 'seq', [(j, j ^ slot) for j in range(2 * half)])  22 us
    pallas_call x1, Pallas kernels, convolve(): pl.pallas_call(functools.partial(convolve_kernel, blocks), in_specs=[pl.B...  11.2 us
    all_to_all x2, starting transfers between devices, exchange(): lax.all_to_all(near, 'seq', split_axis=0, concat_axis=0, axis_index_group...  9.69 us
    pallas_call x1, Pallas kernels, arrange(): pl.pallas_call(functools.partial(arrange_kernel, pieces, blocks), in_spec...  3.7 us
    pallas_call x1, Pallas kernels, gate_and_project(): pl.pallas_call(functools.partial(gate_kernel, len(slots)), in_specs=[pl.B...  3.38 us
    pallas_call x1, Pallas kernels, project_kept(): pl.pallas_call(kept_kernel, in_specs=[pl.BlockSpec(memory_space=pltpu.SME...  2.69 us
  transfers between devices with their start and end apart: 19, of which 8 were waited for; matrix products, arithmetic and copies ran while one was open for 0% of the time, Pallas kernels for 2%

profile of v10, /device:TPU:0, one launch (start us, length us, event | category | flops | bytes accessed | tf_op | source)
XLA Modules:
  0.0 110.7 jit_solution(1305909807040698591)
XLA Ops:
  0.0 3.7 %arrange_rows.1 = (bf16[8,256,256]{2,1,0:T(8,128)(2,1)}, bf16[256,256]{1,0:T(8,128)(2,1)}, bf16[256,256]{1,0:T(8,128)(2,1)}, bf16[256,256]{1,0:T(8,128)(2,1)}, b...) custom-call(s32[1]{0:T(128)} %bitcast.1.me_ref, ...), custom_call_target="tpu_custom_call" | custom-call | flops 536870912 | bytes 4194304 | tf_op jit(solution)/shard_map/arrange_rows/pallas_call | solution.py:237
  3.7 6.2 %all-to-all-start = ((bf16[8,256,256]{2,1,0:T(8,128)(2,1)}), bf16[8,256,256]{2,1,0:T(8,128)(2,1)S(1)}, u32[]{:S(2)}, u32[]{:S(2)}) async-start(bf16[8,256,256]{2,1,0:T(8,128)(2,1)} %get-tuple-element.25), calls=%async_computation | async-start | bytes 2097152 | tf_op jit(solution)/shard_map/all_to_all | solution.py:618
  9.9 2.6 %collective-permute-start = (bf16[256,256]{1,0:T(8,128)(2,1)}, bf16[256,256]{1,0:T(8,128)(2,1)S(1)}, u32[]{:S(2)}, u32[]{:S(2)}) collective-permute-start(bf16[256,256]{1,0:T(8,128)(2,1)} %get-tuple-element.26), channel_id=1, source_target_pairs={{0,16},{2,18},{4,20},{6,22},{8,24},{10,26},{12,28},{14,30},{16,0},... | collective-permute-start | bytes 393224 | tf_op jit(solution)/shard_map/ppermute | solution.py:620
  12.5 1.8 %collective-permute-start.1 = (bf16[256,256]{1,0:T(8,128)(2,1)}, bf16[256,256]{1,0:T(8,128)(2,1)S(1)}, u32[]{:S(2)}, u32[]{:S(2)}) collective-permute-start(bf16[256,256]{1,0:T(8,128)(2,1)} %get-tuple-element.27), channel_id=1, source_target_pairs={{0,24},{2,26},{4,28},{6,30},{8,16},{10,18},{12,20},{14,22},{16,8},... | collective-permute-start | bytes 393224 | tf_op jit(solution)/shard_map/ppermute | solution.py:620
  14.3 2.6 %collective-permute-start.2 = (bf16[256,256]{1,0:T(8,128)(2,1)}, bf16[256,256]{1,0:T(8,128)(2,1)S(1)}, u32[]{:S(2)}, u32[]{:S(2)}) collective-permute-start(bf16[256,256]{1,0:T(8,128)(2,1)} %get-tuple-element.28), channel_id=1, source_target_pairs={{0,18},{2,16},{4,22},{6,20},{8,26},{10,24},{12,30},{14,28},{16,2},... | collective-permute-start | bytes 393224 | tf_op jit(solution)/shard_map/ppermute | solution.py:620
  17.8 2.9 %collective-permute-start.4 = (bf16[256,256]{1,0:T(8,128)(2,1)}, bf16[256,256]{1,0:T(8,128)(2,1)S(1)}, u32[]{:S(2)}, u32[]{:S(2)}) collective-permute-start(bf16[256,256]{1,0:T(8,128)(2,1)} %get-tuple-element.30), channel_id=1, source_target_pairs={{0,20},{2,22},{4,16},{6,18},{8,28},{10,30},{12,24},{14,26},{16,4},... | collective-permute-start | bytes 393224 | tf_op jit(solution)/shard_map/ppermute | solution.py:620
  20.7 4.7 %collective-permute-done.rest_0_ = bf16[256,256]{1,0:T(8,128)(2,1)S(1)} collective-permute-done((bf16[256,256]{1,0:T(8,128)(2,1)}, bf16[256,256]{1,0:T(8,128)(2,1)S(1)}, u32[]{:S(2)}, u32[]{:S(2)}) %collective-permute-start) | collective-permute-done | bytes 131104 | tf_op jit(solution)/shard_map/ppermute | solution.py:620
  25.4 5.0 %collective-permute-start.5 = (bf16[256,256]{1,0:T(8,128)(2,1)}, bf16[256,256]{1,0:T(8,128)(2,1)S(1)}, u32[]{:S(2)}, u32[]{:S(2)}) collective-permute-start(bf16[256,256]{1,0:T(8,128)(2,1)} %get-tuple-element.31), channel_id=1, source_target_pairs={{0,28},{2,30},{4,24},{6,26},{8,20},{10,22},{12,16},{14,18},{16,12}... | collective-permute-start | bytes 393224 | tf_op jit(solution)/shard_map/ppermute | solution.py:620
  30.4 2.3 %collective-permute-done.1.rest_1_ = bf16[256,256]{1,0:T(8,128)(2,1)S(1)} collective-permute-done((bf16[256,256]{1,0:T(8,128)(2,1)}, bf16[256,256]{1,0:T(8,128)(2,1)S(1)}, u32[]{:S(2)}, u32[]{:S(2)}) %collective-permute-start.1) | collective-permute-done | bytes 131104 | tf_op jit(solution)/shard_map/ppermute | solution.py:620
  33.7 16.2 %collective-permute-start.7 = (bf16[256,256]{1,0:T(8,128)(2,1)}, bf16[256,256]{1,0:T(8,128)(2,1)S(1)}, u32[]{:S(2)}, u32[]{:S(2)}) collective-permute-start(bf16[256,256]{1,0:T(8,128)(2,1)} %get-tuple-element.33), channel_id=1, source_target_pairs={{0,30},{2,28},{4,26},{6,24},{8,22},{10,20},{12,18},{14,16},{16,14}... | collective-permute-start | bytes 393224 | tf_op jit(solution)/shard_map/ppermute | solution.py:620
  51.0 7.9 %collective-permute-done.6.rest_6_ = bf16[256,256]{1,0:T(8,128)(2,1)S(1)} collective-permute-done((bf16[256,256]{1,0:T(8,128)(2,1)}, bf16[256,256]{1,0:T(8,128)(2,1)S(1)}, u32[]{:S(2)}, u32[]{:S(2)}) %collective-permute-start.6) | collective-permute-done | bytes 131104 | tf_op jit(solution)/shard_map/ppermute | solution.py:620
  58.9 11.2 %long_convolution.1 = (bf16[8,256,128]{2,1,0:T(8,128)(2,1)}, bf16[256,128]{1,0:T(8,128)(2,1)S(1)}, bf16[256,128]{1,0:T(8,128)(2,1)S(1)}, bf16[256,128]{1,0:T(8,1...) custom-call(s32[1]{0:T(128)} %bitcast.1.me_ref, ...), custom_call_target="tpu_custom_call" | custom-call | flops 5000000000 | bytes 9000000 | tf_op jit(solution)/shard_map/long_convolution/pallas_call | solution.py:456
  71.3 3.5 %all-to-all-start.1 = ((bf16[8,256,128]{2,1,0:T(8,128)(2,1)}), bf16[8,256,128]{2,1,0:T(8,128)(2,1)S(1)}, u32[]{:S(2)}, u32[]{:S(2)}) async-start(bf16[8,256,128]{2,1,0:T(8,128)(2,1)} %get-tuple-element.34), calls=%async_computation.1 | async-start | bytes 1048576 | tf_op jit(solution)/shard_map/all_to_all | solution.py:618
  74.8 4.0 %collective-permute-start.8 = (bf16[256,128]{1,0:T(8,128)(2,1)}, bf16[256,128]{1,0:T(8,128)(2,1)S(1)}, u32[]{:S(2)}, u32[]{:S(2)}) collective-permute-start(bf16[256,128]{1,0:T(8,128)(2,1)} %copy-done.3), channel_id=1, source_target_pairs={{0,16},{2,18},{4,20},{6,22},{8,24},{10,26},{12,28},{14,30},{16,0},... | collective-permute-start | bytes 196616 | tf_op jit(solution)/shard_map/ppermute | solution.py:620
  78.8 1.3 %collective-permute-start.9 = (bf16[256,128]{1,0:T(8,128)(2,1)}, bf16[256,128]{1,0:T(8,128)(2,1)S(1)}, u32[]{:S(2)}, u32[]{:S(2)}) collective-permute-start(bf16[256,128]{1,0:T(8,128)(2,1)} %copy-done.2), channel_id=1, source_target_pairs={{0,24},{2,26},{4,28},{6,30},{8,16},{10,18},{12,20},{14,22},{16,8},... | collective-permute-start | bytes 196616 | tf_op jit(solution)/shard_map/ppermute | solution.py:620
  80.1 2.9 %collective-permute-start.10 = (bf16[256,128]{1,0:T(8,128)(2,1)S(1)}, bf16[256,128]{1,0:T(8,128)(2,1)S(1)}, u32[]{:S(2)}, u32[]{:S(2)}) collective-permute-start(bf16[256,128]{1,0:T(8,128)(2,1)S(1)} %get-tuple-element.37), channel_id=1, source_target_pairs={{0,18},{2,16},{4,22},{6,20},{8,26},{10,24},{12,30},{14,28},{16,2},... | collective-permute-start | bytes 196616 | tf_op jit(solution)/shard_map/ppermute | solution.py:620
  84.0 2.9 %collective-permute-start.12 = (bf16[256,128]{1,0:T(8,128)(2,1)S(1)}, bf16[256,128]{1,0:T(8,128)(2,1)S(1)}, u32[]{:S(2)}, u32[]{:S(2)}) collective-permute-start(bf16[256,128]{1,0:T(8,128)(2,1)S(1)} %get-tuple-element.39), channel_id=1, source_target_pairs={{0,20},{2,22},{4,16},{6,18},{8,28},{10,30},{12,24},{14,26},{16,4},... | collective-permute-start | bytes 196616 | tf_op jit(solution)/shard_map/ppermute | solution.py:620
  86.9 7.3 %collective-permute-start.13 = (bf16[256,128]{1,0:T(8,128)(2,1)S(1)}, bf16[256,128]{1,0:T(8,128)(2,1)S(1)}, u32[]{:S(2)}, u32[]{:S(2)}) collective-permute-start(bf16[256,128]{1,0:T(8,128)(2,1)S(1)} %get-tuple-element.40), channel_id=1, source_target_pairs={{0,28},{2,30},{4,24},{6,26},{8,20},{10,22},{12,16},{14,18},{16,12}... | collective-permute-start | bytes 196616 | tf_op jit(solution)/shard_map/ppermute | solution.py:620
  94.1 1.3 %collective-permute-start.14 = (bf16[256,128]{1,0:T(8,128)(2,1)S(1)}, bf16[256,128]{1,0:T(8,128)(2,1)S(1)}, u32[]{:S(2)}, u32[]{:S(2)}) collective-permute-start(bf16[256,128]{1,0:T(8,128)(2,1)S(1)} %get-tuple-element.41), channel_id=1, source_target_pairs={{0,22},{2,20},{4,18},{6,16},{8,30},{10,28},{12,26},{14,24},{16,6},... | collective-permute-start | bytes 196616 | tf_op jit(solution)/shard_map/ppermute | solution.py:620
  95.7 2.2 %collective-permute-start.15 = (bf16[256,128]{1,0:T(8,128)(2,1)S(1)}, bf16[256,128]{1,0:T(8,128)(2,1)S(1)}, u32[]{:S(2)}, u32[]{:S(2)}) collective-permute-start(bf16[256,128]{1,0:T(8,128)(2,1)S(1)} %get-tuple-element.42), channel_id=1, source_target_pairs={{0,30},{2,28},{4,26},{6,24},{8,22},{10,20},{12,18},{14,16},{16,14}... | collective-permute-start | bytes 196616 | tf_op jit(solution)/shard_map/ppermute | solution.py:620
  97.8 2.0 %collective-permute-done.12.rest_4_ = bf16[256,128]{1,0:T(8,128)(2,1)S(1)} collective-permute-done((bf16[256,128]{1,0:T(8,128)(2,1)S(1)}, bf16[256,128]{1,0:T(8,128)(2,1)S(1)}, u32[]{:S(2)}, u32[]{:S(2)}) %collective-permute-start.12) | collective-permute-done | bytes 65568 | tf_op jit(solution)/shard_map/ppermute | solution.py:620
  99.9 2.8 %collective-permute-done.14.rest_6_ = bf16[256,128]{1,0:T(8,128)(2,1)S(1)} collective-permute-done((bf16[256,128]{1,0:T(8,128)(2,1)S(1)}, bf16[256,128]{1,0:T(8,128)(2,1)S(1)}, u32[]{:S(2)}, u32[]{:S(2)}) %collective-permute-start.14) | collective-permute-done | bytes 65568 | tf_op jit(solution)/shard_map/ppermute | solution.py:620
  103.6 3.4 %gate_project_sent.1 = (bf16[256,2048]{1,0:T(8,128)(2,1)S(1)}, f32[256,1024]{1,0:T(8,128)S(1)}) custom-call(s32[1]{0:T(128)} %bitcast.1.me_ref, s32[1]{0:T(128)} %bitcast.half_ref, bf16[8,256,128]{2,1,0:T(8,128)(2,1)S(1)} %all-to-all-done.1.near_ref, bf16[256,2048]{1,0:T(8,128)(2,1)S(1)} %copy-done, bf16[256,2048]{1,0:T(8,128)(2,1)} %values_hbm.3, ...), custom_call_target="tpu_custom_call" | custom-call | flops 1073741824 | bytes 4194304 | tf_op jit(solution)/shard_map/gate_project_sent/pallas_call | solution.py:543
  107.1 2.7 %project_kept.1.kept_ref = f32[256,1024]{1,0:T(8,128)S(1)} custom-call(s32[1]{0:T(128)} %bitcast.half_ref, bf16[256,2048]{1,0:T(8,128)(2,1)S(1)} %get-tuple-element.43.gated_ref, bf16[2048,2048]{1,0:T(8,128)(2,1)} %weight_hbm.3), custom_call_target="tpu_custom_call" | custom-call | flops 1073741824 | bytes 4194304 | tf_op jit(solution)/shard_map/project_kept/pallas_call | solution.py:576
  (27 shorter events, 7.2 us)
Async XLA Ops:
  3.7 55.2 %all-to-all-start = ((bf16[8,256,256]{2,1,0:T(8,128)(2,1)}), bf16[8,256,256]{2,1,0:T(8,128)(2,1)S(1)}, u32[]{:S(2)}, u32[]{:S(2)}) async-start(bf16[8,256,256]{2,1,0:T(8,128)(2,1)} %get-tuple-element.25), calls=%async_computation | async-start | bytes 2097152 | tf_op jit(solution)/shard_map/all_to_all | solution.py:618
  9.9 15.5 %collective-permute-start = (bf16[256,256]{1,0:T(8,128)(2,1)}, bf16[256,256]{1,0:T(8,128)(2,1)S(1)}, u32[]{:S(2)}, u32[]{:S(2)}) collective-permute-start(bf16[256,256]{1,0:T(8,128)(2,1)} %get-tuple-element.26), channel_id=1, source_target_pairs={{0,16},{2,18},{4,20},{6,22},{8,24},{10,26},{12,28},{14,30},{16,0},... | collective-permute-start | bytes 393224 | tf_op jit(solution)/shard_map/ppermute | solution.py:620
  12.5 20.2 %collective-permute-start.1 = (bf16[256,256]{1,0:T(8,128)(2,1)}, bf16[256,256]{1,0:T(8,128)(2,1)S(1)}, u32[]{:S(2)}, u32[]{:S(2)}) collective-permute-start(bf16[256,256]{1,0:T(8,128)(2,1)} %get-tuple-element.27), channel_id=1, source_target_pairs={{0,24},{2,26},{4,28},{6,30},{8,16},{10,18},{12,20},{14,22},{16,8},... | collective-permute-start | bytes 393224 | tf_op jit(solution)/shard_map/ppermute | solution.py:620
  14.3 19.4 %collective-permute-start.2 = (bf16[256,256]{1,0:T(8,128)(2,1)}, bf16[256,256]{1,0:T(8,128)(2,1)S(1)}, u32[]{:S(2)}, u32[]{:S(2)}) collective-permute-start(bf16[256,256]{1,0:T(8,128)(2,1)} %get-tuple-element.28), channel_id=1, source_target_pairs={{0,18},{2,16},{4,22},{6,20},{8,26},{10,24},{12,30},{14,28},{16,2},... | collective-permute-start | bytes 393224 | tf_op jit(solution)/shard_map/ppermute | solution.py:620
  16.9 33.1 %collective-permute-start.3 = (bf16[256,256]{1,0:T(8,128)(2,1)}, bf16[256,256]{1,0:T(8,128)(2,1)S(1)}, u32[]{:S(2)}, u32[]{:S(2)}) collective-permute-start(bf16[256,256]{1,0:T(8,128)(2,1)} %get-tuple-element.29), channel_id=1, source_target_pairs={{0,26},{2,24},{4,30},{6,28},{8,18},{10,16},{12,22},{14,20},{16,10}... | collective-permute-start | bytes 393224 | tf_op jit(solution)/shard_map/ppermute | solution.py:620
  17.8 33.2 %collective-permute-start.4 = (bf16[256,256]{1,0:T(8,128)(2,1)}, bf16[256,256]{1,0:T(8,128)(2,1)S(1)}, u32[]{:S(2)}, u32[]{:S(2)}) collective-permute-start(bf16[256,256]{1,0:T(8,128)(2,1)} %get-tuple-element.30), channel_id=1, source_target_pairs={{0,20},{2,22},{4,16},{6,18},{8,28},{10,30},{12,24},{14,26},{16,4},... | collective-permute-start | bytes 393224 | tf_op jit(solution)/shard_map/ppermute | solution.py:620
  25.4 25.6 %collective-permute-start.5 = (bf16[256,256]{1,0:T(8,128)(2,1)}, bf16[256,256]{1,0:T(8,128)(2,1)S(1)}, u32[]{:S(2)}, u32[]{:S(2)}) collective-permute-start(bf16[256,256]{1,0:T(8,128)(2,1)} %get-tuple-element.31), channel_id=1, source_target_pairs={{0,28},{2,30},{4,24},{6,26},{8,20},{10,22},{12,16},{14,18},{16,12}... | collective-permute-start | bytes 393224 | tf_op jit(solution)/shard_map/ppermute | solution.py:620
  32.7 26.2 %collective-permute-start.6 = (bf16[256,256]{1,0:T(8,128)(2,1)}, bf16[256,256]{1,0:T(8,128)(2,1)S(1)}, u32[]{:S(2)}, u32[]{:S(2)}) collective-permute-start(bf16[256,256]{1,0:T(8,128)(2,1)} %get-tuple-element.32), channel_id=1, source_target_pairs={{0,22},{2,20},{4,18},{6,16},{8,30},{10,28},{12,26},{14,24},{16,6},... | collective-permute-start | bytes 393224 | tf_op jit(solution)/shard_map/ppermute | solution.py:620
  33.7 69.9 %copy-start = (bf16[256,2048]{1,0:T(8,128)(2,1)S(1)}, bf16[256,2048]{1,0:T(8,128)(2,1)}, u32[]{:S(2)}) copy-start(bf16[256,2048]{1,0:T(8,128)(2,1)} %gates_hbm.1) | copy-start | bytes 3145732
  33.7 69.9 %copy-start.1 = (f32[2048]{0:T(1024)S(1)}, f32[2048]{0:T(1024)}, u32[]{:S(2)}) copy-start(f32[2048]{0:T(1024)} %param.9) | copy-start | bytes 24580
  33.7 25.2 %collective-permute-start.7 = (bf16[256,256]{1,0:T(8,128)(2,1)}, bf16[256,256]{1,0:T(8,128)(2,1)S(1)}, u32[]{:S(2)}, u32[]{:S(2)}) collective-permute-start(bf16[256,256]{1,0:T(8,128)(2,1)} %get-tuple-element.33), channel_id=1, source_target_pairs={{0,30},{2,28},{4,26},{6,24},{8,22},{10,20},{12,18},{14,16},{16,14}... | collective-permute-start | bytes 393224 | tf_op jit(solution)/shard_map/ppermute | solution.py:620
  70.1 0.6 copy-start.2
  70.7 0.6 copy-start.3
  71.3 32.3 %all-to-all-start.1 = ((bf16[8,256,128]{2,1,0:T(8,128)(2,1)}), bf16[8,256,128]{2,1,0:T(8,128)(2,1)S(1)}, u32[]{:S(2)}, u32[]{:S(2)}) async-start(bf16[8,256,128]{2,1,0:T(8,128)(2,1)} %get-tuple-element.34), calls=%async_computation.1 | async-start | bytes 1048576 | tf_op jit(solution)/shard_map/all_to_all | solution.py:618
  74.8 12.0 %collective-permute-start.8 = (bf16[256,128]{1,0:T(8,128)(2,1)}, bf16[256,128]{1,0:T(8,128)(2,1)S(1)}, u32[]{:S(2)}, u32[]{:S(2)}) collective-permute-start(bf16[256,128]{1,0:T(8,128)(2,1)} %copy-done.3), channel_id=1, source_target_pairs={{0,16},{2,18},{4,20},{6,22},{8,24},{10,26},{12,28},{14,30},{16,0},... | collective-permute-start | bytes 196616 | tf_op jit(solution)/shard_map/ppermute | solution.py:620
  78.8 15.3 %collective-permute-start.9 = (bf16[256,128]{1,0:T(8,128)(2,1)}, bf16[256,128]{1,0:T(8,128)(2,1)S(1)}, u32[]{:S(2)}, u32[]{:S(2)}) collective-permute-start(bf16[256,128]{1,0:T(8,128)(2,1)} %copy-done.2), channel_id=1, source_target_pairs={{0,24},{2,26},{4,28},{6,30},{8,16},{10,18},{12,20},{14,22},{16,8},... | collective-permute-start | bytes 196616 | tf_op jit(solution)/shard_map/ppermute | solution.py:620
  80.1 15.5 %collective-permute-start.10 = (bf16[256,128]{1,0:T(8,128)(2,1)S(1)}, bf16[256,128]{1,0:T(8,128)(2,1)S(1)}, u32[]{:S(2)}, u32[]{:S(2)}) collective-permute-start(bf16[256,128]{1,0:T(8,128)(2,1)S(1)} %get-tuple-element.37), channel_id=1, source_target_pairs={{0,18},{2,16},{4,22},{6,20},{8,26},{10,24},{12,30},{14,28},{16,2},... | collective-permute-start | bytes 196616 | tf_op jit(solution)/shard_map/ppermute | solution.py:620
  83.1 14.8 %collective-permute-start.11 = (bf16[256,128]{1,0:T(8,128)(2,1)S(1)}, bf16[256,128]{1,0:T(8,128)(2,1)S(1)}, u32[]{:S(2)}, u32[]{:S(2)}) collective-permute-start(bf16[256,128]{1,0:T(8,128)(2,1)S(1)} %get-tuple-element.38), channel_id=1, source_target_pairs={{0,26},{2,24},{4,30},{6,28},{8,18},{10,16},{12,22},{14,20},{16,10}... | collective-permute-start | bytes 196616 | tf_op jit(solution)/shard_map/ppermute | solution.py:620
  84.0 15.9 %collective-permute-start.12 = (bf16[256,128]{1,0:T(8,128)(2,1)S(1)}, bf16[256,128]{1,0:T(8,128)(2,1)S(1)}, u32[]{:S(2)}, u32[]{:S(2)}) collective-permute-start(bf16[256,128]{1,0:T(8,128)(2,1)S(1)} %get-tuple-element.39), channel_id=1, source_target_pairs={{0,20},{2,22},{4,16},{6,18},{8,28},{10,30},{12,24},{14,26},{16,4},... | collective-permute-start | bytes 196616 | tf_op jit(solution)/shard_map/ppermute | solution.py:620
  86.9 13.0 %collective-permute-start.13 = (bf16[256,128]{1,0:T(8,128)(2,1)S(1)}, bf16[256,128]{1,0:T(8,128)(2,1)S(1)}, u32[]{:S(2)}, u32[]{:S(2)}) collective-permute-start(bf16[256,128]{1,0:T(8,128)(2,1)S(1)} %get-tuple-element.40), channel_id=1, source_target_pairs={{0,28},{2,30},{4,24},{6,26},{8,20},{10,22},{12,16},{14,18},{16,12}... | collective-permute-start | bytes 196616 | tf_op jit(solution)/shard_map/ppermute | solution.py:620
  94.1 8.5 %collective-permute-start.14 = (bf16[256,128]{1,0:T(8,128)(2,1)S(1)}, bf16[256,128]{1,0:T(8,128)(2,1)S(1)}, u32[]{:S(2)}, u32[]{:S(2)}) collective-permute-start(bf16[256,128]{1,0:T(8,128)(2,1)S(1)} %get-tuple-element.41), channel_id=1, source_target_pairs={{0,22},{2,20},{4,18},{6,16},{8,30},{10,28},{12,26},{14,24},{16,6},... | collective-permute-start | bytes 196616 | tf_op jit(solution)/shard_map/ppermute | solution.py:620
  95.7 8.0 %collective-permute-start.15 = (bf16[256,128]{1,0:T(8,128)(2,1)S(1)}, bf16[256,128]{1,0:T(8,128)(2,1)S(1)}, u32[]{:S(2)}, u32[]{:S(2)}) collective-permute-start(bf16[256,128]{1,0:T(8,128)(2,1)S(1)} %get-tuple-element.42), channel_id=1, source_target_pairs={{0,30},{2,28},{4,26},{6,24},{8,22},{10,20},{12,18},{14,16},{16,14}... | collective-permute-start | bytes 196616 | tf_op jit(solution)/shard_map/ppermute | solution.py:620
  107.0 2.8 %collective-permute-start.16 = (f32[256,1024]{1,0:T(8,128)S(1)}, f32[256,1024]{1,0:T(8,128)S(1)}, u32[]{:S(2)}, u32[]{:S(2)}) collective-permute-start(f32[256,1024]{1,0:T(8,128)S(1)} %get-tuple-element.44), channel_id=1, source_target_pairs={{0,1},{1,0},{2,3},{3,2},{4,5},{5,4},{6,7},{7,6},{8,9},{9,8},{10,11... | collective-permute-start | bytes 3145736 | tf_op jit(solution)/shard_map/ppermute | solution.py:633

commit v11 on v9

--- a/solution.py
+++ b/solution.py
@@ -15,7 +15,7 @@
 RADIX = 16
 LANES = 128
 Q_ORDER = [low + 4 * high for low in range(4) for high in range(4)]
-ARRANGE_BYTES = 60 * 1024 * 1024
+ARRANGE_BYTES = 12 * 1024 * 1024
 CONV_BYTES = 49 * 1024 * 1024
 TAIL_BYTES = 49 * 1024 * 1024
 
@@ -242,12 +242,11 @@
 
 
 def convolve_kernel(blocks, me_ref, *rest):
-    slots = rest[:blocks]
-    convolve_blocks(me_ref, slots, *rest[blocks:])
+    convolve_blocks(me_ref, rest[:blocks], rest[blocks], rest[blocks + 1 : 2 * blocks + 1], *rest[2 * blocks + 1 :])
 
 
 def convolve_blocks(
-    me_ref, slots, tables_hbm, out_hbm,
+    me_ref, slots, tables_hbm, outs,
     streams, turns_ref, fixed, stages, raw_even, raw_odd, columns, mixed, halves_even, halves_odd, signals, sems,
 ):
     blocks, rows, _ = streams.shape
@@ -261,14 +260,22 @@
     load_fixed = pltpu.make_async_copy(tables_hbm.at[pl.ds(2 * RADIX, count)], fixed, sems.at[0])
     load_turns, stores = [], []
     for low in range(4):
-        taken = pl.ds(low * group, group)
         eight = pl.ds(8 * low, 8)
         load_turns.append(pltpu.make_async_copy(tables_hbm.at[eight], turns_ref.at[eight], sems.at[1 + low]))
-        stores.append(pltpu.make_async_copy(signals.at[:, taken], out_hbm.at[:, taken], sems.at[5 + low]))
+    for part in range(2):
+        taken = pl.ds(2 * part * group, 2 * group)
+        stores.append(
+            [
+                pltpu.make_async_copy(
+                    signals.at[me_ref[0] ^ slot, taken], out.at[taken], sems.at[6 + part * blocks + i]
+                )
+                for i, (out, slot) in enumerate(zip(outs, slot_order(blocks)))
+            ]
+        )
     load_fixed.start()
     for load in load_turns:
         load.start()
-    own = pltpu.make_async_copy(slots[-1], streams.at[me_ref[0]], sems.at[9])
+    own = pltpu.make_async_copy(slots[-1], streams.at[me_ref[0]], sems.at[5])
     own.start()
     for slot, source in zip(slot_order(blocks)[:-1], slots[:-1]):
         streams[me_ref[0] ^ slot] = source[...]
@@ -418,8 +425,10 @@
             return carry
 
         lax.fori_loop(0, 2, back, 0)
-        stores[low].start()
-    for store in stores:
+        if low % 2:
+            for store in stores[low // 2]:
+                store.start()
+    for store in stores[0] + stores[1]:
         store.wait()
 
 
@@ -434,8 +443,8 @@
         in_specs=[pl.BlockSpec(memory_space=pltpu.SMEM)]
         + [pl.BlockSpec(memory_space=pltpu.VMEM)] * (blocks - 1)
         + [pl.BlockSpec(memory_space=pl.ANY)] * 2,
-        out_specs=pl.BlockSpec(memory_space=pl.ANY),
-        out_shape=jax.ShapeDtypeStruct((blocks, rows, LANES), jnp.bfloat16),
+        out_specs=[pl.BlockSpec(memory_space=pl.ANY)] * blocks,
+        out_shape=[jax.ShapeDtypeStruct((rows, LANES), jnp.bfloat16)] * blocks,
         scratch_shapes=[
             pltpu.VMEM((blocks, rows, lanes), jnp.bfloat16),
             pltpu.VMEM((2 * RADIX, inner, LANES), jnp.float32),
@@ -448,7 +457,7 @@
             pltpu.VMEM((4, 2, inner, lanes), jnp.bfloat16),
             pltpu.VMEM((4, 2, inner, lanes), jnp.bfloat16),
             pltpu.VMEM((blocks, rows, LANES), jnp.bfloat16),
-            pltpu.SemaphoreType.DMA((10,)),
+            pltpu.SemaphoreType.DMA((6 + 2 * blocks,)),
         ],
         compiler_params=pltpu.CompilerParams(vmem_limit_bytes=CONV_BYTES),
         cost_estimate=pl.CostEstimate(flops=5 * 10**9, bytes_accessed=9 * 10**6, transcendentals=0),
@@ -471,19 +480,22 @@
     return loads
 
 
-def gate_kernel(
-    half_ref, conv_ref, gates_hbm, values_hbm, skip_ref, weight_hbm, gated_ref, out_ref,
-    gates_ref, values_ref, weight_ref, sems,
-):
+def gate_kernel(count, me_ref, half_ref, gates_hbm, values_hbm, skip_ref, weight_hbm, *rest):
+    slots = rest[:count]
+    gated_ref, out_ref, conv_ref, gates_ref, values_ref, weight_ref, sems = rest[count:]
     blocks, rows, lanes = conv_ref.shape
+    me = me_ref[0]
     streams = [
         pltpu.make_async_copy(gates_hbm, gates_ref, sems.at[PIECES]),
         pltpu.make_async_copy(values_hbm, values_ref, sems.at[PIECES + 1]),
+        pltpu.make_async_copy(slots[-1], conv_ref.at[me], sems.at[PIECES + 2]),
     ]
     for stream in streams:
         stream.start()
     loads = weight_loads(weight_hbm, weight_ref, 1 - half_ref[0], sems)
     order = row_order(rows, True)
+    for slot, source in zip(slot_order(blocks)[:-1], slots[:-1]):
+        conv_ref[me ^ slot] = source[...]
     for stream in streams:
         stream.wait()
     group = blocks // PIECES
@@ -506,30 +518,34 @@
         out_ref[...] = term if part == 0 else out_ref[...] + term
 
 
-def gate_and_project(half, conv, gates, values, skip_gain, weight):
+def gate_and_project(me, half, slots, gates, values, skip_gain, weight):
     rows, width = gates.shape
     features = weight.shape[1] // 2
     anywhere, inside = pl.BlockSpec(memory_space=pl.ANY), pl.BlockSpec(memory_space=pltpu.VMEM)
     return pl.pallas_call(
-        gate_kernel,
-        in_specs=[pl.BlockSpec(memory_space=pltpu.SMEM), inside, anywhere, anywhere, inside, anywhere],
+        functools.partial(gate_kernel, len(slots)),
+        in_specs=[pl.BlockSpec(memory_space=pltpu.SMEM)] * 2
+        + [anywhere, anywhere, inside, anywhere]
+        + [inside] * (len(slots) - 1)
+        + [anywhere],
         out_specs=[inside] * 2,
         out_shape=[
             jax.ShapeDtypeStruct((rows, width), jnp.bfloat16),
             jax.ShapeDtypeStruct((rows, features), jnp.float32),
         ],
         scratch_shapes=[
+            pltpu.VMEM((len(slots), rows, LANES), jnp.bfloat16),
             pltpu.VMEM((rows, width), jnp.bfloat16),
             pltpu.VMEM((rows, width), jnp.bfloat16),
             pltpu.VMEM((width, features), jnp.bfloat16),
-            pltpu.SemaphoreType.DMA((PIECES + 2,)),
+            pltpu.SemaphoreType.DMA((PIECES + 3,)),
         ],
         compiler_params=pltpu.CompilerParams(vmem_limit_bytes=TAIL_BYTES),
         cost_estimate=pl.CostEstimate(
             flops=2 * rows * width * features, bytes_accessed=2 * width * features, transcendentals=0
         ),
         name="gate_project_sent",
-    )(half, conv, gates, values, skip_gain[None, :], weight)
+    )(me, half, gates, values, skip_gain[None, :], weight, *slots)
 
 
 def kept_kernel(half_ref, gated_ref, weight_hbm, out_ref, weight_ref, sems):
@@ -579,10 +595,6 @@
     )(kept, came)
 
 
-def swap_blocks(array):
-    return lax.all_to_all(array, "seq", split_axis=0, concat_axis=0, tiled=True)
-
-
 def exchange(slots):
     blocks = len(slots)
     return [
@@ -596,7 +608,7 @@
     me = lax.axis_index("seq").astype(jnp.int32)[None]
     half = lax.axis_index("chan").astype(jnp.int32)[None]
     conv = convolve(me, exchange(arrange(me, values, filter_taps, blocks)))
-    gated, sent = gate_and_project(half, swap_blocks(conv), gates, values, skip_gain, out_weight)
+    gated, sent = gate_and_project(me, half, exchange(conv), gates, values, skip_gain, out_weight)
     other = lax.ppermute(sent, "chan", [(0, 1), (1, 0)])
     kept = project_kept(half, gated, out_weight)
     return join(kept, other)

time: 104 us -> 106 us (1.019)
  starting transfers between devices: 34.6 us -> 55.3 us
  waiting for transfers between devices: 46.6 us -> 27.1 us
  local copies, waits for them, and re-layouts: 0.91 us -> 2.46 us
    ppermute x15 -> x30, starting transfers between devices: 28.2 us -> 55.2 us  [exchange(): lax.ppermute(source, 'seq', [(j, j ^ slot) for j in range(blocks)])]
    all_to_all x1 -> x0, waiting for transfers between devices: 24.6 us -> none  [swap_blocks(): return lax.all_to_all(array, 'seq', split_axis=0, concat_axis=0, tiled=True)]
    all_to_all x1 -> x0, starting transfers between devices: 6.32 us -> none  [swap_blocks(): return lax.all_to_all(array, 'seq', split_axis=0, concat_axis=0, tiled=True)]
    ppermute x15 -> x30, waiting for transfers between devices: 22 us -> 27.1 us  [exchange(): lax.ppermute(source, 'seq', [(j, j ^ slot) for j in range(blocks)])]
    pallas_call x1, Pallas kernels: 3.63 us -> 1.78 us  [arrange(): pl.pallas_call(functools.partial(arrange_kernel, pieces, blocks), in_spec...]
    unnamed x6 -> x8, local copies, waits for them, and re-layouts: 0.91 us -> 2.46 us
    pallas_call x1, Pallas kernels: 10.5 us -> 11.8 us  [convolve(): pl.pallas_call(functools.partial(convolve_kernel, blocks), in_specs=[pl.B...]
  transfers between devices with their start and end apart: 17 -> 31, of which waited for: 9 -> 13; matrix products, arithmetic and copies ran while one was open for 0% -> 0% of each run, Pallas kernels for 3% -> 3%
where the time goes in v11:
time: 106 us; the launch traced here: 105 us
  starting transfers between devices  55.3 us (52%)
  waiting for transfers between devices  27.1 us (26%)
  Pallas kernels  20.5 us (19%)
  local copies, waits for them, and re-layouts  2.46 us (2%)
    ppermute x30, starting transfers between devices, exchange(): lax.ppermute(source, 'seq', [(j, j ^ slot) for j in range(blocks)])  55.2 us
    ppermute x30, waiting for transfers between devices, exchange(): lax.ppermute(source, 'seq', [(j, j ^ slot) for j in range(blocks)])  27.1 us
    pallas_call x1, Pallas kernels, convolve(): pl.pallas_call(functools.partial(convolve_kernel, blocks), in_specs=[pl.B...  11.8 us
    pallas_call x1, Pallas kernels, gate_and_project(): pl.pallas_call(functools.partial(gate_kernel, len(slots)), in_specs=[pl.B...  3.32 us
    pallas_call x1, Pallas kernels, project_kept(): pl.pallas_call(kept_kernel, in_specs=[pl.BlockSpec(memory_space=pltpu.SME...  2.7 us
    unnamed x8, local copies, waits for them, and re-layouts  2.46 us
  transfers between devices with their start and end apart: 31, of which 13 were waited for; matrix products, arithmetic and copies ran while one was open for 0% of the time, Pallas kernels for 3%

profile of v11, /device:TPU:0, one launch (start us, length us, event | category | flops | bytes accessed | tf_op | source)
XLA Modules:
  0.0 105.4 jit_solution(11337786934107462571)
XLA Ops:
  2.5 1.8 %arrange_rows.1 = (bf16[256,256]{1,0:T(8,128)(2,1)S(1)}, bf16[256,256]{1,0:T(8,128)(2,1)S(1)}, bf16[256,256]{1,0:T(8,128)(2,1)S(1)}, bf16[256,256]{1,0:T(8,128)(...) custom-call(s32[1]{0:T(128)} %bitcast.1.me_ref, ...), custom_call_target="tpu_custom_call" | custom-call | flops 536870912 | bytes 4194304 | tf_op jit(solution)/shard_map/arrange_rows/pallas_call | solution.py:225
  4.2 4.1 %collective-permute-start = (bf16[256,256]{1,0:T(8,128)(2,1)S(1)}, bf16[256,256]{1,0:T(8,128)(2,1)S(1)}, u32[]{:S(2)}, u32[]{:S(2)}) collective-permute-start(bf16[256,256]{1,0:T(8,128)(2,1)S(1)} %get-tuple-element.39), channel_id=1, source_target_pairs={{0,16},{2,18},{4,20},{6,22},{8,24},{10,26},{12,28},{14,30},{16,0},... | collective-permute-start | bytes 393224 | tf_op jit(solution)/shard_map/ppermute | solution.py:601
  8.3 1.5 %collective-permute-start.1 = (bf16[256,256]{1,0:T(8,128)(2,1)S(1)}, bf16[256,256]{1,0:T(8,128)(2,1)S(1)}, u32[]{:S(2)}, u32[]{:S(2)}) collective-permute-start(bf16[256,256]{1,0:T(8,128)(2,1)S(1)} %get-tuple-element.40), channel_id=1, source_target_pairs={{0,2},{2,0},{4,6},{6,4},{8,10},{10,8},{12,14},{14,12},{16,18},{18,... | collective-permute-start | bytes 393224 | tf_op jit(solution)/shard_map/ppermute | solution.py:601
  11.2 1.5 %collective-permute-start.3 = (bf16[256,256]{1,0:T(8,128)(2,1)S(1)}, bf16[256,256]{1,0:T(8,128)(2,1)S(1)}, u32[]{:S(2)}, u32[]{:S(2)}) collective-permute-start(bf16[256,256]{1,0:T(8,128)(2,1)S(1)} %get-tuple-element.42), channel_id=1, source_target_pairs={{0,4},{2,6},{4,0},{6,2},{8,12},{10,14},{12,8},{14,10},{16,20},{18,... | collective-permute-start | bytes 393224 | tf_op jit(solution)/shard_map/ppermute | solution.py:601
  12.7 1.7 %collective-permute-start.4 = (bf16[256,256]{1,0:T(8,128)(2,1)S(1)}, bf16[256,256]{1,0:T(8,128)(2,1)S(1)}, u32[]{:S(2)}, u32[]{:S(2)}) collective-permute-start(bf16[256,256]{1,0:T(8,128)(2,1)S(1)} %get-tuple-element.43), channel_id=1, source_target_pairs={{0,18},{2,16},{4,22},{6,20},{8,26},{10,24},{12,30},{14,28},{16,2},... | collective-permute-start | bytes 393224 | tf_op jit(solution)/shard_map/ppermute | solution.py:601
  14.4 6.7 %collective-permute-done.rest_0_ = bf16[256,256]{1,0:T(8,128)(2,1)S(1)} collective-permute-done((bf16[256,256]{1,0:T(8,128)(2,1)S(1)}, bf16[256,256]{1,0:T(8,128)(2,1)S(1)}, u32[]{:S(2)}, u32[]{:S(2)}) %collective-permute-start) | collective-permute-done | bytes 131104 | tf_op jit(solution)/shard_map/ppermute | solution.py:601
  21.1 2.8 %collective-permute-start.5 = (bf16[256,256]{1,0:T(8,128)(2,1)S(1)}, bf16[256,256]{1,0:T(8,128)(2,1)S(1)}, u32[]{:S(2)}, u32[]{:S(2)}) collective-permute-start(bf16[256,256]{1,0:T(8,128)(2,1)S(1)} %get-tuple-element.44), channel_id=1, source_target_pairs={{0,6},{2,4},{4,2},{6,0},{8,14},{10,12},{12,10},{14,8},{16,22},{18,... | collective-permute-start | bytes 393224 | tf_op jit(solution)/shard_map/ppermute | solution.py:601
  23.9 2.4 %collective-permute-start.6 = (bf16[256,256]{1,0:T(8,128)(2,1)S(1)}, bf16[256,256]{1,0:T(8,128)(2,1)S(1)}, u32[]{:S(2)}, u32[]{:S(2)}) collective-permute-start(bf16[256,256]{1,0:T(8,128)(2,1)S(1)} %get-tuple-element.45), channel_id=1, source_target_pairs={{0,26},{2,24},{4,30},{6,28},{8,18},{10,16},{12,22},{14,20},{16,10}... | collective-permute-start | bytes 393224 | tf_op jit(solution)/shard_map/ppermute | solution.py:601
  26.3 1.5 %collective-permute-start.8 = (bf16[256,256]{1,0:T(8,128)(2,1)S(1)}, bf16[256,256]{1,0:T(8,128)(2,1)S(1)}, u32[]{:S(2)}, u32[]{:S(2)}) collective-permute-start(bf16[256,256]{1,0:T(8,128)(2,1)S(1)} %get-tuple-element.47), channel_id=1, source_target_pairs={{0,20},{2,22},{4,16},{6,18},{8,28},{10,30},{12,24},{14,26},{16,4},... | collective-permute-start | bytes 393224 | tf_op jit(solution)/shard_map/ppermute | solution.py:601
  30.4 7.1 %collective-permute-start.10 = (bf16[256,256]{1,0:T(8,128)(2,1)S(1)}, bf16[256,256]{1,0:T(8,128)(2,1)S(1)}, u32[]{:S(2)}, u32[]{:S(2)}) collective-permute-start(bf16[256,256]{1,0:T(8,128)(2,1)S(1)} %get-tuple-element.49), channel_id=1, source_target_pairs={{0,28},{2,30},{4,24},{6,26},{8,20},{10,22},{12,16},{14,18},{16,12}... | collective-permute-start | bytes 393224 | tf_op jit(solution)/shard_map/ppermute | solution.py:601
  38.1 3.9 %collective-permute-done.8.rest_8_ = bf16[256,256]{1,0:T(8,128)(2,1)S(1)} collective-permute-done((bf16[256,256]{1,0:T(8,128)(2,1)S(1)}, bf16[256,256]{1,0:T(8,128)(2,1)S(1)}, u32[]{:S(2)}, u32[]{:S(2)}) %collective-permute-start.8) | collective-permute-done | bytes 131104 | tf_op jit(solution)/shard_map/ppermute | solution.py:601
  42.1 2.3 %collective-permute-start.14 = (bf16[256,256]{1,0:T(8,128)(2,1)S(1)}, bf16[256,256]{1,0:T(8,128)(2,1)S(1)}, u32[]{:S(2)}, u32[]{:S(2)}) collective-permute-start(bf16[256,256]{1,0:T(8,128)(2,1)S(1)} %get-tuple-element.53), channel_id=1, source_target_pairs={{0,30},{2,28},{4,26},{6,24},{8,22},{10,20},{12,18},{14,16},{16,14}... | collective-permute-start | bytes 393224 | tf_op jit(solution)/shard_map/ppermute | solution.py:601
  44.4 1.4 %collective-permute-done.11.rest_11_ = bf16[256,256]{1,0:T(8,128)(2,1)S(1)} collective-permute-done((bf16[256,256]{1,0:T(8,128)(2,1)S(1)}, bf16[256,256]{1,0:T(8,128)(2,1)S(1)}, u32[]{:S(2)}, u32[]{:S(2)}) %collective-permute-start.11) | collective-permute-done | bytes 131104 | tf_op jit(solution)/shard_map/ppermute | solution.py:601
  45.8 6.3 %collective-permute-done.12.rest_12_ = bf16[256,256]{1,0:T(8,128)(2,1)S(1)} collective-permute-done((bf16[256,256]{1,0:T(8,128)(2,1)S(1)}, bf16[256,256]{1,0:T(8,128)(2,1)S(1)}, u32[]{:S(2)}, u32[]{:S(2)}) %collective-permute-start.12) | collective-permute-done | bytes 131104 | tf_op jit(solution)/shard_map/ppermute | solution.py:601
  52.1 2.4 %collective-permute-done.14.rest_14_ = bf16[256,256]{1,0:T(8,128)(2,1)S(1)} collective-permute-done((bf16[256,256]{1,0:T(8,128)(2,1)S(1)}, bf16[256,256]{1,0:T(8,128)(2,1)S(1)}, u32[]{:S(2)}, u32[]{:S(2)}) %collective-permute-start.14) | collective-permute-done | bytes 131104 | tf_op jit(solution)/shard_map/ppermute | solution.py:601
  54.5 11.8 %long_convolution.1 = (bf16[256,128]{1,0:T(8,128)(2,1)S(1)}, bf16[256,128]{1,0:T(8,128)(2,1)S(1)}, bf16[256,128]{1,0:T(8,128)(2,1)S(1)}, bf16[256,128]{1,0:T(8,1...) custom-call(s32[1]{0:T(128)} %bitcast.1.me_ref, ...), custom_call_target="tpu_custom_call" | custom-call | flops 5000000000 | bytes 9000000 | tf_op jit(solution)/shard_map/long_convolution/pallas_call | solution.py:441
  66.3 4.7 %collective-permute-start.15 = (bf16[256,128]{1,0:T(8,128)(2,1)S(1)}, bf16[256,128]{1,0:T(8,128)(2,1)S(1)}, u32[]{:S(2)}, u32[]{:S(2)}) collective-permute-start(bf16[256,128]{1,0:T(8,128)(2,1)S(1)} %get-tuple-element.55), channel_id=1, source_target_pairs={{0,16},{2,18},{4,20},{6,22},{8,24},{10,26},{12,28},{14,30},{16,0},... | collective-permute-start | bytes 196616 | tf_op jit(solution)/shard_map/ppermute | solution.py:601
  75.3 5.3 %collective-permute-start.21 = (bf16[256,128]{1,0:T(8,128)(2,1)S(1)}, bf16[256,128]{1,0:T(8,128)(2,1)S(1)}, u32[]{:S(2)}, u32[]{:S(2)}) collective-permute-start(bf16[256,128]{1,0:T(8,128)(2,1)S(1)} %get-tuple-element.61), channel_id=1, source_target_pairs={{0,26},{2,24},{4,30},{6,28},{8,18},{10,16},{12,22},{14,20},{16,10}... | collective-permute-start | bytes 196616 | tf_op jit(solution)/shard_map/ppermute | solution.py:601
  82.8 3.2 %collective-permute-start.25 = (bf16[256,128]{1,0:T(8,128)(2,1)S(1)}, bf16[256,128]{1,0:T(8,128)(2,1)S(1)}, u32[]{:S(2)}, u32[]{:S(2)}) collective-permute-start(bf16[256,128]{1,0:T(8,128)(2,1)S(1)} %get-tuple-element.65), channel_id=1, source_target_pairs={{0,28},{2,30},{4,24},{6,26},{8,20},{10,22},{12,16},{14,18},{16,12}... | collective-permute-start | bytes 196616 | tf_op jit(solution)/shard_map/ppermute | solution.py:601
  86.5 3.9 %collective-permute-start.27 = (bf16[256,128]{1,0:T(8,128)(2,1)S(1)}, bf16[256,128]{1,0:T(8,128)(2,1)S(1)}, u32[]{:S(2)}, u32[]{:S(2)}) collective-permute-start(bf16[256,128]{1,0:T(8,128)(2,1)S(1)} %get-tuple-element.67), channel_id=1, source_target_pairs={{0,22},{2,20},{4,18},{6,16},{8,30},{10,28},{12,26},{14,24},{16,6},... | collective-permute-start | bytes 196616 | tf_op jit(solution)/shard_map/ppermute | solution.py:601
  90.4 4.6 %collective-permute-start.29 = (bf16[256,128]{1,0:T(8,128)(2,1)S(1)}, bf16[256,128]{1,0:T(8,128)(2,1)S(1)}, u32[]{:S(2)}, u32[]{:S(2)}) collective-permute-start(bf16[256,128]{1,0:T(8,128)(2,1)S(1)} %get-tuple-element.69), channel_id=1, source_target_pairs={{0,30},{2,28},{4,26},{6,24},{8,22},{10,20},{12,18},{14,16},{16,14}... | collective-permute-start | bytes 196616 | tf_op jit(solution)/shard_map/ppermute | solution.py:601
  96.4 1.9 %collective-permute-done.29.rest_14_ = bf16[256,128]{1,0:T(8,128)(2,1)S(1)} collective-permute-done((bf16[256,128]{1,0:T(8,128)(2,1)S(1)}, bf16[256,128]{1,0:T(8,128)(2,1)S(1)}, u32[]{:S(2)}, u32[]{:S(2)}) %collective-permute-start.29) | collective-permute-done | bytes 65568 | tf_op jit(solution)/shard_map/ppermute | solution.py:601
  98.3 3.3 %gate_project_sent.1 = (bf16[256,2048]{1,0:T(8,128)(2,1)S(1)}, f32[256,1024]{1,0:T(8,128)S(1)}) custom-call(s32[1]{0:T(128)} %bitcast.1.me_ref, s32[1]{0:T(128)} %bitcast.half_ref, bf16[256,2048]{1,0:T(8,128)(2,1)S(1)} %copy-done.2, bf16[256,2048]{1,0:T(8,128)(2,1)} %values_hbm.3, f32[1,2048]{1,0:T(1,128)S(1)} %bitcast.3, bf16[2048,2048]{1,0:T(8,128)(2,1)} %weight_hbm.3, ...), custom_call_target="tpu_custom_call" | custom-call | flops 1073741824 | bytes 4194304 | tf_op jit(solution)/shard_map/gate_project_sent/pallas_call | solution.py:525
  101.7 2.7 %project_kept.1.kept_ref = f32[256,1024]{1,0:T(8,128)S(1)} custom-call(s32[1]{0:T(128)} %bitcast.half_ref, bf16[256,2048]{1,0:T(8,128)(2,1)S(1)} %get-tuple-element.71.gated_ref, bf16[2048,2048]{1,0:T(8,128)(2,1)} %weight_hbm.3), custom_call_target="tpu_custom_call" | custom-call | flops 1073741824 | bytes 4194304 | tf_op jit(solution)/shard_map/project_kept/pallas_call | solution.py:559
  (51 shorter events, 16.4 us)
Async XLA Ops:
  4.2 16.9 %collective-permute-start = (bf16[256,256]{1,0:T(8,128)(2,1)S(1)}, bf16[256,256]{1,0:T(8,128)(2,1)S(1)}, u32[]{:S(2)}, u32[]{:S(2)}) collective-permute-start(bf16[256,256]{1,0:T(8,128)(2,1)S(1)} %get-tuple-element.39), channel_id=1, source_target_pairs={{0,16},{2,18},{4,20},{6,22},{8,24},{10,26},{12,28},{14,30},{16,0},... | collective-permute-start | bytes 393224 | tf_op jit(solution)/shard_map/ppermute | solution.py:601
  8.3 15.5 %collective-permute-start.1 = (bf16[256,256]{1,0:T(8,128)(2,1)S(1)}, bf16[256,256]{1,0:T(8,128)(2,1)S(1)}, u32[]{:S(2)}, u32[]{:S(2)}) collective-permute-start(bf16[256,256]{1,0:T(8,128)(2,1)S(1)} %get-tuple-element.40), channel_id=1, source_target_pairs={{0,2},{2,0},{4,6},{6,4},{8,10},{10,8},{12,14},{14,12},{16,18},{18,... | collective-permute-start | bytes 393224 | tf_op jit(solution)/shard_map/ppermute | solution.py:601
  9.8 16.5 %collective-permute-start.2 = (bf16[256,256]{1,0:T(8,128)(2,1)S(1)}, bf16[256,256]{1,0:T(8,128)(2,1)S(1)}, u32[]{:S(2)}, u32[]{:S(2)}) collective-permute-start(bf16[256,256]{1,0:T(8,128)(2,1)S(1)} %get-tuple-element.41), channel_id=1, source_target_pairs={{0,24},{2,26},{4,28},{6,30},{8,16},{10,18},{12,20},{14,22},{16,8},... | collective-permute-start | bytes 393224 | tf_op jit(solution)/shard_map/ppermute | solution.py:601
  11.2 15.1 %collective-permute-start.3 = (bf16[256,256]{1,0:T(8,128)(2,1)S(1)}, bf16[256,256]{1,0:T(8,128)(2,1)S(1)}, u32[]{:S(2)}, u32[]{:S(2)}) collective-permute-start(bf16[256,256]{1,0:T(8,128)(2,1)S(1)} %get-tuple-element.42), channel_id=1, source_target_pairs={{0,4},{2,6},{4,0},{6,2},{8,12},{10,14},{12,8},{14,10},{16,20},{18,... | collective-permute-start | bytes 393224 | tf_op jit(solution)/shard_map/ppermute | solution.py:601
  12.7 16.2 %collective-permute-start.4 = (bf16[256,256]{1,0:T(8,128)(2,1)S(1)}, bf16[256,256]{1,0:T(8,128)(2,1)S(1)}, u32[]{:S(2)}, u32[]{:S(2)}) collective-permute-start(bf16[256,256]{1,0:T(8,128)(2,1)S(1)} %get-tuple-element.43), channel_id=1, source_target_pairs={{0,18},{2,16},{4,22},{6,20},{8,26},{10,24},{12,30},{14,28},{16,2},... | collective-permute-start | bytes 393224 | tf_op jit(solution)/shard_map/ppermute | solution.py:601
  21.1 9.3 %collective-permute-start.5 = (bf16[256,256]{1,0:T(8,128)(2,1)S(1)}, bf16[256,256]{1,0:T(8,128)(2,1)S(1)}, u32[]{:S(2)}, u32[]{:S(2)}) collective-permute-start(bf16[256,256]{1,0:T(8,128)(2,1)S(1)} %get-tuple-element.44), channel_id=1, source_target_pairs={{0,6},{2,4},{4,2},{6,0},{8,14},{10,12},{12,10},{14,8},{16,22},{18,... | collective-permute-start | bytes 393224 | tf_op jit(solution)/shard_map/ppermute | solution.py:601
  23.9 13.6 %collective-permute-start.6 = (bf16[256,256]{1,0:T(8,128)(2,1)S(1)}, bf16[256,256]{1,0:T(8,128)(2,1)S(1)}, u32[]{:S(2)}, u32[]{:S(2)}) collective-permute-start(bf16[256,256]{1,0:T(8,128)(2,1)S(1)} %get-tuple-element.45), channel_id=1, source_target_pairs={{0,26},{2,24},{4,30},{6,28},{8,18},{10,16},{12,22},{14,20},{16,10}... | collective-permute-start | bytes 393224 | tf_op jit(solution)/shard_map/ppermute | solution.py:601
  26.3 11.2 %collective-permute-start.7 = (bf16[256,256]{1,0:T(8,128)(2,1)S(1)}, bf16[256,256]{1,0:T(8,128)(2,1)S(1)}, u32[]{:S(2)}, u32[]{:S(2)}) collective-permute-start(bf16[256,256]{1,0:T(8,128)(2,1)S(1)} %get-tuple-element.46), channel_id=1, source_target_pairs={{0,8},{2,10},{4,12},{6,14},{8,0},{10,2},{12,4},{14,6},{16,24},{18,... | collective-permute-start | bytes 393224 | tf_op jit(solution)/shard_map/ppermute | solution.py:601
  26.3 15.7 %collective-permute-start.8 = (bf16[256,256]{1,0:T(8,128)(2,1)S(1)}, bf16[256,256]{1,0:T(8,128)(2,1)S(1)}, u32[]{:S(2)}, u32[]{:S(2)}) collective-permute-start(bf16[256,256]{1,0:T(8,128)(2,1)S(1)} %get-tuple-element.47), channel_id=1, source_target_pairs={{0,20},{2,22},{4,16},{6,18},{8,28},{10,30},{12,24},{14,26},{16,4},... | collective-permute-start | bytes 393224 | tf_op jit(solution)/shard_map/ppermute | solution.py:601
  28.9 13.1 %collective-permute-start.9 = (bf16[256,256]{1,0:T(8,128)(2,1)S(1)}, bf16[256,256]{1,0:T(8,128)(2,1)S(1)}, u32[]{:S(2)}, u32[]{:S(2)}) collective-permute-start(bf16[256,256]{1,0:T(8,128)(2,1)S(1)} %get-tuple-element.48), channel_id=1, source_target_pairs={{0,10},{2,8},{4,14},{6,12},{8,2},{10,0},{12,6},{14,4},{16,26},{18,... | collective-permute-start | bytes 393224 | tf_op jit(solution)/shard_map/ppermute | solution.py:601
  30.4 14.0 %collective-permute-start.10 = (bf16[256,256]{1,0:T(8,128)(2,1)S(1)}, bf16[256,256]{1,0:T(8,128)(2,1)S(1)}, u32[]{:S(2)}, u32[]{:S(2)}) collective-permute-start(bf16[256,256]{1,0:T(8,128)(2,1)S(1)} %get-tuple-element.49), channel_id=1, source_target_pairs={{0,28},{2,30},{4,24},{6,26},{8,20},{10,22},{12,16},{14,18},{16,12}... | collective-permute-start | bytes 393224 | tf_op jit(solution)/shard_map/ppermute | solution.py:601
  37.5 14.6 %collective-permute-start.12 = (bf16[256,256]{1,0:T(8,128)(2,1)S(1)}, bf16[256,256]{1,0:T(8,128)(2,1)S(1)}, u32[]{:S(2)}, u32[]{:S(2)}) collective-permute-start(bf16[256,256]{1,0:T(8,128)(2,1)S(1)} %get-tuple-element.51), channel_id=1, source_target_pairs={{0,22},{2,20},{4,18},{6,16},{8,30},{10,28},{12,26},{14,24},{16,6},... | collective-permute-start | bytes 393224 | tf_op jit(solution)/shard_map/ppermute | solution.py:601
  42.1 10.1 %collective-permute-start.13 = (bf16[256,256]{1,0:T(8,128)(2,1)S(1)}, bf16[256,256]{1,0:T(8,128)(2,1)S(1)}, u32[]{:S(2)}, u32[]{:S(2)}) collective-permute-start(bf16[256,256]{1,0:T(8,128)(2,1)S(1)} %get-tuple-element.52), channel_id=1, source_target_pairs={{0,14},{2,12},{4,10},{6,8},{8,6},{10,4},{12,2},{14,0},{16,30},{18,... | collective-permute-start | bytes 393224 | tf_op jit(solution)/shard_map/ppermute | solution.py:601
  42.1 12.4 %collective-permute-start.14 = (bf16[256,256]{1,0:T(8,128)(2,1)S(1)}, bf16[256,256]{1,0:T(8,128)(2,1)S(1)}, u32[]{:S(2)}, u32[]{:S(2)}) collective-permute-start(bf16[256,256]{1,0:T(8,128)(2,1)S(1)} %get-tuple-element.53), channel_id=1, source_target_pairs={{0,30},{2,28},{4,26},{6,24},{8,22},{10,20},{12,18},{14,16},{16,14}... | collective-permute-start | bytes 393224 | tf_op jit(solution)/shard_map/ppermute | solution.py:601
  71.0 9.6 %collective-permute-start.17 = (bf16[256,128]{1,0:T(8,128)(2,1)S(1)}, bf16[256,128]{1,0:T(8,128)(2,1)S(1)}, u32[]{:S(2)}, u32[]{:S(2)}) collective-permute-start(bf16[256,128]{1,0:T(8,128)(2,1)S(1)} %get-tuple-element.57), channel_id=1, source_target_pairs={{0,24},{2,26},{4,28},{6,30},{8,16},{10,18},{12,20},{14,22},{16,8},... | collective-permute-start | bytes 196616 | tf_op jit(solution)/shard_map/ppermute | solution.py:601
  72.1 8.5 %collective-permute-start.18 = (bf16[256,128]{1,0:T(8,128)(2,1)S(1)}, bf16[256,128]{1,0:T(8,128)(2,1)S(1)}, u32[]{:S(2)}, u32[]{:S(2)}) collective-permute-start(bf16[256,128]{1,0:T(8,128)(2,1)S(1)} %get-tuple-element.58), channel_id=1, source_target_pairs={{0,4},{2,6},{4,0},{6,2},{8,12},{10,14},{12,8},{14,10},{16,20},{18,... | collective-permute-start | bytes 196616 | tf_op jit(solution)/shard_map/ppermute | solution.py:601
  72.6 8.8 %collective-permute-start.19 = (bf16[256,128]{1,0:T(8,128)(2,1)S(1)}, bf16[256,128]{1,0:T(8,128)(2,1)S(1)}, u32[]{:S(2)}, u32[]{:S(2)}) collective-permute-start(bf16[256,128]{1,0:T(8,128)(2,1)S(1)} %get-tuple-element.59), channel_id=1, source_target_pairs={{0,18},{2,16},{4,22},{6,20},{8,26},{10,24},{12,30},{14,28},{16,2},... | collective-permute-start | bytes 196616 | tf_op jit(solution)/shard_map/ppermute | solution.py:601
  74.3 8.4 %collective-permute-start.20 = (bf16[256,128]{1,0:T(8,128)(2,1)S(1)}, bf16[256,128]{1,0:T(8,128)(2,1)S(1)}, u32[]{:S(2)}, u32[]{:S(2)}) collective-permute-start(bf16[256,128]{1,0:T(8,128)(2,1)S(1)} %get-tuple-element.60), channel_id=1, source_target_pairs={{0,6},{2,4},{4,2},{6,0},{8,14},{10,12},{12,10},{14,8},{16,22},{18,... | collective-permute-start | bytes 196616 | tf_op jit(solution)/shard_map/ppermute | solution.py:601
  75.3 10.7 %collective-permute-start.21 = (bf16[256,128]{1,0:T(8,128)(2,1)S(1)}, bf16[256,128]{1,0:T(8,128)(2,1)S(1)}, u32[]{:S(2)}, u32[]{:S(2)}) collective-permute-start(bf16[256,128]{1,0:T(8,128)(2,1)S(1)} %get-tuple-element.61), channel_id=1, source_target_pairs={{0,26},{2,24},{4,30},{6,28},{8,18},{10,16},{12,22},{14,20},{16,10}... | collective-permute-start | bytes 196616 | tf_op jit(solution)/shard_map/ppermute | solution.py:601
  80.6 9.8 %collective-permute-start.23 = (bf16[256,128]{1,0:T(8,128)(2,1)S(1)}, bf16[256,128]{1,0:T(8,128)(2,1)S(1)}, u32[]{:S(2)}, u32[]{:S(2)}) collective-permute-start(bf16[256,128]{1,0:T(8,128)(2,1)S(1)} %get-tuple-element.63), channel_id=1, source_target_pairs={{0,20},{2,22},{4,16},{6,18},{8,28},{10,30},{12,24},{14,26},{16,4},... | collective-permute-start | bytes 196616 | tf_op jit(solution)/shard_map/ppermute | solution.py:601
  81.4 9.0 %collective-permute-start.24 = (bf16[256,128]{1,0:T(8,128)(2,1)S(1)}, bf16[256,128]{1,0:T(8,128)(2,1)S(1)}, u32[]{:S(2)}, u32[]{:S(2)}) collective-permute-start(bf16[256,128]{1,0:T(8,128)(2,1)S(1)} %get-tuple-element.64), channel_id=1, source_target_pairs={{0,10},{2,8},{4,14},{6,12},{8,2},{10,0},{12,6},{14,4},{16,26},{18,... | collective-permute-start | bytes 196616 | tf_op jit(solution)/shard_map/ppermute | solution.py:601
  82.8 12.2 %collective-permute-start.25 = (bf16[256,128]{1,0:T(8,128)(2,1)S(1)}, bf16[256,128]{1,0:T(8,128)(2,1)S(1)}, u32[]{:S(2)}, u32[]{:S(2)}) collective-permute-start(bf16[256,128]{1,0:T(8,128)(2,1)S(1)} %get-tuple-element.65), channel_id=1, source_target_pairs={{0,28},{2,30},{4,24},{6,26},{8,20},{10,22},{12,16},{14,18},{16,12}... | collective-permute-start | bytes 196616 | tf_op jit(solution)/shard_map/ppermute | solution.py:601
  86.0 9.1 %collective-permute-start.26 = (bf16[256,128]{1,0:T(8,128)(2,1)S(1)}, bf16[256,128]{1,0:T(8,128)(2,1)S(1)}, u32[]{:S(2)}, u32[]{:S(2)}) collective-permute-start(bf16[256,128]{1,0:T(8,128)(2,1)S(1)} %get-tuple-element.66), channel_id=1, source_target_pairs={{0,12},{2,14},{4,8},{6,10},{8,4},{10,6},{12,0},{14,2},{16,28},{18,... | collective-permute-start | bytes 196616 | tf_op jit(solution)/shard_map/ppermute | solution.py:601
  86.5 8.9 %collective-permute-start.27 = (bf16[256,128]{1,0:T(8,128)(2,1)S(1)}, bf16[256,128]{1,0:T(8,128)(2,1)S(1)}, u32[]{:S(2)}, u32[]{:S(2)}) collective-permute-start(bf16[256,128]{1,0:T(8,128)(2,1)S(1)} %get-tuple-element.67), channel_id=1, source_target_pairs={{0,22},{2,20},{4,18},{6,16},{8,30},{10,28},{12,26},{14,24},{16,6},... | collective-permute-start | bytes 196616 | tf_op jit(solution)/shard_map/ppermute | solution.py:601
  (11 other events, 133.4 us)

commit v12 on v9

--- a/solution.py
+++ b/solution.py
@@ -15,7 +15,8 @@
 RADIX = 16
 LANES = 128
 Q_ORDER = [low + 4 * high for low in range(4) for high in range(4)]
-ARRANGE_BYTES = 60 * 1024 * 1024
+FIRST_BYTES = 60 * 1024 * 1024
+ARRANGE_BYTES = 12 * 1024 * 1024
 CONV_BYTES = 49 * 1024 * 1024
 TAIL_BYTES = 49 * 1024 * 1024
 
@@ -193,9 +194,29 @@
     return [slot for pair in zip(across, near) for slot in pair]
 
 
+LEAD = 4
+
+
+def lead_kernel(blocks, me_ref, values_hbm, taps_hbm, *rest):
+    outs, (streams, sems) = rest[:LEAD], rest[LEAD:]
+    loads = []
+    for i, slot in enumerate(slot_order(blocks)[:LEAD]):
+        lanes = pl.ds(pl.multiple_of((me_ref[0] ^ slot) * LANES, LANES), LANES)
+        for side, source in enumerate((values_hbm, taps_hbm)):
+            to = pl.ds((2 * i + side) * LANES, LANES)
+            loads.append(pltpu.make_async_copy(source.at[:, lanes], streams.at[:, to], sems.at[2 * i + side]))
+    for load in loads:
+        load.start()
+    order = row_order(streams.shape[0])
+    for load in loads:
+        load.wait()
+    moved = jnp.dot(order, streams[...], preferred_element_type=jnp.float32).astype(jnp.bfloat16)
+    for i, out in enumerate(outs):
+        out[...] = moved[:, 2 * i * LANES : 2 * (i + 1) * LANES]
+
+
 def arrange_kernel(pieces, blocks, me_ref, values_hbm, taps_hbm, *rest):
-    outs = rest[:blocks]
-    values_ref, taps_ref, packed, sems = rest[blocks:]
+    outs, (values_ref, taps_ref, packed, sems) = rest[: blocks - LEAD], rest[blocks - LEAD :]
     piece = values_ref.shape[1] // pieces
     loads = []
     for part in range(pieces):
@@ -215,18 +236,35 @@
             for side in range(2):
                 start = side * piece + block * LANES
                 packed[part * piece // LANES + block, :, pl.ds(side * LANES, LANES)] = moved[:, start : start + LANES]
-    for out, slot in zip(outs, slot_order(blocks)):
+    for out, slot in zip(outs, slot_order(blocks)[LEAD:]):
         out[...] = packed[me_ref[0] ^ slot]
 
 
 def arrange(me, values, taps, blocks):
     rows, wide = values.shape
     pieces = 4
-    return pl.pallas_call(
+    block = jax.ShapeDtypeStruct((rows, 2 * LANES), jnp.bfloat16)
+    in_specs = [pl.BlockSpec(memory_space=pltpu.SMEM)] + [pl.BlockSpec(memory_space=pl.ANY)] * 2
+    lead = pl.pallas_call(
+        functools.partial(lead_kernel, blocks),
+        in_specs=in_specs,
+        out_specs=[pl.BlockSpec(memory_space=pltpu.VMEM)] * LEAD,
+        out_shape=[block] * LEAD,
+        scratch_shapes=[
+            pltpu.VMEM((rows, 2 * LEAD * LANES), jnp.bfloat16),
+            pltpu.SemaphoreType.DMA((2 * LEAD,)),
+        ],
+        compiler_params=pltpu.CompilerParams(vmem_limit_bytes=FIRST_BYTES),
+        cost_estimate=pl.CostEstimate(
+            flops=4 * rows * rows * LEAD * LANES, bytes_accessed=8 * rows * LEAD * LANES, transcendentals=0
+        ),
+        name="arrange_lead",
+    )(me, values, taps)
+    others = pl.pallas_call(
         functools.partial(arrange_kernel, pieces, blocks),
-        in_specs=[pl.BlockSpec(memory_space=pltpu.SMEM)] + [pl.BlockSpec(memory_space=pl.ANY)] * 2,
-        out_specs=[pl.BlockSpec(memory_space=pltpu.VMEM)] * blocks,
-        out_shape=[jax.ShapeDtypeStruct((rows, 2 * LANES), jnp.bfloat16)] * blocks,
+        in_specs=in_specs,
+        out_specs=[pl.BlockSpec(memory_space=pltpu.VMEM)] * (blocks - LEAD),
+        out_shape=[block] * (blocks - LEAD),
         scratch_shapes=[
             pltpu.VMEM((rows, wide), jnp.bfloat16),
             pltpu.VMEM((rows, wide), jnp.bfloat16),
@@ -237,8 +275,9 @@
         cost_estimate=pl.CostEstimate(
             flops=4 * rows * rows * wide, bytes_accessed=8 * rows * wide, transcendentals=0
         ),
-        name="arrange_rows",
+        name="arrange_others",
     )(me, values, taps)
+    return [*lead, *others]
 
 
 def convolve_kernel(blocks, me_ref, *rest):
@@ -258,26 +297,35 @@
     raws = (raw_even, raw_odd)
     halves = (halves_even, halves_odd)
     count = fixed.shape[0]
-    load_fixed = pltpu.make_async_copy(tables_hbm.at[pl.ds(2 * RADIX, count)], fixed, sems.at[0])
+    load_fixed = []
+    for part in range(2):
+        taken = pl.ds(part * count // 2, count // 2)
+        source = tables_hbm.at[pl.ds(2 * RADIX + part * count // 2, count // 2)]
+        load_fixed.append(pltpu.make_async_copy(source, fixed.at[taken], sems.at[10 * part]))
     load_turns, stores = [], []
     for low in range(4):
         taken = pl.ds(low * group, group)
         eight = pl.ds(8 * low, 8)
         load_turns.append(pltpu.make_async_copy(tables_hbm.at[eight], turns_ref.at[eight], sems.at[1 + low]))
         stores.append(pltpu.make_async_copy(signals.at[:, taken], out_hbm.at[:, taken], sems.at[5 + low]))
-    load_fixed.start()
+    load_fixed[0].start()
     for load in load_turns:
         load.start()
+    load_fixed[1].start()
     own = pltpu.make_async_copy(slots[-1], streams.at[me_ref[0]], sems.at[9])
     own.start()
     for slot, source in zip(slot_order(blocks)[:-1], slots[:-1]):
         streams[me_ref[0] ^ slot] = source[...]
     own.wait()
-    load_fixed.wait()
     width = inner // LANES
-    for table in range(4):
-        for block in range(width):
-            stages[table, :, pl.ds(block * LANES, LANES)] = fixed[table * width + block].astype(jnp.bfloat16)
+
+    def take_stages(part):
+        load_fixed[part].wait()
+        for table in range(2 * part, 2 * part + 2):
+            for block in range(width):
+                stages[table, :, pl.ds(block * LANES, LANES)] = fixed[table * width + block].astype(jnp.bfloat16)
+
+    take_stages(0)
 
     def transform(low, pair):
         sides = [[], []]
@@ -408,6 +456,7 @@
         last_rows(0, index * steps, steps // 16)
         return carry
 
+    take_stages(1)
     lax.fori_loop(0, 2, prepare, 0)
     for low in range(4):
 
@@ -448,7 +497,7 @@
             pltpu.VMEM((4, 2, inner, lanes), jnp.bfloat16),
             pltpu.VMEM((4, 2, inner, lanes), jnp.bfloat16),
             pltpu.VMEM((blocks, rows, LANES), jnp.bfloat16),
-            pltpu.SemaphoreType.DMA((10,)),
+            pltpu.SemaphoreType.DMA((11,)),
         ],
         compiler_params=pltpu.CompilerParams(vmem_limit_bytes=CONV_BYTES),
         cost_estimate=pl.CostEstimate(flops=5 * 10**9, bytes_accessed=9 * 10**6, transcendentals=0),

time: 104 us -> 103 us (level)
  waiting for transfers between devices: 46.6 us -> 37.3 us
  starting transfers between devices: 34.6 us -> 40.7 us
  local copies, waits for them, and re-layouts: 0.91 us -> 2.46 us
    ppermute x15, waiting for transfers between devices: 22 us -> 12.7 us  [exchange(): lax.ppermute(source, 'seq', [(j, j ^ slot) for j in range(blocks)])]
    ppermute x15, starting transfers between devices: 28.2 us -> 35 us  [exchange(): lax.ppermute(source, 'seq', [(j, j ^ slot) for j in range(blocks)])]
    pallas_call x0 -> x1, Pallas kernels: none -> 2.17 us  [arrange(): pl.pallas_call(functools.partial(lead_kernel, blocks), in_specs=in_specs,...]
    pallas_call x1, Pallas kernels: 3.63 us -> 1.74 us  [arrange(): pl.pallas_call(functools.partial(arrange_kernel, pieces, blocks), in_spec...]
    unnamed x6 -> x8, local copies, waits for them, and re-layouts: 0.91 us -> 2.46 us
  transfers between devices with their start and end apart: 17 -> 17, of which waited for: 9 -> 7; matrix products, arithmetic and copies ran while one was open for 0% -> 0% of each run, Pallas kernels for 3% -> 4%
where the time goes in v12:
time: 103 us; the launch traced here: 102 us
  starting transfers between devices  40.7 us (40%)
  waiting for transfers between devices  37.3 us (36%)
  Pallas kernels  21.1 us (20%)
  local copies, waits for them, and re-layouts  2.46 us (2%)
    ppermute x15, starting transfers between devices, exchange(): lax.ppermute(source, 'seq', [(j, j ^ slot) for j in range(blocks)])  35 us
    all_to_all x1, waiting for transfers between devices, swap_blocks(): return lax.all_to_all(array, 'seq', split_axis=0, concat_axis=0, tiled=True)  24.6 us
    ppermute x15, waiting for transfers between devices, exchange(): lax.ppermute(source, 'seq', [(j, j ^ slot) for j in range(blocks)])  12.7 us
    pallas_call x1, Pallas kernels, convolve(): pl.pallas_call(functools.partial(convolve_kernel, blocks), in_specs=[pl.B...  10.3 us
    all_to_all x1, starting transfers between devices, swap_blocks(): return lax.all_to_all(array, 'seq', split_axis=0, concat_axis=0, tiled=True)  5.62 us
    pallas_call x1, Pallas kernels, gate_and_project(): pl.pallas_call(gate_kernel, in_specs=[pl.BlockSpec(memory_space=pltpu.SME...  3.31 us
    pallas_call x1, Pallas kernels, project_kept(): pl.pallas_call(kept_kernel, in_specs=[pl.BlockSpec(memory_space=pltpu.SME...  2.68 us
    unnamed x8, local copies, waits for them, and re-layouts  2.46 us
  transfers between devices with their start and end apart: 17, of which 7 were waited for; matrix products, arithmetic and copies ran while one was open for 0% of the time, Pallas kernels for 4%

profile of v12, /device:TPU:0, one launch (start us, length us, event | category | flops | bytes accessed | tf_op | source)
XLA Modules:
  0.0 101.6 jit_solution(12472082902074831229)
XLA Ops:
  0.0 2.2 %arrange_lead.1 = (bf16[256,256]{1,0:T(8,128)(2,1)}, bf16[256,256]{1,0:T(8,128)(2,1)}, bf16[256,256]{1,0:T(8,128)(2,1)}, bf16[256,256]{1,0:T(8,128)(2,1)}) custom-call(s32[1]{0:T(128)} %bitcast.1.me_ref, bf16[256,2048]{1,0:T(8,128)(2,1)} %values_hbm.5, bf16[256,2048]{1,0:T(8,128)(2,1)} %taps_hbm.3), custom_call_target="tpu_custom_call" | custom-call | flops 134217728 | bytes 1048576 | tf_op jit(solution)/shard_map/arrange_lead/pallas_call | solution.py:248
  2.2 4.1 %collective-permute-start = (bf16[256,256]{1,0:T(8,128)(2,1)}, bf16[256,256]{1,0:T(8,128)(2,1)S(1)}, u32[]{:S(2)}, u32[]{:S(2)}) collective-permute-start(bf16[256,256]{1,0:T(8,128)(2,1)} %get-tuple-element.23), channel_id=1, source_target_pairs={{0,16},{2,18},{4,20},{6,22},{8,24},{10,26},{12,28},{14,30},{16,0},... | collective-permute-start | bytes 393224 | tf_op jit(solution)/shard_map/ppermute | solution.py:638
  6.3 1.5 %collective-permute-start.1 = (bf16[256,256]{1,0:T(8,128)(2,1)}, bf16[256,256]{1,0:T(8,128)(2,1)S(1)}, u32[]{:S(2)}, u32[]{:S(2)}) collective-permute-start(bf16[256,256]{1,0:T(8,128)(2,1)} %get-tuple-element.24), channel_id=1, source_target_pairs={{0,2},{2,0},{4,6},{6,4},{8,10},{10,8},{12,14},{14,12},{16,18},{18,... | collective-permute-start | bytes 393224 | tf_op jit(solution)/shard_map/ppermute | solution.py:638
  7.8 1.3 %collective-permute-start.2 = (bf16[256,256]{1,0:T(8,128)(2,1)}, bf16[256,256]{1,0:T(8,128)(2,1)S(1)}, u32[]{:S(2)}, u32[]{:S(2)}) collective-permute-start(bf16[256,256]{1,0:T(8,128)(2,1)} %get-tuple-element.25), channel_id=1, source_target_pairs={{0,24},{2,26},{4,28},{6,30},{8,16},{10,18},{12,20},{14,22},{16,8},... | collective-permute-start | bytes 393224 | tf_op jit(solution)/shard_map/ppermute | solution.py:638
  9.1 1.5 %collective-permute-start.3 = (bf16[256,256]{1,0:T(8,128)(2,1)}, bf16[256,256]{1,0:T(8,128)(2,1)S(1)}, u32[]{:S(2)}, u32[]{:S(2)}) collective-permute-start(bf16[256,256]{1,0:T(8,128)(2,1)} %get-tuple-element.26), channel_id=1, source_target_pairs={{0,4},{2,6},{4,0},{6,2},{8,12},{10,14},{12,8},{14,10},{16,20},{18,... | collective-permute-start | bytes 393224 | tf_op jit(solution)/shard_map/ppermute | solution.py:638
  13.1 1.7 %arrange_others.1 = (bf16[256,256]{1,0:T(8,128)(2,1)S(1)}, bf16[256,256]{1,0:T(8,128)(2,1)S(1)}, bf16[256,256]{1,0:T(8,128)(2,1)S(1)}, bf16[256,256]{1,0:T(8,128...) custom-call(s32[1]{0:T(128)} %bitcast.1.me_ref, ...), custom_call_target="tpu_custom_call" | custom-call | flops 536870912 | bytes 4194304 | tf_op jit(solution)/shard_map/arrange_others/pallas_call | solution.py:263
  14.8 1.7 %collective-permute-start.4 = (bf16[256,256]{1,0:T(8,128)(2,1)S(1)}, bf16[256,256]{1,0:T(8,128)(2,1)S(1)}, u32[]{:S(2)}, u32[]{:S(2)}) collective-permute-start(bf16[256,256]{1,0:T(8,128)(2,1)S(1)} %get-tuple-element.27), channel_id=1, source_target_pairs={{0,18},{2,16},{4,22},{6,20},{8,26},{10,24},{12,30},{14,28},{16,2},... | collective-permute-start | bytes 393224 | tf_op jit(solution)/shard_map/ppermute | solution.py:638
  16.6 5.5 %collective-permute-start.5 = (bf16[256,256]{1,0:T(8,128)(2,1)S(1)}, bf16[256,256]{1,0:T(8,128)(2,1)S(1)}, u32[]{:S(2)}, u32[]{:S(2)}) collective-permute-start(bf16[256,256]{1,0:T(8,128)(2,1)S(1)} %get-tuple-element.28), channel_id=1, source_target_pairs={{0,6},{2,4},{4,2},{6,0},{8,14},{10,12},{12,10},{14,8},{16,22},{18,... | collective-permute-start | bytes 393224 | tf_op jit(solution)/shard_map/ppermute | solution.py:638
  23.1 2.8 %collective-permute-start.8 = (bf16[256,256]{1,0:T(8,128)(2,1)S(1)}, bf16[256,256]{1,0:T(8,128)(2,1)S(1)}, u32[]{:S(2)}, u32[]{:S(2)}) collective-permute-start(bf16[256,256]{1,0:T(8,128)(2,1)S(1)} %get-tuple-element.31), channel_id=1, source_target_pairs={{0,20},{2,22},{4,16},{6,18},{8,28},{10,30},{12,24},{14,26},{16,4},... | collective-permute-start | bytes 393224 | tf_op jit(solution)/shard_map/ppermute | solution.py:638
  25.9 1.7 %collective-permute-done.4.rest_4_ = bf16[256,256]{1,0:T(8,128)(2,1)S(1)} collective-permute-done((bf16[256,256]{1,0:T(8,128)(2,1)S(1)}, bf16[256,256]{1,0:T(8,128)(2,1)S(1)}, u32[]{:S(2)}, u32[]{:S(2)}) %collective-permute-start.4) | collective-permute-done | bytes 131104 | tf_op jit(solution)/shard_map/ppermute | solution.py:638
  27.9 1.7 %collective-permute-done.5.rest_5_ = bf16[256,256]{1,0:T(8,128)(2,1)S(1)} collective-permute-done((bf16[256,256]{1,0:T(8,128)(2,1)S(1)}, bf16[256,256]{1,0:T(8,128)(2,1)S(1)}, u32[]{:S(2)}, u32[]{:S(2)}) %collective-permute-start.5) | collective-permute-done | bytes 131104 | tf_op jit(solution)/shard_map/ppermute | solution.py:638
  29.6 4.2 %collective-permute-start.10 = (bf16[256,256]{1,0:T(8,128)(2,1)S(1)}, bf16[256,256]{1,0:T(8,128)(2,1)S(1)}, u32[]{:S(2)}, u32[]{:S(2)}) collective-permute-start(bf16[256,256]{1,0:T(8,128)(2,1)S(1)} %get-tuple-element.33), channel_id=1, source_target_pairs={{0,28},{2,30},{4,24},{6,26},{8,20},{10,22},{12,16},{14,18},{16,12}... | collective-permute-start | bytes 393224 | tf_op jit(solution)/shard_map/ppermute | solution.py:638
  33.8 2.3 %collective-permute-start.11 = (bf16[256,256]{1,0:T(8,128)(2,1)S(1)}, bf16[256,256]{1,0:T(8,128)(2,1)S(1)}, u32[]{:S(2)}, u32[]{:S(2)}) collective-permute-start(bf16[256,256]{1,0:T(8,128)(2,1)S(1)} %get-tuple-element.34), channel_id=1, source_target_pairs={{0,12},{2,14},{4,8},{6,10},{8,4},{10,6},{12,0},{14,2},{16,28},{18,... | collective-permute-start | bytes 393224 | tf_op jit(solution)/shard_map/ppermute | solution.py:638
  36.1 1.9 %collective-permute-start.12 = (bf16[256,256]{1,0:T(8,128)(2,1)S(1)}, bf16[256,256]{1,0:T(8,128)(2,1)S(1)}, u32[]{:S(2)}, u32[]{:S(2)}) collective-permute-start(bf16[256,256]{1,0:T(8,128)(2,1)S(1)} %get-tuple-element.35), channel_id=1, source_target_pairs={{0,22},{2,20},{4,18},{6,16},{8,30},{10,28},{12,26},{14,24},{16,6},... | collective-permute-start | bytes 393224 | tf_op jit(solution)/shard_map/ppermute | solution.py:638
  38.0 4.6 %collective-permute-start.13 = (bf16[256,256]{1,0:T(8,128)(2,1)S(1)}, bf16[256,256]{1,0:T(8,128)(2,1)S(1)}, u32[]{:S(2)}, u32[]{:S(2)}) collective-permute-start(bf16[256,256]{1,0:T(8,128)(2,1)S(1)} %get-tuple-element.36), channel_id=1, source_target_pairs={{0,14},{2,12},{4,10},{6,8},{8,6},{10,4},{12,2},{14,0},{16,30},{18,... | collective-permute-start | bytes 393224 | tf_op jit(solution)/shard_map/ppermute | solution.py:638
  42.7 2.1 %collective-permute-start.14 = (bf16[256,256]{1,0:T(8,128)(2,1)S(1)}, bf16[256,256]{1,0:T(8,128)(2,1)S(1)}, u32[]{:S(2)}, u32[]{:S(2)}) collective-permute-start(bf16[256,256]{1,0:T(8,128)(2,1)S(1)} %get-tuple-element.37), channel_id=1, source_target_pairs={{0,30},{2,28},{4,26},{6,24},{8,22},{10,20},{12,18},{14,16},{16,14}... | collective-permute-start | bytes 393224 | tf_op jit(solution)/shard_map/ppermute | solution.py:638
  44.7 2.4 %collective-permute-done.11.rest_11_ = bf16[256,256]{1,0:T(8,128)(2,1)S(1)} collective-permute-done((bf16[256,256]{1,0:T(8,128)(2,1)S(1)}, bf16[256,256]{1,0:T(8,128)(2,1)S(1)}, u32[]{:S(2)}, u32[]{:S(2)}) %collective-permute-start.11) | collective-permute-done | bytes 131104 | tf_op jit(solution)/shard_map/ppermute | solution.py:638
  47.1 2.5 %collective-permute-done.12.rest_12_ = bf16[256,256]{1,0:T(8,128)(2,1)S(1)} collective-permute-done((bf16[256,256]{1,0:T(8,128)(2,1)S(1)}, bf16[256,256]{1,0:T(8,128)(2,1)S(1)}, u32[]{:S(2)}, u32[]{:S(2)}) %collective-permute-start.12) | collective-permute-done | bytes 131104 | tf_op jit(solution)/shard_map/ppermute | solution.py:638
  49.9 4.1 %collective-permute-done.14.rest_14_ = bf16[256,256]{1,0:T(8,128)(2,1)S(1)} collective-permute-done((bf16[256,256]{1,0:T(8,128)(2,1)S(1)}, bf16[256,256]{1,0:T(8,128)(2,1)S(1)}, u32[]{:S(2)}, u32[]{:S(2)}) %collective-permute-start.14) | collective-permute-done | bytes 131104 | tf_op jit(solution)/shard_map/ppermute | solution.py:638
  54.1 10.3 %long_convolution.1 = bf16[16,256,128]{2,1,0:T(8,128)(2,1)} custom-call(s32[1]{0:T(128)} %bitcast.1.me_ref, bf16[256,256]{1,0:T(8,128)(2,1)S(1)} %collective-permute-done.rest_0_, bf16[256,256]{1,0:T(8,128)(2,1)S(1)} %collective-permute-done.1.rest_1_, bf16[256,256]{1,0:T(8,128)(2,1)S(1)} %collective-permute-done.2.rest_2_, ...), custom_call_target="tpu_custom_call" | custom-call | flops 5000000000 | bytes 9000000 | tf_op jit(solution)/shard_map/long_convolution/pallas_call | solution.py:481
  64.4 5.6 %all-to-all-start = ((bf16[16,256,128]{2,1,0:T(8,128)(2,1)}), bf16[16,256,128]{2,1,0:T(8,128)(2,1)S(1)}, u32[]{:S(2)}, u32[]{:S(2)}) async-start(bf16[16,256,128]{2,1,0:T(8,128)(2,1)} %long_convolution.1), calls=%async_computation | async-start | bytes 2097152 | tf_op jit(solution)/shard_map/all_to_all | solution.py:632
  70.0 24.6 %all-to-all-done.conv_ref = bf16[16,256,128]{2,1,0:T(8,128)(2,1)S(1)} async-done(((bf16[16,256,128]{2,1,0:T(8,128)(2,1)}), bf16[16,256,128]{2,1,0:T(8,128)(2,1)S(1)}, u32[]{:S(2)}, u32[]{:S(2)}) %all-to-all-start) | async-done | bytes 1048608 | tf_op jit(solution)/shard_map/all_to_all | solution.py:632
  94.6 3.3 %gate_project_sent.1 = (bf16[256,2048]{1,0:T(8,128)(2,1)S(1)}, f32[256,1024]{1,0:T(8,128)S(1)}) custom-call(s32[1]{0:T(128)} %bitcast.half_ref, bf16[16,256,128]{2,1,0:T(8,128)(2,1)S(1)} %all-to-all-done.conv_ref, bf16[256,2048]{1,0:T(8,128)(2,1)S(1)} %copy-done.2, bf16[256,2048]{1,0:T(8,128)(2,1)} %values_hbm.5, f32[1,2048]{1,0:T(1,128)S(1)} %bitcast.3, ...), custom_call_target="tpu_custom_call" | custom-call | flops 1073741824 | bytes 4194304 | tf_op jit(solution)/shard_map/gate_project_sent/pallas_call | solution.py:562
  98.0 2.7 %project_kept.1.kept_ref = f32[256,1024]{1,0:T(8,128)S(1)} custom-call(s32[1]{0:T(128)} %bitcast.half_ref, bf16[256,2048]{1,0:T(8,128)(2,1)S(1)} %get-tuple-element.39.gated_ref, bf16[2048,2048]{1,0:T(8,128)(2,1)} %weight_hbm.3), custom_call_target="tpu_custom_call" | custom-call | flops 1073741824 | bytes 4194304 | tf_op jit(solution)/shard_map/project_kept/pallas_call | solution.py:592
  (24 shorter events, 5.1 us)
Async XLA Ops:
  2.2 14.4 %collective-permute-start = (bf16[256,256]{1,0:T(8,128)(2,1)}, bf16[256,256]{1,0:T(8,128)(2,1)S(1)}, u32[]{:S(2)}, u32[]{:S(2)}) collective-permute-start(bf16[256,256]{1,0:T(8,128)(2,1)} %get-tuple-element.23), channel_id=1, source_target_pairs={{0,16},{2,18},{4,20},{6,22},{8,24},{10,26},{12,28},{14,30},{16,0},... | collective-permute-start | bytes 393224 | tf_op jit(solution)/shard_map/ppermute | solution.py:638
  6.3 15.8 %collective-permute-start.1 = (bf16[256,256]{1,0:T(8,128)(2,1)}, bf16[256,256]{1,0:T(8,128)(2,1)S(1)}, u32[]{:S(2)}, u32[]{:S(2)}) collective-permute-start(bf16[256,256]{1,0:T(8,128)(2,1)} %get-tuple-element.24), channel_id=1, source_target_pairs={{0,2},{2,0},{4,6},{6,4},{8,10},{10,8},{12,14},{14,12},{16,18},{18,... | collective-permute-start | bytes 393224 | tf_op jit(solution)/shard_map/ppermute | solution.py:638
  7.8 15.3 %collective-permute-start.2 = (bf16[256,256]{1,0:T(8,128)(2,1)}, bf16[256,256]{1,0:T(8,128)(2,1)S(1)}, u32[]{:S(2)}, u32[]{:S(2)}) collective-permute-start(bf16[256,256]{1,0:T(8,128)(2,1)} %get-tuple-element.25), channel_id=1, source_target_pairs={{0,24},{2,26},{4,28},{6,30},{8,16},{10,18},{12,20},{14,22},{16,8},... | collective-permute-start | bytes 393224 | tf_op jit(solution)/shard_map/ppermute | solution.py:638
  9.1 14.0 %collective-permute-start.3 = (bf16[256,256]{1,0:T(8,128)(2,1)}, bf16[256,256]{1,0:T(8,128)(2,1)S(1)}, u32[]{:S(2)}, u32[]{:S(2)}) collective-permute-start(bf16[256,256]{1,0:T(8,128)(2,1)} %get-tuple-element.26), channel_id=1, source_target_pairs={{0,4},{2,6},{4,0},{6,2},{8,12},{10,14},{12,8},{14,10},{16,20},{18,... | collective-permute-start | bytes 393224 | tf_op jit(solution)/shard_map/ppermute | solution.py:638
  10.6 1.2 %copy-start = (bf16[256,2048]{1,0:T(8,128)(2,1)S(1)}, bf16[256,2048]{1,0:T(8,128)(2,1)}, u32[]{:S(2)}) copy-start(bf16[256,2048]{1,0:T(8,128)(2,1)} %values_hbm.5) | copy-start | bytes 3145732
  11.9 1.2 %copy-start.1 = (bf16[256,2048]{1,0:T(8,128)(2,1)S(1)}, bf16[256,2048]{1,0:T(8,128)(2,1)}, u32[]{:S(2)}) copy-start(bf16[256,2048]{1,0:T(8,128)(2,1)} %taps_hbm.3) | copy-start | bytes 3145732
  14.8 12.7 %collective-permute-start.4 = (bf16[256,256]{1,0:T(8,128)(2,1)S(1)}, bf16[256,256]{1,0:T(8,128)(2,1)S(1)}, u32[]{:S(2)}, u32[]{:S(2)}) collective-permute-start(bf16[256,256]{1,0:T(8,128)(2,1)S(1)} %get-tuple-element.27), channel_id=1, source_target_pairs={{0,18},{2,16},{4,22},{6,20},{8,26},{10,24},{12,30},{14,28},{16,2},... | collective-permute-start | bytes 393224 | tf_op jit(solution)/shard_map/ppermute | solution.py:638
  16.6 13.0 %collective-permute-start.5 = (bf16[256,256]{1,0:T(8,128)(2,1)S(1)}, bf16[256,256]{1,0:T(8,128)(2,1)S(1)}, u32[]{:S(2)}, u32[]{:S(2)}) collective-permute-start(bf16[256,256]{1,0:T(8,128)(2,1)S(1)} %get-tuple-element.28), channel_id=1, source_target_pairs={{0,6},{2,4},{4,2},{6,0},{8,14},{10,12},{12,10},{14,8},{16,22},{18,... | collective-permute-start | bytes 393224 | tf_op jit(solution)/shard_map/ppermute | solution.py:638
  22.0 11.8 %collective-permute-start.6 = (bf16[256,256]{1,0:T(8,128)(2,1)S(1)}, bf16[256,256]{1,0:T(8,128)(2,1)S(1)}, u32[]{:S(2)}, u32[]{:S(2)}) collective-permute-start(bf16[256,256]{1,0:T(8,128)(2,1)S(1)} %get-tuple-element.29), channel_id=1, source_target_pairs={{0,26},{2,24},{4,30},{6,28},{8,18},{10,16},{12,22},{14,20},{16,10}... | collective-permute-start | bytes 393224 | tf_op jit(solution)/shard_map/ppermute | solution.py:638
  23.1 13.0 %collective-permute-start.7 = (bf16[256,256]{1,0:T(8,128)(2,1)S(1)}, bf16[256,256]{1,0:T(8,128)(2,1)S(1)}, u32[]{:S(2)}, u32[]{:S(2)}) collective-permute-start(bf16[256,256]{1,0:T(8,128)(2,1)S(1)} %get-tuple-element.30), channel_id=1, source_target_pairs={{0,8},{2,10},{4,12},{6,14},{8,0},{10,2},{12,4},{14,6},{16,24},{18,... | collective-permute-start | bytes 393224 | tf_op jit(solution)/shard_map/ppermute | solution.py:638
  23.1 15.0 %collective-permute-start.8 = (bf16[256,256]{1,0:T(8,128)(2,1)S(1)}, bf16[256,256]{1,0:T(8,128)(2,1)S(1)}, u32[]{:S(2)}, u32[]{:S(2)}) collective-permute-start(bf16[256,256]{1,0:T(8,128)(2,1)S(1)} %get-tuple-element.31), channel_id=1, source_target_pairs={{0,20},{2,22},{4,16},{6,18},{8,28},{10,30},{12,24},{14,26},{16,4},... | collective-permute-start | bytes 393224 | tf_op jit(solution)/shard_map/ppermute | solution.py:638
  27.5 15.1 %collective-permute-start.9 = (bf16[256,256]{1,0:T(8,128)(2,1)S(1)}, bf16[256,256]{1,0:T(8,128)(2,1)S(1)}, u32[]{:S(2)}, u32[]{:S(2)}) collective-permute-start(bf16[256,256]{1,0:T(8,128)(2,1)S(1)} %get-tuple-element.32), channel_id=1, source_target_pairs={{0,10},{2,8},{4,14},{6,12},{8,2},{10,0},{12,6},{14,4},{16,26},{18,... | collective-permute-start | bytes 393224 | tf_op jit(solution)/shard_map/ppermute | solution.py:638
  29.6 15.2 %collective-permute-start.10 = (bf16[256,256]{1,0:T(8,128)(2,1)S(1)}, bf16[256,256]{1,0:T(8,128)(2,1)S(1)}, u32[]{:S(2)}, u32[]{:S(2)}) collective-permute-start(bf16[256,256]{1,0:T(8,128)(2,1)S(1)} %get-tuple-element.33), channel_id=1, source_target_pairs={{0,28},{2,30},{4,24},{6,26},{8,20},{10,22},{12,16},{14,18},{16,12}... | collective-permute-start | bytes 393224 | tf_op jit(solution)/shard_map/ppermute | solution.py:638
  33.8 13.3 %collective-permute-start.11 = (bf16[256,256]{1,0:T(8,128)(2,1)S(1)}, bf16[256,256]{1,0:T(8,128)(2,1)S(1)}, u32[]{:S(2)}, u32[]{:S(2)}) collective-permute-start(bf16[256,256]{1,0:T(8,128)(2,1)S(1)} %get-tuple-element.34), channel_id=1, source_target_pairs={{0,12},{2,14},{4,8},{6,10},{8,4},{10,6},{12,0},{14,2},{16,28},{18,... | collective-permute-start | bytes 393224 | tf_op jit(solution)/shard_map/ppermute | solution.py:638
  36.1 13.6 %collective-permute-start.12 = (bf16[256,256]{1,0:T(8,128)(2,1)S(1)}, bf16[256,256]{1,0:T(8,128)(2,1)S(1)}, u32[]{:S(2)}, u32[]{:S(2)}) collective-permute-start(bf16[256,256]{1,0:T(8,128)(2,1)S(1)} %get-tuple-element.35), channel_id=1, source_target_pairs={{0,22},{2,20},{4,18},{6,16},{8,30},{10,28},{12,26},{14,24},{16,6},... | collective-permute-start | bytes 393224 | tf_op jit(solution)/shard_map/ppermute | solution.py:638
  38.0 11.9 %collective-permute-start.13 = (bf16[256,256]{1,0:T(8,128)(2,1)S(1)}, bf16[256,256]{1,0:T(8,128)(2,1)S(1)}, u32[]{:S(2)}, u32[]{:S(2)}) collective-permute-start(bf16[256,256]{1,0:T(8,128)(2,1)S(1)} %get-tuple-element.36), channel_id=1, source_target_pairs={{0,14},{2,12},{4,10},{6,8},{8,6},{10,4},{12,2},{14,0},{16,30},{18,... | collective-permute-start | bytes 393224 | tf_op jit(solution)/shard_map/ppermute | solution.py:638
  42.7 11.4 %collective-permute-start.14 = (bf16[256,256]{1,0:T(8,128)(2,1)S(1)}, bf16[256,256]{1,0:T(8,128)(2,1)S(1)}, u32[]{:S(2)}, u32[]{:S(2)}) collective-permute-start(bf16[256,256]{1,0:T(8,128)(2,1)S(1)} %get-tuple-element.37), channel_id=1, source_target_pairs={{0,30},{2,28},{4,26},{6,24},{8,22},{10,20},{12,18},{14,16},{16,14}... | collective-permute-start | bytes 393224 | tf_op jit(solution)/shard_map/ppermute | solution.py:638
  54.1 40.6 %copy-start.2 = (bf16[256,2048]{1,0:T(8,128)(2,1)S(1)}, bf16[256,2048]{1,0:T(8,128)(2,1)}, u32[]{:S(2)}) copy-start(bf16[256,2048]{1,0:T(8,128)(2,1)} %gates_hbm.1) | copy-start | bytes 3145732
  54.1 40.6 %copy-start.3 = (f32[2048]{0:T(1024)S(1)}, f32[2048]{0:T(1024)}, u32[]{:S(2)}) copy-start(f32[2048]{0:T(1024)} %param.9) | copy-start | bytes 24580
  64.4 30.2 %all-to-all-start = ((bf16[16,256,128]{2,1,0:T(8,128)(2,1)}), bf16[16,256,128]{2,1,0:T(8,128)(2,1)S(1)}, u32[]{:S(2)}, u32[]{:S(2)}) async-start(bf16[16,256,128]{2,1,0:T(8,128)(2,1)} %long_convolution.1), calls=%async_computation | async-start | bytes 2097152 | tf_op jit(solution)/shard_map/all_to_all | solution.py:632
  97.9 2.8 %collective-permute-start.15 = (f32[256,1024]{1,0:T(8,128)S(1)}, f32[256,1024]{1,0:T(8,128)S(1)}, u32[]{:S(2)}, u32[]{:S(2)}) collective-permute-start(f32[256,1024]{1,0:T(8,128)S(1)} %get-tuple-element.40), channel_id=1, source_target_pairs={{0,1},{1,0},{2,3},{3,2},{4,5},{5,4},{6,7},{7,6},{8,9},{9,8},{10,11... | collective-permute-start | bytes 3145736 | tf_op jit(solution)/shard_map/ppermute | solution.py:649

commit v13 on v12

--- a/solution.py
+++ b/solution.py
@@ -194,7 +194,7 @@
     return [slot for pair in zip(across, near) for slot in pair]
 
 
-LEAD = 4
+LEAD = 5
 
 
 def lead_kernel(blocks, me_ref, values_hbm, taps_hbm, *rest):

time: 103 us -> 102 us (level)
  starting transfers between devices: 40.7 us -> 33.9 us
  waiting for transfers between devices: 37.3 us -> 43.1 us
    ppermute x15, starting transfers between devices: 35 us -> 27.8 us  [exchange(): lax.ppermute(source, 'seq', [(j, j ^ slot) for j in range(blocks)])]
    ppermute x15, waiting for transfers between devices: 12.7 us -> 18.5 us  [exchange(): lax.ppermute(source, 'seq', [(j, j ^ slot) for j in range(blocks)])]
  transfers between devices with their start and end apart: 17 -> 17, of which waited for: 7 -> 8; matrix products, arithmetic and copies ran while one was open for 0% -> 0% of each run, Pallas kernels for 4% -> 4%
where the time goes in v13:
time: 102 us; the launch traced here: 101 us
  waiting for transfers between devices  43.1 us (42%)
  starting transfers between devices  33.9 us (33%)
  Pallas kernels  21.3 us (21%)
  local copies, waits for them, and re-layouts  2.46 us (2%)
    ppermute x15, starting transfers between devices, exchange(): lax.ppermute(source, 'seq', [(j, j ^ slot) for j in range(blocks)])  27.8 us
    all_to_all x1, waiting for transfers between devices, swap_blocks(): return lax.all_to_all(array, 'seq', split_axis=0, concat_axis=0, tiled=True)  24.6 us
    ppermute x15, waiting for transfers between devices, exchange(): lax.ppermute(source, 'seq', [(j, j ^ slot) for j in range(blocks)])  18.5 us
    pallas_call x1, Pallas kernels, convolve(): pl.pallas_call(functools.partial(convolve_kernel, blocks), in_specs=[pl.B...  10.3 us
    all_to_all x1, starting transfers between devices, swap_blocks(): return lax.all_to_all(array, 'seq', split_axis=0, concat_axis=0, tiled=True)  6.04 us
    pallas_call x1, Pallas kernels, gate_and_project(): pl.pallas_call(gate_kernel, in_specs=[pl.BlockSpec(memory_space=pltpu.SME...  3.31 us
    pallas_call x1, Pallas kernels, project_kept(): pl.pallas_call(kept_kernel, in_specs=[pl.BlockSpec(memory_space=pltpu.SME...  2.68 us
    unnamed x8, local copies, waits for them, and re-layouts  2.46 us
  transfers between devices with their start and end apart: 17, of which 8 were waited for; matrix products, arithmetic and copies ran while one was open for 0% of the time, Pallas kernels for 4%

profile of v13, /device:TPU:0, one launch (start us, length us, event | category | flops | bytes accessed | tf_op | source)
XLA Modules:
  0.0 100.8 jit_solution(8120711087398392324)
XLA Ops:
  0.0 2.3 %arrange_lead.1 = (bf16[256,256]{1,0:T(8,128)(2,1)}, bf16[256,256]{1,0:T(8,128)(2,1)}, bf16[256,256]{1,0:T(8,128)(2,1)}, bf16[256,256]{1,0:T(8,128)(2,1)}, bf16[256,256]{1,0:T(8,128)(2,1)}) custom-call(s32[1]{0:T(128)} %bitcast.1.me_ref, bf16[256,2048]{1,0:T(8,128)(2,1)} %values_hbm.5, bf16[256,2048]{1,0:T(8,128)(2,1)} %taps_hbm.3), custom_call_target="tpu_custom_call" | custom-call | flops 167772160 | bytes 1310720 | tf_op jit(solution)/shard_map/arrange_lead/pallas_call | solution.py:248
  2.3 4.1 %collective-permute-start = (bf16[256,256]{1,0:T(8,128)(2,1)}, bf16[256,256]{1,0:T(8,128)(2,1)S(1)}, u32[]{:S(2)}, u32[]{:S(2)}) collective-permute-start(bf16[256,256]{1,0:T(8,128)(2,1)} %get-tuple-element.23), channel_id=1, source_target_pairs={{0,16},{2,18},{4,20},{6,22},{8,24},{10,26},{12,28},{14,30},{16,0},... | collective-permute-start | bytes 393224 | tf_op jit(solution)/shard_map/ppermute | solution.py:638
  6.4 1.5 %collective-permute-start.1 = (bf16[256,256]{1,0:T(8,128)(2,1)}, bf16[256,256]{1,0:T(8,128)(2,1)S(1)}, u32[]{:S(2)}, u32[]{:S(2)}) collective-permute-start(bf16[256,256]{1,0:T(8,128)(2,1)} %get-tuple-element.24), channel_id=1, source_target_pairs={{0,2},{2,0},{4,6},{6,4},{8,10},{10,8},{12,14},{14,12},{16,18},{18,... | collective-permute-start | bytes 393224 | tf_op jit(solution)/shard_map/ppermute | solution.py:638
  7.9 1.3 %collective-permute-start.2 = (bf16[256,256]{1,0:T(8,128)(2,1)}, bf16[256,256]{1,0:T(8,128)(2,1)S(1)}, u32[]{:S(2)}, u32[]{:S(2)}) collective-permute-start(bf16[256,256]{1,0:T(8,128)(2,1)} %get-tuple-element.25), channel_id=1, source_target_pairs={{0,24},{2,26},{4,28},{6,30},{8,16},{10,18},{12,20},{14,22},{16,8},... | collective-permute-start | bytes 393224 | tf_op jit(solution)/shard_map/ppermute | solution.py:638
  9.2 1.5 %collective-permute-start.3 = (bf16[256,256]{1,0:T(8,128)(2,1)}, bf16[256,256]{1,0:T(8,128)(2,1)S(1)}, u32[]{:S(2)}, u32[]{:S(2)}) collective-permute-start(bf16[256,256]{1,0:T(8,128)(2,1)} %get-tuple-element.26), channel_id=1, source_target_pairs={{0,4},{2,6},{4,0},{6,2},{8,12},{10,14},{12,8},{14,10},{16,20},{18,... | collective-permute-start | bytes 393224 | tf_op jit(solution)/shard_map/ppermute | solution.py:638
  10.8 1.7 %collective-permute-start.4 = (bf16[256,256]{1,0:T(8,128)(2,1)}, bf16[256,256]{1,0:T(8,128)(2,1)S(1)}, u32[]{:S(2)}, u32[]{:S(2)}) collective-permute-start(bf16[256,256]{1,0:T(8,128)(2,1)} %get-tuple-element.27), channel_id=1, source_target_pairs={{0,18},{2,16},{4,22},{6,20},{8,26},{10,24},{12,30},{14,28},{16,2},... | collective-permute-start | bytes 393224 | tf_op jit(solution)/shard_map/ppermute | solution.py:638
  12.4 1.2 %copy-done = bf16[256,2048]{1,0:T(8,128)(2,1)S(1)} copy-done((bf16[256,2048]{1,0:T(8,128)(2,1)S(1)}, bf16[256,2048]{1,0:T(8,128)(2,1)}, u32[]{:S(2)}) %copy-start) | copy-done | bytes 1048600
  13.7 1.2 %copy-done.1 = bf16[256,2048]{1,0:T(8,128)(2,1)S(1)} copy-done((bf16[256,2048]{1,0:T(8,128)(2,1)S(1)}, bf16[256,2048]{1,0:T(8,128)(2,1)}, u32[]{:S(2)}) %copy-start.1) | copy-done | bytes 1048600
  14.9 1.7 %arrange_others.1 = (bf16[256,256]{1,0:T(8,128)(2,1)S(1)}, bf16[256,256]{1,0:T(8,128)(2,1)S(1)}, bf16[256,256]{1,0:T(8,128)(2,1)S(1)}, bf16[256,256]{1,0:T(8,128...) custom-call(s32[1]{0:T(128)} %bitcast.1.me_ref, ...), custom_call_target="tpu_custom_call" | custom-call | flops 536870912 | bytes 4194304 | tf_op jit(solution)/shard_map/arrange_others/pallas_call | solution.py:263
  16.6 2.7 %collective-permute-done.rest_0_ = bf16[256,256]{1,0:T(8,128)(2,1)S(1)} collective-permute-done((bf16[256,256]{1,0:T(8,128)(2,1)}, bf16[256,256]{1,0:T(8,128)(2,1)S(1)}, u32[]{:S(2)}, u32[]{:S(2)}) %collective-permute-start) | collective-permute-done | bytes 131104 | tf_op jit(solution)/shard_map/ppermute | solution.py:638
  19.4 2.8 %collective-permute-start.5 = (bf16[256,256]{1,0:T(8,128)(2,1)S(1)}, bf16[256,256]{1,0:T(8,128)(2,1)S(1)}, u32[]{:S(2)}, u32[]{:S(2)}) collective-permute-start(bf16[256,256]{1,0:T(8,128)(2,1)S(1)} %get-tuple-element.28), channel_id=1, source_target_pairs={{0,6},{2,4},{4,2},{6,0},{8,14},{10,12},{12,10},{14,8},{16,22},{18,... | collective-permute-start | bytes 393224 | tf_op jit(solution)/shard_map/ppermute | solution.py:638
  22.2 2.4 %collective-permute-start.6 = (bf16[256,256]{1,0:T(8,128)(2,1)S(1)}, bf16[256,256]{1,0:T(8,128)(2,1)S(1)}, u32[]{:S(2)}, u32[]{:S(2)}) collective-permute-start(bf16[256,256]{1,0:T(8,128)(2,1)S(1)} %get-tuple-element.29), channel_id=1, source_target_pairs={{0,26},{2,24},{4,30},{6,28},{8,18},{10,16},{12,22},{14,20},{16,10}... | collective-permute-start | bytes 393224 | tf_op jit(solution)/shard_map/ppermute | solution.py:638
  24.6 1.5 %collective-permute-start.8 = (bf16[256,256]{1,0:T(8,128)(2,1)S(1)}, bf16[256,256]{1,0:T(8,128)(2,1)S(1)}, u32[]{:S(2)}, u32[]{:S(2)}) collective-permute-start(bf16[256,256]{1,0:T(8,128)(2,1)S(1)} %get-tuple-element.31), channel_id=1, source_target_pairs={{0,20},{2,22},{4,16},{6,18},{8,28},{10,30},{12,24},{14,26},{16,4},... | collective-permute-start | bytes 393224 | tf_op jit(solution)/shard_map/ppermute | solution.py:638
  28.7 7.1 %collective-permute-start.10 = (bf16[256,256]{1,0:T(8,128)(2,1)S(1)}, bf16[256,256]{1,0:T(8,128)(2,1)S(1)}, u32[]{:S(2)}, u32[]{:S(2)}) collective-permute-start(bf16[256,256]{1,0:T(8,128)(2,1)S(1)} %get-tuple-element.33), channel_id=1, source_target_pairs={{0,28},{2,30},{4,24},{6,26},{8,20},{10,22},{12,16},{14,18},{16,12}... | collective-permute-start | bytes 393224 | tf_op jit(solution)/shard_map/ppermute | solution.py:638
  36.4 3.9 %collective-permute-done.8.rest_8_ = bf16[256,256]{1,0:T(8,128)(2,1)S(1)} collective-permute-done((bf16[256,256]{1,0:T(8,128)(2,1)S(1)}, bf16[256,256]{1,0:T(8,128)(2,1)S(1)}, u32[]{:S(2)}, u32[]{:S(2)}) %collective-permute-start.8) | collective-permute-done | bytes 131104 | tf_op jit(solution)/shard_map/ppermute | solution.py:638
  40.3 2.4 %collective-permute-start.14 = (bf16[256,256]{1,0:T(8,128)(2,1)S(1)}, bf16[256,256]{1,0:T(8,128)(2,1)S(1)}, u32[]{:S(2)}, u32[]{:S(2)}) collective-permute-start(bf16[256,256]{1,0:T(8,128)(2,1)S(1)} %get-tuple-element.37), channel_id=1, source_target_pairs={{0,30},{2,28},{4,26},{6,24},{8,22},{10,20},{12,18},{14,16},{16,14}... | collective-permute-start | bytes 393224 | tf_op jit(solution)/shard_map/ppermute | solution.py:638
  42.7 1.4 %collective-permute-done.11.rest_11_ = bf16[256,256]{1,0:T(8,128)(2,1)S(1)} collective-permute-done((bf16[256,256]{1,0:T(8,128)(2,1)S(1)}, bf16[256,256]{1,0:T(8,128)(2,1)S(1)}, u32[]{:S(2)}, u32[]{:S(2)}) %collective-permute-start.11) | collective-permute-done | bytes 131104 | tf_op jit(solution)/shard_map/ppermute | solution.py:638
  44.1 6.3 %collective-permute-done.12.rest_12_ = bf16[256,256]{1,0:T(8,128)(2,1)S(1)} collective-permute-done((bf16[256,256]{1,0:T(8,128)(2,1)S(1)}, bf16[256,256]{1,0:T(8,128)(2,1)S(1)}, u32[]{:S(2)}, u32[]{:S(2)}) %collective-permute-start.12) | collective-permute-done | bytes 131104 | tf_op jit(solution)/shard_map/ppermute | solution.py:638
  50.4 2.4 %collective-permute-done.14.rest_14_ = bf16[256,256]{1,0:T(8,128)(2,1)S(1)} collective-permute-done((bf16[256,256]{1,0:T(8,128)(2,1)S(1)}, bf16[256,256]{1,0:T(8,128)(2,1)S(1)}, u32[]{:S(2)}, u32[]{:S(2)}) %collective-permute-start.14) | collective-permute-done | bytes 131104 | tf_op jit(solution)/shard_map/ppermute | solution.py:638
  52.8 10.3 %long_convolution.1 = bf16[16,256,128]{2,1,0:T(8,128)(2,1)} custom-call(s32[1]{0:T(128)} %bitcast.1.me_ref, bf16[256,256]{1,0:T(8,128)(2,1)S(1)} %collective-permute-done.rest_0_, bf16[256,256]{1,0:T(8,128)(2,1)S(1)} %collective-permute-done.1.rest_1_, bf16[256,256]{1,0:T(8,128)(2,1)S(1)} %collective-permute-done.2.rest_2_, ...), custom_call_target="tpu_custom_call" | custom-call | flops 5000000000 | bytes 9000000 | tf_op jit(solution)/shard_map/long_convolution/pallas_call | solution.py:481
  63.1 6.0 %all-to-all-start = ((bf16[16,256,128]{2,1,0:T(8,128)(2,1)}), bf16[16,256,128]{2,1,0:T(8,128)(2,1)S(1)}, u32[]{:S(2)}, u32[]{:S(2)}) async-start(bf16[16,256,128]{2,1,0:T(8,128)(2,1)} %long_convolution.1), calls=%async_computation | async-start | bytes 2097152 | tf_op jit(solution)/shard_map/all_to_all | solution.py:632
  69.2 24.6 %all-to-all-done.conv_ref = bf16[16,256,128]{2,1,0:T(8,128)(2,1)S(1)} async-done(((bf16[16,256,128]{2,1,0:T(8,128)(2,1)}), bf16[16,256,128]{2,1,0:T(8,128)(2,1)S(1)}, u32[]{:S(2)}, u32[]{:S(2)}) %all-to-all-start) | async-done | bytes 1048608 | tf_op jit(solution)/shard_map/all_to_all | solution.py:632
  93.8 3.3 %gate_project_sent.1 = (bf16[256,2048]{1,0:T(8,128)(2,1)S(1)}, f32[256,1024]{1,0:T(8,128)S(1)}) custom-call(s32[1]{0:T(128)} %bitcast.half_ref, bf16[16,256,128]{2,1,0:T(8,128)(2,1)S(1)} %all-to-all-done.conv_ref, bf16[256,2048]{1,0:T(8,128)(2,1)S(1)} %copy-done.2, bf16[256,2048]{1,0:T(8,128)(2,1)} %values_hbm.5, f32[1,2048]{1,0:T(1,128)S(1)} %bitcast.3, ...), custom_call_target="tpu_custom_call" | custom-call | flops 1073741824 | bytes 4194304 | tf_op jit(solution)/shard_map/gate_project_sent/pallas_call | solution.py:562
  97.2 2.7 %project_kept.1.kept_ref = f32[256,1024]{1,0:T(8,128)S(1)} custom-call(s32[1]{0:T(128)} %bitcast.half_ref, bf16[256,2048]{1,0:T(8,128)(2,1)S(1)} %get-tuple-element.39.gated_ref, bf16[2048,2048]{1,0:T(8,128)(2,1)} %weight_hbm.3), custom_call_target="tpu_custom_call" | custom-call | flops 1073741824 | bytes 4194304 | tf_op jit(solution)/shard_map/project_kept/pallas_call | solution.py:592
  (24 shorter events, 4.2 us)
Async XLA Ops:
  2.3 17.1 %collective-permute-start = (bf16[256,256]{1,0:T(8,128)(2,1)}, bf16[256,256]{1,0:T(8,128)(2,1)S(1)}, u32[]{:S(2)}, u32[]{:S(2)}) collective-permute-start(bf16[256,256]{1,0:T(8,128)(2,1)} %get-tuple-element.23), channel_id=1, source_target_pairs={{0,16},{2,18},{4,20},{6,22},{8,24},{10,26},{12,28},{14,30},{16,0},... | collective-permute-start | bytes 393224 | tf_op jit(solution)/shard_map/ppermute | solution.py:638
  6.4 15.8 %collective-permute-start.1 = (bf16[256,256]{1,0:T(8,128)(2,1)}, bf16[256,256]{1,0:T(8,128)(2,1)S(1)}, u32[]{:S(2)}, u32[]{:S(2)}) collective-permute-start(bf16[256,256]{1,0:T(8,128)(2,1)} %get-tuple-element.24), channel_id=1, source_target_pairs={{0,2},{2,0},{4,6},{6,4},{8,10},{10,8},{12,14},{14,12},{16,18},{18,... | collective-permute-start | bytes 393224 | tf_op jit(solution)/shard_map/ppermute | solution.py:638
  7.9 16.7 %collective-permute-start.2 = (bf16[256,256]{1,0:T(8,128)(2,1)}, bf16[256,256]{1,0:T(8,128)(2,1)S(1)}, u32[]{:S(2)}, u32[]{:S(2)}) collective-permute-start(bf16[256,256]{1,0:T(8,128)(2,1)} %get-tuple-element.25), channel_id=1, source_target_pairs={{0,24},{2,26},{4,28},{6,30},{8,16},{10,18},{12,20},{14,22},{16,8},... | collective-permute-start | bytes 393224 | tf_op jit(solution)/shard_map/ppermute | solution.py:638
  9.2 15.4 %collective-permute-start.3 = (bf16[256,256]{1,0:T(8,128)(2,1)}, bf16[256,256]{1,0:T(8,128)(2,1)S(1)}, u32[]{:S(2)}, u32[]{:S(2)}) collective-permute-start(bf16[256,256]{1,0:T(8,128)(2,1)} %get-tuple-element.26), channel_id=1, source_target_pairs={{0,4},{2,6},{4,0},{6,2},{8,12},{10,14},{12,8},{14,10},{16,20},{18,... | collective-permute-start | bytes 393224 | tf_op jit(solution)/shard_map/ppermute | solution.py:638
  10.8 16.4 %collective-permute-start.4 = (bf16[256,256]{1,0:T(8,128)(2,1)}, bf16[256,256]{1,0:T(8,128)(2,1)S(1)}, u32[]{:S(2)}, u32[]{:S(2)}) collective-permute-start(bf16[256,256]{1,0:T(8,128)(2,1)} %get-tuple-element.27), channel_id=1, source_target_pairs={{0,18},{2,16},{4,22},{6,20},{8,26},{10,24},{12,30},{14,28},{16,2},... | collective-permute-start | bytes 393224 | tf_op jit(solution)/shard_map/ppermute | solution.py:638
  12.4 1.2 %copy-start = (bf16[256,2048]{1,0:T(8,128)(2,1)S(1)}, bf16[256,2048]{1,0:T(8,128)(2,1)}, u32[]{:S(2)}) copy-start(bf16[256,2048]{1,0:T(8,128)(2,1)} %values_hbm.5) | copy-start | bytes 3145732
  13.7 1.2 %copy-start.1 = (bf16[256,2048]{1,0:T(8,128)(2,1)S(1)}, bf16[256,2048]{1,0:T(8,128)(2,1)}, u32[]{:S(2)}) copy-start(bf16[256,2048]{1,0:T(8,128)(2,1)} %taps_hbm.3) | copy-start | bytes 3145732
  19.4 9.4 %collective-permute-start.5 = (bf16[256,256]{1,0:T(8,128)(2,1)S(1)}, bf16[256,256]{1,0:T(8,128)(2,1)S(1)}, u32[]{:S(2)}, u32[]{:S(2)}) collective-permute-start(bf16[256,256]{1,0:T(8,128)(2,1)S(1)} %get-tuple-element.28), channel_id=1, source_target_pairs={{0,6},{2,4},{4,2},{6,0},{8,14},{10,12},{12,10},{14,8},{16,22},{18,... | collective-permute-start | bytes 393224 | tf_op jit(solution)/shard_map/ppermute | solution.py:638
  22.2 13.6 %collective-permute-start.6 = (bf16[256,256]{1,0:T(8,128)(2,1)S(1)}, bf16[256,256]{1,0:T(8,128)(2,1)S(1)}, u32[]{:S(2)}, u32[]{:S(2)}) collective-permute-start(bf16[256,256]{1,0:T(8,128)(2,1)S(1)} %get-tuple-element.29), channel_id=1, source_target_pairs={{0,26},{2,24},{4,30},{6,28},{8,18},{10,16},{12,22},{14,20},{16,10}... | collective-permute-start | bytes 393224 | tf_op jit(solution)/shard_map/ppermute | solution.py:638
  24.6 11.2 %collective-permute-start.7 = (bf16[256,256]{1,0:T(8,128)(2,1)S(1)}, bf16[256,256]{1,0:T(8,128)(2,1)S(1)}, u32[]{:S(2)}, u32[]{:S(2)}) collective-permute-start(bf16[256,256]{1,0:T(8,128)(2,1)S(1)} %get-tuple-element.30), channel_id=1, source_target_pairs={{0,8},{2,10},{4,12},{6,14},{8,0},{10,2},{12,4},{14,6},{16,24},{18,... | collective-permute-start | bytes 393224 | tf_op jit(solution)/shard_map/ppermute | solution.py:638
  24.6 15.7 %collective-permute-start.8 = (bf16[256,256]{1,0:T(8,128)(2,1)S(1)}, bf16[256,256]{1,0:T(8,128)(2,1)S(1)}, u32[]{:S(2)}, u32[]{:S(2)}) collective-permute-start(bf16[256,256]{1,0:T(8,128)(2,1)S(1)} %get-tuple-element.31), channel_id=1, source_target_pairs={{0,20},{2,22},{4,16},{6,18},{8,28},{10,30},{12,24},{14,26},{16,4},... | collective-permute-start | bytes 393224 | tf_op jit(solution)/shard_map/ppermute | solution.py:638
  27.1 13.2 %collective-permute-start.9 = (bf16[256,256]{1,0:T(8,128)(2,1)S(1)}, bf16[256,256]{1,0:T(8,128)(2,1)S(1)}, u32[]{:S(2)}, u32[]{:S(2)}) collective-permute-start(bf16[256,256]{1,0:T(8,128)(2,1)S(1)} %get-tuple-element.32), channel_id=1, source_target_pairs={{0,10},{2,8},{4,14},{6,12},{8,2},{10,0},{12,6},{14,4},{16,26},{18,... | collective-permute-start | bytes 393224 | tf_op jit(solution)/shard_map/ppermute | solution.py:638
  28.7 14.0 %collective-permute-start.10 = (bf16[256,256]{1,0:T(8,128)(2,1)S(1)}, bf16[256,256]{1,0:T(8,128)(2,1)S(1)}, u32[]{:S(2)}, u32[]{:S(2)}) collective-permute-start(bf16[256,256]{1,0:T(8,128)(2,1)S(1)} %get-tuple-element.33), channel_id=1, source_target_pairs={{0,28},{2,30},{4,24},{6,26},{8,20},{10,22},{12,16},{14,18},{16,12}... | collective-permute-start | bytes 393224 | tf_op jit(solution)/shard_map/ppermute | solution.py:638
  35.8 8.3 %collective-permute-start.11 = (bf16[256,256]{1,0:T(8,128)(2,1)S(1)}, bf16[256,256]{1,0:T(8,128)(2,1)S(1)}, u32[]{:S(2)}, u32[]{:S(2)}) collective-permute-start(bf16[256,256]{1,0:T(8,128)(2,1)S(1)} %get-tuple-element.34), channel_id=1, source_target_pairs={{0,12},{2,14},{4,8},{6,10},{8,4},{10,6},{12,0},{14,2},{16,28},{18,... | collective-permute-start | bytes 393224 | tf_op jit(solution)/shard_map/ppermute | solution.py:638
  35.8 14.6 %collective-permute-start.12 = (bf16[256,256]{1,0:T(8,128)(2,1)S(1)}, bf16[256,256]{1,0:T(8,128)(2,1)S(1)}, u32[]{:S(2)}, u32[]{:S(2)}) collective-permute-start(bf16[256,256]{1,0:T(8,128)(2,1)S(1)} %get-tuple-element.35), channel_id=1, source_target_pairs={{0,22},{2,20},{4,18},{6,16},{8,30},{10,28},{12,26},{14,24},{16,6},... | collective-permute-start | bytes 393224 | tf_op jit(solution)/shard_map/ppermute | solution.py:638
  40.3 10.1 %collective-permute-start.13 = (bf16[256,256]{1,0:T(8,128)(2,1)S(1)}, bf16[256,256]{1,0:T(8,128)(2,1)S(1)}, u32[]{:S(2)}, u32[]{:S(2)}) collective-permute-start(bf16[256,256]{1,0:T(8,128)(2,1)S(1)} %get-tuple-element.36), channel_id=1, source_target_pairs={{0,14},{2,12},{4,10},{6,8},{8,6},{10,4},{12,2},{14,0},{16,30},{18,... | collective-permute-start | bytes 393224 | tf_op jit(solution)/shard_map/ppermute | solution.py:638
  40.3 12.4 %collective-permute-start.14 = (bf16[256,256]{1,0:T(8,128)(2,1)S(1)}, bf16[256,256]{1,0:T(8,128)(2,1)S(1)}, u32[]{:S(2)}, u32[]{:S(2)}) collective-permute-start(bf16[256,256]{1,0:T(8,128)(2,1)S(1)} %get-tuple-element.37), channel_id=1, source_target_pairs={{0,30},{2,28},{4,26},{6,24},{8,22},{10,20},{12,18},{14,16},{16,14}... | collective-permute-start | bytes 393224 | tf_op jit(solution)/shard_map/ppermute | solution.py:638
  52.8 41.0 %copy-start.2 = (bf16[256,2048]{1,0:T(8,128)(2,1)S(1)}, bf16[256,2048]{1,0:T(8,128)(2,1)}, u32[]{:S(2)}) copy-start(bf16[256,2048]{1,0:T(8,128)(2,1)} %gates_hbm.1) | copy-start | bytes 3145732
  52.8 41.0 %copy-start.3 = (f32[2048]{0:T(1024)S(1)}, f32[2048]{0:T(1024)}, u32[]{:S(2)}) copy-start(f32[2048]{0:T(1024)} %param.9) | copy-start | bytes 24580
  63.1 30.6 %all-to-all-start = ((bf16[16,256,128]{2,1,0:T(8,128)(2,1)}), bf16[16,256,128]{2,1,0:T(8,128)(2,1)S(1)}, u32[]{:S(2)}, u32[]{:S(2)}) async-start(bf16[16,256,128]{2,1,0:T(8,128)(2,1)} %long_convolution.1), calls=%async_computation | async-start | bytes 2097152 | tf_op jit(solution)/shard_map/all_to_all | solution.py:632
  97.1 2.8 %collective-permute-start.15 = (f32[256,1024]{1,0:T(8,128)S(1)}, f32[256,1024]{1,0:T(8,128)S(1)}, u32[]{:S(2)}, u32[]{:S(2)}) collective-permute-start(f32[256,1024]{1,0:T(8,128)S(1)} %get-tuple-element.40), channel_id=1, source_target_pairs={{0,1},{1,0},{2,3},{3,2},{4,5},{5,4},{6,7},{7,6},{8,9},{9,8},{10,11... | collective-permute-start | bytes 3145736 | tf_op jit(solution)/shard_map/ppermute | solution.py:649

commit v14 on v13

--- a/solution.py
+++ b/solution.py
@@ -191,7 +191,8 @@
     half = blocks // 2
     across = [half + (i // 2 if i % 2 == 0 else half // 2 + i // 2) for i in range(half)]
     near = list(range(1, half)) + [0]
-    return [slot for pair in zip(across, near) for slot in pair]
+    lead = [across[0], near[0], across[1], near[1], across[2]]
+    return lead + [slot for pair in zip(across[3:], near[2:]) for slot in pair] + near[half - 1 :]
 
 
 LEAD = 5

time: 102 us -> 104 us (1.020)
  starting transfers between devices: 33.9 us -> 37.3 us
  waiting for transfers between devices: 43.1 us -> 41.7 us
    ppermute x15, starting transfers between devices: 27.8 us -> 31 us  [exchange(): lax.ppermute(source, 'seq', [(j, j ^ slot) for j in range(blocks)])]
where the time goes in v14:
time: 104 us; the launch traced here: 103 us
  waiting for transfers between devices  41.7 us (40%)
  starting transfers between devices  37.3 us (36%)
  Pallas kernels  21.3 us (20%)
  local copies, waits for them, and re-layouts  2.46 us (2%)
    ppermute x15, starting transfers between devices, exchange(): lax.ppermute(source, 'seq', [(j, j ^ slot) for j in range(blocks)])  31 us
    all_to_all x1, waiting for transfers between devices, swap_blocks(): return lax.all_to_all(array, 'seq', split_axis=0, concat_axis=0, tiled=True)  24.3 us
    ppermute x15, waiting for transfers between devices, exchange(): lax.ppermute(source, 'seq', [(j, j ^ slot) for j in range(blocks)])  17.5 us
    pallas_call x1, Pallas kernels, convolve(): pl.pallas_call(functools.partial(convolve_kernel, blocks), in_specs=[pl.B...  10.3 us
    all_to_all x1, starting transfers between devices, swap_blocks(): return lax.all_to_all(array, 'seq', split_axis=0, concat_axis=0, tiled=True)  6.19 us
    pallas_call x1, Pallas kernels, gate_and_project(): pl.pallas_call(gate_kernel, in_specs=[pl.BlockSpec(memory_space=pltpu.SME...  3.31 us
    pallas_call x1, Pallas kernels, project_kept(): pl.pallas_call(kept_kernel, in_specs=[pl.BlockSpec(memory_space=pltpu.SME...  2.68 us
    unnamed x8, local copies, waits for them, and re-layouts  2.46 us
  transfers between devices with their start and end apart: 17, of which 8 were waited for; matrix products, arithmetic and copies ran while one was open for 0% of the time, Pallas kernels for 4%

profile of v14, /device:TPU:0, one launch (start us, length us, event | category | flops | bytes accessed | tf_op | source)
XLA Modules:
  0.0 102.8 jit_solution(4918583501148881711)
XLA Ops:
  0.0 2.3 %arrange_lead.1 = (bf16[256,256]{1,0:T(8,128)(2,1)}, bf16[256,256]{1,0:T(8,128)(2,1)}, bf16[256,256]{1,0:T(8,128)(2,1)}, bf16[256,256]{1,0:T(8,128)(2,1)}, bf16[256,256]{1,0:T(8,128)(2,1)}) custom-call(s32[1]{0:T(128)} %bitcast.1.me_ref, bf16[256,2048]{1,0:T(8,128)(2,1)} %values_hbm.5, bf16[256,2048]{1,0:T(8,128)(2,1)} %taps_hbm.3), custom_call_target="tpu_custom_call" | custom-call | flops 167772160 | bytes 1310720 | tf_op jit(solution)/shard_map/arrange_lead/pallas_call | solution.py:249
  2.3 4.1 %collective-permute-start = (bf16[256,256]{1,0:T(8,128)(2,1)}, bf16[256,256]{1,0:T(8,128)(2,1)S(1)}, u32[]{:S(2)}, u32[]{:S(2)}) collective-permute-start(bf16[256,256]{1,0:T(8,128)(2,1)} %get-tuple-element.23), channel_id=1, source_target_pairs={{0,16},{2,18},{4,20},{6,22},{8,24},{10,26},{12,28},{14,30},{16,0},... | collective-permute-start | bytes 393224 | tf_op jit(solution)/shard_map/ppermute | solution.py:639
  6.4 1.5 %collective-permute-start.1 = (bf16[256,256]{1,0:T(8,128)(2,1)}, bf16[256,256]{1,0:T(8,128)(2,1)S(1)}, u32[]{:S(2)}, u32[]{:S(2)}) collective-permute-start(bf16[256,256]{1,0:T(8,128)(2,1)} %get-tuple-element.24), channel_id=1, source_target_pairs={{0,2},{2,0},{4,6},{6,4},{8,10},{10,8},{12,14},{14,12},{16,18},{18,... | collective-permute-start | bytes 393224 | tf_op jit(solution)/shard_map/ppermute | solution.py:639
  7.9 1.3 %collective-permute-start.2 = (bf16[256,256]{1,0:T(8,128)(2,1)}, bf16[256,256]{1,0:T(8,128)(2,1)S(1)}, u32[]{:S(2)}, u32[]{:S(2)}) collective-permute-start(bf16[256,256]{1,0:T(8,128)(2,1)} %get-tuple-element.25), channel_id=1, source_target_pairs={{0,24},{2,26},{4,28},{6,30},{8,16},{10,18},{12,20},{14,22},{16,8},... | collective-permute-start | bytes 393224 | tf_op jit(solution)/shard_map/ppermute | solution.py:639
  9.2 1.5 %collective-permute-start.3 = (bf16[256,256]{1,0:T(8,128)(2,1)}, bf16[256,256]{1,0:T(8,128)(2,1)S(1)}, u32[]{:S(2)}, u32[]{:S(2)}) collective-permute-start(bf16[256,256]{1,0:T(8,128)(2,1)} %get-tuple-element.26), channel_id=1, source_target_pairs={{0,4},{2,6},{4,0},{6,2},{8,12},{10,14},{12,8},{14,10},{16,20},{18,... | collective-permute-start | bytes 393224 | tf_op jit(solution)/shard_map/ppermute | solution.py:639
  10.8 1.7 %collective-permute-start.4 = (bf16[256,256]{1,0:T(8,128)(2,1)}, bf16[256,256]{1,0:T(8,128)(2,1)S(1)}, u32[]{:S(2)}, u32[]{:S(2)}) collective-permute-start(bf16[256,256]{1,0:T(8,128)(2,1)} %get-tuple-element.27), channel_id=1, source_target_pairs={{0,18},{2,16},{4,22},{6,20},{8,26},{10,24},{12,30},{14,28},{16,2},... | collective-permute-start | bytes 393224 | tf_op jit(solution)/shard_map/ppermute | solution.py:639
  14.9 1.7 %arrange_others.1 = (bf16[256,256]{1,0:T(8,128)(2,1)S(1)}, bf16[256,256]{1,0:T(8,128)(2,1)S(1)}, bf16[256,256]{1,0:T(8,128)(2,1)S(1)}, bf16[256,256]{1,0:T(8,128...) custom-call(s32[1]{0:T(128)} %bitcast.1.me_ref, ...), custom_call_target="tpu_custom_call" | custom-call | flops 536870912 | bytes 4194304 | tf_op jit(solution)/shard_map/arrange_others/pallas_call | solution.py:264
  16.6 2.7 %collective-permute-done.rest_0_ = bf16[256,256]{1,0:T(8,128)(2,1)S(1)} collective-permute-done((bf16[256,256]{1,0:T(8,128)(2,1)}, bf16[256,256]{1,0:T(8,128)(2,1)S(1)}, u32[]{:S(2)}, u32[]{:S(2)}) %collective-permute-start) | collective-permute-done | bytes 131104 | tf_op jit(solution)/shard_map/ppermute | solution.py:639
  19.4 3.7 %collective-permute-start.5 = (bf16[256,256]{1,0:T(8,128)(2,1)S(1)}, bf16[256,256]{1,0:T(8,128)(2,1)S(1)}, u32[]{:S(2)}, u32[]{:S(2)}) collective-permute-start(bf16[256,256]{1,0:T(8,128)(2,1)S(1)} %get-tuple-element.28), channel_id=1, source_target_pairs={{0,26},{2,24},{4,30},{6,28},{8,18},{10,16},{12,22},{14,20},{16,10}... | collective-permute-start | bytes 393224 | tf_op jit(solution)/shard_map/ppermute | solution.py:639
  23.1 1.5 %collective-permute-start.6 = (bf16[256,256]{1,0:T(8,128)(2,1)S(1)}, bf16[256,256]{1,0:T(8,128)(2,1)S(1)}, u32[]{:S(2)}, u32[]{:S(2)}) collective-permute-start(bf16[256,256]{1,0:T(8,128)(2,1)S(1)} %get-tuple-element.29), channel_id=1, source_target_pairs={{0,6},{2,4},{4,2},{6,0},{8,14},{10,12},{12,10},{14,8},{16,22},{18,... | collective-permute-start | bytes 393224 | tf_op jit(solution)/shard_map/ppermute | solution.py:639
  26.1 5.8 %collective-permute-done.4.rest_4_ = bf16[256,256]{1,0:T(8,128)(2,1)S(1)} collective-permute-done((bf16[256,256]{1,0:T(8,128)(2,1)}, bf16[256,256]{1,0:T(8,128)(2,1)S(1)}, u32[]{:S(2)}, u32[]{:S(2)}) %collective-permute-start.4) | collective-permute-done | bytes 131104 | tf_op jit(solution)/shard_map/ppermute | solution.py:639
  31.9 3.4 %collective-permute-start.9 = (bf16[256,256]{1,0:T(8,128)(2,1)S(1)}, bf16[256,256]{1,0:T(8,128)(2,1)S(1)}, u32[]{:S(2)}, u32[]{:S(2)}) collective-permute-start(bf16[256,256]{1,0:T(8,128)(2,1)S(1)} %get-tuple-element.32), channel_id=1, source_target_pairs={{0,28},{2,30},{4,24},{6,26},{8,20},{10,22},{12,16},{14,18},{16,12}... | collective-permute-start | bytes 393224 | tf_op jit(solution)/shard_map/ppermute | solution.py:639
  35.3 2.8 %collective-permute-start.11 = (bf16[256,256]{1,0:T(8,128)(2,1)S(1)}, bf16[256,256]{1,0:T(8,128)(2,1)S(1)}, u32[]{:S(2)}, u32[]{:S(2)}) collective-permute-start(bf16[256,256]{1,0:T(8,128)(2,1)S(1)} %get-tuple-element.34), channel_id=1, source_target_pairs={{0,22},{2,20},{4,18},{6,16},{8,30},{10,28},{12,26},{14,24},{16,6},... | collective-permute-start | bytes 393224 | tf_op jit(solution)/shard_map/ppermute | solution.py:639
  38.1 2.3 %collective-permute-done.7.rest_7_ = bf16[256,256]{1,0:T(8,128)(2,1)S(1)} collective-permute-done((bf16[256,256]{1,0:T(8,128)(2,1)S(1)}, bf16[256,256]{1,0:T(8,128)(2,1)S(1)}, u32[]{:S(2)}, u32[]{:S(2)}) %collective-permute-start.7) | collective-permute-done | bytes 131104 | tf_op jit(solution)/shard_map/ppermute | solution.py:639
  40.3 3.4 %collective-permute-start.13 = (bf16[256,256]{1,0:T(8,128)(2,1)S(1)}, bf16[256,256]{1,0:T(8,128)(2,1)S(1)}, u32[]{:S(2)}, u32[]{:S(2)}) collective-permute-start(bf16[256,256]{1,0:T(8,128)(2,1)S(1)} %get-tuple-element.36), channel_id=1, source_target_pairs={{0,30},{2,28},{4,26},{6,24},{8,22},{10,20},{12,18},{14,16},{16,14}... | collective-permute-start | bytes 393224 | tf_op jit(solution)/shard_map/ppermute | solution.py:639
  43.7 4.6 %collective-permute-start.14 = (bf16[256,256]{1,0:T(8,128)(2,1)S(1)}, bf16[256,256]{1,0:T(8,128)(2,1)S(1)}, u32[]{:S(2)}, u32[]{:S(2)}) collective-permute-start(bf16[256,256]{1,0:T(8,128)(2,1)S(1)} %get-tuple-element.37), channel_id=1, source_target_pairs={{0,14},{2,12},{4,10},{6,8},{8,6},{10,4},{12,2},{14,0},{16,30},{18,... | collective-permute-start | bytes 393224 | tf_op jit(solution)/shard_map/ppermute | solution.py:639
  48.3 2.2 %collective-permute-done.11.rest_11_ = bf16[256,256]{1,0:T(8,128)(2,1)S(1)} collective-permute-done((bf16[256,256]{1,0:T(8,128)(2,1)S(1)}, bf16[256,256]{1,0:T(8,128)(2,1)S(1)}, u32[]{:S(2)}, u32[]{:S(2)}) %collective-permute-start.11) | collective-permute-done | bytes 131104 | tf_op jit(solution)/shard_map/ppermute | solution.py:639
  50.5 1.3 %collective-permute-done.12.rest_12_ = bf16[256,256]{1,0:T(8,128)(2,1)S(1)} collective-permute-done((bf16[256,256]{1,0:T(8,128)(2,1)S(1)}, bf16[256,256]{1,0:T(8,128)(2,1)S(1)}, u32[]{:S(2)}, u32[]{:S(2)}) %collective-permute-start.12) | collective-permute-done | bytes 131104 | tf_op jit(solution)/shard_map/ppermute | solution.py:639
  51.8 2.8 %collective-permute-done.13.rest_13_ = bf16[256,256]{1,0:T(8,128)(2,1)S(1)} collective-permute-done((bf16[256,256]{1,0:T(8,128)(2,1)S(1)}, bf16[256,256]{1,0:T(8,128)(2,1)S(1)}, u32[]{:S(2)}, u32[]{:S(2)}) %collective-permute-start.13) | collective-permute-done | bytes 131104 | tf_op jit(solution)/shard_map/ppermute | solution.py:639
  55.0 10.3 %long_convolution.1 = bf16[16,256,128]{2,1,0:T(8,128)(2,1)} custom-call(s32[1]{0:T(128)} %bitcast.1.me_ref, bf16[256,256]{1,0:T(8,128)(2,1)S(1)} %collective-permute-done.rest_0_, bf16[256,256]{1,0:T(8,128)(2,1)S(1)} %collective-permute-done.1.rest_1_, bf16[256,256]{1,0:T(8,128)(2,1)S(1)} %collective-permute-done.2.rest_2_, ...), custom_call_target="tpu_custom_call" | custom-call | flops 5000000000 | bytes 9000000 | tf_op jit(solution)/shard_map/long_convolution/pallas_call | solution.py:482
  65.4 6.2 %all-to-all-start = ((bf16[16,256,128]{2,1,0:T(8,128)(2,1)}), bf16[16,256,128]{2,1,0:T(8,128)(2,1)S(1)}, u32[]{:S(2)}, u32[]{:S(2)}) async-start(bf16[16,256,128]{2,1,0:T(8,128)(2,1)} %long_convolution.1), calls=%async_computation | async-start | bytes 2097152 | tf_op jit(solution)/shard_map/all_to_all | solution.py:633
  71.6 24.3 %all-to-all-done.conv_ref = bf16[16,256,128]{2,1,0:T(8,128)(2,1)S(1)} async-done(((bf16[16,256,128]{2,1,0:T(8,128)(2,1)}), bf16[16,256,128]{2,1,0:T(8,128)(2,1)S(1)}, u32[]{:S(2)}, u32[]{:S(2)}) %all-to-all-start) | async-done | bytes 1048608 | tf_op jit(solution)/shard_map/all_to_all | solution.py:633
  95.8 3.3 %gate_project_sent.1 = (bf16[256,2048]{1,0:T(8,128)(2,1)S(1)}, f32[256,1024]{1,0:T(8,128)S(1)}) custom-call(s32[1]{0:T(128)} %bitcast.half_ref, bf16[16,256,128]{2,1,0:T(8,128)(2,1)S(1)} %all-to-all-done.conv_ref, bf16[256,2048]{1,0:T(8,128)(2,1)S(1)} %copy-done.2, bf16[256,2048]{1,0:T(8,128)(2,1)} %values_hbm.5, f32[1,2048]{1,0:T(1,128)S(1)} %bitcast.3, ...), custom_call_target="tpu_custom_call" | custom-call | flops 1073741824 | bytes 4194304 | tf_op jit(solution)/shard_map/gate_project_sent/pallas_call | solution.py:563
  99.2 2.7 %project_kept.1.kept_ref = f32[256,1024]{1,0:T(8,128)S(1)} custom-call(s32[1]{0:T(128)} %bitcast.half_ref, bf16[256,2048]{1,0:T(8,128)(2,1)S(1)} %get-tuple-element.39.gated_ref, bf16[2048,2048]{1,0:T(8,128)(2,1)} %weight_hbm.3), custom_call_target="tpu_custom_call" | custom-call | flops 1073741824 | bytes 4194304 | tf_op jit(solution)/shard_map/project_kept/pallas_call | solution.py:593
  (24 shorter events, 5.5 us)
Async XLA Ops:
  2.3 17.1 %collective-permute-start = (bf16[256,256]{1,0:T(8,128)(2,1)}, bf16[256,256]{1,0:T(8,128)(2,1)S(1)}, u32[]{:S(2)}, u32[]{:S(2)}) collective-permute-start(bf16[256,256]{1,0:T(8,128)(2,1)} %get-tuple-element.23), channel_id=1, source_target_pairs={{0,16},{2,18},{4,20},{6,22},{8,24},{10,26},{12,28},{14,30},{16,0},... | collective-permute-start | bytes 393224 | tf_op jit(solution)/shard_map/ppermute | solution.py:639
  6.4 16.7 %collective-permute-start.1 = (bf16[256,256]{1,0:T(8,128)(2,1)}, bf16[256,256]{1,0:T(8,128)(2,1)S(1)}, u32[]{:S(2)}, u32[]{:S(2)}) collective-permute-start(bf16[256,256]{1,0:T(8,128)(2,1)} %get-tuple-element.24), channel_id=1, source_target_pairs={{0,2},{2,0},{4,6},{6,4},{8,10},{10,8},{12,14},{14,12},{16,18},{18,... | collective-permute-start | bytes 393224 | tf_op jit(solution)/shard_map/ppermute | solution.py:639
  7.9 16.7 %collective-permute-start.2 = (bf16[256,256]{1,0:T(8,128)(2,1)}, bf16[256,256]{1,0:T(8,128)(2,1)S(1)}, u32[]{:S(2)}, u32[]{:S(2)}) collective-permute-start(bf16[256,256]{1,0:T(8,128)(2,1)} %get-tuple-element.25), channel_id=1, source_target_pairs={{0,24},{2,26},{4,28},{6,30},{8,16},{10,18},{12,20},{14,22},{16,8},... | collective-permute-start | bytes 393224 | tf_op jit(solution)/shard_map/ppermute | solution.py:639
  9.2 15.8 %collective-permute-start.3 = (bf16[256,256]{1,0:T(8,128)(2,1)}, bf16[256,256]{1,0:T(8,128)(2,1)S(1)}, u32[]{:S(2)}, u32[]{:S(2)}) collective-permute-start(bf16[256,256]{1,0:T(8,128)(2,1)} %get-tuple-element.26), channel_id=1, source_target_pairs={{0,4},{2,6},{4,0},{6,2},{8,12},{10,14},{12,8},{14,10},{16,20},{18,... | collective-permute-start | bytes 393224 | tf_op jit(solution)/shard_map/ppermute | solution.py:639
  10.8 21.1 %collective-permute-start.4 = (bf16[256,256]{1,0:T(8,128)(2,1)}, bf16[256,256]{1,0:T(8,128)(2,1)S(1)}, u32[]{:S(2)}, u32[]{:S(2)}) collective-permute-start(bf16[256,256]{1,0:T(8,128)(2,1)} %get-tuple-element.27), channel_id=1, source_target_pairs={{0,18},{2,16},{4,22},{6,20},{8,26},{10,24},{12,30},{14,28},{16,2},... | collective-permute-start | bytes 393224 | tf_op jit(solution)/shard_map/ppermute | solution.py:639
  12.4 1.2 %copy-start = (bf16[256,2048]{1,0:T(8,128)(2,1)S(1)}, bf16[256,2048]{1,0:T(8,128)(2,1)}, u32[]{:S(2)}) copy-start(bf16[256,2048]{1,0:T(8,128)(2,1)} %values_hbm.5) | copy-start | bytes 3145732
  13.7 1.2 %copy-start.1 = (bf16[256,2048]{1,0:T(8,128)(2,1)S(1)}, bf16[256,2048]{1,0:T(8,128)(2,1)}, u32[]{:S(2)}) copy-start(bf16[256,2048]{1,0:T(8,128)(2,1)} %taps_hbm.3) | copy-start | bytes 3145732
  19.4 15.9 %collective-permute-start.5 = (bf16[256,256]{1,0:T(8,128)(2,1)S(1)}, bf16[256,256]{1,0:T(8,128)(2,1)S(1)}, u32[]{:S(2)}, u32[]{:S(2)}) collective-permute-start(bf16[256,256]{1,0:T(8,128)(2,1)S(1)} %get-tuple-element.28), channel_id=1, source_target_pairs={{0,26},{2,24},{4,30},{6,28},{8,18},{10,16},{12,22},{14,20},{16,10}... | collective-permute-start | bytes 393224 | tf_op jit(solution)/shard_map/ppermute | solution.py:639
  23.1 12.2 %collective-permute-start.6 = (bf16[256,256]{1,0:T(8,128)(2,1)S(1)}, bf16[256,256]{1,0:T(8,128)(2,1)S(1)}, u32[]{:S(2)}, u32[]{:S(2)}) collective-permute-start(bf16[256,256]{1,0:T(8,128)(2,1)S(1)} %get-tuple-element.29), channel_id=1, source_target_pairs={{0,6},{2,4},{4,2},{6,0},{8,14},{10,12},{12,10},{14,8},{16,22},{18,... | collective-permute-start | bytes 393224 | tf_op jit(solution)/shard_map/ppermute | solution.py:639
  24.6 15.7 %collective-permute-start.7 = (bf16[256,256]{1,0:T(8,128)(2,1)S(1)}, bf16[256,256]{1,0:T(8,128)(2,1)S(1)}, u32[]{:S(2)}, u32[]{:S(2)}) collective-permute-start(bf16[256,256]{1,0:T(8,128)(2,1)S(1)} %get-tuple-element.30), channel_id=1, source_target_pairs={{0,20},{2,22},{4,16},{6,18},{8,28},{10,30},{12,24},{14,26},{16,4},... | collective-permute-start | bytes 393224 | tf_op jit(solution)/shard_map/ppermute | solution.py:639
  25.0 15.3 %collective-permute-start.8 = (bf16[256,256]{1,0:T(8,128)(2,1)S(1)}, bf16[256,256]{1,0:T(8,128)(2,1)S(1)}, u32[]{:S(2)}, u32[]{:S(2)}) collective-permute-start(bf16[256,256]{1,0:T(8,128)(2,1)S(1)} %get-tuple-element.31), channel_id=1, source_target_pairs={{0,8},{2,10},{4,12},{6,14},{8,0},{10,2},{12,4},{14,6},{16,24},{18,... | collective-permute-start | bytes 393224 | tf_op jit(solution)/shard_map/ppermute | solution.py:639
  31.9 11.8 %collective-permute-start.9 = (bf16[256,256]{1,0:T(8,128)(2,1)S(1)}, bf16[256,256]{1,0:T(8,128)(2,1)S(1)}, u32[]{:S(2)}, u32[]{:S(2)}) collective-permute-start(bf16[256,256]{1,0:T(8,128)(2,1)S(1)} %get-tuple-element.32), channel_id=1, source_target_pairs={{0,28},{2,30},{4,24},{6,26},{8,20},{10,22},{12,16},{14,18},{16,12}... | collective-permute-start | bytes 393224 | tf_op jit(solution)/shard_map/ppermute | solution.py:639
  35.3 13.0 %collective-permute-start.10 = (bf16[256,256]{1,0:T(8,128)(2,1)S(1)}, bf16[256,256]{1,0:T(8,128)(2,1)S(1)}, u32[]{:S(2)}, u32[]{:S(2)}) collective-permute-start(bf16[256,256]{1,0:T(8,128)(2,1)S(1)} %get-tuple-element.33), channel_id=1, source_target_pairs={{0,10},{2,8},{4,14},{6,12},{8,2},{10,0},{12,6},{14,4},{16,26},{18,... | collective-permute-start | bytes 393224 | tf_op jit(solution)/shard_map/ppermute | solution.py:639
  35.3 15.2 %collective-permute-start.11 = (bf16[256,256]{1,0:T(8,128)(2,1)S(1)}, bf16[256,256]{1,0:T(8,128)(2,1)S(1)}, u32[]{:S(2)}, u32[]{:S(2)}) collective-permute-start(bf16[256,256]{1,0:T(8,128)(2,1)S(1)} %get-tuple-element.34), channel_id=1, source_target_pairs={{0,22},{2,20},{4,18},{6,16},{8,30},{10,28},{12,26},{14,24},{16,6},... | collective-permute-start | bytes 393224 | tf_op jit(solution)/shard_map/ppermute | solution.py:639
  40.3 11.5 %collective-permute-start.12 = (bf16[256,256]{1,0:T(8,128)(2,1)S(1)}, bf16[256,256]{1,0:T(8,128)(2,1)S(1)}, u32[]{:S(2)}, u32[]{:S(2)}) collective-permute-start(bf16[256,256]{1,0:T(8,128)(2,1)S(1)} %get-tuple-element.35), channel_id=1, source_target_pairs={{0,12},{2,14},{4,8},{6,10},{8,4},{10,6},{12,0},{14,2},{16,28},{18,... | collective-permute-start | bytes 393224 | tf_op jit(solution)/shard_map/ppermute | solution.py:639
  40.3 14.2 %collective-permute-start.13 = (bf16[256,256]{1,0:T(8,128)(2,1)S(1)}, bf16[256,256]{1,0:T(8,128)(2,1)S(1)}, u32[]{:S(2)}, u32[]{:S(2)}) collective-permute-start(bf16[256,256]{1,0:T(8,128)(2,1)S(1)} %get-tuple-element.36), channel_id=1, source_target_pairs={{0,30},{2,28},{4,26},{6,24},{8,22},{10,20},{12,18},{14,16},{16,14}... | collective-permute-start | bytes 393224 | tf_op jit(solution)/shard_map/ppermute | solution.py:639
  43.7 11.3 %collective-permute-start.14 = (bf16[256,256]{1,0:T(8,128)(2,1)S(1)}, bf16[256,256]{1,0:T(8,128)(2,1)S(1)}, u32[]{:S(2)}, u32[]{:S(2)}) collective-permute-start(bf16[256,256]{1,0:T(8,128)(2,1)S(1)} %get-tuple-element.37), channel_id=1, source_target_pairs={{0,14},{2,12},{4,10},{6,8},{8,6},{10,4},{12,2},{14,0},{16,30},{18,... | collective-permute-start | bytes 393224 | tf_op jit(solution)/shard_map/ppermute | solution.py:639
  55.0 40.8 %copy-start.2 = (bf16[256,2048]{1,0:T(8,128)(2,1)S(1)}, bf16[256,2048]{1,0:T(8,128)(2,1)}, u32[]{:S(2)}) copy-start(bf16[256,2048]{1,0:T(8,128)(2,1)} %gates_hbm.1) | copy-start | bytes 3145732
  55.0 40.8 %copy-start.3 = (f32[2048]{0:T(1024)S(1)}, f32[2048]{0:T(1024)}, u32[]{:S(2)}) copy-start(f32[2048]{0:T(1024)} %param.9) | copy-start | bytes 24580
  65.4 30.5 %all-to-all-start = ((bf16[16,256,128]{2,1,0:T(8,128)(2,1)}), bf16[16,256,128]{2,1,0:T(8,128)(2,1)S(1)}, u32[]{:S(2)}, u32[]{:S(2)}) async-start(bf16[16,256,128]{2,1,0:T(8,128)(2,1)} %long_convolution.1), calls=%async_computation | async-start | bytes 2097152 | tf_op jit(solution)/shard_map/all_to_all | solution.py:633
  99.2 2.8 %collective-permute-start.15 = (f32[256,1024]{1,0:T(8,128)S(1)}, f32[256,1024]{1,0:T(8,128)S(1)}, u32[]{:S(2)}, u32[]{:S(2)}) collective-permute-start(f32[256,1024]{1,0:T(8,128)S(1)} %get-tuple-element.40), channel_id=1, source_target_pairs={{0,1},{1,0},{2,3},{3,2},{4,5},{5,4},{6,7},{7,6},{8,9},{9,8},{10,11... | collective-permute-start | bytes 3145736 | tf_op jit(solution)/shard_map/ppermute | solution.py:650

commit v15 on v13

--- a/solution.py
+++ b/solution.py
@@ -18,7 +18,7 @@
 FIRST_BYTES = 60 * 1024 * 1024
 ARRANGE_BYTES = 12 * 1024 * 1024
 CONV_BYTES = 49 * 1024 * 1024
-TAIL_BYTES = 49 * 1024 * 1024
+TAIL_BYTES = 46 * 1024 * 1024
 
 
 def angle_table(first, second, period):
@@ -189,7 +189,7 @@
 
 def slot_order(blocks):
     half = blocks // 2
-    across = [half + (i // 2 if i % 2 == 0 else half // 2 + i // 2) for i in range(half)]
+    across = list(range(half, blocks))
     near = list(range(1, half)) + [0]
     return [slot for pair in zip(across, near) for slot in pair]
 

time: 102 us -> 102 us (level)
  starting transfers between devices: 33.9 us -> 42.4 us
  waiting for transfers between devices: 43.1 us -> 35 us
  Pallas kernels: 21.3 us -> 20.2 us
    ppermute x15, starting transfers between devices: 27.8 us -> 35.9 us  [exchange(): lax.ppermute(source, 'seq', [(j, j ^ slot) for j in range(blocks)])]
    ppermute x15, waiting for transfers between devices: 18.5 us -> 10.4 us  [exchange(): lax.ppermute(source, 'seq', [(j, j ^ slot) for j in range(blocks)])]
    unnamed x8 -> x12, local copies, waits for them, and re-layouts: 2.46 us -> 3.47 us
  transfers between devices with their start and end apart: 17 -> 17, of which waited for: 8 -> 6; matrix products, arithmetic and copies ran while one was open for 0% -> 0% of each run, Pallas kernels for 4% -> 4%
where the time goes in v15:
time: 102 us; the launch traced here: 101 us
  starting transfers between devices  42.4 us (42%)
  waiting for transfers between devices  35 us (34%)
  Pallas kernels  20.2 us (20%)
  local copies, waits for them, and re-layouts  3.47 us (3%)
    ppermute x15, starting transfers between devices, exchange(): lax.ppermute(source, 'seq', [(j, j ^ slot) for j in range(blocks)])  35.9 us
    all_to_all x1, waiting for transfers between devices, swap_blocks(): return lax.all_to_all(array, 'seq', split_axis=0, concat_axis=0, tiled=True)  24.5 us
    ppermute x15, waiting for transfers between devices, exchange(): lax.ppermute(source, 'seq', [(j, j ^ slot) for j in range(blocks)])  10.4 us
    pallas_call x1, Pallas kernels, convolve(): pl.pallas_call(functools.partial(convolve_kernel, blocks), in_specs=[pl.B...  9.73 us
    all_to_all x1, starting transfers between devices, swap_blocks(): return lax.all_to_all(array, 'seq', split_axis=0, concat_axis=0, tiled=True)  6.38 us
    unnamed x12, local copies, waits for them, and re-layouts  3.47 us
    pallas_call x1, Pallas kernels, gate_and_project(): pl.pallas_call(gate_kernel, in_specs=[pl.BlockSpec(memory_space=pltpu.SME...  2.85 us
    pallas_call x1, Pallas kernels, project_kept(): pl.pallas_call(kept_kernel, in_specs=[pl.BlockSpec(memory_space=pltpu.SME...  2.68 us
  transfers between devices with their start and end apart: 17, of which 6 were waited for; matrix products, arithmetic and copies ran while one was open for 0% of the time, Pallas kernels for 4%

profile of v15, /device:TPU:0, one launch (start us, length us, event | category | flops | bytes accessed | tf_op | source)
XLA Modules:
  0.0 101.2 jit_solution(5989214326480125120)
XLA Ops:
  0.0 2.3 %arrange_lead.1 = (bf16[256,256]{1,0:T(8,128)(2,1)}, bf16[256,256]{1,0:T(8,128)(2,1)}, bf16[256,256]{1,0:T(8,128)(2,1)}, bf16[256,256]{1,0:T(8,128)(2,1)}, bf16[256,256]{1,0:T(8,128)(2,1)}) custom-call(s32[1]{0:T(128)} %bitcast.1.me_ref, bf16[256,2048]{1,0:T(8,128)(2,1)} %values_hbm.5, bf16[256,2048]{1,0:T(8,128)(2,1)} %taps_hbm.3), custom_call_target="tpu_custom_call" | custom-call | flops 167772160 | bytes 1310720 | tf_op jit(solution)/shard_map/arrange_lead/pallas_call | solution.py:248
  2.3 4.1 %collective-permute-start = (bf16[256,256]{1,0:T(8,128)(2,1)}, bf16[256,256]{1,0:T(8,128)(2,1)S(1)}, u32[]{:S(2)}, u32[]{:S(2)}) collective-permute-start(bf16[256,256]{1,0:T(8,128)(2,1)} %get-tuple-element.23), channel_id=1, source_target_pairs={{0,16},{2,18},{4,20},{6,22},{8,24},{10,26},{12,28},{14,30},{16,0},... | collective-permute-start | bytes 393224 | tf_op jit(solution)/shard_map/ppermute | solution.py:638
  6.4 1.5 %collective-permute-start.1 = (bf16[256,256]{1,0:T(8,128)(2,1)}, bf16[256,256]{1,0:T(8,128)(2,1)S(1)}, u32[]{:S(2)}, u32[]{:S(2)}) collective-permute-start(bf16[256,256]{1,0:T(8,128)(2,1)} %get-tuple-element.24), channel_id=1, source_target_pairs={{0,2},{2,0},{4,6},{6,4},{8,10},{10,8},{12,14},{14,12},{16,18},{18,... | collective-permute-start | bytes 393224 | tf_op jit(solution)/shard_map/ppermute | solution.py:638
  7.9 1.8 %collective-permute-start.3 = (bf16[256,256]{1,0:T(8,128)(2,1)}, bf16[256,256]{1,0:T(8,128)(2,1)S(1)}, u32[]{:S(2)}, u32[]{:S(2)}) collective-permute-start(bf16[256,256]{1,0:T(8,128)(2,1)} %get-tuple-element.26), channel_id=1, source_target_pairs={{0,4},{2,6},{4,0},{6,2},{8,12},{10,14},{12,8},{14,10},{16,20},{18,... | collective-permute-start | bytes 393224 | tf_op jit(solution)/shard_map/ppermute | solution.py:638
  9.7 2.5 %collective-permute-start.4 = (bf16[256,256]{1,0:T(8,128)(2,1)}, bf16[256,256]{1,0:T(8,128)(2,1)S(1)}, u32[]{:S(2)}, u32[]{:S(2)}) collective-permute-start(bf16[256,256]{1,0:T(8,128)(2,1)} %get-tuple-element.27), channel_id=1, source_target_pairs={{0,20},{2,22},{4,16},{6,18},{8,28},{10,30},{12,24},{14,26},{16,4},... | collective-permute-start | bytes 393224 | tf_op jit(solution)/shard_map/ppermute | solution.py:638
  12.2 1.2 %copy-done = bf16[256,2048]{1,0:T(8,128)(2,1)S(1)} copy-done((bf16[256,2048]{1,0:T(8,128)(2,1)S(1)}, bf16[256,2048]{1,0:T(8,128)(2,1)}, u32[]{:S(2)}) %copy-start) | copy-done | bytes 1048600
  14.7 1.7 %arrange_others.1 = (bf16[256,256]{1,0:T(8,128)(2,1)S(1)}, bf16[256,256]{1,0:T(8,128)(2,1)S(1)}, bf16[256,256]{1,0:T(8,128)(2,1)S(1)}, bf16[256,256]{1,0:T(8,128...) custom-call(s32[1]{0:T(128)} %bitcast.1.me_ref, ...), custom_call_target="tpu_custom_call" | custom-call | flops 536870912 | bytes 4194304 | tf_op jit(solution)/shard_map/arrange_others/pallas_call | solution.py:263
  16.4 2.9 %collective-permute-done.rest_0_ = bf16[256,256]{1,0:T(8,128)(2,1)S(1)} collective-permute-done((bf16[256,256]{1,0:T(8,128)(2,1)}, bf16[256,256]{1,0:T(8,128)(2,1)S(1)}, u32[]{:S(2)}, u32[]{:S(2)}) %collective-permute-start) | collective-permute-done | bytes 131104 | tf_op jit(solution)/shard_map/ppermute | solution.py:638
  19.3 2.8 %collective-permute-start.5 = (bf16[256,256]{1,0:T(8,128)(2,1)S(1)}, bf16[256,256]{1,0:T(8,128)(2,1)S(1)}, u32[]{:S(2)}, u32[]{:S(2)}) collective-permute-start(bf16[256,256]{1,0:T(8,128)(2,1)S(1)} %get-tuple-element.28), channel_id=1, source_target_pairs={{0,6},{2,4},{4,2},{6,0},{8,14},{10,12},{12,10},{14,8},{16,22},{18,... | collective-permute-start | bytes 393224 | tf_op jit(solution)/shard_map/ppermute | solution.py:638
  22.1 1.3 %collective-permute-done.2.rest_2_ = bf16[256,256]{1,0:T(8,128)(2,1)S(1)} collective-permute-done((bf16[256,256]{1,0:T(8,128)(2,1)}, bf16[256,256]{1,0:T(8,128)(2,1)S(1)}, u32[]{:S(2)}, u32[]{:S(2)}) %collective-permute-start.2) | collective-permute-done | bytes 131104 | tf_op jit(solution)/shard_map/ppermute | solution.py:638
  23.4 1.7 %collective-permute-start.7 = (bf16[256,256]{1,0:T(8,128)(2,1)S(1)}, bf16[256,256]{1,0:T(8,128)(2,1)S(1)}, u32[]{:S(2)}, u32[]{:S(2)}) collective-permute-start(bf16[256,256]{1,0:T(8,128)(2,1)S(1)} %get-tuple-element.30), channel_id=1, source_target_pairs={{0,8},{2,10},{4,12},{6,14},{8,0},{10,2},{12,4},{14,6},{16,24},{18,... | collective-permute-start | bytes 393224 | tf_op jit(solution)/shard_map/ppermute | solution.py:638
  25.1 2.2 %collective-permute-start.8 = (bf16[256,256]{1,0:T(8,128)(2,1)S(1)}, bf16[256,256]{1,0:T(8,128)(2,1)S(1)}, u32[]{:S(2)}, u32[]{:S(2)}) collective-permute-start(bf16[256,256]{1,0:T(8,128)(2,1)S(1)} %get-tuple-element.31), channel_id=1, source_target_pairs={{0,24},{2,26},{4,28},{6,30},{8,16},{10,18},{12,20},{14,22},{16,8},... | collective-permute-start | bytes 393224 | tf_op jit(solution)/shard_map/ppermute | solution.py:638
  27.3 1.6 %collective-permute-start.9 = (bf16[256,256]{1,0:T(8,128)(2,1)S(1)}, bf16[256,256]{1,0:T(8,128)(2,1)S(1)}, u32[]{:S(2)}, u32[]{:S(2)}) collective-permute-start(bf16[256,256]{1,0:T(8,128)(2,1)S(1)} %get-tuple-element.32), channel_id=1, source_target_pairs={{0,10},{2,8},{4,14},{6,12},{8,2},{10,0},{12,6},{14,4},{16,26},{18,... | collective-permute-start | bytes 393224 | tf_op jit(solution)/shard_map/ppermute | solution.py:638
  28.9 4.9 %collective-permute-start.10 = (bf16[256,256]{1,0:T(8,128)(2,1)S(1)}, bf16[256,256]{1,0:T(8,128)(2,1)S(1)}, u32[]{:S(2)}, u32[]{:S(2)}) collective-permute-start(bf16[256,256]{1,0:T(8,128)(2,1)S(1)} %get-tuple-element.33), channel_id=1, source_target_pairs={{0,26},{2,24},{4,30},{6,28},{8,18},{10,16},{12,22},{14,20},{16,10}... | collective-permute-start | bytes 393224 | tf_op jit(solution)/shard_map/ppermute | solution.py:638
  33.9 1.8 %collective-permute-done.6.rest_6_ = bf16[256,256]{1,0:T(8,128)(2,1)S(1)} collective-permute-done((bf16[256,256]{1,0:T(8,128)(2,1)S(1)}, bf16[256,256]{1,0:T(8,128)(2,1)S(1)}, u32[]{:S(2)}, u32[]{:S(2)}) %collective-permute-start.6) | collective-permute-done | bytes 131104 | tf_op jit(solution)/shard_map/ppermute | solution.py:638
  35.7 6.9 %collective-permute-start.12 = (bf16[256,256]{1,0:T(8,128)(2,1)S(1)}, bf16[256,256]{1,0:T(8,128)(2,1)S(1)}, u32[]{:S(2)}, u32[]{:S(2)}) collective-permute-start(bf16[256,256]{1,0:T(8,128)(2,1)S(1)} %get-tuple-element.35), channel_id=1, source_target_pairs={{0,28},{2,30},{4,24},{6,26},{8,20},{10,22},{12,16},{14,18},{16,12}... | collective-permute-start | bytes 393224 | tf_op jit(solution)/shard_map/ppermute | solution.py:638
  42.6 5.9 %collective-permute-start.14 = (bf16[256,256]{1,0:T(8,128)(2,1)S(1)}, bf16[256,256]{1,0:T(8,128)(2,1)S(1)}, u32[]{:S(2)}, u32[]{:S(2)}) collective-permute-start(bf16[256,256]{1,0:T(8,128)(2,1)S(1)} %get-tuple-element.37), channel_id=1, source_target_pairs={{0,30},{2,28},{4,26},{6,24},{8,22},{10,20},{12,18},{14,16},{16,14}... | collective-permute-start | bytes 393224 | tf_op jit(solution)/shard_map/ppermute | solution.py:638
  48.5 2.6 %collective-permute-done.13.rest_13_ = bf16[256,256]{1,0:T(8,128)(2,1)S(1)} collective-permute-done((bf16[256,256]{1,0:T(8,128)(2,1)S(1)}, bf16[256,256]{1,0:T(8,128)(2,1)S(1)}, u32[]{:S(2)}, u32[]{:S(2)}) %collective-permute-start.13) | collective-permute-done | bytes 131104 | tf_op jit(solution)/shard_map/ppermute | solution.py:638
  51.1 1.8 %collective-permute-done.14.rest_14_ = bf16[256,256]{1,0:T(8,128)(2,1)S(1)} collective-permute-done((bf16[256,256]{1,0:T(8,128)(2,1)S(1)}, bf16[256,256]{1,0:T(8,128)(2,1)S(1)}, u32[]{:S(2)}, u32[]{:S(2)}) %collective-permute-start.14) | collective-permute-done | bytes 131104 | tf_op jit(solution)/shard_map/ppermute | solution.py:638
  52.9 9.7 %long_convolution.1 = bf16[16,256,128]{2,1,0:T(8,128)(2,1)S(1)} custom-call(s32[1]{0:T(128)} %bitcast.1.me_ref, bf16[256,256]{1,0:T(8,128)(2,1)S(1)} %collective-permute-done.rest_0_, bf16[256,256]{1,0:T(8,128)(2,1)S(1)} %collective-permute-done.1.rest_1_, bf16[256,256]{1,0:T(8,128)(2,1)S(1)} %collective-permute-done.2.rest_2_, ...), custom_call_target="tpu_custom_call" | custom-call | flops 5000000000 | bytes 9000000 | tf_op jit(solution)/shard_map/long_convolution/pallas_call | solution.py:481
  63.7 6.4 %all-to-all-start = ((bf16[16,256,128]{2,1,0:T(8,128)(2,1)}), bf16[16,256,128]{2,1,0:T(8,128)(2,1)S(1)}, u32[]{:S(2)}, u32[]{:S(2)}) async-start(bf16[16,256,128]{2,1,0:T(8,128)(2,1)} %copy-done.4), calls=%async_computation | async-start | bytes 2097152 | tf_op jit(solution)/shard_map/all_to_all | solution.py:632
  70.0 24.5 %all-to-all-done.conv_ref = bf16[16,256,128]{2,1,0:T(8,128)(2,1)S(1)} async-done(((bf16[16,256,128]{2,1,0:T(8,128)(2,1)}), bf16[16,256,128]{2,1,0:T(8,128)(2,1)S(1)}, u32[]{:S(2)}, u32[]{:S(2)}) %all-to-all-start) | async-done | bytes 1048608 | tf_op jit(solution)/shard_map/all_to_all | solution.py:632
  94.6 2.8 %gate_project_sent.1 = (bf16[256,2048]{1,0:T(8,128)(2,1)S(1)}, f32[256,1024]{1,0:T(8,128)S(1)}) custom-call(s32[1]{0:T(128)} %bitcast.half_ref, bf16[16,256,128]{2,1,0:T(8,128)(2,1)S(1)} %all-to-all-done.conv_ref, bf16[256,2048]{1,0:T(8,128)(2,1)S(1)} %copy-done.3, bf16[256,2048]{1,0:T(8,128)(2,1)S(1)} %copy-done.1, f32[1,2048]{1,0:T(1,128)S(1)} %bitcast.3, ...), custom_call_target="tpu_custom_call" | custom-call | flops 1073741824 | bytes 4194304 | tf_op jit(solution)/shard_map/gate_project_sent/pallas_call | solution.py:562
  97.5 2.7 %project_kept.1.kept_ref = f32[256,1024]{1,0:T(8,128)S(1)} custom-call(s32[1]{0:T(128)} %bitcast.half_ref, bf16[256,2048]{1,0:T(8,128)(2,1)S(1)} %get-tuple-element.39.gated_ref, bf16[2048,2048]{1,0:T(8,128)(2,1)} %weight_hbm.3), custom_call_target="tpu_custom_call" | custom-call | flops 1073741824 | bytes 4194304 | tf_op jit(solution)/shard_map/project_kept/pallas_call | solution.py:592
  (28 shorter events, 3.3 us)
Async XLA Ops:
  2.3 17.1 %collective-permute-start = (bf16[256,256]{1,0:T(8,128)(2,1)}, bf16[256,256]{1,0:T(8,128)(2,1)S(1)}, u32[]{:S(2)}, u32[]{:S(2)}) collective-permute-start(bf16[256,256]{1,0:T(8,128)(2,1)} %get-tuple-element.23), channel_id=1, source_target_pairs={{0,16},{2,18},{4,20},{6,22},{8,24},{10,26},{12,28},{14,30},{16,0},... | collective-permute-start | bytes 393224 | tf_op jit(solution)/shard_map/ppermute | solution.py:638
  6.4 15.8 %collective-permute-start.1 = (bf16[256,256]{1,0:T(8,128)(2,1)}, bf16[256,256]{1,0:T(8,128)(2,1)S(1)}, u32[]{:S(2)}, u32[]{:S(2)}) collective-permute-start(bf16[256,256]{1,0:T(8,128)(2,1)} %get-tuple-element.24), channel_id=1, source_target_pairs={{0,2},{2,0},{4,6},{6,4},{8,10},{10,8},{12,14},{14,12},{16,18},{18,... | collective-permute-start | bytes 393224 | tf_op jit(solution)/shard_map/ppermute | solution.py:638
  7.9 15.6 %collective-permute-start.2 = (bf16[256,256]{1,0:T(8,128)(2,1)}, bf16[256,256]{1,0:T(8,128)(2,1)S(1)}, u32[]{:S(2)}, u32[]{:S(2)}) collective-permute-start(bf16[256,256]{1,0:T(8,128)(2,1)} %get-tuple-element.25), channel_id=1, source_target_pairs={{0,18},{2,16},{4,22},{6,20},{8,26},{10,24},{12,30},{14,28},{16,2},... | collective-permute-start | bytes 393224 | tf_op jit(solution)/shard_map/ppermute | solution.py:638
  7.9 17.2 %collective-permute-start.3 = (bf16[256,256]{1,0:T(8,128)(2,1)}, bf16[256,256]{1,0:T(8,128)(2,1)S(1)}, u32[]{:S(2)}, u32[]{:S(2)}) collective-permute-start(bf16[256,256]{1,0:T(8,128)(2,1)} %get-tuple-element.26), channel_id=1, source_target_pairs={{0,4},{2,6},{4,0},{6,2},{8,12},{10,14},{12,8},{14,10},{16,20},{18,... | collective-permute-start | bytes 393224 | tf_op jit(solution)/shard_map/ppermute | solution.py:638
  9.7 17.6 %collective-permute-start.4 = (bf16[256,256]{1,0:T(8,128)(2,1)}, bf16[256,256]{1,0:T(8,128)(2,1)S(1)}, u32[]{:S(2)}, u32[]{:S(2)}) collective-permute-start(bf16[256,256]{1,0:T(8,128)(2,1)} %get-tuple-element.27), channel_id=1, source_target_pairs={{0,20},{2,22},{4,16},{6,18},{8,28},{10,30},{12,24},{14,26},{16,4},... | collective-permute-start | bytes 393224 | tf_op jit(solution)/shard_map/ppermute | solution.py:638
  12.2 1.2 %copy-start = (bf16[256,2048]{1,0:T(8,128)(2,1)S(1)}, bf16[256,2048]{1,0:T(8,128)(2,1)}, u32[]{:S(2)}) copy-start(bf16[256,2048]{1,0:T(8,128)(2,1)} %values_hbm.5) | copy-start | bytes 3145732
  13.5 1.2 %copy-start.2 = (bf16[256,2048]{1,0:T(8,128)(2,1)S(1)}, bf16[256,2048]{1,0:T(8,128)(2,1)}, u32[]{:S(2)}) copy-start(bf16[256,2048]{1,0:T(8,128)(2,1)} %taps_hbm.3) | copy-start | bytes 3145732
  19.3 9.6 %collective-permute-start.5 = (bf16[256,256]{1,0:T(8,128)(2,1)S(1)}, bf16[256,256]{1,0:T(8,128)(2,1)S(1)}, u32[]{:S(2)}, u32[]{:S(2)}) collective-permute-start(bf16[256,256]{1,0:T(8,128)(2,1)S(1)} %get-tuple-element.28), channel_id=1, source_target_pairs={{0,6},{2,4},{4,2},{6,0},{8,14},{10,12},{12,10},{14,8},{16,22},{18,... | collective-permute-start | bytes 393224 | tf_op jit(solution)/shard_map/ppermute | solution.py:638
  22.1 13.5 %collective-permute-start.6 = (bf16[256,256]{1,0:T(8,128)(2,1)S(1)}, bf16[256,256]{1,0:T(8,128)(2,1)S(1)}, u32[]{:S(2)}, u32[]{:S(2)}) collective-permute-start(bf16[256,256]{1,0:T(8,128)(2,1)S(1)} %get-tuple-element.29), channel_id=1, source_target_pairs={{0,22},{2,20},{4,18},{6,16},{8,30},{10,28},{12,26},{14,24},{16,6},... | collective-permute-start | bytes 393224 | tf_op jit(solution)/shard_map/ppermute | solution.py:638
  23.4 12.2 %collective-permute-start.7 = (bf16[256,256]{1,0:T(8,128)(2,1)S(1)}, bf16[256,256]{1,0:T(8,128)(2,1)S(1)}, u32[]{:S(2)}, u32[]{:S(2)}) collective-permute-start(bf16[256,256]{1,0:T(8,128)(2,1)S(1)} %get-tuple-element.30), channel_id=1, source_target_pairs={{0,8},{2,10},{4,12},{6,14},{8,0},{10,2},{12,4},{14,6},{16,24},{18,... | collective-permute-start | bytes 393224 | tf_op jit(solution)/shard_map/ppermute | solution.py:638
  25.1 17.5 %collective-permute-start.8 = (bf16[256,256]{1,0:T(8,128)(2,1)S(1)}, bf16[256,256]{1,0:T(8,128)(2,1)S(1)}, u32[]{:S(2)}, u32[]{:S(2)}) collective-permute-start(bf16[256,256]{1,0:T(8,128)(2,1)S(1)} %get-tuple-element.31), channel_id=1, source_target_pairs={{0,24},{2,26},{4,28},{6,30},{8,16},{10,18},{12,20},{14,22},{16,8},... | collective-permute-start | bytes 393224 | tf_op jit(solution)/shard_map/ppermute | solution.py:638
  27.3 15.3 %collective-permute-start.9 = (bf16[256,256]{1,0:T(8,128)(2,1)S(1)}, bf16[256,256]{1,0:T(8,128)(2,1)S(1)}, u32[]{:S(2)}, u32[]{:S(2)}) collective-permute-start(bf16[256,256]{1,0:T(8,128)(2,1)S(1)} %get-tuple-element.32), channel_id=1, source_target_pairs={{0,10},{2,8},{4,14},{6,12},{8,2},{10,0},{12,6},{14,4},{16,26},{18,... | collective-permute-start | bytes 393224 | tf_op jit(solution)/shard_map/ppermute | solution.py:638
  28.9 19.5 %collective-permute-start.10 = (bf16[256,256]{1,0:T(8,128)(2,1)S(1)}, bf16[256,256]{1,0:T(8,128)(2,1)S(1)}, u32[]{:S(2)}, u32[]{:S(2)}) collective-permute-start(bf16[256,256]{1,0:T(8,128)(2,1)S(1)} %get-tuple-element.33), channel_id=1, source_target_pairs={{0,26},{2,24},{4,30},{6,28},{8,18},{10,16},{12,22},{14,20},{16,10}... | collective-permute-start | bytes 393224 | tf_op jit(solution)/shard_map/ppermute | solution.py:638
  35.7 12.8 %collective-permute-start.11 = (bf16[256,256]{1,0:T(8,128)(2,1)S(1)}, bf16[256,256]{1,0:T(8,128)(2,1)S(1)}, u32[]{:S(2)}, u32[]{:S(2)}) collective-permute-start(bf16[256,256]{1,0:T(8,128)(2,1)S(1)} %get-tuple-element.34), channel_id=1, source_target_pairs={{0,12},{2,14},{4,8},{6,10},{8,4},{10,6},{12,0},{14,2},{16,28},{18,... | collective-permute-start | bytes 393224 | tf_op jit(solution)/shard_map/ppermute | solution.py:638
  35.7 12.8 %collective-permute-start.12 = (bf16[256,256]{1,0:T(8,128)(2,1)S(1)}, bf16[256,256]{1,0:T(8,128)(2,1)S(1)}, u32[]{:S(2)}, u32[]{:S(2)}) collective-permute-start(bf16[256,256]{1,0:T(8,128)(2,1)S(1)} %get-tuple-element.35), channel_id=1, source_target_pairs={{0,28},{2,30},{4,24},{6,26},{8,20},{10,22},{12,16},{14,18},{16,12}... | collective-permute-start | bytes 393224 | tf_op jit(solution)/shard_map/ppermute | solution.py:638
  42.6 8.5 %collective-permute-start.13 = (bf16[256,256]{1,0:T(8,128)(2,1)S(1)}, bf16[256,256]{1,0:T(8,128)(2,1)S(1)}, u32[]{:S(2)}, u32[]{:S(2)}) collective-permute-start(bf16[256,256]{1,0:T(8,128)(2,1)S(1)} %get-tuple-element.36), channel_id=1, source_target_pairs={{0,14},{2,12},{4,10},{6,8},{8,6},{10,4},{12,2},{14,0},{16,30},{18,... | collective-permute-start | bytes 393224 | tf_op jit(solution)/shard_map/ppermute | solution.py:638
  42.6 10.3 %collective-permute-start.14 = (bf16[256,256]{1,0:T(8,128)(2,1)S(1)}, bf16[256,256]{1,0:T(8,128)(2,1)S(1)}, u32[]{:S(2)}, u32[]{:S(2)}) collective-permute-start(bf16[256,256]{1,0:T(8,128)(2,1)S(1)} %get-tuple-element.37), channel_id=1, source_target_pairs={{0,30},{2,28},{4,26},{6,24},{8,22},{10,20},{12,18},{14,16},{16,14}... | collective-permute-start | bytes 393224 | tf_op jit(solution)/shard_map/ppermute | solution.py:638
  52.9 41.7 %copy-start.1 = (bf16[256,2048]{1,0:T(8,128)(2,1)S(1)}, bf16[256,2048]{1,0:T(8,128)(2,1)}, u32[]{:S(2)}) copy-start(bf16[256,2048]{1,0:T(8,128)(2,1)} %values_hbm.5) | copy-start | bytes 3145732
  52.9 41.7 %copy-start.3 = (bf16[256,2048]{1,0:T(8,128)(2,1)S(1)}, bf16[256,2048]{1,0:T(8,128)(2,1)}, u32[]{:S(2)}) copy-start(bf16[256,2048]{1,0:T(8,128)(2,1)} %gates_hbm.1) | copy-start | bytes 3145732
  52.9 41.7 %copy-start.5 = (f32[2048]{0:T(1024)S(1)}, f32[2048]{0:T(1024)}, u32[]{:S(2)}) copy-start(f32[2048]{0:T(1024)} %param.9) | copy-start | bytes 24580
  62.6 1.0 %copy-start.4 = (bf16[16,256,128]{2,1,0:T(8,128)(2,1)}, bf16[16,256,128]{2,1,0:T(8,128)(2,1)S(1)}, u32[]{:S(2)}) copy-start(bf16[16,256,128]{2,1,0:T(8,128)(2,1)S(1)} %long_convolution.1) | copy-start | bytes 3145732
  63.7 30.9 %all-to-all-start = ((bf16[16,256,128]{2,1,0:T(8,128)(2,1)}), bf16[16,256,128]{2,1,0:T(8,128)(2,1)S(1)}, u32[]{:S(2)}, u32[]{:S(2)}) async-start(bf16[16,256,128]{2,1,0:T(8,128)(2,1)} %copy-done.4), calls=%async_computation | async-start | bytes 2097152 | tf_op jit(solution)/shard_map/all_to_all | solution.py:632
  97.5 2.8 %collective-permute-start.15 = (f32[256,1024]{1,0:T(8,128)S(1)}, f32[256,1024]{1,0:T(8,128)S(1)}, u32[]{:S(2)}, u32[]{:S(2)}) collective-permute-start(f32[256,1024]{1,0:T(8,128)S(1)} %get-tuple-element.40), channel_id=1, source_target_pairs={{0,1},{1,0},{2,3},{3,2},{4,5},{5,4},{6,7},{7,6},{8,9},{9,8},{10,11... | collective-permute-start | bytes 3145736 | tf_op jit(solution)/shard_map/ppermute | solution.py:649

commit v16 on v13

--- a/solution.py
+++ b/solution.py
@@ -18,7 +18,7 @@
 FIRST_BYTES = 60 * 1024 * 1024
 ARRANGE_BYTES = 12 * 1024 * 1024
 CONV_BYTES = 49 * 1024 * 1024
-TAIL_BYTES = 49 * 1024 * 1024
+TAIL_BYTES = 48 * 1024 * 1024
 
 
 def angle_table(first, second, period):

time: 102 us -> 102 us (level)
  Pallas kernels: 21.3 us -> 20.2 us
    unnamed x8 -> x12, local copies, waits for them, and re-layouts: 2.46 us -> 3.47 us
where the time goes in v16:
time: 102 us; the launch traced here: 101 us
  waiting for transfers between devices  43.1 us (42%)
  starting transfers between devices  33.9 us (33%)
  Pallas kernels  20.2 us (20%)
  local copies, waits for them, and re-layouts  3.47 us (3%)
    ppermute x15, starting transfers between devices, exchange(): lax.ppermute(source, 'seq', [(j, j ^ slot) for j in range(blocks)])  27.8 us
    all_to_all x1, waiting for transfers between devices, swap_blocks(): return lax.all_to_all(array, 'seq', split_axis=0, concat_axis=0, tiled=True)  24.6 us
    ppermute x15, waiting for transfers between devices, exchange(): lax.ppermute(source, 'seq', [(j, j ^ slot) for j in range(blocks)])  18.5 us
    pallas_call x1, Pallas kernels, convolve(): pl.pallas_call(functools.partial(convolve_kernel, blocks), in_specs=[pl.B...  9.74 us
    all_to_all x1, starting transfers between devices, swap_blocks(): return lax.all_to_all(array, 'seq', split_axis=0, concat_axis=0, tiled=True)  6.02 us
    unnamed x12, local copies, waits for them, and re-layouts  3.47 us
    pallas_call x1, Pallas kernels, gate_and_project(): pl.pallas_call(gate_kernel, in_specs=[pl.BlockSpec(memory_space=pltpu.SME...  2.85 us
    pallas_call x1, Pallas kernels, project_kept(): pl.pallas_call(kept_kernel, in_specs=[pl.BlockSpec(memory_space=pltpu.SME...  2.68 us
  transfers between devices with their start and end apart: 17, of which 8 were waited for; matrix products, arithmetic and copies ran while one was open for 0% of the time, Pallas kernels for 4%

profile of v16, /device:TPU:0, one launch (start us, length us, event | category | flops | bytes accessed | tf_op | source)
XLA Modules:
  0.0 100.7 jit_solution(13640446425243302098)
XLA Ops:
  0.0 2.3 %arrange_lead.1 = (bf16[256,256]{1,0:T(8,128)(2,1)}, bf16[256,256]{1,0:T(8,128)(2,1)}, bf16[256,256]{1,0:T(8,128)(2,1)}, bf16[256,256]{1,0:T(8,128)(2,1)}, bf16[256,256]{1,0:T(8,128)(2,1)}) custom-call(s32[1]{0:T(128)} %bitcast.1.me_ref, bf16[256,2048]{1,0:T(8,128)(2,1)} %values_hbm.5, bf16[256,2048]{1,0:T(8,128)(2,1)} %taps_hbm.3), custom_call_target="tpu_custom_call" | custom-call | flops 167772160 | bytes 1310720 | tf_op jit(solution)/shard_map/arrange_lead/pallas_call | solution.py:248
  2.3 4.1 %collective-permute-start = (bf16[256,256]{1,0:T(8,128)(2,1)}, bf16[256,256]{1,0:T(8,128)(2,1)S(1)}, u32[]{:S(2)}, u32[]{:S(2)}) collective-permute-start(bf16[256,256]{1,0:T(8,128)(2,1)} %get-tuple-element.23), channel_id=1, source_target_pairs={{0,16},{2,18},{4,20},{6,22},{8,24},{10,26},{12,28},{14,30},{16,0},... | collective-permute-start | bytes 393224 | tf_op jit(solution)/shard_map/ppermute | solution.py:638
  6.4 1.5 %collective-permute-start.1 = (bf16[256,256]{1,0:T(8,128)(2,1)}, bf16[256,256]{1,0:T(8,128)(2,1)S(1)}, u32[]{:S(2)}, u32[]{:S(2)}) collective-permute-start(bf16[256,256]{1,0:T(8,128)(2,1)} %get-tuple-element.24), channel_id=1, source_target_pairs={{0,2},{2,0},{4,6},{6,4},{8,10},{10,8},{12,14},{14,12},{16,18},{18,... | collective-permute-start | bytes 393224 | tf_op jit(solution)/shard_map/ppermute | solution.py:638
  7.9 1.3 %collective-permute-start.2 = (bf16[256,256]{1,0:T(8,128)(2,1)}, bf16[256,256]{1,0:T(8,128)(2,1)S(1)}, u32[]{:S(2)}, u32[]{:S(2)}) collective-permute-start(bf16[256,256]{1,0:T(8,128)(2,1)} %get-tuple-element.25), channel_id=1, source_target_pairs={{0,24},{2,26},{4,28},{6,30},{8,16},{10,18},{12,20},{14,22},{16,8},... | collective-permute-start | bytes 393224 | tf_op jit(solution)/shard_map/ppermute | solution.py:638
  9.2 1.5 %collective-permute-start.3 = (bf16[256,256]{1,0:T(8,128)(2,1)}, bf16[256,256]{1,0:T(8,128)(2,1)S(1)}, u32[]{:S(2)}, u32[]{:S(2)}) collective-permute-start(bf16[256,256]{1,0:T(8,128)(2,1)} %get-tuple-element.26), channel_id=1, source_target_pairs={{0,4},{2,6},{4,0},{6,2},{8,12},{10,14},{12,8},{14,10},{16,20},{18,... | collective-permute-start | bytes 393224 | tf_op jit(solution)/shard_map/ppermute | solution.py:638
  10.7 1.7 %collective-permute-start.4 = (bf16[256,256]{1,0:T(8,128)(2,1)}, bf16[256,256]{1,0:T(8,128)(2,1)S(1)}, u32[]{:S(2)}, u32[]{:S(2)}) collective-permute-start(bf16[256,256]{1,0:T(8,128)(2,1)} %get-tuple-element.27), channel_id=1, source_target_pairs={{0,18},{2,16},{4,22},{6,20},{8,26},{10,24},{12,30},{14,28},{16,2},... | collective-permute-start | bytes 393224 | tf_op jit(solution)/shard_map/ppermute | solution.py:638
  12.4 1.2 %copy-done = bf16[256,2048]{1,0:T(8,128)(2,1)S(1)} copy-done((bf16[256,2048]{1,0:T(8,128)(2,1)S(1)}, bf16[256,2048]{1,0:T(8,128)(2,1)}, u32[]{:S(2)}) %copy-start) | copy-done | bytes 1048600
  13.6 1.2 %copy-done.2 = bf16[256,2048]{1,0:T(8,128)(2,1)S(1)} copy-done((bf16[256,2048]{1,0:T(8,128)(2,1)S(1)}, bf16[256,2048]{1,0:T(8,128)(2,1)}, u32[]{:S(2)}) %copy-start.2) | copy-done | bytes 1048600
  14.9 1.7 %arrange_others.1 = (bf16[256,256]{1,0:T(8,128)(2,1)S(1)}, bf16[256,256]{1,0:T(8,128)(2,1)S(1)}, bf16[256,256]{1,0:T(8,128)(2,1)S(1)}, bf16[256,256]{1,0:T(8,128...) custom-call(s32[1]{0:T(128)} %bitcast.1.me_ref, ...), custom_call_target="tpu_custom_call" | custom-call | flops 536870912 | bytes 4194304 | tf_op jit(solution)/shard_map/arrange_others/pallas_call | solution.py:263
  16.6 2.7 %collective-permute-done.rest_0_ = bf16[256,256]{1,0:T(8,128)(2,1)S(1)} collective-permute-done((bf16[256,256]{1,0:T(8,128)(2,1)}, bf16[256,256]{1,0:T(8,128)(2,1)S(1)}, u32[]{:S(2)}, u32[]{:S(2)}) %collective-permute-start) | collective-permute-done | bytes 131104 | tf_op jit(solution)/shard_map/ppermute | solution.py:638
  19.3 2.8 %collective-permute-start.5 = (bf16[256,256]{1,0:T(8,128)(2,1)S(1)}, bf16[256,256]{1,0:T(8,128)(2,1)S(1)}, u32[]{:S(2)}, u32[]{:S(2)}) collective-permute-start(bf16[256,256]{1,0:T(8,128)(2,1)S(1)} %get-tuple-element.28), channel_id=1, source_target_pairs={{0,6},{2,4},{4,2},{6,0},{8,14},{10,12},{12,10},{14,8},{16,22},{18,... | collective-permute-start | bytes 393224 | tf_op jit(solution)/shard_map/ppermute | solution.py:638
  22.1 2.4 %collective-permute-start.6 = (bf16[256,256]{1,0:T(8,128)(2,1)S(1)}, bf16[256,256]{1,0:T(8,128)(2,1)S(1)}, u32[]{:S(2)}, u32[]{:S(2)}) collective-permute-start(bf16[256,256]{1,0:T(8,128)(2,1)S(1)} %get-tuple-element.29), channel_id=1, source_target_pairs={{0,26},{2,24},{4,30},{6,28},{8,18},{10,16},{12,22},{14,20},{16,10}... | collective-permute-start | bytes 393224 | tf_op jit(solution)/shard_map/ppermute | solution.py:638
  24.6 1.5 %collective-permute-start.8 = (bf16[256,256]{1,0:T(8,128)(2,1)S(1)}, bf16[256,256]{1,0:T(8,128)(2,1)S(1)}, u32[]{:S(2)}, u32[]{:S(2)}) collective-permute-start(bf16[256,256]{1,0:T(8,128)(2,1)S(1)} %get-tuple-element.31), channel_id=1, source_target_pairs={{0,20},{2,22},{4,16},{6,18},{8,28},{10,30},{12,24},{14,26},{16,4},... | collective-permute-start | bytes 393224 | tf_op jit(solution)/shard_map/ppermute | solution.py:638
  28.7 7.1 %collective-permute-start.10 = (bf16[256,256]{1,0:T(8,128)(2,1)S(1)}, bf16[256,256]{1,0:T(8,128)(2,1)S(1)}, u32[]{:S(2)}, u32[]{:S(2)}) collective-permute-start(bf16[256,256]{1,0:T(8,128)(2,1)S(1)} %get-tuple-element.33), channel_id=1, source_target_pairs={{0,28},{2,30},{4,24},{6,26},{8,20},{10,22},{12,16},{14,18},{16,12}... | collective-permute-start | bytes 393224 | tf_op jit(solution)/shard_map/ppermute | solution.py:638
  36.4 3.9 %collective-permute-done.8.rest_8_ = bf16[256,256]{1,0:T(8,128)(2,1)S(1)} collective-permute-done((bf16[256,256]{1,0:T(8,128)(2,1)S(1)}, bf16[256,256]{1,0:T(8,128)(2,1)S(1)}, u32[]{:S(2)}, u32[]{:S(2)}) %collective-permute-start.8) | collective-permute-done | bytes 131104 | tf_op jit(solution)/shard_map/ppermute | solution.py:638
  40.3 2.4 %collective-permute-start.14 = (bf16[256,256]{1,0:T(8,128)(2,1)S(1)}, bf16[256,256]{1,0:T(8,128)(2,1)S(1)}, u32[]{:S(2)}, u32[]{:S(2)}) collective-permute-start(bf16[256,256]{1,0:T(8,128)(2,1)S(1)} %get-tuple-element.37), channel_id=1, source_target_pairs={{0,30},{2,28},{4,26},{6,24},{8,22},{10,20},{12,18},{14,16},{16,14}... | collective-permute-start | bytes 393224 | tf_op jit(solution)/shard_map/ppermute | solution.py:638
  42.7 1.4 %collective-permute-done.11.rest_11_ = bf16[256,256]{1,0:T(8,128)(2,1)S(1)} collective-permute-done((bf16[256,256]{1,0:T(8,128)(2,1)S(1)}, bf16[256,256]{1,0:T(8,128)(2,1)S(1)}, u32[]{:S(2)}, u32[]{:S(2)}) %collective-permute-start.11) | collective-permute-done | bytes 131104 | tf_op jit(solution)/shard_map/ppermute | solution.py:638
  44.1 6.3 %collective-permute-done.12.rest_12_ = bf16[256,256]{1,0:T(8,128)(2,1)S(1)} collective-permute-done((bf16[256,256]{1,0:T(8,128)(2,1)S(1)}, bf16[256,256]{1,0:T(8,128)(2,1)S(1)}, u32[]{:S(2)}, u32[]{:S(2)}) %collective-permute-start.12) | collective-permute-done | bytes 131104 | tf_op jit(solution)/shard_map/ppermute | solution.py:638
  50.4 2.4 %collective-permute-done.14.rest_14_ = bf16[256,256]{1,0:T(8,128)(2,1)S(1)} collective-permute-done((bf16[256,256]{1,0:T(8,128)(2,1)S(1)}, bf16[256,256]{1,0:T(8,128)(2,1)S(1)}, u32[]{:S(2)}, u32[]{:S(2)}) %collective-permute-start.14) | collective-permute-done | bytes 131104 | tf_op jit(solution)/shard_map/ppermute | solution.py:638
  52.8 9.7 %long_convolution.1 = bf16[16,256,128]{2,1,0:T(8,128)(2,1)S(1)} custom-call(s32[1]{0:T(128)} %bitcast.1.me_ref, bf16[256,256]{1,0:T(8,128)(2,1)S(1)} %collective-permute-done.rest_0_, bf16[256,256]{1,0:T(8,128)(2,1)S(1)} %collective-permute-done.1.rest_1_, bf16[256,256]{1,0:T(8,128)(2,1)S(1)} %collective-permute-done.2.rest_2_, ...), custom_call_target="tpu_custom_call" | custom-call | flops 5000000000 | bytes 9000000 | tf_op jit(solution)/shard_map/long_convolution/pallas_call | solution.py:481
  63.5 6.0 %all-to-all-start = ((bf16[16,256,128]{2,1,0:T(8,128)(2,1)}), bf16[16,256,128]{2,1,0:T(8,128)(2,1)S(1)}, u32[]{:S(2)}, u32[]{:S(2)}) async-start(bf16[16,256,128]{2,1,0:T(8,128)(2,1)} %copy-done.4), calls=%async_computation | async-start | bytes 2097152 | tf_op jit(solution)/shard_map/all_to_all | solution.py:632
  69.6 24.6 %all-to-all-done.conv_ref = bf16[16,256,128]{2,1,0:T(8,128)(2,1)S(1)} async-done(((bf16[16,256,128]{2,1,0:T(8,128)(2,1)}), bf16[16,256,128]{2,1,0:T(8,128)(2,1)S(1)}, u32[]{:S(2)}, u32[]{:S(2)}) %all-to-all-start) | async-done | bytes 1048608 | tf_op jit(solution)/shard_map/all_to_all | solution.py:632
  94.2 2.9 %gate_project_sent.1 = (bf16[256,2048]{1,0:T(8,128)(2,1)S(1)}, f32[256,1024]{1,0:T(8,128)S(1)}) custom-call(s32[1]{0:T(128)} %bitcast.half_ref, bf16[16,256,128]{2,1,0:T(8,128)(2,1)S(1)} %all-to-all-done.conv_ref, bf16[256,2048]{1,0:T(8,128)(2,1)S(1)} %copy-done.3, bf16[256,2048]{1,0:T(8,128)(2,1)S(1)} %copy-done.1, f32[1,2048]{1,0:T(1,128)S(1)} %bitcast.3, ...), custom_call_target="tpu_custom_call" | custom-call | flops 1073741824 | bytes 4194304 | tf_op jit(solution)/shard_map/gate_project_sent/pallas_call | solution.py:562
  97.1 2.7 %project_kept.1.kept_ref = f32[256,1024]{1,0:T(8,128)S(1)} custom-call(s32[1]{0:T(128)} %bitcast.half_ref, bf16[256,2048]{1,0:T(8,128)(2,1)S(1)} %get-tuple-element.39.gated_ref, bf16[2048,2048]{1,0:T(8,128)(2,1)} %weight_hbm.3), custom_call_target="tpu_custom_call" | custom-call | flops 1073741824 | bytes 4194304 | tf_op jit(solution)/shard_map/project_kept/pallas_call | solution.py:592
  (28 shorter events, 5.2 us)
Async XLA Ops:
  2.3 17.1 %collective-permute-start = (bf16[256,256]{1,0:T(8,128)(2,1)}, bf16[256,256]{1,0:T(8,128)(2,1)S(1)}, u32[]{:S(2)}, u32[]{:S(2)}) collective-permute-start(bf16[256,256]{1,0:T(8,128)(2,1)} %get-tuple-element.23), channel_id=1, source_target_pairs={{0,16},{2,18},{4,20},{6,22},{8,24},{10,26},{12,28},{14,30},{16,0},... | collective-permute-start | bytes 393224 | tf_op jit(solution)/shard_map/ppermute | solution.py:638
  6.4 15.8 %collective-permute-start.1 = (bf16[256,256]{1,0:T(8,128)(2,1)}, bf16[256,256]{1,0:T(8,128)(2,1)S(1)}, u32[]{:S(2)}, u32[]{:S(2)}) collective-permute-start(bf16[256,256]{1,0:T(8,128)(2,1)} %get-tuple-element.24), channel_id=1, source_target_pairs={{0,2},{2,0},{4,6},{6,4},{8,10},{10,8},{12,14},{14,12},{16,18},{18,... | collective-permute-start | bytes 393224 | tf_op jit(solution)/shard_map/ppermute | solution.py:638
  7.9 16.7 %collective-permute-start.2 = (bf16[256,256]{1,0:T(8,128)(2,1)}, bf16[256,256]{1,0:T(8,128)(2,1)S(1)}, u32[]{:S(2)}, u32[]{:S(2)}) collective-permute-start(bf16[256,256]{1,0:T(8,128)(2,1)} %get-tuple-element.25), channel_id=1, source_target_pairs={{0,24},{2,26},{4,28},{6,30},{8,16},{10,18},{12,20},{14,22},{16,8},... | collective-permute-start | bytes 393224 | tf_op jit(solution)/shard_map/ppermute | solution.py:638
  9.2 15.4 %collective-permute-start.3 = (bf16[256,256]{1,0:T(8,128)(2,1)}, bf16[256,256]{1,0:T(8,128)(2,1)S(1)}, u32[]{:S(2)}, u32[]{:S(2)}) collective-permute-start(bf16[256,256]{1,0:T(8,128)(2,1)} %get-tuple-element.26), channel_id=1, source_target_pairs={{0,4},{2,6},{4,0},{6,2},{8,12},{10,14},{12,8},{14,10},{16,20},{18,... | collective-permute-start | bytes 393224 | tf_op jit(solution)/shard_map/ppermute | solution.py:638
  10.7 16.4 %collective-permute-start.4 = (bf16[256,256]{1,0:T(8,128)(2,1)}, bf16[256,256]{1,0:T(8,128)(2,1)S(1)}, u32[]{:S(2)}, u32[]{:S(2)}) collective-permute-start(bf16[256,256]{1,0:T(8,128)(2,1)} %get-tuple-element.27), channel_id=1, source_target_pairs={{0,18},{2,16},{4,22},{6,20},{8,26},{10,24},{12,30},{14,28},{16,2},... | collective-permute-start | bytes 393224 | tf_op jit(solution)/shard_map/ppermute | solution.py:638
  12.4 1.2 %copy-start = (bf16[256,2048]{1,0:T(8,128)(2,1)S(1)}, bf16[256,2048]{1,0:T(8,128)(2,1)}, u32[]{:S(2)}) copy-start(bf16[256,2048]{1,0:T(8,128)(2,1)} %values_hbm.5) | copy-start | bytes 3145732
  13.6 1.2 %copy-start.2 = (bf16[256,2048]{1,0:T(8,128)(2,1)S(1)}, bf16[256,2048]{1,0:T(8,128)(2,1)}, u32[]{:S(2)}) copy-start(bf16[256,2048]{1,0:T(8,128)(2,1)} %taps_hbm.3) | copy-start | bytes 3145732
  19.3 9.4 %collective-permute-start.5 = (bf16[256,256]{1,0:T(8,128)(2,1)S(1)}, bf16[256,256]{1,0:T(8,128)(2,1)S(1)}, u32[]{:S(2)}, u32[]{:S(2)}) collective-permute-start(bf16[256,256]{1,0:T(8,128)(2,1)S(1)} %get-tuple-element.28), channel_id=1, source_target_pairs={{0,6},{2,4},{4,2},{6,0},{8,14},{10,12},{12,10},{14,8},{16,22},{18,... | collective-permute-start | bytes 393224 | tf_op jit(solution)/shard_map/ppermute | solution.py:638
  22.1 13.6 %collective-permute-start.6 = (bf16[256,256]{1,0:T(8,128)(2,1)S(1)}, bf16[256,256]{1,0:T(8,128)(2,1)S(1)}, u32[]{:S(2)}, u32[]{:S(2)}) collective-permute-start(bf16[256,256]{1,0:T(8,128)(2,1)S(1)} %get-tuple-element.29), channel_id=1, source_target_pairs={{0,26},{2,24},{4,30},{6,28},{8,18},{10,16},{12,22},{14,20},{16,10}... | collective-permute-start | bytes 393224 | tf_op jit(solution)/shard_map/ppermute | solution.py:638
  24.6 11.2 %collective-permute-start.7 = (bf16[256,256]{1,0:T(8,128)(2,1)S(1)}, bf16[256,256]{1,0:T(8,128)(2,1)S(1)}, u32[]{:S(2)}, u32[]{:S(2)}) collective-permute-start(bf16[256,256]{1,0:T(8,128)(2,1)S(1)} %get-tuple-element.30), channel_id=1, source_target_pairs={{0,8},{2,10},{4,12},{6,14},{8,0},{10,2},{12,4},{14,6},{16,24},{18,... | collective-permute-start | bytes 393224 | tf_op jit(solution)/shard_map/ppermute | solution.py:638
  24.6 15.7 %collective-permute-start.8 = (bf16[256,256]{1,0:T(8,128)(2,1)S(1)}, bf16[256,256]{1,0:T(8,128)(2,1)S(1)}, u32[]{:S(2)}, u32[]{:S(2)}) collective-permute-start(bf16[256,256]{1,0:T(8,128)(2,1)S(1)} %get-tuple-element.31), channel_id=1, source_target_pairs={{0,20},{2,22},{4,16},{6,18},{8,28},{10,30},{12,24},{14,26},{16,4},... | collective-permute-start | bytes 393224 | tf_op jit(solution)/shard_map/ppermute | solution.py:638
  27.1 13.2 %collective-permute-start.9 = (bf16[256,256]{1,0:T(8,128)(2,1)S(1)}, bf16[256,256]{1,0:T(8,128)(2,1)S(1)}, u32[]{:S(2)}, u32[]{:S(2)}) collective-permute-start(bf16[256,256]{1,0:T(8,128)(2,1)S(1)} %get-tuple-element.32), channel_id=1, source_target_pairs={{0,10},{2,8},{4,14},{6,12},{8,2},{10,0},{12,6},{14,4},{16,26},{18,... | collective-permute-start | bytes 393224 | tf_op jit(solution)/shard_map/ppermute | solution.py:638
  28.7 14.0 %collective-permute-start.10 = (bf16[256,256]{1,0:T(8,128)(2,1)S(1)}, bf16[256,256]{1,0:T(8,128)(2,1)S(1)}, u32[]{:S(2)}, u32[]{:S(2)}) collective-permute-start(bf16[256,256]{1,0:T(8,128)(2,1)S(1)} %get-tuple-element.33), channel_id=1, source_target_pairs={{0,28},{2,30},{4,24},{6,26},{8,20},{10,22},{12,16},{14,18},{16,12}... | collective-permute-start | bytes 393224 | tf_op jit(solution)/shard_map/ppermute | solution.py:638
  35.8 8.3 %collective-permute-start.11 = (bf16[256,256]{1,0:T(8,128)(2,1)S(1)}, bf16[256,256]{1,0:T(8,128)(2,1)S(1)}, u32[]{:S(2)}, u32[]{:S(2)}) collective-permute-start(bf16[256,256]{1,0:T(8,128)(2,1)S(1)} %get-tuple-element.34), channel_id=1, source_target_pairs={{0,12},{2,14},{4,8},{6,10},{8,4},{10,6},{12,0},{14,2},{16,28},{18,... | collective-permute-start | bytes 393224 | tf_op jit(solution)/shard_map/ppermute | solution.py:638
  35.8 14.6 %collective-permute-start.12 = (bf16[256,256]{1,0:T(8,128)(2,1)S(1)}, bf16[256,256]{1,0:T(8,128)(2,1)S(1)}, u32[]{:S(2)}, u32[]{:S(2)}) collective-permute-start(bf16[256,256]{1,0:T(8,128)(2,1)S(1)} %get-tuple-element.35), channel_id=1, source_target_pairs={{0,22},{2,20},{4,18},{6,16},{8,30},{10,28},{12,26},{14,24},{16,6},... | collective-permute-start | bytes 393224 | tf_op jit(solution)/shard_map/ppermute | solution.py:638
  40.3 10.1 %collective-permute-start.13 = (bf16[256,256]{1,0:T(8,128)(2,1)S(1)}, bf16[256,256]{1,0:T(8,128)(2,1)S(1)}, u32[]{:S(2)}, u32[]{:S(2)}) collective-permute-start(bf16[256,256]{1,0:T(8,128)(2,1)S(1)} %get-tuple-element.36), channel_id=1, source_target_pairs={{0,14},{2,12},{4,10},{6,8},{8,6},{10,4},{12,2},{14,0},{16,30},{18,... | collective-permute-start | bytes 393224 | tf_op jit(solution)/shard_map/ppermute | solution.py:638
  40.3 12.4 %collective-permute-start.14 = (bf16[256,256]{1,0:T(8,128)(2,1)S(1)}, bf16[256,256]{1,0:T(8,128)(2,1)S(1)}, u32[]{:S(2)}, u32[]{:S(2)}) collective-permute-start(bf16[256,256]{1,0:T(8,128)(2,1)S(1)} %get-tuple-element.37), channel_id=1, source_target_pairs={{0,30},{2,28},{4,26},{6,24},{8,22},{10,20},{12,18},{14,16},{16,14}... | collective-permute-start | bytes 393224 | tf_op jit(solution)/shard_map/ppermute | solution.py:638
  52.8 41.4 %copy-start.1 = (bf16[256,2048]{1,0:T(8,128)(2,1)S(1)}, bf16[256,2048]{1,0:T(8,128)(2,1)}, u32[]{:S(2)}) copy-start(bf16[256,2048]{1,0:T(8,128)(2,1)} %values_hbm.5) | copy-start | bytes 3145732
  52.8 41.4 %copy-start.3 = (bf16[256,2048]{1,0:T(8,128)(2,1)S(1)}, bf16[256,2048]{1,0:T(8,128)(2,1)}, u32[]{:S(2)}) copy-start(bf16[256,2048]{1,0:T(8,128)(2,1)} %gates_hbm.1) | copy-start | bytes 3145732
  52.8 41.4 %copy-start.5 = (f32[2048]{0:T(1024)S(1)}, f32[2048]{0:T(1024)}, u32[]{:S(2)}) copy-start(f32[2048]{0:T(1024)} %param.9) | copy-start | bytes 24580
  62.5 1.0 %copy-start.4 = (bf16[16,256,128]{2,1,0:T(8,128)(2,1)}, bf16[16,256,128]{2,1,0:T(8,128)(2,1)S(1)}, u32[]{:S(2)}) copy-start(bf16[16,256,128]{2,1,0:T(8,128)(2,1)S(1)} %long_convolution.1) | copy-start | bytes 3145732
  63.5 30.6 %all-to-all-start = ((bf16[16,256,128]{2,1,0:T(8,128)(2,1)}), bf16[16,256,128]{2,1,0:T(8,128)(2,1)S(1)}, u32[]{:S(2)}, u32[]{:S(2)}) async-start(bf16[16,256,128]{2,1,0:T(8,128)(2,1)} %copy-done.4), calls=%async_computation | async-start | bytes 2097152 | tf_op jit(solution)/shard_map/all_to_all | solution.py:632
  97.0 2.8 %collective-permute-start.15 = (f32[256,1024]{1,0:T(8,128)S(1)}, f32[256,1024]{1,0:T(8,128)S(1)}, u32[]{:S(2)}, u32[]{:S(2)}) collective-permute-start(f32[256,1024]{1,0:T(8,128)S(1)} %get-tuple-element.40), channel_id=1, source_target_pairs={{0,1},{1,0},{2,3},{3,2},{4,5},{5,4},{6,7},{7,6},{8,9},{9,8},{10,11... | collective-permute-start | bytes 3145736 | tf_op jit(solution)/shard_map/ppermute | solution.py:649

commit v17 on v13

--- a/solution.py
+++ b/solution.py
@@ -374,7 +374,7 @@
         transform(0, pair)
         return carry
 
-    lax.fori_loop(0, 2, alone, 0)
+    lax.fori_loop(0, 2, alone, 0, unroll=True)
     for low in range(1, 4):
         load_turns[low - 1].wait()
 
@@ -408,7 +408,7 @@
                     mixed[4 * high + k, lower] = point[1]
         return carry
 
-    lax.fori_loop(0, part_rows // 8, middle, 0)
+    lax.fori_loop(0, part_rows // 8, middle, 0, unroll=2)
 
     def last_pass(low, start):
         target = halves[low % 2]

time: 102 us -> 102 us (level)
  no operation moved by 1% of the time
where the time goes in v17:
time: 102 us; the launch traced here: 101 us
  waiting for transfers between devices  43.1 us (42%)
  starting transfers between devices  33.9 us (33%)
  Pallas kernels  21 us (21%)
  local copies, waits for them, and re-layouts  2.46 us (2%)
    ppermute x15, starting transfers between devices, exchange(): lax.ppermute(source, 'seq', [(j, j ^ slot) for j in range(blocks)])  27.8 us
    all_to_all x1, waiting for transfers between devices, swap_blocks(): return lax.all_to_all(array, 'seq', split_axis=0, concat_axis=0, tiled=True)  24.6 us
    ppermute x15, waiting for transfers between devices, exchange(): lax.ppermute(source, 'seq', [(j, j ^ slot) for j in range(blocks)])  18.5 us
    pallas_call x1, Pallas kernels, convolve(): pl.pallas_call(functools.partial(convolve_kernel, blocks), in_specs=[pl.B...  10.1 us
    all_to_all x1, starting transfers between devices, swap_blocks(): return lax.all_to_all(array, 'seq', split_axis=0, concat_axis=0, tiled=True)  6.02 us
    pallas_call x1, Pallas kernels, gate_and_project(): pl.pallas_call(gate_kernel, in_specs=[pl.BlockSpec(memory_space=pltpu.SME...  3.3 us
    pallas_call x1, Pallas kernels, project_kept(): pl.pallas_call(kept_kernel, in_specs=[pl.BlockSpec(memory_space=pltpu.SME...  2.69 us
    unnamed x8, local copies, waits for them, and re-layouts  2.46 us
  transfers between devices with their start and end apart: 17, of which 8 were waited for; matrix products, arithmetic and copies ran while one was open for 0% of the time, Pallas kernels for 4%

profile of v17, /device:TPU:0, one launch (start us, length us, event | category | flops | bytes accessed | tf_op | source)
XLA Modules:
  0.0 100.5 jit_solution(7721734768905421290)
XLA Ops:
  0.0 2.3 %arrange_lead.1 = (bf16[256,256]{1,0:T(8,128)(2,1)}, bf16[256,256]{1,0:T(8,128)(2,1)}, bf16[256,256]{1,0:T(8,128)(2,1)}, bf16[256,256]{1,0:T(8,128)(2,1)}, bf16[256,256]{1,0:T(8,128)(2,1)}) custom-call(s32[1]{0:T(128)} %bitcast.1.me_ref, bf16[256,2048]{1,0:T(8,128)(2,1)} %values_hbm.5, bf16[256,2048]{1,0:T(8,128)(2,1)} %taps_hbm.3), custom_call_target="tpu_custom_call" | custom-call | flops 167772160 | bytes 1310720 | tf_op jit(solution)/shard_map/arrange_lead/pallas_call | solution.py:248
  2.3 4.1 %collective-permute-start = (bf16[256,256]{1,0:T(8,128)(2,1)}, bf16[256,256]{1,0:T(8,128)(2,1)S(1)}, u32[]{:S(2)}, u32[]{:S(2)}) collective-permute-start(bf16[256,256]{1,0:T(8,128)(2,1)} %get-tuple-element.23), channel_id=1, source_target_pairs={{0,16},{2,18},{4,20},{6,22},{8,24},{10,26},{12,28},{14,30},{16,0},... | collective-permute-start | bytes 393224 | tf_op jit(solution)/shard_map/ppermute | solution.py:638
  6.4 1.5 %collective-permute-start.1 = (bf16[256,256]{1,0:T(8,128)(2,1)}, bf16[256,256]{1,0:T(8,128)(2,1)S(1)}, u32[]{:S(2)}, u32[]{:S(2)}) collective-permute-start(bf16[256,256]{1,0:T(8,128)(2,1)} %get-tuple-element.24), channel_id=1, source_target_pairs={{0,2},{2,0},{4,6},{6,4},{8,10},{10,8},{12,14},{14,12},{16,18},{18,... | collective-permute-start | bytes 393224 | tf_op jit(solution)/shard_map/ppermute | solution.py:638
  7.9 1.3 %collective-permute-start.2 = (bf16[256,256]{1,0:T(8,128)(2,1)}, bf16[256,256]{1,0:T(8,128)(2,1)S(1)}, u32[]{:S(2)}, u32[]{:S(2)}) collective-permute-start(bf16[256,256]{1,0:T(8,128)(2,1)} %get-tuple-element.25), channel_id=1, source_target_pairs={{0,24},{2,26},{4,28},{6,30},{8,16},{10,18},{12,20},{14,22},{16,8},... | collective-permute-start | bytes 393224 | tf_op jit(solution)/shard_map/ppermute | solution.py:638
  9.2 1.5 %collective-permute-start.3 = (bf16[256,256]{1,0:T(8,128)(2,1)}, bf16[256,256]{1,0:T(8,128)(2,1)S(1)}, u32[]{:S(2)}, u32[]{:S(2)}) collective-permute-start(bf16[256,256]{1,0:T(8,128)(2,1)} %get-tuple-element.26), channel_id=1, source_target_pairs={{0,4},{2,6},{4,0},{6,2},{8,12},{10,14},{12,8},{14,10},{16,20},{18,... | collective-permute-start | bytes 393224 | tf_op jit(solution)/shard_map/ppermute | solution.py:638
  10.8 1.7 %collective-permute-start.4 = (bf16[256,256]{1,0:T(8,128)(2,1)}, bf16[256,256]{1,0:T(8,128)(2,1)S(1)}, u32[]{:S(2)}, u32[]{:S(2)}) collective-permute-start(bf16[256,256]{1,0:T(8,128)(2,1)} %get-tuple-element.27), channel_id=1, source_target_pairs={{0,18},{2,16},{4,22},{6,20},{8,26},{10,24},{12,30},{14,28},{16,2},... | collective-permute-start | bytes 393224 | tf_op jit(solution)/shard_map/ppermute | solution.py:638
  12.4 1.2 %copy-done = bf16[256,2048]{1,0:T(8,128)(2,1)S(1)} copy-done((bf16[256,2048]{1,0:T(8,128)(2,1)S(1)}, bf16[256,2048]{1,0:T(8,128)(2,1)}, u32[]{:S(2)}) %copy-start) | copy-done | bytes 1048600
  13.7 1.2 %copy-done.1 = bf16[256,2048]{1,0:T(8,128)(2,1)S(1)} copy-done((bf16[256,2048]{1,0:T(8,128)(2,1)S(1)}, bf16[256,2048]{1,0:T(8,128)(2,1)}, u32[]{:S(2)}) %copy-start.1) | copy-done | bytes 1048600
  14.9 1.7 %arrange_others.1 = (bf16[256,256]{1,0:T(8,128)(2,1)S(1)}, bf16[256,256]{1,0:T(8,128)(2,1)S(1)}, bf16[256,256]{1,0:T(8,128)(2,1)S(1)}, bf16[256,256]{1,0:T(8,128...) custom-call(s32[1]{0:T(128)} %bitcast.1.me_ref, ...), custom_call_target="tpu_custom_call" | custom-call | flops 536870912 | bytes 4194304 | tf_op jit(solution)/shard_map/arrange_others/pallas_call | solution.py:263
  16.6 2.7 %collective-permute-done.rest_0_ = bf16[256,256]{1,0:T(8,128)(2,1)S(1)} collective-permute-done((bf16[256,256]{1,0:T(8,128)(2,1)}, bf16[256,256]{1,0:T(8,128)(2,1)S(1)}, u32[]{:S(2)}, u32[]{:S(2)}) %collective-permute-start) | collective-permute-done | bytes 131104 | tf_op jit(solution)/shard_map/ppermute | solution.py:638
  19.4 2.8 %collective-permute-start.5 = (bf16[256,256]{1,0:T(8,128)(2,1)S(1)}, bf16[256,256]{1,0:T(8,128)(2,1)S(1)}, u32[]{:S(2)}, u32[]{:S(2)}) collective-permute-start(bf16[256,256]{1,0:T(8,128)(2,1)S(1)} %get-tuple-element.28), channel_id=1, source_target_pairs={{0,6},{2,4},{4,2},{6,0},{8,14},{10,12},{12,10},{14,8},{16,22},{18,... | collective-permute-start | bytes 393224 | tf_op jit(solution)/shard_map/ppermute | solution.py:638
  22.2 2.4 %collective-permute-start.6 = (bf16[256,256]{1,0:T(8,128)(2,1)S(1)}, bf16[256,256]{1,0:T(8,128)(2,1)S(1)}, u32[]{:S(2)}, u32[]{:S(2)}) collective-permute-start(bf16[256,256]{1,0:T(8,128)(2,1)S(1)} %get-tuple-element.29), channel_id=1, source_target_pairs={{0,26},{2,24},{4,30},{6,28},{8,18},{10,16},{12,22},{14,20},{16,10}... | collective-permute-start | bytes 393224 | tf_op jit(solution)/shard_map/ppermute | solution.py:638
  24.6 1.5 %collective-permute-start.8 = (bf16[256,256]{1,0:T(8,128)(2,1)S(1)}, bf16[256,256]{1,0:T(8,128)(2,1)S(1)}, u32[]{:S(2)}, u32[]{:S(2)}) collective-permute-start(bf16[256,256]{1,0:T(8,128)(2,1)S(1)} %get-tuple-element.31), channel_id=1, source_target_pairs={{0,20},{2,22},{4,16},{6,18},{8,28},{10,30},{12,24},{14,26},{16,4},... | collective-permute-start | bytes 393224 | tf_op jit(solution)/shard_map/ppermute | solution.py:638
  28.7 7.1 %collective-permute-start.10 = (bf16[256,256]{1,0:T(8,128)(2,1)S(1)}, bf16[256,256]{1,0:T(8,128)(2,1)S(1)}, u32[]{:S(2)}, u32[]{:S(2)}) collective-permute-start(bf16[256,256]{1,0:T(8,128)(2,1)S(1)} %get-tuple-element.33), channel_id=1, source_target_pairs={{0,28},{2,30},{4,24},{6,26},{8,20},{10,22},{12,16},{14,18},{16,12}... | collective-permute-start | bytes 393224 | tf_op jit(solution)/shard_map/ppermute | solution.py:638
  36.4 3.9 %collective-permute-done.8.rest_8_ = bf16[256,256]{1,0:T(8,128)(2,1)S(1)} collective-permute-done((bf16[256,256]{1,0:T(8,128)(2,1)S(1)}, bf16[256,256]{1,0:T(8,128)(2,1)S(1)}, u32[]{:S(2)}, u32[]{:S(2)}) %collective-permute-start.8) | collective-permute-done | bytes 131104 | tf_op jit(solution)/shard_map/ppermute | solution.py:638
  40.3 2.4 %collective-permute-start.14 = (bf16[256,256]{1,0:T(8,128)(2,1)S(1)}, bf16[256,256]{1,0:T(8,128)(2,1)S(1)}, u32[]{:S(2)}, u32[]{:S(2)}) collective-permute-start(bf16[256,256]{1,0:T(8,128)(2,1)S(1)} %get-tuple-element.37), channel_id=1, source_target_pairs={{0,30},{2,28},{4,26},{6,24},{8,22},{10,20},{12,18},{14,16},{16,14}... | collective-permute-start | bytes 393224 | tf_op jit(solution)/shard_map/ppermute | solution.py:638
  42.7 1.4 %collective-permute-done.11.rest_11_ = bf16[256,256]{1,0:T(8,128)(2,1)S(1)} collective-permute-done((bf16[256,256]{1,0:T(8,128)(2,1)S(1)}, bf16[256,256]{1,0:T(8,128)(2,1)S(1)}, u32[]{:S(2)}, u32[]{:S(2)}) %collective-permute-start.11) | collective-permute-done | bytes 131104 | tf_op jit(solution)/shard_map/ppermute | solution.py:638
  44.1 6.3 %collective-permute-done.12.rest_12_ = bf16[256,256]{1,0:T(8,128)(2,1)S(1)} collective-permute-done((bf16[256,256]{1,0:T(8,128)(2,1)S(1)}, bf16[256,256]{1,0:T(8,128)(2,1)S(1)}, u32[]{:S(2)}, u32[]{:S(2)}) %collective-permute-start.12) | collective-permute-done | bytes 131104 | tf_op jit(solution)/shard_map/ppermute | solution.py:638
  50.4 2.4 %collective-permute-done.14.rest_14_ = bf16[256,256]{1,0:T(8,128)(2,1)S(1)} collective-permute-done((bf16[256,256]{1,0:T(8,128)(2,1)S(1)}, bf16[256,256]{1,0:T(8,128)(2,1)S(1)}, u32[]{:S(2)}, u32[]{:S(2)}) %collective-permute-start.14) | collective-permute-done | bytes 131104 | tf_op jit(solution)/shard_map/ppermute | solution.py:638
  52.8 10.1 %long_convolution.1 = bf16[16,256,128]{2,1,0:T(8,128)(2,1)} custom-call(s32[1]{0:T(128)} %bitcast.1.me_ref, bf16[256,256]{1,0:T(8,128)(2,1)S(1)} %collective-permute-done.rest_0_, bf16[256,256]{1,0:T(8,128)(2,1)S(1)} %collective-permute-done.1.rest_1_, bf16[256,256]{1,0:T(8,128)(2,1)S(1)} %collective-permute-done.2.rest_2_, ...), custom_call_target="tpu_custom_call" | custom-call | flops 5000000000 | bytes 9000000 | tf_op jit(solution)/shard_map/long_convolution/pallas_call | solution.py:481
  62.9 6.0 %all-to-all-start = ((bf16[16,256,128]{2,1,0:T(8,128)(2,1)}), bf16[16,256,128]{2,1,0:T(8,128)(2,1)S(1)}, u32[]{:S(2)}, u32[]{:S(2)}) async-start(bf16[16,256,128]{2,1,0:T(8,128)(2,1)} %long_convolution.1), calls=%async_computation | async-start | bytes 2097152 | tf_op jit(solution)/shard_map/all_to_all | solution.py:632
  68.9 24.6 %all-to-all-done.conv_ref = bf16[16,256,128]{2,1,0:T(8,128)(2,1)S(1)} async-done(((bf16[16,256,128]{2,1,0:T(8,128)(2,1)}), bf16[16,256,128]{2,1,0:T(8,128)(2,1)S(1)}, u32[]{:S(2)}, u32[]{:S(2)}) %all-to-all-start) | async-done | bytes 1048608 | tf_op jit(solution)/shard_map/all_to_all | solution.py:632
  93.5 3.3 %gate_project_sent.1 = (bf16[256,2048]{1,0:T(8,128)(2,1)S(1)}, f32[256,1024]{1,0:T(8,128)S(1)}) custom-call(s32[1]{0:T(128)} %bitcast.half_ref, bf16[16,256,128]{2,1,0:T(8,128)(2,1)S(1)} %all-to-all-done.conv_ref, bf16[256,2048]{1,0:T(8,128)(2,1)S(1)} %copy-done.2, bf16[256,2048]{1,0:T(8,128)(2,1)} %values_hbm.5, f32[1,2048]{1,0:T(1,128)S(1)} %bitcast.3, ...), custom_call_target="tpu_custom_call" | custom-call | flops 1073741824 | bytes 4194304 | tf_op jit(solution)/shard_map/gate_project_sent/pallas_call | solution.py:562
  96.9 2.7 %project_kept.1.kept_ref = f32[256,1024]{1,0:T(8,128)S(1)} custom-call(s32[1]{0:T(128)} %bitcast.half_ref, bf16[256,2048]{1,0:T(8,128)(2,1)S(1)} %get-tuple-element.39.gated_ref, bf16[2048,2048]{1,0:T(8,128)(2,1)} %weight_hbm.3), custom_call_target="tpu_custom_call" | custom-call | flops 1073741824 | bytes 4194304 | tf_op jit(solution)/shard_map/project_kept/pallas_call | solution.py:592
  (24 shorter events, 4.2 us)
Async XLA Ops:
  2.3 17.1 %collective-permute-start = (bf16[256,256]{1,0:T(8,128)(2,1)}, bf16[256,256]{1,0:T(8,128)(2,1)S(1)}, u32[]{:S(2)}, u32[]{:S(2)}) collective-permute-start(bf16[256,256]{1,0:T(8,128)(2,1)} %get-tuple-element.23), channel_id=1, source_target_pairs={{0,16},{2,18},{4,20},{6,22},{8,24},{10,26},{12,28},{14,30},{16,0},... | collective-permute-start | bytes 393224 | tf_op jit(solution)/shard_map/ppermute | solution.py:638
  6.4 15.8 %collective-permute-start.1 = (bf16[256,256]{1,0:T(8,128)(2,1)}, bf16[256,256]{1,0:T(8,128)(2,1)S(1)}, u32[]{:S(2)}, u32[]{:S(2)}) collective-permute-start(bf16[256,256]{1,0:T(8,128)(2,1)} %get-tuple-element.24), channel_id=1, source_target_pairs={{0,2},{2,0},{4,6},{6,4},{8,10},{10,8},{12,14},{14,12},{16,18},{18,... | collective-permute-start | bytes 393224 | tf_op jit(solution)/shard_map/ppermute | solution.py:638
  7.9 16.7 %collective-permute-start.2 = (bf16[256,256]{1,0:T(8,128)(2,1)}, bf16[256,256]{1,0:T(8,128)(2,1)S(1)}, u32[]{:S(2)}, u32[]{:S(2)}) collective-permute-start(bf16[256,256]{1,0:T(8,128)(2,1)} %get-tuple-element.25), channel_id=1, source_target_pairs={{0,24},{2,26},{4,28},{6,30},{8,16},{10,18},{12,20},{14,22},{16,8},... | collective-permute-start | bytes 393224 | tf_op jit(solution)/shard_map/ppermute | solution.py:638
  9.2 15.4 %collective-permute-start.3 = (bf16[256,256]{1,0:T(8,128)(2,1)}, bf16[256,256]{1,0:T(8,128)(2,1)S(1)}, u32[]{:S(2)}, u32[]{:S(2)}) collective-permute-start(bf16[256,256]{1,0:T(8,128)(2,1)} %get-tuple-element.26), channel_id=1, source_target_pairs={{0,4},{2,6},{4,0},{6,2},{8,12},{10,14},{12,8},{14,10},{16,20},{18,... | collective-permute-start | bytes 393224 | tf_op jit(solution)/shard_map/ppermute | solution.py:638
  10.8 16.4 %collective-permute-start.4 = (bf16[256,256]{1,0:T(8,128)(2,1)}, bf16[256,256]{1,0:T(8,128)(2,1)S(1)}, u32[]{:S(2)}, u32[]{:S(2)}) collective-permute-start(bf16[256,256]{1,0:T(8,128)(2,1)} %get-tuple-element.27), channel_id=1, source_target_pairs={{0,18},{2,16},{4,22},{6,20},{8,26},{10,24},{12,30},{14,28},{16,2},... | collective-permute-start | bytes 393224 | tf_op jit(solution)/shard_map/ppermute | solution.py:638
  12.4 1.2 %copy-start = (bf16[256,2048]{1,0:T(8,128)(2,1)S(1)}, bf16[256,2048]{1,0:T(8,128)(2,1)}, u32[]{:S(2)}) copy-start(bf16[256,2048]{1,0:T(8,128)(2,1)} %values_hbm.5) | copy-start | bytes 3145732
  13.7 1.2 %copy-start.1 = (bf16[256,2048]{1,0:T(8,128)(2,1)S(1)}, bf16[256,2048]{1,0:T(8,128)(2,1)}, u32[]{:S(2)}) copy-start(bf16[256,2048]{1,0:T(8,128)(2,1)} %taps_hbm.3) | copy-start | bytes 3145732
  19.4 9.4 %collective-permute-start.5 = (bf16[256,256]{1,0:T(8,128)(2,1)S(1)}, bf16[256,256]{1,0:T(8,128)(2,1)S(1)}, u32[]{:S(2)}, u32[]{:S(2)}) collective-permute-start(bf16[256,256]{1,0:T(8,128)(2,1)S(1)} %get-tuple-element.28), channel_id=1, source_target_pairs={{0,6},{2,4},{4,2},{6,0},{8,14},{10,12},{12,10},{14,8},{16,22},{18,... | collective-permute-start | bytes 393224 | tf_op jit(solution)/shard_map/ppermute | solution.py:638
  22.2 13.6 %collective-permute-start.6 = (bf16[256,256]{1,0:T(8,128)(2,1)S(1)}, bf16[256,256]{1,0:T(8,128)(2,1)S(1)}, u32[]{:S(2)}, u32[]{:S(2)}) collective-permute-start(bf16[256,256]{1,0:T(8,128)(2,1)S(1)} %get-tuple-element.29), channel_id=1, source_target_pairs={{0,26},{2,24},{4,30},{6,28},{8,18},{10,16},{12,22},{14,20},{16,10}... | collective-permute-start | bytes 393224 | tf_op jit(solution)/shard_map/ppermute | solution.py:638
  24.6 11.2 %collective-permute-start.7 = (bf16[256,256]{1,0:T(8,128)(2,1)S(1)}, bf16[256,256]{1,0:T(8,128)(2,1)S(1)}, u32[]{:S(2)}, u32[]{:S(2)}) collective-permute-start(bf16[256,256]{1,0:T(8,128)(2,1)S(1)} %get-tuple-element.30), channel_id=1, source_target_pairs={{0,8},{2,10},{4,12},{6,14},{8,0},{10,2},{12,4},{14,6},{16,24},{18,... | collective-permute-start | bytes 393224 | tf_op jit(solution)/shard_map/ppermute | solution.py:638
  24.6 15.7 %collective-permute-start.8 = (bf16[256,256]{1,0:T(8,128)(2,1)S(1)}, bf16[256,256]{1,0:T(8,128)(2,1)S(1)}, u32[]{:S(2)}, u32[]{:S(2)}) collective-permute-start(bf16[256,256]{1,0:T(8,128)(2,1)S(1)} %get-tuple-element.31), channel_id=1, source_target_pairs={{0,20},{2,22},{4,16},{6,18},{8,28},{10,30},{12,24},{14,26},{16,4},... | collective-permute-start | bytes 393224 | tf_op jit(solution)/shard_map/ppermute | solution.py:638
  27.1 13.2 %collective-permute-start.9 = (bf16[256,256]{1,0:T(8,128)(2,1)S(1)}, bf16[256,256]{1,0:T(8,128)(2,1)S(1)}, u32[]{:S(2)}, u32[]{:S(2)}) collective-permute-start(bf16[256,256]{1,0:T(8,128)(2,1)S(1)} %get-tuple-element.32), channel_id=1, source_target_pairs={{0,10},{2,8},{4,14},{6,12},{8,2},{10,0},{12,6},{14,4},{16,26},{18,... | collective-permute-start | bytes 393224 | tf_op jit(solution)/shard_map/ppermute | solution.py:638
  28.7 14.0 %collective-permute-start.10 = (bf16[256,256]{1,0:T(8,128)(2,1)S(1)}, bf16[256,256]{1,0:T(8,128)(2,1)S(1)}, u32[]{:S(2)}, u32[]{:S(2)}) collective-permute-start(bf16[256,256]{1,0:T(8,128)(2,1)S(1)} %get-tuple-element.33), channel_id=1, source_target_pairs={{0,28},{2,30},{4,24},{6,26},{8,20},{10,22},{12,16},{14,18},{16,12}... | collective-permute-start | bytes 393224 | tf_op jit(solution)/shard_map/ppermute | solution.py:638
  35.8 8.3 %collective-permute-start.11 = (bf16[256,256]{1,0:T(8,128)(2,1)S(1)}, bf16[256,256]{1,0:T(8,128)(2,1)S(1)}, u32[]{:S(2)}, u32[]{:S(2)}) collective-permute-start(bf16[256,256]{1,0:T(8,128)(2,1)S(1)} %get-tuple-element.34), channel_id=1, source_target_pairs={{0,12},{2,14},{4,8},{6,10},{8,4},{10,6},{12,0},{14,2},{16,28},{18,... | collective-permute-start | bytes 393224 | tf_op jit(solution)/shard_map/ppermute | solution.py:638
  35.8 14.6 %collective-permute-start.12 = (bf16[256,256]{1,0:T(8,128)(2,1)S(1)}, bf16[256,256]{1,0:T(8,128)(2,1)S(1)}, u32[]{:S(2)}, u32[]{:S(2)}) collective-permute-start(bf16[256,256]{1,0:T(8,128)(2,1)S(1)} %get-tuple-element.35), channel_id=1, source_target_pairs={{0,22},{2,20},{4,18},{6,16},{8,30},{10,28},{12,26},{14,24},{16,6},... | collective-permute-start | bytes 393224 | tf_op jit(solution)/shard_map/ppermute | solution.py:638
  40.3 10.1 %collective-permute-start.13 = (bf16[256,256]{1,0:T(8,128)(2,1)S(1)}, bf16[256,256]{1,0:T(8,128)(2,1)S(1)}, u32[]{:S(2)}, u32[]{:S(2)}) collective-permute-start(bf16[256,256]{1,0:T(8,128)(2,1)S(1)} %get-tuple-element.36), channel_id=1, source_target_pairs={{0,14},{2,12},{4,10},{6,8},{8,6},{10,4},{12,2},{14,0},{16,30},{18,... | collective-permute-start | bytes 393224 | tf_op jit(solution)/shard_map/ppermute | solution.py:638
  40.3 12.4 %collective-permute-start.14 = (bf16[256,256]{1,0:T(8,128)(2,1)S(1)}, bf16[256,256]{1,0:T(8,128)(2,1)S(1)}, u32[]{:S(2)}, u32[]{:S(2)}) collective-permute-start(bf16[256,256]{1,0:T(8,128)(2,1)S(1)} %get-tuple-element.37), channel_id=1, source_target_pairs={{0,30},{2,28},{4,26},{6,24},{8,22},{10,20},{12,18},{14,16},{16,14}... | collective-permute-start | bytes 393224 | tf_op jit(solution)/shard_map/ppermute | solution.py:638
  52.8 40.7 %copy-start.2 = (bf16[256,2048]{1,0:T(8,128)(2,1)S(1)}, bf16[256,2048]{1,0:T(8,128)(2,1)}, u32[]{:S(2)}) copy-start(bf16[256,2048]{1,0:T(8,128)(2,1)} %gates_hbm.1) | copy-start | bytes 3145732
  52.8 40.7 %copy-start.3 = (f32[2048]{0:T(1024)S(1)}, f32[2048]{0:T(1024)}, u32[]{:S(2)}) copy-start(f32[2048]{0:T(1024)} %param.9) | copy-start | bytes 24580
  62.9 30.6 %all-to-all-start = ((bf16[16,256,128]{2,1,0:T(8,128)(2,1)}), bf16[16,256,128]{2,1,0:T(8,128)(2,1)S(1)}, u32[]{:S(2)}, u32[]{:S(2)}) async-start(bf16[16,256,128]{2,1,0:T(8,128)(2,1)} %long_convolution.1), calls=%async_computation | async-start | bytes 2097152 | tf_op jit(solution)/shard_map/all_to_all | solution.py:632
  96.8 2.8 %collective-permute-start.15 = (f32[256,1024]{1,0:T(8,128)S(1)}, f32[256,1024]{1,0:T(8,128)S(1)}, u32[]{:S(2)}, u32[]{:S(2)}) collective-permute-start(f32[256,1024]{1,0:T(8,128)S(1)} %get-tuple-element.40), channel_id=1, source_target_pairs={{0,1},{1,0},{2,3},{3,2},{4,5},{5,4},{6,7},{7,6},{8,9},{9,8},{10,11... | collective-permute-start | bytes 3145736 | tf_op jit(solution)/shard_map/ppermute | solution.py:649
